TPU v7x, 512 devices: a whole 4x4x16 slice. The times are simulated.
512 devices in a mesh: prompt: 32 (over z, core), rollout: 16 (over y, x).
Axes of the slice: x: 4, y: 4, z: 16, core: 2. Of those that a mesh axis runs over, the one named last changes fastest.
Arguments:
- row_grads: bfloat16 [32, 16, 50, 8192], P('prompt', 'rollout'), may hold values from -6 to 6
- used_ids: int32 [32, 16, 50], P('prompt', 'rollout'), may hold values from 0 to 383, as said below
- used_count: int32 [32, 16], P('prompt', 'rollout'), may hold values from 20 to 50
- pre_act: bfloat16 [12288, 5120], P('prompt', 'rollout'), may hold values from -8 to 8
- patches: bfloat16 [12288, 5120], P(('prompt', 'rollout')), may hold values from -6 to 6
- ln_gain: float32 [1280], replicated, may hold values from 0.25 to 1.75
- w_fc2: bfloat16 [5120, 8192], P('rollout', 'prompt'), may hold values from -0.078125 to 0.078125
- w_fc1: bfloat16 [5120, 5120], P('prompt', 'rollout'), may hold values from -0.078125 to 0.078125
Outputs:
- patch_grads: bfloat16 [12288, 5120], P(('prompt', 'rollout'))
Inputs may be any that keep to these rules, and one draw needn't show every extreme that they name: `used_ids`: the first used_count entries of each rollout's list are distinct; at most 5 of them lie in one block of 24 rows r * 24 to r * 24 + 23; later entries are ignored.
All inputs are finite; a program needn't handle non-finite values.
Results may differ from a plain program's by a relative error of at most 0.0056.
Values may be sent and summed in bfloat16 or wider, within the bound.
No kernel may reach another device: no remote copies, remote signals or barrier semaphores. Data moves between devices by JAX's collectives and lax.ppermute only.
A program may use at most 64 MiB of HBM per device.

v0:
```python
import jax
import jax.numpy as jnp
from jax import lax
from jax.sharding import PartitionSpec as P

VIT = 1280
MERGE = 4
CAP = 5


def gelu_slope(value):
    return (
        0.5 * (1.0 + jax.scipy.special.erf(value * 0.7071067811865476))
        + value * jnp.exp(-0.5 * value * value) * 0.3989422804014327
    )


def contract_last(left, right):
    return lax.dot_general(
        left, right, (((1,), (1,)), ((), ())), preferred_element_type=jnp.float32
    )


def per_device(row_grads, used_ids, used_count, pre_act, patches, ln_gain, w_fc2, w_fc1):
    rollouts = lax.axis_size("rollout")
    slot_grads = row_grads[0, 0]
    slot_ids = used_ids[0, 0]
    slot_count = used_count[0, 0]
    slot_total = slot_ids.shape[0]
    own_rows = patches.shape[0]
    usable = jnp.arange(slot_total, dtype=jnp.int32) < slot_count
    owners = slot_ids // own_rows
    within = slot_ids % own_rows
    owner_hit = (owners[:, None] == jnp.arange(rollouts, dtype=jnp.int32)[None, :]) & usable[
        :, None
    ]
    hit_count = owner_hit.astype(jnp.int32)
    before = jnp.cumsum(hit_count, axis=0) - hit_count
    placing = jnp.sum(jnp.where(owner_hit, before, 0), axis=1)
    target = owners * CAP + placing
    buckets = rollouts * CAP
    select = (target[None, :] == jnp.arange(buckets, dtype=jnp.int32)[:, None]) & usable[None, :]
    filled = jnp.any(select, axis=1)
    send_rows = jnp.where(filled, jnp.sum(jnp.where(select, within[None, :], 0), axis=1), -1)
    outgoing = jnp.dot(
        select.astype(jnp.bfloat16), slot_grads, preferred_element_type=jnp.float32
    ).astype(jnp.bfloat16)
    outgoing = outgoing.reshape(rollouts, CAP, -1)
    send_rows = send_rows.reshape(rollouts, CAP)
    received, row_targets = (
        lax.all_to_all(outgoing, "rollout", split_axis=0, concat_axis=0, tiled=True),
        lax.all_to_all(send_rows, "rollout", split_axis=0, concat_axis=0, tiled=True),
    )
    matches = (
        row_targets.reshape(-1)[None, :] == jnp.arange(own_rows, dtype=jnp.int32)[:, None]
    ).astype(jnp.bfloat16)
    summed = jnp.dot(
        matches, received.reshape(buckets, -1), preferred_element_type=jnp.float32
    ).astype(jnp.bfloat16)
    all_rows = lax.all_gather(summed, "rollout", axis=0, tiled=True)
    hidden_grad = contract_last(all_rows, lax.all_gather(w_fc2, "prompt", axis=1, tiled=True))
    w1_all = lax.all_gather(w_fc1, "prompt", axis=0, tiled=True)
    act_grad = (hidden_grad * gelu_slope(pre_act.astype(jnp.float32))).astype(jnp.bfloat16)
    w1_outputs = lax.all_to_all(w1_all, "rollout", split_axis=0, concat_axis=1, tiled=True)
    upstream_cols = contract_last(
        lax.all_gather(act_grad, "rollout", axis=1, tiled=True), w1_outputs
    )
    upstream = lax.all_to_all(upstream_cols, "rollout", split_axis=0, concat_axis=1, tiled=True)
    inputs = patches.astype(jnp.float32).reshape(own_rows, MERGE, VIT)
    scaled = upstream.reshape(own_rows, MERGE, VIT) * ln_gain
    inverse = lax.rsqrt(jnp.mean(inputs * inputs, axis=-1, keepdims=True) + 1e-06)
    inner = jnp.mean(scaled * inputs, axis=-1, keepdims=True)
    result = inverse * scaled - inputs * inverse * inverse * inverse * inner
    return result.reshape(own_rows, -1).astype(jnp.bfloat16)


def solution(mesh):
    return jax.shard_map(
        per_device,
        mesh=mesh,
        in_specs=(
            P("prompt", "rollout", None, None),
            P("prompt", "rollout", None),
            P("prompt", "rollout"),
            P("prompt", "rollout"),
            P(("prompt", "rollout"), None),
            P(),
            P("rollout", "prompt"),
            P("prompt", "rollout"),
        ),
        out_specs=P(("prompt", "rollout"), None),
        check_vma=False,
    )
```

profile of v0, /device:TPU:6, one launch (start us, length us, event | category | flops | bytes accessed | tf_op | source)
XLA Modules:
  0.0 372.6 jit_solution(1236579134384252895)
XLA Ops:
  6.5 0.7 all-gather.7.cloned.1.call-update
  7.9 0.7 and_select_fusion
  8.8 0.2 select_reduce_fusion.1
  9.2 0.7 select_n.52
  9.9 9.1 %all-to-all-start = ((s32[16,1,5]{2,1,0:T(1,128)}), s32[16,1,5]{2,1,0:T(1,128)S(1)}, u32[]{:S(2)}, u32[]{:S(2)}) async-start(s32[16,1,5]{2,1,0:T(1,128)} %bitcast.4), calls=%async_computation | async-start | bytes 16384 | tf_op jit(solution)/shard_map/all_to_all | solution.py:52
  19.0 0.6 convolution_convert_fusion
  19.6 1.6 reshape.132
  21.3 3.3 all-to-all-done
  24.5 5.6 %all-to-all-start.1 = ((bf16[16,5,8192]{2,1,0:T(8,128)(2,1)}), bf16[16,5,8192]{2,1,0:T(8,128)(2,1)S(1)}, u32[]{:S(2)}, u32[]{:S(2)}) async-start(bf16[16,5,8192]{2,1,0:T(8,128)(2,1)} %reshape.132), calls=%async_computation.1 | async-start | bytes 4194304 | tf_op jit(solution)/shard_map/all_to_all | solution.py:51
  30.2 0.5 broadcast.118
  30.7 0.7 reduce.3
  31.5 21.6 %all-to-all-done.1 = bf16[16,5,8192]{2,1,0:T(8,128)(2,1)S(1)} async-done(((bf16[16,5,8192]{2,1,0:T(8,128)(2,1)}), bf16[16,5,8192]{2,1,0:T(8,128)(2,1)S(1)}, u32[]{:S(2)}, u32[]{:S(2)}) %all-to-all-start.1) | async-done | bytes 1310752 | tf_op jit(solution)/shard_map/all_to_all | solution.py:51
  53.1 1.5 reshape.133
  54.5 2.4 convolution_convert_fusion.1
  57.0 0.7 all-gather.11.cloned.1.call-update
  57.8 40.2 %all-gather.7.cloned.1.call-done = bf16[320,8192]{1,0:T(8,128)(2,1)} async-done(((bf16[320,256]{1,0:T(8,128)(2,1)}), bf16[320,8192]{1,0:T(8,128)(2,1)}) %all-gather.7.cloned.1.call-update) | async-done | bytes 5242896 | tf_op jit(solution)/shard_map/all_gather | solution.py:61
  98.0 75.5 %all-gather.5.cloned.1.call-done = bf16[384,8192]{1,0:T(8,128)(2,1)} async-done(((bf16[24,8192]{1,0:T(8,128)(2,1)}), bf16[384,8192]{1,0:T(8,128)(2,1)}) %all-gather.5.cloned.1.call-update) | async-done | bytes 6291472 | tf_op jit(solution)/shard_map/all_gather | solution.py:60
  173.5 7.9 %fusion = bf16[384,320]{0,1:T(8,128)(2,1)} fusion(bf16[384,8192]{1,0:T(8,128)(2,1)} %all-gather.5.cloned.1.call-done, bf16[320,8192]{1,0:T(8,128)(2,1)} %all-gather.7.cloned.1.call-done, bf16[384,320]{0,1:T(8,128)(2,1)S(1)} %copy-done.3), kind=kOutput, calls=%fused_computation.3 | convolution fusion | flops 2014617600 | bytes 12025856 | tf_op jit(solution)/shard_map/dot_general | solution.py:19
  181.5 67.8 %all-gather.11.cloned.1.call-done = bf16[5120,320]{1,0:T(8,128)(2,1)} async-done(((bf16[160,320]{1,0:T(8,128)(2,1)}), bf16[5120,320]{1,0:T(8,128)(2,1)}) %all-gather.11.cloned.1.call-update) | async-done | bytes 3276816 | tf_op jit(solution)/shard_map/all_gather | solution.py:62
  249.2 57.1 %all_to_all.43 = bf16[16,320,320]{2,1,0:T(8,128)(2,1)S(1)} all-to-all(bf16[16,320,320]{2,1,0:T(8,128)(2,1)} %bitcast.29), channel_id=1, replica_groups=mesh['prompt'=32,'rollout'=16] {'rollout'}, dimensions={0} | all-to-all | bytes 6553600 | tf_op jit(solution)/shard_map/all_to_all | solution.py:64
  306.3 4.2 %copy.22 = bf16[320,16,320]{2,1,0:T(8,128)(2,1)} copy(bf16[320,16,320]{2,0,1:T(8,128)(2,1)S(1)} %bitcast.28) | data formatting | bytes 6553600 | tf_op jit(solution)/shard_map/all_to_all | solution.py:64
  310.6 7.4 %reshape.136 = bf16[320,5120,1]{1,0,2:T(8,128)(2,1)} reshape(bf16[320,16,320]{2,1,0:T(8,128)(2,1)} %copy.22) | data formatting | bytes 6553600 | tf_op jit(solution)/shard_map/all_to_all | solution.py:64
  318.0 17.9 %all-gather.9.cloned.1.call-done = bf16[384,5120]{0,1:T(8,128)(2,1)} async-done(((bf16[384,320]{0,1:T(8,128)(2,1)}), bf16[384,5120]{0,1:T(8,128)(2,1)}) %all-gather.9.cloned.1.call-update) | async-done | bytes 3932176 | tf_op jit(solution)/shard_map/all_gather | solution.py:66
  335.9 6.3 %copy.21 = bf16[384,5120]{1,0:T(8,128)(2,1)} copy(bf16[384,5120]{0,1:T(8,128)(2,1)} %all-gather.9.cloned.1.call-done) | data formatting | bytes 7864320 | tf_op jit(solution)/shard_map/all_gather | solution.py:66
  342.2 6.2 %fusion.20 = f32[16,24,320]{2,1,0:T(8,128)} fusion(bf16[16,24,5120]{2,1,0:T(8,128)(2,1)} %bitcast.30, bf16[320,5120,1]{1,0,2:T(8,128)(2,1)} %reshape.136), kind=kOutput, calls=%fused_computation.41 | convolution fusion | flops 1258291200 | bytes 7700480 | tf_op jit(solution)/shard_map/dot_general | solution.py:19
  348.4 5.7 %all-to-all-start.3 = ((f32[16,24,320]{2,1,0:T(8,128)}), f32[16,24,320]{2,1,0:T(8,128)S(1)}, u32[]{:S(2)}, u32[]{:S(2)}) async-start(f32[16,24,320]{2,1,0:T(8,128)} %fusion.20), calls=%async_computation.3 | async-start | bytes 1179648 | tf_op jit(solution)/shard_map/all_to_all | solution.py:68
  354.1 0.2 reshape.131
  354.4 9.3 %all-to-all-done.3 = f32[16,24,320]{2,1,0:T(8,128)S(1)} async-done(((f32[16,24,320]{2,1,0:T(8,128)}), f32[16,24,320]{2,1,0:T(8,128)S(1)}, u32[]{:S(2)}, u32[]{:S(2)}) %all-to-all-start.3) | async-done | bytes 491552 | tf_op jit(solution)/shard_map/all_to_all | solution.py:68
  363.8 0.4 reshape.135
  364.2 0.2 reshape.134
  364.4 0.3 multiply_reduce_fusion.1
  365.2 0.8 fusion.4
  (30 shorter events, 1.2 us)
Async XLA Ops:
  6.5 12.5 %copy-start = (bf16[1,1,50,8192]{3,2,1,0:T(8,128)(2,1)S(1)}, bf16[1,1,50,8192]{3,2,1,0:T(8,128)(2,1)}, u32[]{:S(2)}) copy-start(bf16[1,1,50,8192]{3,2,1,0:T(8,128)(2,1)} %param.8) | copy-start | bytes 2457604
  6.5 91.4 %all-gather.7.cloned.1.call-start = ((), (), s32[]{:S(2)}) async-start(), calls=%async_computation.5 | async-start | bytes 5406720 | tf_op jit(solution)/shard_map/all_gather | solution.py:61
  9.9 14.7 %all-to-all-start = ((s32[16,1,5]{2,1,0:T(1,128)}), s32[16,1,5]{2,1,0:T(1,128)S(1)}, u32[]{:S(2)}, u32[]{:S(2)}) async-start(s32[16,1,5]{2,1,0:T(1,128)} %bitcast.4), calls=%async_computation | async-start | bytes 16384 | tf_op jit(solution)/shard_map/all_to_all | solution.py:52
  21.3 152.2 %copy-start.3 = (bf16[384,320]{0,1:T(8,128)(2,1)S(1)}, bf16[384,320]{0,1:T(8,128)(2,1)}, u32[]{:S(2)}) copy-start(bf16[384,320]{0,1:T(8,128)(2,1)} %param.11) | copy-start | bytes 737284
  24.5 28.5 %all-to-all-start.1 = ((bf16[16,5,8192]{2,1,0:T(8,128)(2,1)}), bf16[16,5,8192]{2,1,0:T(8,128)(2,1)S(1)}, u32[]{:S(2)}, u32[]{:S(2)}) async-start(bf16[16,5,8192]{2,1,0:T(8,128)(2,1)} %reshape.132), calls=%async_computation.1 | async-start | bytes 4194304 | tf_op jit(solution)/shard_map/all_to_all | solution.py:51
  30.1 143.4 %all-gather.5.cloned.1.call-start = ((), (), s32[]{:S(2)}) async-start(), calls=%async_computation.4 | async-start | bytes 6684672 | tf_op jit(solution)/shard_map/all_gather | solution.py:60
  57.0 192.3 %all-gather.11.cloned.1.call-start = ((), (), s32[]{:S(2)}) async-start(), calls=%async_computation.7 | async-start | bytes 4055040 | tf_op jit(solution)/shard_map/all_gather | solution.py:62
  57.7 278.2 %all-gather.9.cloned.1.call-start = ((), (), s32[]{:S(2)}) async-start(), calls=%async_computation.6 | async-start | bytes 4177920 | tf_op jit(solution)/shard_map/all_gather | solution.py:66
  342.2 11.9 %copy-start.1 = (bf16[24,5120]{1,0:T(8,128)(2,1)S(1)}, bf16[24,5120]{1,0:T(8,128)(2,1)}, u32[]{:S(2)}) copy-start(bf16[24,5120]{1,0:T(8,128)(2,1)} %param.12) | copy-start | bytes 737284
  342.2 12.2 %copy-start.2 = (f32[1280]{0:T(1024)S(1)}, f32[1280]{0:T(1024)}, u32[]{:S(2)}) copy-start(f32[1280]{0:T(1024)} %param.13) | copy-start | bytes 15364
  348.4 15.3 %all-to-all-start.3 = ((f32[16,24,320]{2,1,0:T(8,128)}), f32[16,24,320]{2,1,0:T(8,128)S(1)}, u32[]{:S(2)}, u32[]{:S(2)}) async-start(f32[16,24,320]{2,1,0:T(8,128)} %fusion.20), calls=%async_computation.3 | async-start | bytes 1179648 | tf_op jit(solution)/shard_map/all_to_all | solution.py:68
Sparse Core Ops, SparseCore 0:
  9.4 88.5 all-gather.6
  101.0 72.4 all-gather.4
  175.6 73.5 all-gather.10
  252.1 83.7 all-gather.8
where the time goes:
time: 375 us; the launch traced here: 373 us
  waiting for transfers between devices  237 us (63%)
  blocking collectives  57.1 us (15%)
  local copies, waits for them, and re-layouts  23.7 us (6%)
  starting transfers between devices  20.5 us (5%)
  matrix products  17.2 us (5%)
  between operations  13.9 us (4%)
    all_gather x1, waiting for transfers between devices, per_device(): all_rows = lax.all_gather(summed, 'rollout', axis=0, tiled=True)  75.5 us
    all_gather x1, waiting for transfers between devices, per_device(): w1_all = lax.all_gather(w_fc1, 'prompt', axis=0, tiled=True)  67.8 us
    all_to_all x1, blocking collectives, per_device(): lax.all_to_all(w1_all, 'rollout', split_axis=0, concat_axis=1, tiled=True)  57.1 us
    all_gather x1, waiting for transfers between devices, per_device(): lax.all_gather(w_fc2, 'prompt', axis=1, tiled=True)  40.2 us
    all_to_all x1, waiting for transfers between devices, per_device(): lax.all_to_all(outgoing, 'rollout', split_axis=0, concat_axis=0, tiled=True)  21.6 us
    all_gather x1, waiting for transfers between devices, per_device(): lax.all_gather(act_grad, 'rollout', axis=1, tiled=True)  17.9 us
    dot_general x2, matrix products, contract_last(): lax.dot_general(left, right, (((1,), (1,)), ((), ())), preferred_element_...  14.1 us
    all_to_all x2, local copies, waits for them, and re-layouts, per_device(): lax.all_to_all(w1_all, 'rollout', split_axis=0, concat_axis=1, tiled=True)  11.6 us
  transfers between devices with their start and end apart: 7, of which 7 were waited for; matrix products, arithmetic and copies ran while one was open for 8% of the time, Pallas kernels for 0%

commit v1 on v0

v1 whole, which is shorter than its diff:
```python
import jax
import jax.numpy as jnp
from jax import lax
from jax.experimental import pallas as pl
from jax.experimental.pallas import tpu as pltpu
from jax.sharding import PartitionSpec as P

VIT = 1280
MERGE = 4
PROMPTS = 32
ROLLOUTS = 16
SIDE = 4
SLOTS = 50
PAD_SLOTS = 64
OWN = 24
ROWS = OWN * ROLLOUTS
D_LLM = 8192
COLS = D_LLM // ROLLOUTS
HID = 5120
HID_OWN = HID // ROLLOUTS
IN_OWN = HID // PROMPTS
W2_COLS = D_LLM // PROMPTS
TAIL = IN_OWN // 2
W_ROWS = HID_OWN + IN_OWN + TAIL
AXES = ("prompt", "rollout")
F32 = jnp.float32
BF16 = jnp.bfloat16


def gelu_slope(value):
    return (
        0.5 * (1.0 + jax.scipy.special.erf(value * 0.7071067811865476))
        + value * jnp.exp(-0.5 * value * value) * 0.3989422804014327
    )


def dot_t(left, right):
    return lax.dot_general(left, right, (((1,), (1,)), ((), ())), preferred_element_type=F32)


def line_groups(phase):
    groups = []
    for prompt in range(PROMPTS):
        for other in range(SIDE):
            along_x = (prompt % 2 == 0) == (phase == 0)
            line = [(other * SIDE + i) if along_x else (i * SIDE + other) for i in range(SIDE)]
            groups.append([prompt * ROLLOUTS + r for r in line])
    return groups


def exchange(blocks, phase):
    return lax.all_to_all(
        blocks, AXES, split_axis=0, concat_axis=0, axis_index_groups=line_groups(phase), tiled=True
    )


def pack_kernel(grads_ref, meta_ref, out_ref):
    for k in range(ROLLOUTS):
        cols = pl.ds(k * COLS, COLS)
        out_ref[k, 0:48, :] = grads_ref[0:48, cols]
        out_ref[k, 48:64, :] = (grads_ref[48:64, cols].astype(F32) + meta_ref[...]).astype(BF16)


def sum_kernel(recv_ref, out_ref):
    rows = (lax.broadcasted_iota(jnp.int32, (ROWS, 4 * PAD_SLOTS), 0) + 1).astype(F32)
    total = jnp.zeros((ROWS, COLS), F32)
    for g in range(ROLLOUTS // 4):
        codes = jnp.zeros((8, 4 * PAD_SLOTS), F32)
        for k in range(4):
            tile = recv_ref[4 * g + k, 48:64, 0 : 4 * PAD_SLOTS].astype(F32)[0:8]
            codes = codes + (pltpu.roll(tile, PAD_SLOTS * k, 1) if k else tile)
        row = codes[2:3] * 16.0 + codes[3:4]
        onehot = jnp.where(rows == row, 1.0, 0.0).astype(BF16)
        block = recv_ref[4 * g : 4 * g + 4].reshape(4 * PAD_SLOTS, COLS)
        total = total + jnp.dot(onehot, block, preferred_element_type=F32)
    value = total.astype(BF16)
    for k in range(SIDE):
        out_ref[k] = value


def mlp_kernel(core_ref, w_ref, s_ref, slope_ref, out_ref, w2, w1a, w1b, sems):
    copies = []
    parts = 4
    step = PROMPTS // parts
    for i in range(parts):
        span = pl.ds(i * step, step)
        copies.append(pltpu.make_async_copy(w_ref.at[span, 0:HID_OWN], w2.at[span], sems.at[i]))
    copies.append(pltpu.make_async_copy(w_ref.at[:, HID_OWN : HID_OWN + IN_OWN], w1a, sems.at[parts]))
    copies.append(pltpu.make_async_copy(w_ref.at[:, HID_OWN + IN_OWN : W_ROWS], w1b, sems.at[parts + 1]))
    for copy in copies:
        copy.start()
    for copy in copies[:parts]:
        copy.wait()
    even = core_ref[0] == 0

    def add(slot, hidden):
        j, k = slot // SIDE, slot % SIDE
        block = jnp.where(even, j * SIDE + k, k * SIDE + j)
        s = s_ref[slot]
        hidden = hidden + dot_t(s[:, :W2_COLS], w2[2 * block])
        return hidden + dot_t(s[:, W2_COLS:], w2[2 * block + 1])

    hidden = lax.fori_loop(0, ROLLOUTS, add, jnp.zeros((ROWS, HID_OWN), F32))
    act = (hidden * slope_ref[...]).astype(BF16)
    for copy in copies[parts:]:
        copy.wait()
    four = 4
    for g in range(PROMPTS // four):
        a = w1a[four * g : four * (g + 1)].reshape(four * IN_OWN, 256)
        b = w1b[four * g : four * (g + 1)]
        b = jnp.concatenate([b[:, :, :128], b[:, :, 128:]], axis=1).reshape(four * IN_OWN, 128)
        part = dot_t(act[:, :256], a) + dot_t(act[:, 256:], b[:, :64])
        out_ref[:, four * IN_OWN * g : four * IN_OWN * (g + 1)] = part.astype(BF16)


def add_kernel(recv_ref, out_ref):
    total = recv_ref[0].astype(F32)
    for k in range(1, SIDE):
        total = total + recv_ref[k].astype(F32)
    out_ref[...] = total.astype(BF16)


def norm_kernel(recv_ref, patches_ref, gain_ref, out_ref):
    for m in range(MERGE):
        cols = slice(m * VIT, (m + 1) * VIT)
        upstream = recv_ref[0, :, cols].astype(F32)
        for k in range(1, SIDE):
            upstream = upstream + recv_ref[k, :, cols].astype(F32)
        inputs = patches_ref[:, cols].astype(F32)
        scaled = upstream * gain_ref[...]
        inverse = lax.rsqrt(jnp.mean(inputs * inputs, axis=-1, keepdims=True) + 1e-06)
        inner = jnp.mean(scaled * inputs, axis=-1, keepdims=True)
        result = inverse * scaled - inputs * inverse * inverse * inverse * inner
        out_ref[:, cols] = result.astype(BF16)


def call(kernel, out_shape, n_in, flops=0, bytes_accessed=0, **kw):
    vmem = pl.BlockSpec(memory_space=pltpu.VMEM)
    return pl.pallas_call(
        kernel,
        out_shape=jax.ShapeDtypeStruct(out_shape, BF16),
        in_specs=kw.pop("in_specs", [vmem] * n_in),
        out_specs=vmem,
        cost_estimate=pl.CostEstimate(flops=flops, bytes_accessed=bytes_accessed, transcendentals=0),
        compiler_params=pltpu.CompilerParams(vmem_limit_bytes=kw.pop("vmem", 16 << 20)),
        **kw,
    )


def per_device(row_grads, used_ids, used_count, pre_act, patches, ln_gain, w_fc2, w_fc1):
    core = lax.axis_index("prompt") % 2
    tail = jnp.pad(w_fc1[:, 256:], ((0, 0), (0, 64)))
    weights = jnp.concatenate(
        [w_fc2, w_fc1[:, :256], jnp.concatenate([tail[:TAIL], tail[TAIL:]], axis=1)], axis=0
    )
    weights = lax.all_gather(weights, "prompt", axis=0, tiled=False)

    ids = used_ids[0]
    owner = ids // OWN
    turned = (owner % SIDE) * SIDE + owner // SIDE
    place = jnp.where(core == 0, turned, owner) * OWN + ids % OWN + 1
    place = jnp.where(jnp.arange(SLOTS, dtype=jnp.int32)[None] < used_count, place, 0)
    place = jnp.pad(place, ((0, 0), (0, COLS - SLOTS)))
    codes = jnp.concatenate([place // 16, place % 16], axis=0).astype(F32)
    meta = jnp.pad(codes, ((2, 12), (0, 0)))
    grads = jnp.pad(row_grads[0, 0], ((0, PAD_SLOTS - SLOTS), (0, 0)))
    outgoing = call(pack_kernel, (ROLLOUTS, PAD_SLOTS, COLS), 2, bytes_accessed=2 << 20)(grads, meta)
    received = lax.all_to_all(outgoing, "rollout", split_axis=0, concat_axis=0, tiled=True)
    summed = call(sum_kernel, (SIDE, ROWS, COLS), 1, flops=1 << 28, bytes_accessed=3 << 20)(received)
    line = exchange(summed, 0)
    plane = exchange(jnp.broadcast_to(line[None], (SIDE, SIDE, ROWS, COLS)), 1)

    slope = gelu_slope(pre_act.astype(F32)).reshape(SIDE, SIDE, OWN, HID_OWN)
    slope = jnp.where(core == 0, slope.transpose(1, 0, 2, 3), slope).reshape(ROWS, HID_OWN)
    vmem = pl.BlockSpec(memory_space=pltpu.VMEM)
    partial = call(
        mlp_kernel,
        (ROWS, HID),
        4,
        flops=3 << 30,
        bytes_accessed=20 << 20,
        vmem=50 << 20,
        in_specs=[
            pl.BlockSpec(memory_space=pltpu.SMEM),
            pl.BlockSpec(memory_space=pl.ANY),
            vmem,
            vmem,
        ],
        scratch_shapes=[
            pltpu.VMEM((PROMPTS, HID_OWN, W2_COLS), BF16),
            pltpu.VMEM((PROMPTS, IN_OWN, 256), BF16),
            pltpu.VMEM((PROMPTS, TAIL, 256), BF16),
            pltpu.SemaphoreType.DMA((6,)),
        ],
    )(core.astype(jnp.int32)[None], weights, plane.reshape(ROLLOUTS, ROWS, COLS), slope)

    halfway = exchange(partial.reshape(SIDE, SIDE * OWN, HID), 0)
    halfway = call(add_kernel, (SIDE * OWN, HID), 1, bytes_accessed=5 << 20, vmem=24 << 20)(halfway)
    last = exchange(halfway.reshape(SIDE, OWN, HID), 1)
    return call(norm_kernel, (OWN, HID), 3, bytes_accessed=2 << 20)(
        last, patches, ln_gain.reshape(1, VIT)
    )


def solution(mesh):
    return jax.shard_map(
        per_device,
        mesh=mesh,
        in_specs=(
            P("prompt", "rollout", None, None),
            P("prompt", "rollout", None),
            P("prompt", "rollout"),
            P("prompt", "rollout"),
            P(("prompt", "rollout"), None),
            P(),
            P("rollout", "prompt"),
            P("prompt", "rollout"),
        ),
        out_specs=P(("prompt", "rollout"), None),
        check_vma=False,
    )
```

time: 375 us -> 172 us (0.46)
  waiting for transfers between devices: 237 us -> 49 us
  Pallas kernels: 0 us -> 19.6 us
  local copies, waits for them, and re-layouts: 23.7 us -> 6.41 us
  matrix products: 17.2 us -> 0 us
  blocking collectives: 57.1 us -> 69 us
  starting transfers between devices: 20.5 us -> 8.88 us
    all_gather x4 -> x1, waiting for transfers between devices: 201 us -> 0.01 us  [per_device(): weights = lax.all_gather(weights, 'prompt', axis=0, tiled=False)]
    pallas_call x0 -> x5, Pallas kernels: none -> 19.6 us  [the longest x1 16.4 us: per_device(): call(mlp_kernel, (ROWS, HID), 4, flops=3 << 30, bytes_accessed=20 << 20,...]
    dot_general x4 -> x0, matrix products: 17.2 us -> none  [the longest x2 14.1 us: contract_last(): lax.dot_general(left, right, (((1,), (1,)), ((), ())), preferred_element_...]
    all_to_all x3 -> x2, waiting for transfers between devices: 34.2 us -> 49 us  [exchange(): lax.all_to_all(blocks, AXES, split_axis=0, concat_axis=0, axis_index_grou...]
    all_to_all x4 -> x0, local copies, waits for them, and re-layouts: 12.3 us -> none  [the longest x2 11.6 us: per_device(): lax.all_to_all(w1_all, 'rollout', split_axis=0, concat_axis=1, tiled=True)]
    all_to_all x1 -> x3, blocking collectives: 57.1 us -> 69 us  [the longest x2 47.2 us: exchange(): lax.all_to_all(blocks, AXES, split_axis=0, concat_axis=0, axis_index_grou...]
    all_to_all x3 -> x2, starting transfers between devices: 20.4 us -> 8.88 us  [exchange(): lax.all_to_all(blocks, AXES, split_axis=0, concat_axis=0, axis_index_grou...]
    all_gather x1 -> x0, local copies, waits for them, and re-layouts: 6.26 us -> none  [per_device(): lax.all_gather(act_grad, 'rollout', axis=1, tiled=True)]
  transfers between devices with their start and end apart: 7 -> 3, of which waited for: 7 -> 2; matrix products, arithmetic and copies ran while one was open for 8% -> 3% of each run, Pallas kernels for 0% -> 0%
where the time goes in v1:
time: 172 us; the launch traced here: 170 us
  blocking collectives  69 us (40%)
  waiting for transfers between devices  49 us (28%)
  Pallas kernels  19.6 us (11%)
  between operations  14.2 us (8%)
  starting transfers between devices  8.88 us (5%)
  local copies, waits for them, and re-layouts  6.41 us (4%)
  other arithmetic  2.64 us (2%)
    all_to_all x2, waiting for transfers between devices, exchange(): lax.all_to_all(blocks, AXES, split_axis=0, concat_axis=0, axis_index_grou...  49 us
    all_to_all x2, blocking collectives, exchange(): lax.all_to_all(blocks, AXES, split_axis=0, concat_axis=0, axis_index_grou...  47.2 us
    all_to_all x1, blocking collectives, per_device(): lax.all_to_all(outgoing, 'rollout', split_axis=0, concat_axis=0, tiled=True)  21.7 us
    pallas_call x1, Pallas kernels, per_device(): call(mlp_kernel, (ROWS, HID), 4, flops=3 << 30, bytes_accessed=20 << 20,...  16.4 us
    all_to_all x2, starting transfers between devices, exchange(): lax.all_to_all(blocks, AXES, split_axis=0, concat_axis=0, axis_index_grou...  8.88 us
  transfers between devices with their start and end apart: 3, of which 2 were waited for; matrix products, arithmetic and copies ran while one was open for 3% of the time, Pallas kernels for 0%

profile of v1, /device:TPU:6, one launch (start us, length us, event | category | flops | bytes accessed | tf_op | source)
XLA Modules:
  0.0 169.6 jit_solution(8160761470875692979)
XLA Ops:
  6.5 0.0 all-gather.3.cloned.1.call-start
  6.5 0.8 slice.13
  7.3 0.9 slice.12
  8.2 1.6 maximum_maximum_fusion
  9.9 0.0 all-gather.3.cloned.1.call-update
  10.6 0.7 compare_select_fusion.3
  11.3 1.3 pad.17.grads_ref
  12.6 0.1 shard_map.82
  12.7 21.7 %all_to_all.25.recv_ref = bf16[16,64,512]{2,1,0:T(8,128)(2,1)S(1)} all-to-all(bf16[16,64,512]{2,1,0:T(8,128)(2,1)S(1)} %shard_map.82), channel_id=1, replica_groups=mesh['prompt'=32,'rollout'=16] {'rollout'}, dimensions={0} | all-to-all | bytes 2097152 | tf_op jit(solution)/shard_map/all_to_all | solution.py:168
  34.4 0.6 shard_map.83
  35.0 17.1 %all_to_all.26 = bf16[4,384,512]{2,1,0:T(8,128)(2,1)S(1)} all-to-all(bf16[4,384,512]{2,1,0:T(8,128)(2,1)S(1)} %shard_map.83), channel_id=1, replica_groups={{0,1,2,3},{4,5,6,7},{8,9,10,11},{12,13,14,15},{16,20,24,28},{17,21,25,2..., dimensions={0} | all-to-all | bytes 3145728 | tf_op jit(solution)/shard_map/all_to_all | solution.py:52
  52.1 3.2 %broadcast_in_dim.7 = bf16[4,4,384,512]{3,2,1,0:T(8,128)(2,1)} broadcast(bf16[4,384,512]{2,1,0:T(8,128)(2,1)S(1)} %all_to_all.26), dimensions={1,2,3} | broadcast | bytes 7864320 | tf_op jit(solution)/shard_map/broadcast_in_dim | solution.py:171
  55.3 0.0 copy-start.1
  55.3 5.4 %all-to-all-start.2 = ((bf16[4,4,384,512]{3,2,1,0:T(8,128)(2,1)}), bf16[4,4,384,512]{3,2,1,0:T(8,128)(2,1)}, u32[]{:S(2)}, u32[]{:S(2)}) async-start(bf16[4,4,384,512]{3,2,1,0:T(8,128)(2,1)} %broadcast_in_dim.7), calls=%async_computation.2 | async-start | bytes 12582912 | tf_op jit(solution)/shard_map/all_to_all | solution.py:52
  60.7 0.0 copy-done.1
  60.7 0.2 copy.11
  60.9 0.2 fusion.3
  61.2 38.5 %all-to-all-done.2 = bf16[4,4,384,512]{3,2,1,0:T(8,128)(2,1)} async-done(((bf16[4,4,384,512]{3,2,1,0:T(8,128)(2,1)}), bf16[4,4,384,512]{3,2,1,0:T(8,128)(2,1)}, u32[]{:S(2)}, u32[]{:S(2)}) %all-to-all-start.2) | async-done | bytes 6291488 | tf_op jit(solution)/shard_map/all_to_all | solution.py:52
  99.7 0.0 all-gather.3.cloned.1.call-done
  99.7 16.4 %shard_map.84 = bf16[384,5120]{1,0:T(8,128)(2,1)} custom-call(s32[1]{0:T(128)} %bitcast.core_ref, bf16[32,560,256]{2,1,0:T(8,128)(2,1)} %bitcast.35, bf16[16,384,512]{2,1,0:T(8,128)(2,1)} %bitcast.7.s_ref, f32[384,320]{1,0:T(8,128)S(1)} %bitcast.33), custom_call_target="tpu_custom_call" | custom-call | flops 3221225472 | bytes 20971520 | tf_op jit(solution)/shard_map/pallas_call | solution.py:176
  116.1 30.1 %all_to_all.27.recv_ref = bf16[4,96,5120]{2,1,0:T(8,128)(2,1)S(1)} all-to-all(bf16[4,96,5120]{2,1,0:T(8,128)(2,1)} %bitcast.34), channel_id=1, replica_groups={{0,1,2,3},{4,5,6,7},{8,9,10,11},{12,13,14,15},{16,20,24,28},{17,21,25,2..., dimensions={0} | all-to-all | bytes 7864320 | tf_op jit(solution)/shard_map/all_to_all | solution.py:52
  146.3 0.0 copy-start.2
  146.3 0.0 copy-start
  146.3 1.4 shard_map.85
  147.7 3.5 %all-to-all-start.4 = ((bf16[4,24,5120]{2,1,0:T(8,128)(2,1)}), bf16[4,24,5120]{2,1,0:T(8,128)(2,1)S(1)}, u32[]{:S(2)}, u32[]{:S(2)}) async-start(bf16[4,24,5120]{2,1,0:T(8,128)(2,1)} %bitcast.12), calls=%async_computation.4 | async-start | bytes 1966080 | tf_op jit(solution)/shard_map/all_to_all | solution.py:52
  151.2 0.0 copy-done.2
  151.3 10.5 %all-to-all-done.4.recv_ref = bf16[4,24,5120]{2,1,0:T(8,128)(2,1)S(1)} async-done(((bf16[4,24,5120]{2,1,0:T(8,128)(2,1)}), bf16[4,24,5120]{2,1,0:T(8,128)(2,1)S(1)}, u32[]{:S(2)}, u32[]{:S(2)}) %all-to-all-start.4) | async-done | bytes 983072 | tf_op jit(solution)/shard_map/all_to_all | solution.py:52
  161.7 0.0 copy-done
  161.7 1.0 shard_map.86
  (7 shorter events, 0.1 us)
Async XLA Ops:
  6.5 93.2 %all-gather.3.cloned.1.call-start = ((), (), s32[]{:S(2)}) async-start(), calls=%async_computation.5 | async-start | bytes 9461760 | tf_op jit(solution)/shard_map/all_gather | solution.py:156
  55.3 5.4 %copy-start.1 = (bf16[384,320]{0,1:T(8,128)(2,1)S(1)}, bf16[384,320]{0,1:T(8,128)(2,1)}, u32[]{:S(2)}) copy-start(bf16[384,320]{0,1:T(8,128)(2,1)} %param.11) | copy-start | bytes 737284
  55.3 44.4 %all-to-all-start.2 = ((bf16[4,4,384,512]{3,2,1,0:T(8,128)(2,1)}), bf16[4,4,384,512]{3,2,1,0:T(8,128)(2,1)}, u32[]{:S(2)}, u32[]{:S(2)}) async-start(bf16[4,4,384,512]{3,2,1,0:T(8,128)(2,1)} %broadcast_in_dim.7), calls=%async_computation.2 | async-start | bytes 12582912 | tf_op jit(solution)/shard_map/all_to_all | solution.py:52
  146.3 4.9 %copy-start.2 = (f32[1280]{0:T(1024)S(1)}, f32[1280]{0:T(1024)}, u32[]{:S(2)}) copy-start(f32[1280]{0:T(1024)} %param.13) | copy-start | bytes 15364
  146.3 15.4 %copy-start = (bf16[24,5120]{1,0:T(8,128)(2,1)S(1)}, bf16[24,5120]{1,0:T(8,128)(2,1)}, u32[]{:S(2)}) copy-start(bf16[24,5120]{1,0:T(8,128)(2,1)} %patches_ref.1) | copy-start | bytes 737284
  147.7 14.0 %all-to-all-start.4 = ((bf16[4,24,5120]{2,1,0:T(8,128)(2,1)}), bf16[4,24,5120]{2,1,0:T(8,128)(2,1)S(1)}, u32[]{:S(2)}, u32[]{:S(2)}) async-start(bf16[4,24,5120]{2,1,0:T(8,128)(2,1)} %bitcast.12), calls=%async_computation.4 | async-start | bytes 1966080 | tf_op jit(solution)/shard_map/all_to_all | solution.py:52
Sparse Core Ops, SparseCore 0:
  10.0 85.0 all-gather.2

commit v2 on v1

v2 whole, which is shorter than its diff:
```python
import jax
import jax.numpy as jnp
from jax import lax
from jax.experimental import pallas as pl
from jax.experimental.pallas import tpu as pltpu
from jax.sharding import PartitionSpec as P

VIT = 1280
MERGE = 4
PROMPTS = 32
ROLLOUTS = 16
SIDE = 4
SLOTS = 50
PAD_SLOTS = 64
OWN = 24
ROWS = OWN * ROLLOUTS
D_LLM = 8192
COLS = D_LLM // ROLLOUTS
HID = 5120
HID_OWN = HID // ROLLOUTS
IN_OWN = HID // PROMPTS
W2_COLS = D_LLM // PROMPTS
TAIL = IN_OWN // 2
W_ROWS = HID_OWN + IN_OWN + TAIL
AXES = ("prompt", "rollout")
F32 = jnp.float32
BF16 = jnp.bfloat16


def gelu_slope(value):
    return (
        0.5 * (1.0 + jax.scipy.special.erf(value * 0.7071067811865476))
        + value * jnp.exp(-0.5 * value * value) * 0.3989422804014327
    )


def dot_t(left, right):
    return lax.dot_general(left, right, (((1,), (1,)), ((), ())), preferred_element_type=F32)


def line_groups(phase):
    groups = []
    for prompt in range(PROMPTS):
        for other in range(SIDE):
            along_x = (prompt % 2 == 0) == (phase == 0)
            line = [(other * SIDE + i) if along_x else (i * SIDE + other) for i in range(SIDE)]
            groups.append([prompt * ROLLOUTS + r for r in line])
    return groups


def exchange(blocks, phase):
    return lax.all_to_all(
        blocks, AXES, split_axis=0, concat_axis=0, axis_index_groups=line_groups(phase), tiled=True
    )


def shift(value, phase, by):
    pairs = []
    for line in line_groups(phase):
        pairs += [(line[i], line[(i + by) % SIDE]) for i in range(SIDE)]
    return lax.ppermute(value, AXES, pairs)


def place_in_plane():
    rollout = lax.axis_index("rollout")
    even = lax.axis_index("prompt") % 2 == 0
    y, x = rollout // SIDE, rollout % SIDE
    return even, jnp.where(even, x, y), jnp.where(even, y, x)


def weights_kernel(w2_ref, w1_ref, out_ref):
    out_ref[0:HID_OWN, :] = w2_ref[...]
    out_ref[HID_OWN : HID_OWN + IN_OWN, :] = w1_ref[:, 0:256]
    base = HID_OWN + IN_OWN
    out_ref[base:W_ROWS, :] = jnp.zeros((TAIL, 256), BF16)
    out_ref[base:W_ROWS, 0:64] = w1_ref[0:TAIL, 256:320]
    out_ref[base:W_ROWS, 128:192] = w1_ref[TAIL:IN_OWN, 256:320]


def pack_kernel(count_ref, ids_ref, grads_ref, out_ref, meta):
    even, _, _ = place_in_plane()
    ids = ids_ref[...]
    owner = (ids * 2731) >> 16
    turned = (owner & 3) * SIDE + (owner >> 2)
    place = jnp.where(even, turned, owner) * OWN + ids - owner * OWN + 1
    live = lax.broadcasted_iota(jnp.int32, (1, SLOTS), 1) < count_ref[0, 0]
    place = jnp.where(live, place, 0)
    meta[...] = jnp.zeros((8, COLS), F32)
    meta[2:3, 0:SLOTS] = (place >> 4).astype(F32)
    meta[3:4, 0:SLOTS] = (place & 15).astype(F32)
    codes = meta[...]
    zeros = jnp.zeros((8, COLS), F32)
    for k in range(ROLLOUTS):
        cols = pl.ds(k * COLS, COLS)
        out_ref[k, 0:48, :] = grads_ref[0:48, cols]
        two = jnp.concatenate([grads_ref[48:SLOTS, cols].astype(F32), zeros[0:6]], axis=0)
        out_ref[k, 48:64, :] = jnp.concatenate([two + codes, zeros], axis=0).astype(BF16)


def sum_kernel(recv_ref, out_ref):
    rows = (lax.broadcasted_iota(jnp.int32, (ROWS, 4 * PAD_SLOTS), 0) + 1).astype(F32)
    total = jnp.zeros((ROWS, COLS), F32)
    for g in range(ROLLOUTS // 4):
        codes = jnp.zeros((8, 4 * PAD_SLOTS), F32)
        for k in range(4):
            tile = recv_ref[4 * g + k, 48:64, 0 : 4 * PAD_SLOTS].astype(F32)[0:8]
            codes = codes + (pltpu.roll(tile, PAD_SLOTS * k, 1) if k else tile)
        row = codes[2:3] * 16.0 + codes[3:4]
        onehot = jnp.where(rows == row, 1.0, 0.0).astype(BF16)
        block = recv_ref[4 * g : 4 * g + 4].reshape(4 * PAD_SLOTS, COLS)
        total = total + jnp.dot(onehot, block, preferred_element_type=F32)
    value = total.astype(BF16)
    for k in range(SIDE):
        out_ref[k] = value


def start_w1(w_ref, w1, sems):
    base = HID_OWN + IN_OWN
    copies = [
        pltpu.make_async_copy(w_ref.at[:, HID_OWN:base], w1.at[:, :, 0:256], sems.at[0]),
        pltpu.make_async_copy(w_ref.at[:, base:W_ROWS, 0:128], w1.at[:, 0:TAIL, 256:384], sems.at[1]),
        pltpu.make_async_copy(w_ref.at[:, base:W_ROWS, 128:256], w1.at[:, TAIL:IN_OWN, 256:384], sems.at[2]),
    ]
    for copy in copies:
        copy.start()
    return copies


def w1_chunk(w1, g, prompts):
    return w1[prompts * g : prompts * (g + 1)].reshape(prompts * IN_OWN, 384)[:, :HID_OWN]


GATHERED = ((0, (0, 1, 2, 3), 0), (1, (0, 1), 3), (2, (2, 3), 3), (3, (2, 3), 1), (4, (0, 1), 1), (5, (0, 1), 2), (6, (2, 3), 2))


def act_kernel(w_ref, *refs):
    sums, (slope_ref, act_ref, low_ref, high_ref, w2, w1, sems2, sems1) = refs[:7], refs[7:]
    even, first, second = place_in_plane()
    slots, copies = [], []
    for operand, places, offset in GATHERED:
        for n, k in enumerate(places):
            s = lax.rem(second + offset, SIDE)
            block = jnp.where(even, s * SIDE + k, k * SIDE + s)
            i = len(slots)
            pair = [
                pltpu.make_async_copy(
                    w_ref.at[2 * block + h, 0:HID_OWN],
                    w2.at[:, pl.ds((2 * i + h) * W2_COLS, W2_COLS)],
                    sems2.at[i, h],
                )
                for h in range(2)
            ]
            for copy in pair:
                copy.start()
            copies.append(pair)
            slots.append((sums[operand], n))
    late = start_w1(w_ref, w1, sems1)
    hidden = None
    for i, (ref, n) in enumerate(slots):
        for copy in copies[i]:
            copy.wait()
        part = dot_t(ref[n], w2[:, i * COLS : (i + 1) * COLS])
        hidden = part if hidden is None else hidden + part
    act_ref[...] = (hidden * slope_ref[...]).astype(BF16)
    far = lax.rem(first + 2, SIDE)
    rows = act_ref[pl.ds(pl.multiple_of(far * 96, 96), 96), :]
    for copy in late:
        copy.wait()
    for g in range(8):
        part = dot_t(rows, w1_chunk(w1, g, 4)).astype(BF16)
        cols = slice(640 * g, 640 * (g + 1))
        low_ref[:, cols] = part[:48]
        high_ref[:, cols] = part[48:]


def rest_kernel(w_ref, act_ref, right_low, right_high, left_low, left_high, own_ref, w1, sems1):
    _, first, _ = place_in_plane()
    late = start_w1(w_ref, w1, sems1)
    blocks = [
        act_ref[pl.ds(pl.multiple_of(lax.rem(first + by, SIDE) * 96, 96), 96), :] for by in (1, 3, 0)
    ]
    rows = jnp.concatenate(blocks, axis=0)
    for copy in late:
        copy.wait()
    for g in range(8):
        part = dot_t(rows, w1_chunk(w1, g, 4)).astype(BF16)
        cols = slice(640 * g, 640 * (g + 1))
        right_low[:, cols] = part[0:48]
        right_high[:, cols] = part[48:96]
        left_low[:, cols] = part[96:144]
        left_high[:, cols] = part[144:192]
        own_ref[:, cols] = part[192:288]


def pair_kernel(a_ref, b_ref, out_ref):
    out_ref[...] = (a_ref[...].astype(F32) + b_ref[...].astype(F32)).astype(BF16)


def join_kernel(own_ref, low_a, low_b, high_a, high_b, out_ref):
    low = own_ref[0:48].astype(F32) + low_a[...].astype(F32) + low_b[...].astype(F32)
    high = own_ref[48:96].astype(F32) + high_a[...].astype(F32) + high_b[...].astype(F32)
    out_ref[0:48] = low.astype(BF16)
    out_ref[48:96] = high.astype(BF16)


def norm_kernel(recv_ref, patches_ref, gain_ref, out_ref):
    for m in range(MERGE):
        cols = slice(m * VIT, (m + 1) * VIT)
        upstream = recv_ref[0, :, cols].astype(F32)
        for k in range(1, SIDE):
            upstream = upstream + recv_ref[k, :, cols].astype(F32)
        inputs = patches_ref[:, cols].astype(F32)
        scaled = upstream * gain_ref[...]
        inverse = lax.rsqrt(jnp.mean(inputs * inputs, axis=-1, keepdims=True) + 1e-06)
        inner = jnp.mean(scaled * inputs, axis=-1, keepdims=True)
        result = inverse * scaled - inputs * inverse * inverse * inverse * inner
        out_ref[:, cols] = result.astype(BF16)


VMEM = pl.BlockSpec(memory_space=pltpu.VMEM)
SMEM = pl.BlockSpec(memory_space=pltpu.SMEM)
ANY = pl.BlockSpec(memory_space=pl.ANY)


def call(kernel, shapes, in_specs, flops=0, moved=0, vmem=16, scratch=()):
    one = not isinstance(shapes[0], tuple)
    shapes = (shapes,) if one else shapes
    run = pl.pallas_call(
        kernel,
        out_shape=[jax.ShapeDtypeStruct(shape, BF16) for shape in shapes],
        in_specs=in_specs,
        out_specs=[VMEM] * len(shapes),
        scratch_shapes=list(scratch),
        cost_estimate=pl.CostEstimate(flops=flops, bytes_accessed=moved, transcendentals=0),
        compiler_params=pltpu.CompilerParams(vmem_limit_bytes=vmem << 20),
    )
    return (lambda *args: run(*args)[0]) if one else run


def per_device(row_grads, used_ids, used_count, pre_act, patches, ln_gain, w_fc2, w_fc1):
    weights = call(weights_kernel, (W_ROWS, 256), [VMEM] * 2)(w_fc2, w_fc1)
    weights = lax.all_gather(weights, "prompt", axis=0, tiled=False)

    outgoing = call(
        pack_kernel, (ROLLOUTS, PAD_SLOTS, COLS), [SMEM, VMEM, VMEM], scratch=[pltpu.VMEM((8, COLS), F32)]
    )(used_count, used_ids[0], row_grads[0, 0])
    received = lax.all_to_all(outgoing, "rollout", split_axis=0, concat_axis=0, tiled=True)
    summed = call(sum_kernel, (SIDE, ROWS, COLS), [VMEM])(received)
    line = exchange(summed, 0)
    a1, b1 = shift(line[:2], 1, 1), shift(line[2:], 1, -1)
    a2, b2 = shift(line[2:], 1, 1), shift(line[:2], 1, -1)
    a3, b3 = shift(a1, 1, 1), shift(b1, 1, -1)

    even = lax.axis_index("prompt") % 2 == 0
    slope = gelu_slope(pre_act.astype(F32)).reshape(SIDE, SIDE, OWN, HID_OWN)
    slope = jnp.where(even, slope.transpose(1, 0, 2, 3), slope).reshape(ROWS, HID_OWN)
    w1_scratch = [pltpu.VMEM((PROMPTS, IN_OWN, 384), BF16), pltpu.SemaphoreType.DMA((3,))]
    act, far_low, far_high = call(
        act_kernel,
        ((ROWS, HID_OWN), (48, HID), (48, HID)),
        [ANY] + [VMEM] * 8,
        flops=5 << 29,
        moved=12 << 20,
        vmem=30,
        scratch=[
            pltpu.VMEM((HID_OWN, D_LLM), BF16),
            w1_scratch[0],
            pltpu.SemaphoreType.DMA((ROLLOUTS, 2)),
            w1_scratch[1],
        ],
    )(weights, line, a1, a2, b1, b2, a3, b3, slope)

    via_right, via_left = shift(far_low, 0, 1), shift(far_high, 0, -1)
    right_low, right_high, left_low, left_high, own = call(
        rest_kernel,
        ((48, HID),) * 4 + ((96, HID),),
        [ANY, VMEM],
        flops=1 << 30,
        moved=8 << 20,
        vmem=20,
        scratch=w1_scratch,
    )(weights, act)
    high_a, low_b = shift(right_high, 0, 1), shift(left_low, 0, -1)
    pair = call(pair_kernel, (48, HID), [VMEM] * 2)
    low_a, high_b = shift(pair(right_low, via_right), 0, 1), shift(pair(left_high, via_left), 0, -1)
    halfway = call(join_kernel, (96, HID), [VMEM] * 5)(own, low_a, low_b, high_a, high_b)
    last = exchange(halfway.reshape(SIDE, OWN, HID), 1)
    return call(norm_kernel, (OWN, HID), [VMEM] * 3)(last, patches, ln_gain.reshape(1, VIT))


def solution(mesh):
    return jax.shard_map(
        per_device,
        mesh=mesh,
        in_specs=(
            P("prompt", "rollout", None, None),
            P("prompt", "rollout", None),
            P("prompt", "rollout"),
            P("prompt", "rollout"),
            P(("prompt", "rollout"), None),
            P(),
            P("rollout", "prompt"),
            P("prompt", "rollout"),
        ),
        out_specs=P(("prompt", "rollout"), None),
        check_vma=False,
    )
```

time: 172 us -> 165 us (0.959)
  starting transfers between devices: 8.88 us -> 47.1 us
  blocking collectives: 69 us -> 38.8 us
  waiting for transfers between devices: 49 us -> 36.8 us
  Pallas kernels: 19.6 us -> 16 us
  other arithmetic: 2.64 us -> 0.28 us
  local copies, waits for them, and re-layouts: 6.41 us -> 8.72 us
    ppermute x0 -> x12, starting transfers between devices: none -> 42.4 us  [shift(): return lax.ppermute(value, AXES, pairs)]
    all_to_all x2 -> x1, waiting for transfers between devices: 49 us -> 10.5 us  [exchange(): lax.all_to_all(blocks, AXES, split_axis=0, concat_axis=0, axis_index_grou...]
    all_to_all x2 -> x1, blocking collectives: 47.2 us -> 17.1 us  [exchange(): lax.all_to_all(blocks, AXES, split_axis=0, concat_axis=0, axis_index_grou...]
    ppermute x0 -> x12, waiting for transfers between devices: none -> 18.2 us  [shift(): return lax.ppermute(value, AXES, pairs)]
    all_gather x1, waiting for transfers between devices: 0.01 us -> 8.1 us  [per_device(): weights = lax.all_gather(weights, 'prompt', axis=0, tiled=False)]
    unnamed x7 -> x19, local copies, waits for them, and re-layouts: 0.23 us -> 7.48 us
    all_to_all x2 -> x1, starting transfers between devices: 8.88 us -> 4.74 us  [exchange(): lax.all_to_all(blocks, AXES, split_axis=0, concat_axis=0, axis_index_grou...]
    pallas_call x5 -> x9, Pallas kernels: 19.6 us -> 16 us  [the longest x1 9.5 us: per_device(): call(act_kernel, ((ROWS, HID_OWN), (48, HID), (48, HID)), [ANY] + [VMEM]...]
  transfers between devices with their start and end apart: 3 -> 14, of which waited for: 2 -> 9; matrix products, arithmetic and copies ran while one was open for 3% -> 1% of each run, Pallas kernels for 0% -> 2%
where the time goes in v2:
time: 165 us; the launch traced here: 162 us
  starting transfers between devices  47.1 us (29%)
  blocking collectives  38.8 us (24%)
  waiting for transfers between devices  36.8 us (22%)
  Pallas kernels  16 us (10%)
  between operations  14.3 us (9%)
  local copies, waits for them, and re-layouts  8.72 us (5%)
    ppermute x12, starting transfers between devices, shift(): return lax.ppermute(value, AXES, pairs)  42.4 us
    all_to_all x1, blocking collectives, per_device(): lax.all_to_all(outgoing, 'rollout', split_axis=0, concat_axis=0, tiled=True)  21.7 us
    ppermute x12, waiting for transfers between devices, shift(): return lax.ppermute(value, AXES, pairs)  18.2 us
    all_to_all x1, blocking collectives, exchange(): lax.all_to_all(blocks, AXES, split_axis=0, concat_axis=0, axis_index_grou...  17.1 us
    all_to_all x1, waiting for transfers between devices, exchange(): lax.all_to_all(blocks, AXES, split_axis=0, concat_axis=0, axis_index_grou...  10.5 us
    pallas_call x1, Pallas kernels, per_device(): call(act_kernel, ((ROWS, HID_OWN), (48, HID), (48, HID)), [ANY] + [VMEM]...  9.5 us
    all_gather x1, waiting for transfers between devices, per_device(): weights = lax.all_gather(weights, 'prompt', axis=0, tiled=False)  8.1 us
    unnamed x19, local copies, waits for them, and re-layouts  7.48 us
  transfers between devices with their start and end apart: 14, of which 9 were waited for; matrix products, arithmetic and copies ran while one was open for 1% of the time, Pallas kernels for 2%

profile of v2, /device:TPU:6, one launch (start us, length us, event | category | flops | bytes accessed | tf_op | source)
XLA Modules:
  0.0 162.1 jit_solution(15323435582240662549)
XLA Ops:
  6.5 0.9 copy-done.4
  7.5 0.9 copy-done.5
  9.8 1.2 copy-done.2
  11.7 21.7 %all_to_all.15.recv_ref = bf16[16,64,512]{2,1,0:T(8,128)(2,1)S(1)} all-to-all(bf16[16,64,512]{2,1,0:T(8,128)(2,1)S(1)} %shard_map.83), channel_id=1, replica_groups=mesh['prompt'=32,'rollout'=16] {'rollout'}, dimensions={0} | all-to-all | bytes 2097152 | tf_op jit(solution)/shard_map/all_to_all | solution.py:247
  34.1 17.1 %all_to_all.16.refs_0_ = bf16[4,384,512]{2,1,0:T(8,128)(2,1)S(1)} all-to-all(bf16[4,384,512]{2,1,0:T(8,128)(2,1)S(1)} %shard_map.84), channel_id=1, replica_groups={{0,1,2,3},{4,5,6,7},{8,9,10,11},{12,13,14,15},{16,20,24,28},{17,21,25,2..., dimensions={0} | all-to-all | bytes 3145728 | tf_op jit(solution)/shard_map/all_to_all | solution.py:52
  51.1 1.2 fusion.6
  52.4 1.9 %collective-permute-start = (bf16[2,384,512]{2,1,0:T(8,128)(2,1)}, bf16[2,384,512]{2,1,0:T(8,128)(2,1)S(1)}, u32[]{:S(2)}, u32[]{:S(2)}) collective-permute-start(bf16[2,384,512]{2,1,0:T(8,128)(2,1)} %get-tuple-element.22), channel_id=1, source_target_pairs={{0,4},{4,8},{8,12},{12,0},{1,5},{5,9},{9,13},{13,1},{2,6},{6,10},{... | collective-permute-start | bytes 2359304 | tf_op jit(solution)/shard_map/ppermute | solution.py:61
  54.3 5.1 %collective-permute-start.2 = (bf16[2,384,512]{2,1,0:T(8,128)(2,1)}, bf16[2,384,512]{2,1,0:T(8,128)(2,1)}, u32[]{:S(2)}, u32[]{:S(2)}) collective-permute-start(bf16[2,384,512]{2,1,0:T(8,128)(2,1)} %get-tuple-element.21), channel_id=1, source_target_pairs={{0,12},{4,0},{8,4},{12,8},{1,13},{5,1},{9,5},{13,9},{2,14},{6,2},{... | collective-permute-start | bytes 2359304 | tf_op jit(solution)/shard_map/ppermute | solution.py:61
  59.4 1.9 %collective-permute-start.1 = (bf16[2,384,512]{2,1,0:T(8,128)(2,1)}, bf16[2,384,512]{2,1,0:T(8,128)(2,1)}, u32[]{:S(2)}, u32[]{:S(2)}) collective-permute-start(bf16[2,384,512]{2,1,0:T(8,128)(2,1)} %get-tuple-element.21), channel_id=1, source_target_pairs={{0,4},{4,8},{8,12},{12,0},{1,5},{5,9},{9,13},{13,1},{2,6},{6,10},{... | collective-permute-start | bytes 2359304 | tf_op jit(solution)/shard_map/ppermute | solution.py:61
  61.4 5.1 %collective-permute-start.3 = (bf16[2,384,512]{2,1,0:T(8,128)(2,1)}, bf16[2,384,512]{2,1,0:T(8,128)(2,1)}, u32[]{:S(2)}, u32[]{:S(2)}) collective-permute-start(bf16[2,384,512]{2,1,0:T(8,128)(2,1)} %get-tuple-element.22), channel_id=1, source_target_pairs={{0,12},{4,0},{8,4},{12,8},{1,13},{5,1},{9,5},{13,9},{2,14},{6,2},{... | collective-permute-start | bytes 2359304 | tf_op jit(solution)/shard_map/ppermute | solution.py:61
  66.5 1.2 collective-permute-done.refs_1_
  67.7 1.9 %collective-permute-start.4 = (bf16[2,384,512]{2,1,0:T(8,128)(2,1)S(1)}, bf16[2,384,512]{2,1,0:T(8,128)(2,1)}, u32[]{:S(2)}, u32[]{:S(2)}) collective-permute-start(bf16[2,384,512]{2,1,0:T(8,128)(2,1)S(1)} %collective-permute-done.refs_1_), channel_id=1, source_target_pairs={{0,4},{4,8},{8,12},{12,0},{1,5},{5,9},{9,13},{13,1},{2,6},{6,10},{... | collective-permute-start | bytes 2359304 | tf_op jit(solution)/shard_map/ppermute | solution.py:61
  69.6 5.2 %collective-permute-start.5 = (bf16[2,384,512]{2,1,0:T(8,128)(2,1)}, bf16[2,384,512]{2,1,0:T(8,128)(2,1)}, u32[]{:S(2)}, u32[]{:S(2)}) collective-permute-start(bf16[2,384,512]{2,1,0:T(8,128)(2,1)} %collective-permute-done.2.refs_3_), channel_id=1, source_target_pairs={{0,12},{4,0},{8,4},{12,8},{1,13},{5,1},{9,5},{13,9},{2,14},{6,2},{... | collective-permute-start | bytes 2359304 | tf_op jit(solution)/shard_map/ppermute | solution.py:61
  76.2 1.5 collective-permute-done.3.refs_4_
  77.7 7.0 %collective-permute-done.4.refs_5_ = bf16[2,384,512]{2,1,0:T(8,128)(2,1)} collective-permute-done((bf16[2,384,512]{2,1,0:T(8,128)(2,1)S(1)}, bf16[2,384,512]{2,1,0:T(8,128)(2,1)}, u32[]{:S(2)}, u32[]{:S(2)}) %collective-permute-start.4) | collective-permute-done | bytes 786464 | tf_op jit(solution)/shard_map/ppermute | solution.py:61
  84.6 1.5 collective-permute-done.5.refs_6_
  86.1 8.1 %all-gather.3.cloned.1.call-done = bf16[17920,256]{1,0:T(8,128)(2,1)} async-done(((bf16[560,256]{1,0:T(8,128)(2,1)}), bf16[17920,256]{1,0:T(8,128)(2,1)}) %all-gather.3.cloned.1.call-update) | async-done | bytes 9175056 | tf_op jit(solution)/shard_map/all_gather | solution.py:242
  94.2 3.6 %copy-done = bf16[17920,256]{1,0:T(8,128)(2,1)S(1)} copy-done((bf16[17920,256]{1,0:T(8,128)(2,1)S(1)}, bf16[17920,256]{1,0:T(8,128)(2,1)}, u32[]{:S(2)}) %copy-start) | copy-done | bytes 9175064
  97.8 9.5 %shard_map.85 = (bf16[384,320]{1,0:T(8,128)(2,1)S(1)}, bf16[48,5120]{1,0:T(8,128)(2,1)S(1)}, bf16[48,5120]{1,0:T(8,128)(2,1)S(1)}) custom-call(bf16[32,560,256]{2,1,0:T(8,128)(2,1)S(1)} %bitcast.8, bf16[4,384,512]{2,1,0:T(8,128)(2,1)S(1)} %all_to_all.16.refs_0_, bf16[2,384,512]{2,1,0:T(8,128)(2,1)S(1)} %collective-permute-done.refs_1_, ...), custom_call_target="tpu_custom_call" | custom-call | flops 2684354560 | bytes 12582912 | tf_op jit(solution)/shard_map/pallas_call | solution.py:258
  107.3 2.8 %collective-permute-start.10 = (bf16[48,5120]{1,0:T(8,128)(2,1)S(1)}, bf16[48,5120]{1,0:T(8,128)(2,1)S(1)}, u32[]{:S(2)}, u32[]{:S(2)}) collective-permute-start(bf16[48,5120]{1,0:T(8,128)(2,1)S(1)} %get-tuple-element.20), channel_id=1, source_target_pairs={{0,3},{1,0},{2,1},{3,2},{4,7},{5,4},{6,5},{7,6},{8,11},{9,8},{10,9... | collective-permute-start | bytes 1474568 | tf_op jit(solution)/shard_map/ppermute | solution.py:61
  110.1 4.2 %collective-permute-start.6 = (bf16[48,5120]{1,0:T(8,128)(2,1)S(1)}, bf16[48,5120]{1,0:T(8,128)(2,1)S(1)}, u32[]{:S(2)}, u32[]{:S(2)}) collective-permute-start(bf16[48,5120]{1,0:T(8,128)(2,1)S(1)} %get-tuple-element.16), channel_id=1, source_target_pairs={{0,1},{1,2},{2,3},{3,0},{4,5},{5,6},{6,7},{7,4},{8,9},{9,10},{10,1... | collective-permute-start | bytes 1474568 | tf_op jit(solution)/shard_map/ppermute | solution.py:61
  114.4 2.5 %shard_map.86 = (bf16[48,5120]{1,0:T(8,128)(2,1)S(1)}, bf16[48,5120]{1,0:T(8,128)(2,1)S(1)}, bf16[48,5120]{1,0:T(8,128)(2,1)S(1)}, bf16[48,5120]{1,0:T(8,128)(2,1)S(1)}, bf16[96,5120]{1,0:T(8,128)(2,1)S(1)}) custom-call(bf16[32,560,256]{2,1,0:T(8,128)(2,1)S(1)} %bitcast.9, bf16[384,320]{1,0:T(8,128)(2,1)S(1)} %get-tuple-element.13.act_ref), custom_call_target="tpu_custom_call" | custom-call | flops 1073741824 | bytes 8388608 | tf_op jit(solution)/shard_map/pallas_call | solution.py:274
  116.9 1.9 %collective-permute-start.8 = (bf16[48,5120]{1,0:T(8,128)(2,1)S(1)}, bf16[48,5120]{1,0:T(8,128)(2,1)S(1)}, u32[]{:S(2)}, u32[]{:S(2)}) collective-permute-start(bf16[48,5120]{1,0:T(8,128)(2,1)S(1)} %get-tuple-element.17), channel_id=1, source_target_pairs={{0,3},{1,0},{2,1},{3,2},{4,7},{5,4},{6,5},{7,6},{8,11},{9,8},{10,9... | collective-permute-start | bytes 1474568 | tf_op jit(solution)/shard_map/ppermute | solution.py:61
  118.8 5.1 %collective-permute-start.9 = (bf16[48,5120]{1,0:T(8,128)(2,1)S(1)}, bf16[48,5120]{1,0:T(8,128)(2,1)S(1)}, u32[]{:S(2)}, u32[]{:S(2)}) collective-permute-start(bf16[48,5120]{1,0:T(8,128)(2,1)S(1)} %get-tuple-element.18), channel_id=1, source_target_pairs={{0,1},{1,2},{2,3},{3,0},{4,5},{5,6},{6,7},{7,4},{8,9},{9,10},{10,1... | collective-permute-start | bytes 1474568 | tf_op jit(solution)/shard_map/ppermute | solution.py:61
  124.1 1.9 %collective-permute-start.11 = (bf16[48,5120]{1,0:T(8,128)(2,1)S(1)}, bf16[48,5120]{1,0:T(8,128)(2,1)S(1)}, u32[]{:S(2)}, u32[]{:S(2)}) collective-permute-start(bf16[48,5120]{1,0:T(8,128)(2,1)S(1)} %shard_map.88), channel_id=1, source_target_pairs={{0,3},{1,0},{2,1},{3,2},{4,7},{5,4},{6,5},{7,6},{8,11},{9,8},{10,9... | collective-permute-start | bytes 1474568 | tf_op jit(solution)/shard_map/ppermute | solution.py:61
  126.1 5.1 %collective-permute-start.7 = (bf16[48,5120]{1,0:T(8,128)(2,1)S(1)}, bf16[48,5120]{1,0:T(8,128)(2,1)S(1)}, u32[]{:S(2)}, u32[]{:S(2)}) collective-permute-start(bf16[48,5120]{1,0:T(8,128)(2,1)S(1)} %shard_map.87), channel_id=1, source_target_pairs={{0,1},{1,2},{2,3},{3,0},{4,5},{5,6},{6,7},{7,4},{8,9},{9,10},{10,1... | collective-permute-start | bytes 1474568 | tf_op jit(solution)/shard_map/ppermute | solution.py:61
  131.3 4.7 %collective-permute-done.11.high_b = bf16[48,5120]{1,0:T(8,128)(2,1)S(1)} collective-permute-done((bf16[48,5120]{1,0:T(8,128)(2,1)S(1)}, bf16[48,5120]{1,0:T(8,128)(2,1)S(1)}, u32[]{:S(2)}, u32[]{:S(2)}) %collective-permute-start.11) | collective-permute-done | bytes 491552 | tf_op jit(solution)/shard_map/ppermute | solution.py:61
  136.0 1.6 collective-permute-done.7.low_a
  137.6 1.3 shard_map.89
  138.9 4.7 %all-to-all-start.2 = ((bf16[4,24,5120]{2,1,0:T(8,128)(2,1)}), bf16[4,24,5120]{2,1,0:T(8,128)(2,1)S(1)}, u32[]{:S(2)}, u32[]{:S(2)}) async-start(bf16[4,24,5120]{2,1,0:T(8,128)(2,1)} %bitcast.6), calls=%async_computation.2 | async-start | bytes 1966080 | tf_op jit(solution)/shard_map/all_to_all | solution.py:52
  143.7 10.5 %all-to-all-done.2.recv_ref = bf16[4,24,5120]{2,1,0:T(8,128)(2,1)S(1)} async-done(((bf16[4,24,5120]{2,1,0:T(8,128)(2,1)}), bf16[4,24,5120]{2,1,0:T(8,128)(2,1)S(1)}, u32[]{:S(2)}, u32[]{:S(2)}) %all-to-all-start.2) | async-done | bytes 983072 | tf_op jit(solution)/shard_map/all_to_all | solution.py:52
  154.2 1.0 shard_map.90
  (31 shorter events, 3.7 us)
Async XLA Ops:
  6.5 87.7 %all-gather.3.cloned.1.call-start = ((), (), s32[]{:S(2)}) async-start(), calls=%async_computation.3 | async-start | bytes 9461760 | tf_op jit(solution)/shard_map/all_gather | solution.py:242
  6.5 0.9 copy-start.4
  7.5 0.9 copy-start.5
  9.8 1.2 copy-start.2
  11.0 0.7 copy-start.6
  51.1 23.7 %copy-start.7 = (bf16[384,320]{0,1:T(8,128)(2,1)S(1)}, bf16[384,320]{0,1:T(8,128)(2,1)}, u32[]{:S(2)}) copy-start(bf16[384,320]{0,1:T(8,128)(2,1)} %param.11) | copy-start | bytes 737284
  52.4 15.3 %collective-permute-start = (bf16[2,384,512]{2,1,0:T(8,128)(2,1)}, bf16[2,384,512]{2,1,0:T(8,128)(2,1)S(1)}, u32[]{:S(2)}, u32[]{:S(2)}) collective-permute-start(bf16[2,384,512]{2,1,0:T(8,128)(2,1)} %get-tuple-element.22), channel_id=1, source_target_pairs={{0,4},{4,8},{8,12},{12,0},{1,5},{5,9},{9,13},{13,1},{2,6},{6,10},{... | collective-permute-start | bytes 2359304 | tf_op jit(solution)/shard_map/ppermute | solution.py:61
  54.3 15.3 %collective-permute-start.2 = (bf16[2,384,512]{2,1,0:T(8,128)(2,1)}, bf16[2,384,512]{2,1,0:T(8,128)(2,1)}, u32[]{:S(2)}, u32[]{:S(2)}) collective-permute-start(bf16[2,384,512]{2,1,0:T(8,128)(2,1)} %get-tuple-element.21), channel_id=1, source_target_pairs={{0,12},{4,0},{8,4},{12,8},{1,13},{5,1},{9,5},{13,9},{2,14},{6,2},{... | collective-permute-start | bytes 2359304 | tf_op jit(solution)/shard_map/ppermute | solution.py:61
  59.4 16.8 %collective-permute-start.1 = (bf16[2,384,512]{2,1,0:T(8,128)(2,1)}, bf16[2,384,512]{2,1,0:T(8,128)(2,1)}, u32[]{:S(2)}, u32[]{:S(2)}) collective-permute-start(bf16[2,384,512]{2,1,0:T(8,128)(2,1)} %get-tuple-element.21), channel_id=1, source_target_pairs={{0,4},{4,8},{8,12},{12,0},{1,5},{5,9},{9,13},{13,1},{2,6},{6,10},{... | collective-permute-start | bytes 2359304 | tf_op jit(solution)/shard_map/ppermute | solution.py:61
  61.4 16.3 %collective-permute-start.3 = (bf16[2,384,512]{2,1,0:T(8,128)(2,1)}, bf16[2,384,512]{2,1,0:T(8,128)(2,1)}, u32[]{:S(2)}, u32[]{:S(2)}) collective-permute-start(bf16[2,384,512]{2,1,0:T(8,128)(2,1)} %get-tuple-element.22), channel_id=1, source_target_pairs={{0,12},{4,0},{8,4},{12,8},{1,13},{5,1},{9,5},{13,9},{2,14},{6,2},{... | collective-permute-start | bytes 2359304 | tf_op jit(solution)/shard_map/ppermute | solution.py:61
  67.7 17.0 %collective-permute-start.4 = (bf16[2,384,512]{2,1,0:T(8,128)(2,1)S(1)}, bf16[2,384,512]{2,1,0:T(8,128)(2,1)}, u32[]{:S(2)}, u32[]{:S(2)}) collective-permute-start(bf16[2,384,512]{2,1,0:T(8,128)(2,1)S(1)} %collective-permute-done.refs_1_), channel_id=1, source_target_pairs={{0,4},{4,8},{8,12},{12,0},{1,5},{5,9},{9,13},{13,1},{2,6},{6,10},{... | collective-permute-start | bytes 2359304 | tf_op jit(solution)/shard_map/ppermute | solution.py:61
  69.6 16.5 %collective-permute-start.5 = (bf16[2,384,512]{2,1,0:T(8,128)(2,1)}, bf16[2,384,512]{2,1,0:T(8,128)(2,1)}, u32[]{:S(2)}, u32[]{:S(2)}) collective-permute-start(bf16[2,384,512]{2,1,0:T(8,128)(2,1)} %collective-permute-done.2.refs_3_), channel_id=1, source_target_pairs={{0,12},{4,0},{8,4},{12,8},{1,13},{5,1},{9,5},{13,9},{2,14},{6,2},{... | collective-permute-start | bytes 2359304 | tf_op jit(solution)/shard_map/ppermute | solution.py:61
  94.2 3.6 %copy-start = (bf16[17920,256]{1,0:T(8,128)(2,1)S(1)}, bf16[17920,256]{1,0:T(8,128)(2,1)}, u32[]{:S(2)}) copy-start(bf16[17920,256]{1,0:T(8,128)(2,1)} %all-gather.3.cloned.1.call-done) | copy-start | bytes 27525124
  97.8 16.6 %copy-start.1 = (bf16[17920,256]{1,0:T(8,128)(2,1)S(1)}, bf16[17920,256]{1,0:T(8,128)(2,1)}, u32[]{:S(2)}) copy-start(bf16[17920,256]{1,0:T(8,128)(2,1)} %all-gather.3.cloned.1.call-done) | copy-start | bytes 27525124
  107.3 16.6 %collective-permute-start.10 = (bf16[48,5120]{1,0:T(8,128)(2,1)S(1)}, bf16[48,5120]{1,0:T(8,128)(2,1)S(1)}, u32[]{:S(2)}, u32[]{:S(2)}) collective-permute-start(bf16[48,5120]{1,0:T(8,128)(2,1)S(1)} %get-tuple-element.20), channel_id=1, source_target_pairs={{0,3},{1,0},{2,1},{3,2},{4,7},{5,4},{6,5},{7,6},{8,11},{9,8},{10,9... | collective-permute-start | bytes 1474568 | tf_op jit(solution)/shard_map/ppermute | solution.py:61
  110.1 15.9 %collective-permute-start.6 = (bf16[48,5120]{1,0:T(8,128)(2,1)S(1)}, bf16[48,5120]{1,0:T(8,128)(2,1)S(1)}, u32[]{:S(2)}, u32[]{:S(2)}) collective-permute-start(bf16[48,5120]{1,0:T(8,128)(2,1)S(1)} %get-tuple-element.16), channel_id=1, source_target_pairs={{0,1},{1,2},{2,3},{3,0},{4,5},{5,6},{6,7},{7,4},{8,9},{9,10},{10,1... | collective-permute-start | bytes 1474568 | tf_op jit(solution)/shard_map/ppermute | solution.py:61
  116.9 14.4 %collective-permute-start.8 = (bf16[48,5120]{1,0:T(8,128)(2,1)S(1)}, bf16[48,5120]{1,0:T(8,128)(2,1)S(1)}, u32[]{:S(2)}, u32[]{:S(2)}) collective-permute-start(bf16[48,5120]{1,0:T(8,128)(2,1)S(1)} %get-tuple-element.17), channel_id=1, source_target_pairs={{0,3},{1,0},{2,1},{3,2},{4,7},{5,4},{6,5},{7,6},{8,11},{9,8},{10,9... | collective-permute-start | bytes 1474568 | tf_op jit(solution)/shard_map/ppermute | solution.py:61
  118.8 12.5 %collective-permute-start.9 = (bf16[48,5120]{1,0:T(8,128)(2,1)S(1)}, bf16[48,5120]{1,0:T(8,128)(2,1)S(1)}, u32[]{:S(2)}, u32[]{:S(2)}) collective-permute-start(bf16[48,5120]{1,0:T(8,128)(2,1)S(1)} %get-tuple-element.18), channel_id=1, source_target_pairs={{0,1},{1,2},{2,3},{3,0},{4,5},{5,6},{6,7},{7,4},{8,9},{9,10},{10,1... | collective-permute-start | bytes 1474568 | tf_op jit(solution)/shard_map/ppermute | solution.py:61
  124.1 11.9 %collective-permute-start.11 = (bf16[48,5120]{1,0:T(8,128)(2,1)S(1)}, bf16[48,5120]{1,0:T(8,128)(2,1)S(1)}, u32[]{:S(2)}, u32[]{:S(2)}) collective-permute-start(bf16[48,5120]{1,0:T(8,128)(2,1)S(1)} %shard_map.88), channel_id=1, source_target_pairs={{0,3},{1,0},{2,1},{3,2},{4,7},{5,4},{6,5},{7,6},{8,11},{9,8},{10,9... | collective-permute-start | bytes 1474568 | tf_op jit(solution)/shard_map/ppermute | solution.py:61
  126.1 11.5 %collective-permute-start.7 = (bf16[48,5120]{1,0:T(8,128)(2,1)S(1)}, bf16[48,5120]{1,0:T(8,128)(2,1)S(1)}, u32[]{:S(2)}, u32[]{:S(2)}) collective-permute-start(bf16[48,5120]{1,0:T(8,128)(2,1)S(1)} %shard_map.87), channel_id=1, source_target_pairs={{0,1},{1,2},{2,3},{3,0},{4,5},{5,6},{6,7},{7,4},{8,9},{9,10},{10,1... | collective-permute-start | bytes 1474568 | tf_op jit(solution)/shard_map/ppermute | solution.py:61
  138.9 4.7 %copy-start.8 = (f32[1280]{0:T(1024)S(1)}, f32[1280]{0:T(1024)}, u32[]{:S(2)}) copy-start(f32[1280]{0:T(1024)} %param.13) | copy-start | bytes 15364
  138.9 15.3 %copy-start.3 = (bf16[24,5120]{1,0:T(8,128)(2,1)S(1)}, bf16[24,5120]{1,0:T(8,128)(2,1)}, u32[]{:S(2)}) copy-start(bf16[24,5120]{1,0:T(8,128)(2,1)} %patches_ref.1) | copy-start | bytes 737284
  138.9 15.3 %all-to-all-start.2 = ((bf16[4,24,5120]{2,1,0:T(8,128)(2,1)}), bf16[4,24,5120]{2,1,0:T(8,128)(2,1)S(1)}, u32[]{:S(2)}, u32[]{:S(2)}) async-start(bf16[4,24,5120]{2,1,0:T(8,128)(2,1)} %bitcast.6), calls=%async_computation.2 | async-start | bytes 1966080 | tf_op jit(solution)/shard_map/all_to_all | solution.py:52
Sparse Core Ops, SparseCore 0:
  9.5 84.6 all-gather.2

commit v3 on v2

v3 whole, which is shorter than its diff:
```python
import jax
import jax.numpy as jnp
from jax import lax
from jax.experimental import pallas as pl
from jax.experimental.pallas import tpu as pltpu
from jax.sharding import PartitionSpec as P

VIT = 1280
MERGE = 4
PROMPTS = 32
ROLLOUTS = 16
SIDE = 4
SLOTS = 50
PAD_SLOTS = 64
OWN = 24
ROWS = OWN * ROLLOUTS
D_LLM = 8192
COLS = D_LLM // ROLLOUTS
HID = 5120
HID_OWN = HID // ROLLOUTS
IN_OWN = HID // PROMPTS
W2_COLS = D_LLM // PROMPTS
PART = IN_OWN // SIDE
PART_PAD = 48
W1_ROWS = SIDE * PART_PAD
W_ROWS = HID_OWN + W1_ROWS + PART_PAD
IN_PAD = PROMPTS * PART_PAD
HALF = IN_PAD // (2 * MERGE)
AXES = ("prompt", "rollout")
F32 = jnp.float32
BF16 = jnp.bfloat16
VMEM = pl.BlockSpec(memory_space=pltpu.VMEM)
SMEM = pl.BlockSpec(memory_space=pltpu.SMEM)
HBM = pl.BlockSpec(memory_space=pltpu.HBM)


def gelu_slope(value):
    return (
        0.5 * (1.0 + jax.scipy.special.erf(value * 0.7071067811865476))
        + value * jnp.exp(-0.5 * value * value) * 0.3989422804014327
    )


def dot_t(left, right):
    return lax.dot_general(left, right, (((1,), (1,)), ((), ())), preferred_element_type=F32)


def line_groups(phase):
    groups = []
    for prompt in range(PROMPTS):
        for other in range(SIDE):
            along_x = (prompt % 2 == 0) == (phase == 0)
            line = [(other * SIDE + i) if along_x else (i * SIDE + other) for i in range(SIDE)]
            groups.append([prompt * ROLLOUTS + r for r in line])
    return groups


def x_groups():
    return [[row * SIDE + i for i in range(SIDE)] for row in range(PROMPTS * SIDE)]


def exchange(blocks, groups):
    return lax.all_to_all(
        blocks, AXES, split_axis=0, concat_axis=0, axis_index_groups=groups, tiled=True
    )


def exchange_all(blocks):
    return lax.all_to_all(blocks, "rollout", split_axis=0, concat_axis=0, tiled=True)


def shift(value, phase, by):
    pairs = []
    for line in line_groups(phase):
        pairs += [(line[i], line[(i + by) % SIDE]) for i in range(SIDE)]
    return lax.ppermute(value, AXES, pairs)


def split_kernel(w1_ref, out_ref):
    rows = w1_ref[...].astype(F32)
    zeros = jnp.zeros((PART_PAD - PART, HID_OWN), F32)
    for i in range(SIDE):
        part = jnp.concatenate([rows[i * PART : (i + 1) * PART], zeros], axis=0)
        out_ref[i] = part.astype(BF16)


def weights_kernel(w2_ref, w1_ref, out_ref):
    out_ref[0:HID_OWN, :] = w2_ref[...]
    for k in range(SIDE):
        base = HID_OWN + k * PART_PAD
        out_ref[base : base + PART_PAD, :] = w1_ref[k, :, 0:256]
    rest = jnp.concatenate([w1_ref[k, :, 256:HID_OWN] for k in range(SIDE)], axis=1)
    out_ref[HID_OWN + W1_ROWS : W_ROWS, :] = rest


def pack_kernel(count_ref, ids_ref, grads_ref, out_ref, meta):
    live = lax.broadcasted_iota(jnp.int32, (1, SLOTS), 1) < count_ref[0, 0]
    place = jnp.where(live, ids_ref[...] + 1, 0)
    meta[...] = jnp.zeros((8, COLS), F32)
    meta[2:3, 0:SLOTS] = (place >> 4).astype(F32)
    meta[3:4, 0:SLOTS] = (place & 15).astype(F32)
    codes = meta[...]
    zeros = jnp.zeros((8, COLS), F32)
    for k in range(ROLLOUTS):
        cols = pl.ds(k * COLS, COLS)
        out_ref[k, 0:48, :] = grads_ref[0:48, cols]
        two = jnp.concatenate([grads_ref[48:SLOTS, cols].astype(F32), zeros[0:6]], axis=0)
        out_ref[k, 48:64, :] = jnp.concatenate([two + codes, zeros], axis=0).astype(BF16)


def sum_kernel(recv_ref, out_ref):
    rows = (lax.broadcasted_iota(jnp.int32, (ROWS, 4 * PAD_SLOTS), 0) + 1).astype(F32)
    total = jnp.zeros((ROWS, COLS), F32)
    for g in range(ROLLOUTS // 4):
        codes = jnp.zeros((8, 4 * PAD_SLOTS), F32)
        for k in range(4):
            tile = recv_ref[4 * g + k, 48:64, 0 : 4 * PAD_SLOTS].astype(F32)[0:8]
            codes = codes + (pltpu.roll(tile, PAD_SLOTS * k, 1) if k else tile)
        row = codes[2:3] * 16.0 + codes[3:4]
        onehot = jnp.where(rows == row, 1.0, 0.0).astype(BF16)
        block = recv_ref[4 * g : 4 * g + 4].reshape(4 * PAD_SLOTS, COLS)
        total = total + jnp.dot(onehot, block, preferred_element_type=F32)
    value = total.astype(BF16)
    for k in range(SIDE):
        out_ref[k] = value


GATHERED = (
    (0, (0, 1, 2, 3), 0),
    (1, (0, 1), 3),
    (2, (2, 3), 3),
    (3, (2, 3), 1),
    (4, (0, 1), 1),
    (5, (0, 1), 2),
    (6, (2, 3), 2),
)


def act_kernel(w_ref, *refs):
    sums, (slope_ref, act_ref, w2, sems) = refs[:7], refs[7:]
    even = lax.axis_index("prompt") % 2 == 0
    rollout = lax.axis_index("rollout")
    own = jnp.where(even, rollout // SIDE, rollout % SIDE)
    slots, copies = [], []
    for operand, places, offset in GATHERED:
        for n, k in enumerate(places):
            other = lax.rem(own + offset, SIDE)
            block = jnp.where(even, other * SIDE + k, k * SIDE + other)
            i = len(slots)
            pair = [
                pltpu.make_async_copy(
                    w_ref.at[2 * block + h, 0:HID_OWN],
                    w2.at[:, pl.ds((2 * i + h) * W2_COLS, W2_COLS)],
                    sems.at[i, h],
                )
                for h in range(2)
            ]
            for copy in pair:
                copy.start()
            copies.append(pair)
            slots.append((sums[operand], n))
    hidden = None
    for i, (ref, n) in enumerate(slots):
        for copy in copies[i]:
            copy.wait()
        part = dot_t(ref[n], w2[:, i * COLS : (i + 1) * COLS])
        hidden = part if hidden is None else hidden + part
    act = (hidden * slope_ref[...]).astype(BF16)
    for k in range(SIDE):
        act_ref[k] = act


def upstream_kernel(w_ref, act_ref, out_ref, w1, sems):
    copies = []
    for m in range(MERGE):
        prompts = pl.ds(m * 8, 8)
        copies.append(pltpu.make_async_copy(w_ref.at[prompts, HID_OWN:W_ROWS], w1.at[prompts], sems.at[m]))
        copies[m].start()
    rest = jnp.concatenate([act_ref[k, :, 256:HID_OWN] for k in range(SIDE)], axis=1)
    for m in range(MERGE):
        copies[m].wait()
        total = None
        for k in range(SIDE + 1):
            w = w1[8 * m : 8 * m + 8, k * PART_PAD : (k + 1) * PART_PAD].reshape(8 * PART_PAD, 256)
            part = dot_t(act_ref[k, :, 0:256] if k < SIDE else rest, w)
            total = part if total is None else total + part
        blocks = total.reshape(ROLLOUTS, OWN, 8 * PART_PAD).astype(BF16)
        out_ref[:, :, 8 * PART_PAD * m : 8 * PART_PAD * (m + 1)] = blocks


def norm_kernel(recv_ref, order_ref, patches_ref, gain_ref, out_ref):
    parts = []
    for i in range(SIDE):
        total = None
        for s in range(SIDE):
            part = recv_ref[s * SIDE + i].astype(F32)
            total = part if total is None else total + part
        parts.append(total)
    rows = []
    for g in range(2 * MERGE):
        whole = jnp.concatenate([part[:, g * HALF : (g + 1) * HALF] for part in parts], axis=1)
        high = whole.astype(BF16)
        rows += [high, (whole - high.astype(F32)).astype(BF16)]
    ordered = jnp.dot(
        jnp.concatenate([r.astype(F32) for r in rows], axis=0).astype(BF16),
        order_ref[...],
        preferred_element_type=F32,
    )
    for m in range(MERGE):
        halves = []
        for g in (2 * m, 2 * m + 1):
            at = 2 * g * OWN
            halves.append(ordered[at : at + OWN] + ordered[at + OWN : at + 2 * OWN])
        upstream = jnp.concatenate(halves, axis=1)
        cols = slice(m * VIT, (m + 1) * VIT)
        inputs = patches_ref[:, cols].astype(F32)
        scaled = upstream * gain_ref[...]
        inverse = lax.rsqrt(jnp.mean(inputs * inputs, axis=-1, keepdims=True) + 1e-06)
        inner = jnp.mean(scaled * inputs, axis=-1, keepdims=True)
        result = inverse * scaled - inputs * inverse * inverse * inverse * inner
        out_ref[:, cols] = result.astype(BF16)


def call(kernel, shape, in_specs, flops=0, moved=0, vmem=16, scratch=()):
    return pl.pallas_call(
        kernel,
        out_shape=jax.ShapeDtypeStruct(shape, BF16),
        in_specs=in_specs,
        out_specs=VMEM,
        scratch_shapes=list(scratch),
        cost_estimate=pl.CostEstimate(flops=flops, bytes_accessed=moved, transcendentals=0),
        compiler_params=pltpu.CompilerParams(vmem_limit_bytes=vmem << 20),
    )


def column_order():
    lane = lax.broadcasted_iota(jnp.int32, (SIDE * HALF, HALF // PART_PAD * IN_OWN), 0)
    col = lax.broadcasted_iota(jnp.int32, lane.shape, 1)
    place, prompt, row = lane // HALF, lane % HALF // PART_PAD, lane % PART_PAD
    return ((prompt * IN_OWN + place * PART + row == col) & (row < PART)).astype(BF16)


def per_device(row_grads, used_ids, used_count, pre_act, patches, ln_gain, w_fc2, w_fc1):
    w1_part = exchange(call(split_kernel, (SIDE, PART_PAD, HID_OWN), [VMEM])(w_fc1), x_groups())
    weights = call(weights_kernel, (W_ROWS, 256), [VMEM] * 2)(w_fc2, w1_part)
    weights = lax.all_gather(weights, "prompt", axis=0, tiled=False)

    outgoing = call(
        pack_kernel, (ROLLOUTS, PAD_SLOTS, COLS), [SMEM, VMEM, VMEM], scratch=[pltpu.VMEM((8, COLS), F32)]
    )(used_count, used_ids[0], row_grads[0, 0])
    summed = call(sum_kernel, (SIDE, ROWS, COLS), [VMEM])(exchange_all(outgoing))
    line = exchange(summed, line_groups(0))
    a1, b1 = shift(line[:2], 1, 1), shift(line[2:], 1, -1)
    a2, b2 = shift(line[2:], 1, 1), shift(line[:2], 1, -1)
    a3, b3 = shift(a1, 1, 1), shift(b1, 1, -1)

    act = call(
        act_kernel,
        (SIDE, ROWS, HID_OWN),
        [HBM] + [VMEM] * 8,
        flops=1 << 31,
        moved=12 << 20,
        vmem=24,
        scratch=[pltpu.VMEM((HID_OWN, D_LLM), BF16), pltpu.SemaphoreType.DMA((ROLLOUTS, 2))],
    )(weights, line, a1, a2, b1, b2, a3, b3, gelu_slope(pre_act.astype(F32)))
    act_line = exchange(act, x_groups())
    partial = call(
        upstream_kernel,
        (ROLLOUTS, OWN, IN_PAD),
        [HBM, VMEM],
        flops=5 << 28,
        moved=6 << 20,
        vmem=24,
        scratch=[
            pltpu.VMEM((PROMPTS, W_ROWS - HID_OWN, 256), BF16),
            pltpu.SemaphoreType.DMA((MERGE,)),
        ],
    )(weights, act_line)
    return call(norm_kernel, (OWN, HID), [VMEM] * 4)(
        exchange_all(partial), column_order(), patches, ln_gain.reshape(1, VIT)
    )


def solution(mesh):
    return jax.shard_map(
        per_device,
        mesh=mesh,
        in_specs=(
            P("prompt", "rollout", None, None),
            P("prompt", "rollout", None),
            P("prompt", "rollout"),
            P("prompt", "rollout"),
            P(("prompt", "rollout"), None),
            P(),
            P("rollout", "prompt"),
            P("prompt", "rollout"),
        ),
        out_specs=P(("prompt", "rollout"), None),
        check_vma=False,
    )
```

time: 165 us -> 175 us (1.061)
  blocking collectives: 38.8 us -> 63 us
  starting transfers between devices: 47.1 us -> 28.5 us
  local copies, waits for them, and re-layouts: 8.72 us -> 14.7 us
  other arithmetic: 0.28 us -> 3.05 us
  waiting for transfers between devices: 36.8 us -> 34.1 us
    all_to_all x1 -> x3, blocking collectives: 17.1 us -> 46.3 us  [exchange(): lax.all_to_all(blocks, AXES, split_axis=0, concat_axis=0, axis_index_grou...]
    ppermute x12 -> x6, starting transfers between devices: 42.4 us -> 21.2 us  [shift(): return lax.ppermute(value, AXES, pairs)]
    ppermute x12 -> x6, waiting for transfers between devices: 18.2 us -> 10.1 us  [shift(): return lax.ppermute(value, AXES, pairs)]
    all_to_all x1, blocking collectives: 21.7 us -> 16.7 us  [exchange_all(): lax.all_to_all(blocks, 'rollout', split_axis=0, concat_axis=0, tiled=True)]
    unnamed x19 -> x22, local copies, waits for them, and re-layouts: 7.48 us -> 10.9 us
    all_to_all x1, waiting for transfers between devices: 10.5 us -> 13.3 us  [exchange_all(): lax.all_to_all(blocks, 'rollout', split_axis=0, concat_axis=0, tiled=True)]
    all_gather x1, waiting for transfers between devices: 8.1 us -> 10.7 us  [per_device(): weights = lax.all_gather(weights, 'prompt', axis=0, tiled=False)]
    all_to_all x1, starting transfers between devices: 4.74 us -> 7.3 us  [exchange_all(): lax.all_to_all(blocks, 'rollout', split_axis=0, concat_axis=0, tiled=True)]
  transfers between devices with their start and end apart: 14 -> 8, of which waited for: 9 -> 6; matrix products, arithmetic and copies ran while one was open for 1% -> 3% of each run, Pallas kernels for 2% -> 0%
where the time goes in v3:
time: 175 us; the launch traced here: 173 us
  blocking collectives  63 us (36%)
  waiting for transfers between devices  34.1 us (19%)
  starting transfers between devices  28.5 us (16%)
  Pallas kernels  14.9 us (9%)
  local copies, waits for them, and re-layouts  14.7 us (8%)
  between operations  14.3 us (8%)
  other arithmetic  3.05 us (2%)
    all_to_all x3, blocking collectives, exchange(): lax.all_to_all(blocks, AXES, split_axis=0, concat_axis=0, axis_index_grou...  46.3 us
    ppermute x6, starting transfers between devices, shift(): return lax.ppermute(value, AXES, pairs)  21.2 us
    all_to_all x1, blocking collectives, exchange_all(): lax.all_to_all(blocks, 'rollout', split_axis=0, concat_axis=0, tiled=True)  16.7 us
    all_to_all x1, waiting for transfers between devices, exchange_all(): lax.all_to_all(blocks, 'rollout', split_axis=0, concat_axis=0, tiled=True)  13.3 us
    unnamed x22, local copies, waits for them, and re-layouts  10.9 us
    all_gather x1, waiting for transfers between devices, per_device(): weights = lax.all_gather(weights, 'prompt', axis=0, tiled=False)  10.7 us
    ppermute x6, waiting for transfers between devices, shift(): return lax.ppermute(value, AXES, pairs)  10.1 us
    pallas_call x1, Pallas kernels, per_device(): call(act_kernel, (SIDE, ROWS, HID_OWN), [HBM] + [VMEM] * 8, flops=1 << 31...  7.56 us
  transfers between devices with their start and end apart: 8, of which 6 were waited for; matrix products, arithmetic and copies ran while one was open for 3% of the time, Pallas kernels for 0%

profile of v3, /device:TPU:6, one launch (start us, length us, event | category | flops | bytes accessed | tf_op | source)
XLA Modules:
  0.0 172.5 jit_solution(15290597499082359941)
XLA Ops:
  6.5 1.0 copy-done.7
  7.5 12.2 %all_to_all.25.w1_ref = bf16[4,48,320]{2,1,0:T(8,128)(2,1)S(1)} all-to-all(bf16[4,48,320]{2,1,0:T(8,128)(2,1)S(1)} %shard_map.82), channel_id=1, replica_groups={{0,1,2,3},{4,5,6,7},{8,9,10,11},{12,13,14,15},{16,17,18,19},{20,21,22,2..., dimensions={0} | all-to-all | bytes 245760 | tf_op jit(solution)/shard_map/all_to_all | solution.py:63
  19.7 0.9 copy-done.6
  20.7 0.8 shard_map.83
  22.1 0.6 copy-done.8
  22.9 16.7 %all_to_all.26.recv_ref = bf16[16,64,512]{2,1,0:T(8,128)(2,1)S(1)} all-to-all(bf16[16,64,512]{2,1,0:T(8,128)(2,1)S(1)} %shard_map.84), channel_id=1, replica_groups=mesh['prompt'=32,'rollout'=16] {'rollout'}, dimensions={0} | all-to-all | bytes 2097152 | tf_op jit(solution)/shard_map/all_to_all | solution.py:69
  40.2 16.8 %all_to_all.27.refs_0_ = bf16[4,384,512]{2,1,0:T(8,128)(2,1)S(1)} all-to-all(bf16[4,384,512]{2,1,0:T(8,128)(2,1)S(1)} %shard_map.85), channel_id=1, replica_groups={{0,1,2,3},{4,5,6,7},{8,9,10,11},{12,13,14,15},{16,20,24,28},{17,21,25,2..., dimensions={0} | all-to-all | bytes 3145728 | tf_op jit(solution)/shard_map/all_to_all | solution.py:63
  57.0 1.3 fusion.22
  58.3 1.9 %collective-permute-start = (bf16[2,384,512]{2,1,0:T(8,128)(2,1)}, bf16[2,384,512]{2,1,0:T(8,128)(2,1)S(1)}, u32[]{:S(2)}, u32[]{:S(2)}) collective-permute-start(bf16[2,384,512]{2,1,0:T(8,128)(2,1)} %get-tuple-element.6), channel_id=1, source_target_pairs={{0,4},{4,8},{8,12},{12,0},{1,5},{5,9},{9,13},{13,1},{2,6},{6,10},{... | collective-permute-start | bytes 2359304 | tf_op jit(solution)/shard_map/ppermute | solution.py:76
  60.2 5.1 %collective-permute-start.2 = (bf16[2,384,512]{2,1,0:T(8,128)(2,1)}, bf16[2,384,512]{2,1,0:T(8,128)(2,1)}, u32[]{:S(2)}, u32[]{:S(2)}) collective-permute-start(bf16[2,384,512]{2,1,0:T(8,128)(2,1)} %get-tuple-element.5), channel_id=1, source_target_pairs={{0,12},{4,0},{8,4},{12,8},{1,13},{5,1},{9,5},{13,9},{2,14},{6,2},{... | collective-permute-start | bytes 2359304 | tf_op jit(solution)/shard_map/ppermute | solution.py:76
  65.3 1.9 %collective-permute-start.1 = (bf16[2,384,512]{2,1,0:T(8,128)(2,1)}, bf16[2,384,512]{2,1,0:T(8,128)(2,1)}, u32[]{:S(2)}, u32[]{:S(2)}) collective-permute-start(bf16[2,384,512]{2,1,0:T(8,128)(2,1)} %get-tuple-element.5), channel_id=1, source_target_pairs={{0,4},{4,8},{8,12},{12,0},{1,5},{5,9},{9,13},{13,1},{2,6},{6,10},{... | collective-permute-start | bytes 2359304 | tf_op jit(solution)/shard_map/ppermute | solution.py:76
  67.3 5.1 %collective-permute-start.3 = (bf16[2,384,512]{2,1,0:T(8,128)(2,1)}, bf16[2,384,512]{2,1,0:T(8,128)(2,1)}, u32[]{:S(2)}, u32[]{:S(2)}) collective-permute-start(bf16[2,384,512]{2,1,0:T(8,128)(2,1)} %get-tuple-element.6), channel_id=1, source_target_pairs={{0,12},{4,0},{8,4},{12,8},{1,13},{5,1},{9,5},{13,9},{2,14},{6,2},{... | collective-permute-start | bytes 2359304 | tf_op jit(solution)/shard_map/ppermute | solution.py:76
  72.4 1.2 collective-permute-done.refs_1_
  73.6 1.9 %collective-permute-start.4 = (bf16[2,384,512]{2,1,0:T(8,128)(2,1)S(1)}, bf16[2,384,512]{2,1,0:T(8,128)(2,1)}, u32[]{:S(2)}, u32[]{:S(2)}) collective-permute-start(bf16[2,384,512]{2,1,0:T(8,128)(2,1)S(1)} %collective-permute-done.refs_1_), channel_id=1, source_target_pairs={{0,4},{4,8},{8,12},{12,0},{1,5},{5,9},{9,13},{13,1},{2,6},{6,10},{... | collective-permute-start | bytes 2359304 | tf_op jit(solution)/shard_map/ppermute | solution.py:76
  75.5 5.2 %collective-permute-start.5 = (bf16[2,384,512]{2,1,0:T(8,128)(2,1)}, bf16[2,384,512]{2,1,0:T(8,128)(2,1)}, u32[]{:S(2)}, u32[]{:S(2)}) collective-permute-start(bf16[2,384,512]{2,1,0:T(8,128)(2,1)} %collective-permute-done.2.refs_3_), channel_id=1, source_target_pairs={{0,12},{4,0},{8,4},{12,8},{1,13},{5,1},{9,5},{13,9},{2,14},{6,2},{... | collective-permute-start | bytes 2359304 | tf_op jit(solution)/shard_map/ppermute | solution.py:76
  80.7 1.0 copy.13
  81.8 1.3 fusion.11.refs_7_
  83.6 7.0 %collective-permute-done.4.refs_5_ = bf16[2,384,512]{2,1,0:T(8,128)(2,1)} collective-permute-done((bf16[2,384,512]{2,1,0:T(8,128)(2,1)S(1)}, bf16[2,384,512]{2,1,0:T(8,128)(2,1)}, u32[]{:S(2)}, u32[]{:S(2)}) %collective-permute-start.4) | collective-permute-done | bytes 786464 | tf_op jit(solution)/shard_map/ppermute | solution.py:76
  90.5 1.5 collective-permute-done.5.refs_6_
  92.0 10.7 %all-gather.3.cloned.1.call-done = bf16[17920,256]{1,0:T(8,128)(2,1)} async-done(((bf16[560,256]{1,0:T(8,128)(2,1)}), bf16[17920,256]{1,0:T(8,128)(2,1)}) %all-gather.3.cloned.1.call-update) | async-done | bytes 9175056 | tf_op jit(solution)/shard_map/all_gather | solution.py:246
  102.7 3.6 %copy-done = bf16[17920,256]{1,0:T(8,128)(2,1)S(1)} copy-done((bf16[17920,256]{1,0:T(8,128)(2,1)S(1)}, bf16[17920,256]{1,0:T(8,128)(2,1)}, u32[]{:S(2)}) %copy-start) | copy-done | bytes 9175064
  106.3 1.1 copy-done.4
  107.4 7.6 %shard_map.86 = bf16[4,384,320]{2,1,0:T(8,128)(2,1)S(1)} custom-call(bf16[32,560,256]{2,1,0:T(8,128)(2,1)S(1)} %bitcast.3, bf16[4,384,512]{2,1,0:T(8,128)(2,1)S(1)} %all_to_all.27.refs_0_, bf16[2,384,512]{2,1,0:T(8,128)(2,1)S(1)} %copy-done.4, bf16[2,384,512]{2,1,0:T(8,128)(2,1)} %collective-permute-done.1.refs_2_, ...), custom_call_target="tpu_custom_call" | custom-call | flops 2147483648 | bytes 12582912 | tf_op jit(solution)/shard_map/pallas_call | solution.py:257
  115.0 0.7 copy.17
  115.7 17.3 %all_to_all.28 = bf16[4,384,320]{1,2,0:T(8,128)(2,1)S(1)} all-to-all(bf16[4,384,320]{1,2,0:T(8,128)(2,1)S(1)} %copy.17), channel_id=1, replica_groups={{0,1,2,3},{4,5,6,7},{8,9,10,11},{12,13,14,15},{16,17,18,19},{20,21,22,2..., dimensions={0} | all-to-all | bytes 1966080 | tf_op jit(solution)/shard_map/all_to_all | solution.py:63
  133.0 0.8 copy.18.act_ref
  133.8 3.6 %copy-done.1 = bf16[17920,256]{1,0:T(8,128)(2,1)S(1)} copy-done((bf16[17920,256]{1,0:T(8,128)(2,1)S(1)}, bf16[17920,256]{1,0:T(8,128)(2,1)}, u32[]{:S(2)}) %copy-start.1) | copy-done | bytes 9175064
  137.4 4.3 %shard_map.87 = bf16[16,24,1536]{2,1,0:T(8,128)(2,1)} custom-call(bf16[32,560,256]{2,1,0:T(8,128)(2,1)S(1)} %bitcast.4, bf16[4,384,320]{2,1,0:T(8,128)(2,1)S(1)} %copy.18.act_ref), custom_call_target="tpu_custom_call" | custom-call | flops 1342177280 | bytes 6291456 | tf_op jit(solution)/shard_map/pallas_call | solution.py:267
  141.8 7.3 %all-to-all-start.4 = ((bf16[16,24,1536]{2,1,0:T(8,128)(2,1)}), bf16[16,24,1536]{2,1,0:T(8,128)(2,1)S(1)}, u32[]{:S(2)}, u32[]{:S(2)}) async-start(bf16[16,24,1536]{2,1,0:T(8,128)(2,1)} %shard_map.87), calls=%async_computation.4 | async-start | bytes 2359296 | tf_op jit(solution)/shard_map/all_to_all | solution.py:69
  149.1 1.7 fusion.7.order_ref
  150.9 13.3 %all-to-all-done.4.recv_ref = bf16[16,24,1536]{2,1,0:T(8,128)(2,1)S(1)} async-done(((bf16[16,24,1536]{2,1,0:T(8,128)(2,1)}), bf16[16,24,1536]{2,1,0:T(8,128)(2,1)S(1)}, u32[]{:S(2)}, u32[]{:S(2)}) %all-to-all-start.4) | async-done | bytes 1179680 | tf_op jit(solution)/shard_map/all_to_all | solution.py:69
  164.2 1.5 shard_map.88
  (30 shorter events, 1.3 us)
Async XLA Ops:
  6.5 15.6 %copy-start.2 = (bf16[1,1,50,8192]{3,2,1,0:T(8,128)(2,1)S(1)}, bf16[1,1,50,8192]{3,2,1,0:T(8,128)(2,1)}, u32[]{:S(2)}) copy-start(bf16[1,1,50,8192]{3,2,1,0:T(8,128)(2,1)} %param.8) | copy-start | bytes 2457604
  6.5 96.2 %all-gather.3.cloned.1.call-start = ((), (), s32[]{:S(2)}) async-start(), calls=%async_computation.5 | async-start | bytes 9461760 | tf_op jit(solution)/shard_map/all_gather | solution.py:246
  6.5 1.0 copy-start.7
  19.7 0.9 copy-start.6
  22.1 0.7 copy-start.8
  57.0 23.7 %copy-start.9 = (bf16[384,320]{0,1:T(8,128)(2,1)S(1)}, bf16[384,320]{0,1:T(8,128)(2,1)}, u32[]{:S(2)}) copy-start(bf16[384,320]{0,1:T(8,128)(2,1)} %param.11) | copy-start | bytes 737284
  58.3 15.3 %collective-permute-start = (bf16[2,384,512]{2,1,0:T(8,128)(2,1)}, bf16[2,384,512]{2,1,0:T(8,128)(2,1)S(1)}, u32[]{:S(2)}, u32[]{:S(2)}) collective-permute-start(bf16[2,384,512]{2,1,0:T(8,128)(2,1)} %get-tuple-element.6), channel_id=1, source_target_pairs={{0,4},{4,8},{8,12},{12,0},{1,5},{5,9},{9,13},{13,1},{2,6},{6,10},{... | collective-permute-start | bytes 2359304 | tf_op jit(solution)/shard_map/ppermute | solution.py:76
  60.2 15.3 %collective-permute-start.2 = (bf16[2,384,512]{2,1,0:T(8,128)(2,1)}, bf16[2,384,512]{2,1,0:T(8,128)(2,1)}, u32[]{:S(2)}, u32[]{:S(2)}) collective-permute-start(bf16[2,384,512]{2,1,0:T(8,128)(2,1)} %get-tuple-element.5), channel_id=1, source_target_pairs={{0,12},{4,0},{8,4},{12,8},{1,13},{5,1},{9,5},{13,9},{2,14},{6,2},{... | collective-permute-start | bytes 2359304 | tf_op jit(solution)/shard_map/ppermute | solution.py:76
  65.3 17.7 %collective-permute-start.1 = (bf16[2,384,512]{2,1,0:T(8,128)(2,1)}, bf16[2,384,512]{2,1,0:T(8,128)(2,1)}, u32[]{:S(2)}, u32[]{:S(2)}) collective-permute-start(bf16[2,384,512]{2,1,0:T(8,128)(2,1)} %get-tuple-element.5), channel_id=1, source_target_pairs={{0,4},{4,8},{8,12},{12,0},{1,5},{5,9},{9,13},{13,1},{2,6},{6,10},{... | collective-permute-start | bytes 2359304 | tf_op jit(solution)/shard_map/ppermute | solution.py:76
  67.3 16.3 %collective-permute-start.3 = (bf16[2,384,512]{2,1,0:T(8,128)(2,1)}, bf16[2,384,512]{2,1,0:T(8,128)(2,1)}, u32[]{:S(2)}, u32[]{:S(2)}) collective-permute-start(bf16[2,384,512]{2,1,0:T(8,128)(2,1)} %get-tuple-element.6), channel_id=1, source_target_pairs={{0,12},{4,0},{8,4},{12,8},{1,13},{5,1},{9,5},{13,9},{2,14},{6,2},{... | collective-permute-start | bytes 2359304 | tf_op jit(solution)/shard_map/ppermute | solution.py:76
  73.6 29.1 %copy-start.3 = (bf16[2,384,512]{2,1,0:T(8,128)(2,1)}, bf16[2,384,512]{2,1,0:T(8,128)(2,1)S(1)}, u32[]{:S(2)}) copy-start(bf16[2,384,512]{2,1,0:T(8,128)(2,1)S(1)} %collective-permute-done.refs_1_) | copy-start | bytes 2359300
  73.6 17.0 %collective-permute-start.4 = (bf16[2,384,512]{2,1,0:T(8,128)(2,1)S(1)}, bf16[2,384,512]{2,1,0:T(8,128)(2,1)}, u32[]{:S(2)}, u32[]{:S(2)}) collective-permute-start(bf16[2,384,512]{2,1,0:T(8,128)(2,1)S(1)} %collective-permute-done.refs_1_), channel_id=1, source_target_pairs={{0,4},{4,8},{8,12},{12,0},{1,5},{5,9},{9,13},{13,1},{2,6},{6,10},{... | collective-permute-start | bytes 2359304 | tf_op jit(solution)/shard_map/ppermute | solution.py:76
  75.5 16.5 %collective-permute-start.5 = (bf16[2,384,512]{2,1,0:T(8,128)(2,1)}, bf16[2,384,512]{2,1,0:T(8,128)(2,1)}, u32[]{:S(2)}, u32[]{:S(2)}) collective-permute-start(bf16[2,384,512]{2,1,0:T(8,128)(2,1)} %collective-permute-done.2.refs_3_), channel_id=1, source_target_pairs={{0,12},{4,0},{8,4},{12,8},{1,13},{5,1},{9,5},{13,9},{2,14},{6,2},{... | collective-permute-start | bytes 2359304 | tf_op jit(solution)/shard_map/ppermute | solution.py:76
  102.7 3.6 %copy-start = (bf16[17920,256]{1,0:T(8,128)(2,1)S(1)}, bf16[17920,256]{1,0:T(8,128)(2,1)}, u32[]{:S(2)}) copy-start(bf16[17920,256]{1,0:T(8,128)(2,1)} %all-gather.3.cloned.1.call-done) | copy-start | bytes 27525124
  106.3 1.1 copy-start.4
  133.8 3.6 %copy-start.1 = (bf16[17920,256]{1,0:T(8,128)(2,1)S(1)}, bf16[17920,256]{1,0:T(8,128)(2,1)}, u32[]{:S(2)}) copy-start(bf16[17920,256]{1,0:T(8,128)(2,1)} %all-gather.3.cloned.1.call-done) | copy-start | bytes 27525124
  141.7 7.3 %copy-start.10 = (f32[1280]{0:T(1024)S(1)}, f32[1280]{0:T(1024)}, u32[]{:S(2)}) copy-start(f32[1280]{0:T(1024)} %param.13) | copy-start | bytes 15364
  141.7 22.4 %copy-start.5 = (bf16[24,5120]{1,0:T(8,128)(2,1)S(1)}, bf16[24,5120]{1,0:T(8,128)(2,1)}, u32[]{:S(2)}) copy-start(bf16[24,5120]{1,0:T(8,128)(2,1)} %patches_ref.1) | copy-start | bytes 737284
  141.8 22.4 %all-to-all-start.4 = ((bf16[16,24,1536]{2,1,0:T(8,128)(2,1)}), bf16[16,24,1536]{2,1,0:T(8,128)(2,1)S(1)}, u32[]{:S(2)}, u32[]{:S(2)}) async-start(bf16[16,24,1536]{2,1,0:T(8,128)(2,1)} %shard_map.87), calls=%async_computation.4 | async-start | bytes 2359296 | tf_op jit(solution)/shard_map/all_to_all | solution.py:69
Sparse Core Ops, SparseCore 0:
  21.6 81.0 all-gather.2

commit v4 on v2

--- a/solution.py
+++ b/solution.py
@@ -64,8 +64,7 @@
 def place_in_plane():
     rollout = lax.axis_index("rollout")
     even = lax.axis_index("prompt") % 2 == 0
-    y, x = rollout // SIDE, rollout % SIDE
-    return even, jnp.where(even, x, y), jnp.where(even, y, x)
+    return even, jnp.where(even, rollout // SIDE, rollout % SIDE)
 
 
 def weights_kernel(w2_ref, w1_ref, out_ref):
@@ -78,7 +77,7 @@
 
 
 def pack_kernel(count_ref, ids_ref, grads_ref, out_ref, meta):
-    even, _, _ = place_in_plane()
+    even, _ = place_in_plane()
     ids = ids_ref[...]
     owner = (ids * 2731) >> 16
     turned = (owner & 3) * SIDE + (owner >> 2)
@@ -133,9 +132,9 @@
 GATHERED = ((0, (0, 1, 2, 3), 0), (1, (0, 1), 3), (2, (2, 3), 3), (3, (2, 3), 1), (4, (0, 1), 1), (5, (0, 1), 2), (6, (2, 3), 2))
 
 
-def act_kernel(w_ref, *refs):
-    sums, (slope_ref, act_ref, low_ref, high_ref, w2, w1, sems2, sems1) = refs[:7], refs[7:]
-    even, first, second = place_in_plane()
+def mlp_kernel(w_ref, *refs):
+    sums, (slope_ref, out_ref, w2, w1, sems2, sems1) = refs[:7], refs[7:]
+    even, second = place_in_plane()
     slots, copies = [], []
     for operand, places, offset in GATHERED:
         for n, k in enumerate(places):
@@ -161,46 +160,18 @@
             copy.wait()
         part = dot_t(ref[n], w2[:, i * COLS : (i + 1) * COLS])
         hidden = part if hidden is None else hidden + part
-    act_ref[...] = (hidden * slope_ref[...]).astype(BF16)
-    far = lax.rem(first + 2, SIDE)
-    rows = act_ref[pl.ds(pl.multiple_of(far * 96, 96), 96), :]
+    act = (hidden * slope_ref[...]).astype(BF16)
     for copy in late:
         copy.wait()
     for g in range(8):
-        part = dot_t(rows, w1_chunk(w1, g, 4)).astype(BF16)
-        cols = slice(640 * g, 640 * (g + 1))
-        low_ref[:, cols] = part[:48]
-        high_ref[:, cols] = part[48:]
-
-
-def rest_kernel(w_ref, act_ref, right_low, right_high, left_low, left_high, own_ref, w1, sems1):
-    _, first, _ = place_in_plane()
-    late = start_w1(w_ref, w1, sems1)
-    blocks = [
-        act_ref[pl.ds(pl.multiple_of(lax.rem(first + by, SIDE) * 96, 96), 96), :] for by in (1, 3, 0)
-    ]
-    rows = jnp.concatenate(blocks, axis=0)
-    for copy in late:
-        copy.wait()
-    for g in range(8):
-        part = dot_t(rows, w1_chunk(w1, g, 4)).astype(BF16)
-        cols = slice(640 * g, 640 * (g + 1))
-        right_low[:, cols] = part[0:48]
-        right_high[:, cols] = part[48:96]
-        left_low[:, cols] = part[96:144]
-        left_high[:, cols] = part[144:192]
-        own_ref[:, cols] = part[192:288]
-
-
-def pair_kernel(a_ref, b_ref, out_ref):
-    out_ref[...] = (a_ref[...].astype(F32) + b_ref[...].astype(F32)).astype(BF16)
-
-
-def join_kernel(own_ref, low_a, low_b, high_a, high_b, out_ref):
-    low = own_ref[0:48].astype(F32) + low_a[...].astype(F32) + low_b[...].astype(F32)
-    high = own_ref[48:96].astype(F32) + high_a[...].astype(F32) + high_b[...].astype(F32)
-    out_ref[0:48] = low.astype(BF16)
-    out_ref[48:96] = high.astype(BF16)
+        out_ref[:, 640 * g : 640 * (g + 1)] = dot_t(act, w1_chunk(w1, g, 4)).astype(BF16)
+
+
+def add_kernel(recv_ref, out_ref):
+    total = recv_ref[0].astype(F32)
+    for k in range(1, SIDE):
+        total = total + recv_ref[k].astype(F32)
+    out_ref[...] = total.astype(BF16)
 
 
 def norm_kernel(recv_ref, patches_ref, gain_ref, out_ref):
@@ -222,19 +193,16 @@
 ANY = pl.BlockSpec(memory_space=pl.ANY)
 
 
-def call(kernel, shapes, in_specs, flops=0, moved=0, vmem=16, scratch=()):
-    one = not isinstance(shapes[0], tuple)
-    shapes = (shapes,) if one else shapes
-    run = pl.pallas_call(
+def call(kernel, shape, in_specs, flops=0, moved=0, vmem=16, scratch=()):
+    return pl.pallas_call(
         kernel,
-        out_shape=[jax.ShapeDtypeStruct(shape, BF16) for shape in shapes],
+        out_shape=jax.ShapeDtypeStruct(shape, BF16),
         in_specs=in_specs,
-        out_specs=[VMEM] * len(shapes),
+        out_specs=VMEM,
         scratch_shapes=list(scratch),
         cost_estimate=pl.CostEstimate(flops=flops, bytes_accessed=moved, transcendentals=0),
         compiler_params=pltpu.CompilerParams(vmem_limit_bytes=vmem << 20),
     )
-    return (lambda *args: run(*args)[0]) if one else run
 
 
 def per_device(row_grads, used_ids, used_count, pre_act, patches, ln_gain, w_fc2, w_fc1):
@@ -254,36 +222,23 @@
     even = lax.axis_index("prompt") % 2 == 0
     slope = gelu_slope(pre_act.astype(F32)).reshape(SIDE, SIDE, OWN, HID_OWN)
     slope = jnp.where(even, slope.transpose(1, 0, 2, 3), slope).reshape(ROWS, HID_OWN)
-    w1_scratch = [pltpu.VMEM((PROMPTS, IN_OWN, 384), BF16), pltpu.SemaphoreType.DMA((3,))]
-    act, far_low, far_high = call(
-        act_kernel,
-        ((ROWS, HID_OWN), (48, HID), (48, HID)),
+    partial = call(
+        mlp_kernel,
+        (ROWS, HID),
         [ANY] + [VMEM] * 8,
-        flops=5 << 29,
-        moved=12 << 20,
-        vmem=30,
+        flops=3 << 30,
+        moved=16 << 20,
+        vmem=50,
         scratch=[
             pltpu.VMEM((HID_OWN, D_LLM), BF16),
-            w1_scratch[0],
+            pltpu.VMEM((PROMPTS, IN_OWN, 384), BF16),
             pltpu.SemaphoreType.DMA((ROLLOUTS, 2)),
-            w1_scratch[1],
+            pltpu.SemaphoreType.DMA((3,)),
         ],
     )(weights, line, a1, a2, b1, b2, a3, b3, slope)
 
-    via_right, via_left = shift(far_low, 0, 1), shift(far_high, 0, -1)
-    right_low, right_high, left_low, left_high, own = call(
-        rest_kernel,
-        ((48, HID),) * 4 + ((96, HID),),
-        [ANY, VMEM],
-        flops=1 << 30,
-        moved=8 << 20,
-        vmem=20,
-        scratch=w1_scratch,
-    )(weights, act)
-    high_a, low_b = shift(right_high, 0, 1), shift(left_low, 0, -1)
-    pair = call(pair_kernel, (48, HID), [VMEM] * 2)
-    low_a, high_b = shift(pair(right_low, via_right), 0, 1), shift(pair(left_high, via_left), 0, -1)
-    halfway = call(join_kernel, (96, HID), [VMEM] * 5)(own, low_a, low_b, high_a, high_b)
+    halfway = exchange(partial.reshape(SIDE, SIDE * OWN, HID), 0)
+    halfway = call(add_kernel, (SIDE * OWN, HID), [VMEM], moved=5 << 20)(halfway)
     last = exchange(halfway.reshape(SIDE, OWN, HID), 1)
     return call(norm_kernel, (OWN, HID), [VMEM] * 3)(last, patches, ln_gain.reshape(1, VIT))
 

time: 165 us -> 162 us (0.982)
  blocking collectives: 38.8 us -> 67.6 us
  starting transfers between devices: 47.1 us -> 25.7 us
  waiting for transfers between devices: 36.8 us -> 30.8 us
  local copies, waits for them, and re-layouts: 8.72 us -> 5.24 us
    all_to_all x1 -> x2, blocking collectives: 17.1 us -> 45.9 us  [exchange(): lax.all_to_all(blocks, AXES, split_axis=0, concat_axis=0, axis_index_grou...]
    ppermute x12 -> x6, starting transfers between devices: 42.4 us -> 21.1 us  [shift(): return lax.ppermute(value, AXES, pairs)]
    ppermute x12 -> x6, waiting for transfers between devices: 18.2 us -> 11.9 us  [shift(): return lax.ppermute(value, AXES, pairs)]
    unnamed x19 -> x17, local copies, waits for them, and re-layouts: 7.48 us -> 3.88 us
    pallas_call x9 -> x6, Pallas kernels: 16 us -> 16.4 us  [the longest x1 12.5 us: per_device(): call(mlp_kernel, (ROWS, HID), [ANY] + [VMEM] * 8, flops=3 << 30, moved=16...]
  transfers between devices with their start and end apart: 14 -> 8, of which waited for: 9 -> 7; matrix products, arithmetic and copies ran while one was open for 1% -> 1% of each run, Pallas kernels for 2% -> 0%
where the time goes in v4:
time: 162 us; the launch traced here: 160 us
  blocking collectives  67.6 us (42%)
  waiting for transfers between devices  30.8 us (19%)
  starting transfers between devices  25.7 us (16%)
  Pallas kernels  16.4 us (10%)
  between operations  14.2 us (9%)
  local copies, waits for them, and re-layouts  5.24 us (3%)
    all_to_all x2, blocking collectives, exchange(): lax.all_to_all(blocks, AXES, split_axis=0, concat_axis=0, axis_index_grou...  45.9 us
    all_to_all x1, blocking collectives, per_device(): lax.all_to_all(outgoing, 'rollout', split_axis=0, concat_axis=0, tiled=True)  21.7 us
    ppermute x6, starting transfers between devices, shift(): return lax.ppermute(value, AXES, pairs)  21.1 us
    pallas_call x1, Pallas kernels, per_device(): call(mlp_kernel, (ROWS, HID), [ANY] + [VMEM] * 8, flops=3 << 30, moved=16...  12.5 us
    ppermute x6, waiting for transfers between devices, shift(): return lax.ppermute(value, AXES, pairs)  11.9 us
    all_to_all x1, waiting for transfers between devices, exchange(): lax.all_to_all(blocks, AXES, split_axis=0, concat_axis=0, axis_index_grou...  10.5 us
    all_gather x1, waiting for transfers between devices, per_device(): weights = lax.all_gather(weights, 'prompt', axis=0, tiled=False)  8.41 us
    all_to_all x1, starting transfers between devices, exchange(): lax.all_to_all(blocks, AXES, split_axis=0, concat_axis=0, axis_index_grou...  4.53 us
  transfers between devices with their start and end apart: 8, of which 7 were waited for; matrix products, arithmetic and copies ran while one was open for 1% of the time, Pallas kernels for 0%

profile of v4, /device:TPU:6, one launch (start us, length us, event | category | flops | bytes accessed | tf_op | source)
XLA Modules:
  0.0 160.3 jit_solution(16514502656085817347)
XLA Ops:
  6.5 0.9 copy-done.2
  7.5 0.9 copy-done.3
  8.4 0.7 shard_map.82
  9.1 0.0 all-gather.3.cloned.1.call-update
  9.8 0.0 copy-start
  9.8 1.2 copy-done
  11.0 0.7 copy-done.4
  11.6 0.1 shard_map.83
  11.7 21.7 %all_to_all.20.recv_ref = bf16[16,64,512]{2,1,0:T(8,128)(2,1)S(1)} all-to-all(bf16[16,64,512]{2,1,0:T(8,128)(2,1)S(1)} %shard_map.83), channel_id=1, replica_groups=mesh['prompt'=32,'rollout'=16] {'rollout'}, dimensions={0} | all-to-all | bytes 2097152 | tf_op jit(solution)/shard_map/all_to_all | solution.py:215
  33.4 0.6 shard_map.84
  34.1 17.1 %all_to_all.21.refs_0_ = bf16[4,384,512]{2,1,0:T(8,128)(2,1)S(1)} all-to-all(bf16[4,384,512]{2,1,0:T(8,128)(2,1)S(1)} %shard_map.84), channel_id=1, replica_groups={{0,1,2,3},{4,5,6,7},{8,9,10,11},{12,13,14,15},{16,20,24,28},{17,21,25,2..., dimensions={0} | all-to-all | bytes 3145728 | tf_op jit(solution)/shard_map/all_to_all | solution.py:52
  51.1 1.4 fusion.6
  52.5 1.9 %collective-permute-start = (bf16[2,384,512]{2,1,0:T(8,128)(2,1)}, bf16[2,384,512]{2,1,0:T(8,128)(2,1)S(1)}, u32[]{:S(2)}, u32[]{:S(2)}) collective-permute-start(bf16[2,384,512]{2,1,0:T(8,128)(2,1)} %get-tuple-element.6), channel_id=1, source_target_pairs={{0,4},{4,8},{8,12},{12,0},{1,5},{5,9},{9,13},{13,1},{2,6},{6,10},{... | collective-permute-start | bytes 2359304 | tf_op jit(solution)/shard_map/ppermute | solution.py:61
  54.4 5.1 %collective-permute-start.2 = (bf16[2,384,512]{2,1,0:T(8,128)(2,1)}, bf16[2,384,512]{2,1,0:T(8,128)(2,1)S(1)}, u32[]{:S(2)}, u32[]{:S(2)}) collective-permute-start(bf16[2,384,512]{2,1,0:T(8,128)(2,1)} %get-tuple-element.5), channel_id=1, source_target_pairs={{0,12},{4,0},{8,4},{12,8},{1,13},{5,1},{9,5},{13,9},{2,14},{6,2},{... | collective-permute-start | bytes 2359304 | tf_op jit(solution)/shard_map/ppermute | solution.py:61
  59.5 1.9 %collective-permute-start.1 = (bf16[2,384,512]{2,1,0:T(8,128)(2,1)}, bf16[2,384,512]{2,1,0:T(8,128)(2,1)S(1)}, u32[]{:S(2)}, u32[]{:S(2)}) collective-permute-start(bf16[2,384,512]{2,1,0:T(8,128)(2,1)} %get-tuple-element.5), channel_id=1, source_target_pairs={{0,4},{4,8},{8,12},{12,0},{1,5},{5,9},{9,13},{13,1},{2,6},{6,10},{... | collective-permute-start | bytes 2359304 | tf_op jit(solution)/shard_map/ppermute | solution.py:61
  61.5 5.1 %collective-permute-start.3 = (bf16[2,384,512]{2,1,0:T(8,128)(2,1)}, bf16[2,384,512]{2,1,0:T(8,128)(2,1)}, u32[]{:S(2)}, u32[]{:S(2)}) collective-permute-start(bf16[2,384,512]{2,1,0:T(8,128)(2,1)} %get-tuple-element.6), channel_id=1, source_target_pairs={{0,12},{4,0},{8,4},{12,8},{1,13},{5,1},{9,5},{13,9},{2,14},{6,2},{... | collective-permute-start | bytes 2359304 | tf_op jit(solution)/shard_map/ppermute | solution.py:61
  66.6 1.2 collective-permute-done.refs_1_
  67.8 1.9 %collective-permute-start.4 = (bf16[2,384,512]{2,1,0:T(8,128)(2,1)S(1)}, bf16[2,384,512]{2,1,0:T(8,128)(2,1)}, u32[]{:S(2)}, u32[]{:S(2)}) collective-permute-start(bf16[2,384,512]{2,1,0:T(8,128)(2,1)S(1)} %collective-permute-done.refs_1_), channel_id=1, source_target_pairs={{0,4},{4,8},{8,12},{12,0},{1,5},{5,9},{9,13},{13,1},{2,6},{6,10},{... | collective-permute-start | bytes 2359304 | tf_op jit(solution)/shard_map/ppermute | solution.py:61
  69.7 5.1 %collective-permute-start.5 = (bf16[2,384,512]{2,1,0:T(8,128)(2,1)S(1)}, bf16[2,384,512]{2,1,0:T(8,128)(2,1)}, u32[]{:S(2)}, u32[]{:S(2)}) collective-permute-start(bf16[2,384,512]{2,1,0:T(8,128)(2,1)S(1)} %collective-permute-done.2.refs_3_), channel_id=1, source_target_pairs={{0,12},{4,0},{8,4},{12,8},{1,13},{5,1},{9,5},{13,9},{2,14},{6,2},{... | collective-permute-start | bytes 2359304 | tf_op jit(solution)/shard_map/ppermute | solution.py:61
  74.9 0.2 copy.11
  75.1 0.2 fusion.3
  75.4 0.8 collective-permute-done.1.refs_2_
  76.2 1.6 collective-permute-done.3.refs_4_
  77.8 7.0 %collective-permute-done.4.refs_5_ = bf16[2,384,512]{2,1,0:T(8,128)(2,1)} collective-permute-done((bf16[2,384,512]{2,1,0:T(8,128)(2,1)S(1)}, bf16[2,384,512]{2,1,0:T(8,128)(2,1)}, u32[]{:S(2)}, u32[]{:S(2)}) %collective-permute-start.4) | collective-permute-done | bytes 786464 | tf_op jit(solution)/shard_map/ppermute | solution.py:61
  84.7 1.4 collective-permute-done.5.refs_6_
  86.1 8.4 %all-gather.3.cloned.1.call-done = bf16[17920,256]{1,0:T(8,128)(2,1)} async-done(((bf16[560,256]{1,0:T(8,128)(2,1)}), bf16[17920,256]{1,0:T(8,128)(2,1)}) %all-gather.3.cloned.1.call-update) | async-done | bytes 9175056 | tf_op jit(solution)/shard_map/all_gather | solution.py:210
  94.5 12.5 %shard_map.85 = bf16[384,5120]{1,0:T(8,128)(2,1)} custom-call(bf16[32,560,256]{2,1,0:T(8,128)(2,1)} %bitcast.13, bf16[4,384,512]{2,1,0:T(8,128)(2,1)} %copy-done.5, bf16[2,384,512]{2,1,0:T(8,128)(2,1)S(1)} %collective-permute-done.refs_1_, bf16[2,384,512]{2,1,0:T(8,128)(2,1)S(1)} %collective-permute-done.1.refs_2_, ...), custom_call_target="tpu_custom_call" | custom-call | flops 3221225472 | bytes 16777216 | tf_op jit(solution)/shard_map/pallas_call | solution.py:225
  107.1 28.8 %all_to_all.22.recv_ref = bf16[4,96,5120]{2,1,0:T(8,128)(2,1)S(1)} all-to-all(bf16[4,96,5120]{2,1,0:T(8,128)(2,1)} %bitcast.12), channel_id=1, replica_groups={{0,1,2,3},{4,5,6,7},{8,9,10,11},{12,13,14,15},{16,20,24,28},{17,21,25,2..., dimensions={0} | all-to-all | bytes 7864320 | tf_op jit(solution)/shard_map/all_to_all | solution.py:52
  135.9 1.4 shard_map.86
  137.3 4.5 %all-to-all-start.3 = ((bf16[4,24,5120]{2,1,0:T(8,128)(2,1)}), bf16[4,24,5120]{2,1,0:T(8,128)(2,1)S(1)}, u32[]{:S(2)}, u32[]{:S(2)}) async-start(bf16[4,24,5120]{2,1,0:T(8,128)(2,1)} %bitcast.7), calls=%async_computation.3 | async-start | bytes 1966080 | tf_op jit(solution)/shard_map/all_to_all | solution.py:52
  141.8 10.5 %all-to-all-done.3.recv_ref = bf16[4,24,5120]{2,1,0:T(8,128)(2,1)S(1)} async-done(((bf16[4,24,5120]{2,1,0:T(8,128)(2,1)}), bf16[4,24,5120]{2,1,0:T(8,128)(2,1)S(1)}, u32[]{:S(2)}, u32[]{:S(2)}) %all-to-all-start.3) | async-done | bytes 983072 | tf_op jit(solution)/shard_map/all_to_all | solution.py:52
  152.4 1.0 shard_map.87
  (15 shorter events, 0.1 us)
Async XLA Ops:
  6.5 88.0 %all-gather.3.cloned.1.call-start = ((), (), s32[]{:S(2)}) async-start(), calls=%async_computation.4 | async-start | bytes 9461760 | tf_op jit(solution)/shard_map/all_gather | solution.py:210
  6.5 0.9 copy-start.2
  7.5 0.9 copy-start.3
  9.8 1.2 copy-start
  10.9 0.7 copy-start.4
  33.4 41.4 %copy-start.6 = (bf16[384,320]{0,1:T(8,128)(2,1)S(1)}, bf16[384,320]{0,1:T(8,128)(2,1)}, u32[]{:S(2)}) copy-start(bf16[384,320]{0,1:T(8,128)(2,1)} %param.11) | copy-start | bytes 737284
  51.1 18.6 %copy-start.5 = (bf16[4,384,512]{2,1,0:T(8,128)(2,1)}, bf16[4,384,512]{2,1,0:T(8,128)(2,1)S(1)}, u32[]{:S(2)}) copy-start(bf16[4,384,512]{2,1,0:T(8,128)(2,1)S(1)} %all_to_all.21.refs_0_) | copy-start | bytes 4718596
  52.5 15.3 %collective-permute-start = (bf16[2,384,512]{2,1,0:T(8,128)(2,1)}, bf16[2,384,512]{2,1,0:T(8,128)(2,1)S(1)}, u32[]{:S(2)}, u32[]{:S(2)}) collective-permute-start(bf16[2,384,512]{2,1,0:T(8,128)(2,1)} %get-tuple-element.6), channel_id=1, source_target_pairs={{0,4},{4,8},{8,12},{12,0},{1,5},{5,9},{9,13},{13,1},{2,6},{6,10},{... | collective-permute-start | bytes 2359304 | tf_op jit(solution)/shard_map/ppermute | solution.py:61
  54.4 15.3 %collective-permute-start.2 = (bf16[2,384,512]{2,1,0:T(8,128)(2,1)}, bf16[2,384,512]{2,1,0:T(8,128)(2,1)S(1)}, u32[]{:S(2)}, u32[]{:S(2)}) collective-permute-start(bf16[2,384,512]{2,1,0:T(8,128)(2,1)} %get-tuple-element.5), channel_id=1, source_target_pairs={{0,12},{4,0},{8,4},{12,8},{1,13},{5,1},{9,5},{13,9},{2,14},{6,2},{... | collective-permute-start | bytes 2359304 | tf_op jit(solution)/shard_map/ppermute | solution.py:61
  59.5 16.7 %collective-permute-start.1 = (bf16[2,384,512]{2,1,0:T(8,128)(2,1)}, bf16[2,384,512]{2,1,0:T(8,128)(2,1)S(1)}, u32[]{:S(2)}, u32[]{:S(2)}) collective-permute-start(bf16[2,384,512]{2,1,0:T(8,128)(2,1)} %get-tuple-element.5), channel_id=1, source_target_pairs={{0,4},{4,8},{8,12},{12,0},{1,5},{5,9},{9,13},{13,1},{2,6},{6,10},{... | collective-permute-start | bytes 2359304 | tf_op jit(solution)/shard_map/ppermute | solution.py:61
  61.5 16.3 %collective-permute-start.3 = (bf16[2,384,512]{2,1,0:T(8,128)(2,1)}, bf16[2,384,512]{2,1,0:T(8,128)(2,1)}, u32[]{:S(2)}, u32[]{:S(2)}) collective-permute-start(bf16[2,384,512]{2,1,0:T(8,128)(2,1)} %get-tuple-element.6), channel_id=1, source_target_pairs={{0,12},{4,0},{8,4},{12,8},{1,13},{5,1},{9,5},{13,9},{2,14},{6,2},{... | collective-permute-start | bytes 2359304 | tf_op jit(solution)/shard_map/ppermute | solution.py:61
  67.8 17.0 %collective-permute-start.4 = (bf16[2,384,512]{2,1,0:T(8,128)(2,1)S(1)}, bf16[2,384,512]{2,1,0:T(8,128)(2,1)}, u32[]{:S(2)}, u32[]{:S(2)}) collective-permute-start(bf16[2,384,512]{2,1,0:T(8,128)(2,1)S(1)} %collective-permute-done.refs_1_), channel_id=1, source_target_pairs={{0,4},{4,8},{8,12},{12,0},{1,5},{5,9},{9,13},{13,1},{2,6},{6,10},{... | collective-permute-start | bytes 2359304 | tf_op jit(solution)/shard_map/ppermute | solution.py:61
  69.7 16.4 %collective-permute-start.5 = (bf16[2,384,512]{2,1,0:T(8,128)(2,1)S(1)}, bf16[2,384,512]{2,1,0:T(8,128)(2,1)}, u32[]{:S(2)}, u32[]{:S(2)}) collective-permute-start(bf16[2,384,512]{2,1,0:T(8,128)(2,1)S(1)} %collective-permute-done.2.refs_3_), channel_id=1, source_target_pairs={{0,12},{4,0},{8,4},{12,8},{1,13},{5,1},{9,5},{13,9},{2,14},{6,2},{... | collective-permute-start | bytes 2359304 | tf_op jit(solution)/shard_map/ppermute | solution.py:61
  135.9 6.0 %copy-start.7 = (f32[1280]{0:T(1024)S(1)}, f32[1280]{0:T(1024)}, u32[]{:S(2)}) copy-start(f32[1280]{0:T(1024)} %param.13) | copy-start | bytes 15364
  135.9 16.5 %copy-start.1 = (bf16[24,5120]{1,0:T(8,128)(2,1)S(1)}, bf16[24,5120]{1,0:T(8,128)(2,1)}, u32[]{:S(2)}) copy-start(bf16[24,5120]{1,0:T(8,128)(2,1)} %patches_ref.1) | copy-start | bytes 737284
  137.3 15.1 %all-to-all-start.3 = ((bf16[4,24,5120]{2,1,0:T(8,128)(2,1)}), bf16[4,24,5120]{2,1,0:T(8,128)(2,1)S(1)}, u32[]{:S(2)}, u32[]{:S(2)}) async-start(bf16[4,24,5120]{2,1,0:T(8,128)(2,1)} %bitcast.7), calls=%async_computation.3 | async-start | bytes 1966080 | tf_op jit(solution)/shard_map/all_to_all | solution.py:52
Sparse Core Ops, SparseCore 0:
  9.5 84.9 all-gather.2

commit v5 on v3

--- a/solution.py
+++ b/solution.py
@@ -20,18 +20,17 @@
 HID_OWN = HID // ROLLOUTS
 IN_OWN = HID // PROMPTS
 W2_COLS = D_LLM // PROMPTS
-PART = IN_OWN // SIDE
-PART_PAD = 48
-W1_ROWS = SIDE * PART_PAD
-W_ROWS = HID_OWN + W1_ROWS + PART_PAD
-IN_PAD = PROMPTS * PART_PAD
-HALF = IN_PAD // (2 * MERGE)
+PART = IN_OWN // 2
+TAIL = 48
+W_ROWS = HID_OWN + 2 * PART + TAIL
+IN_PART = HID // 2
+RUN = 4 * PART
 AXES = ("prompt", "rollout")
 F32 = jnp.float32
 BF16 = jnp.bfloat16
 VMEM = pl.BlockSpec(memory_space=pltpu.VMEM)
 SMEM = pl.BlockSpec(memory_space=pltpu.SMEM)
-HBM = pl.BlockSpec(memory_space=pltpu.HBM)
+ANY = pl.BlockSpec(memory_space=pl.ANY)
 
 
 def gelu_slope(value):
@@ -55,10 +54,6 @@
     return groups
 
 
-def x_groups():
-    return [[row * SIDE + i for i in range(SIDE)] for row in range(PROMPTS * SIDE)]
-
-
 def exchange(blocks, groups):
     return lax.all_to_all(
         blocks, AXES, split_axis=0, concat_axis=0, axis_index_groups=groups, tiled=True
@@ -76,21 +71,24 @@
     return lax.ppermute(value, AXES, pairs)
 
 
-def split_kernel(w1_ref, out_ref):
-    rows = w1_ref[...].astype(F32)
-    zeros = jnp.zeros((PART_PAD - PART, HID_OWN), F32)
-    for i in range(SIDE):
-        part = jnp.concatenate([rows[i * PART : (i + 1) * PART], zeros], axis=0)
-        out_ref[i] = part.astype(BF16)
-
-
-def weights_kernel(w2_ref, w1_ref, out_ref):
+def swap(value):
+    return lax.ppermute(value, "rollout", [(r, r ^ 1) for r in range(ROLLOUTS)])
+
+
+def weights_kernel(w2_ref, mine_ref, theirs_ref, out_ref):
+    odd = lax.axis_index("rollout") % 2 == 1
     out_ref[0:HID_OWN, :] = w2_ref[...]
-    for k in range(SIDE):
-        base = HID_OWN + k * PART_PAD
-        out_ref[base : base + PART_PAD, :] = w1_ref[k, :, 0:256]
-    rest = jnp.concatenate([w1_ref[k, :, 256:HID_OWN] for k in range(SIDE)], axis=1)
-    out_ref[HID_OWN + W1_ROWS : W_ROWS, :] = rest
+    mine = jnp.where(odd, mine_ref[PART:IN_OWN].astype(F32), mine_ref[0:PART].astype(F32))
+    theirs = theirs_ref[...].astype(F32)
+    left = jnp.where(odd, theirs, mine).astype(BF16)
+    right = jnp.where(odd, mine, theirs).astype(BF16)
+    base = HID_OWN + PART
+    out_ref[HID_OWN:base, :] = left[:, 0:256]
+    out_ref[base : base + PART, :] = right[:, 0:256]
+    rest = jnp.concatenate([left[:, 256:HID_OWN], right[:, 256:HID_OWN]], axis=1)
+    out_ref[base + PART : W_ROWS, 0:128] = rest[0:TAIL]
+    low = jnp.concatenate([rest[TAIL:PART], jnp.zeros((2 * TAIL - PART, 128), BF16)], axis=0)
+    out_ref[base + PART : W_ROWS, 128:256] = low
 
 
 def pack_kernel(count_ref, ids_ref, grads_ref, out_ref, meta):
@@ -165,40 +163,42 @@
             copy.wait()
         part = dot_t(ref[n], w2[:, i * COLS : (i + 1) * COLS])
         hidden = part if hidden is None else hidden + part
-    act = (hidden * slope_ref[...]).astype(BF16)
-    for k in range(SIDE):
-        act_ref[k] = act
-
-
-def upstream_kernel(w_ref, act_ref, out_ref, w1, sems):
+    act_ref[...] = (hidden * slope_ref[...]).astype(BF16)
+
+
+def upstream_kernel(w_ref, mine_ref, theirs_ref, out_ref, w1, sems):
     copies = []
     for m in range(MERGE):
         prompts = pl.ds(m * 8, 8)
         copies.append(pltpu.make_async_copy(w_ref.at[prompts, HID_OWN:W_ROWS], w1.at[prompts], sems.at[m]))
         copies[m].start()
-    rest = jnp.concatenate([act_ref[k, :, 256:HID_OWN] for k in range(SIDE)], axis=1)
+    odd = lax.axis_index("rollout") % 2 == 1
+    mine, theirs = mine_ref[...], theirs_ref[...]
+    left, right = jnp.where(odd, theirs, mine), jnp.where(odd, mine, theirs)
+    rest = jnp.concatenate([left[:, 256:HID_OWN], right[:, 256:HID_OWN]], axis=1)
     for m in range(MERGE):
         copies[m].wait()
-        total = None
-        for k in range(SIDE + 1):
-            w = w1[8 * m : 8 * m + 8, k * PART_PAD : (k + 1) * PART_PAD].reshape(8 * PART_PAD, 256)
-            part = dot_t(act_ref[k, :, 0:256] if k < SIDE else rest, w)
-            total = part if total is None else total + part
-        blocks = total.reshape(ROLLOUTS, OWN, 8 * PART_PAD).astype(BF16)
-        out_ref[:, :, 8 * PART_PAD * m : 8 * PART_PAD * (m + 1)] = blocks
+        w = w1[8 * m : 8 * m + 8]
+        fold = w[:, 2 * PART :]
+        tail = jnp.concatenate([fold[:, :, 0:128], fold[:, 0 : PART - TAIL, 128:256]], axis=1)
+        total = dot_t(left[:, 0:256], w[:, 0:PART].reshape(8 * PART, 256))
+        total = total + dot_t(right[:, 0:256], w[:, PART : 2 * PART].reshape(8 * PART, 256))
+        total = total + dot_t(rest, tail.reshape(8 * PART, 128))
+        blocks = total.reshape(ROLLOUTS, OWN, 8 * PART).astype(BF16)
+        out_ref[:, :, 8 * PART * m : 8 * PART * (m + 1)] = blocks
 
 
 def norm_kernel(recv_ref, order_ref, patches_ref, gain_ref, out_ref):
     parts = []
-    for i in range(SIDE):
+    for i in range(2):
         total = None
-        for s in range(SIDE):
-            part = recv_ref[s * SIDE + i].astype(F32)
+        for s in range(ROLLOUTS // 2):
+            part = recv_ref[2 * s + i].astype(F32)
             total = part if total is None else total + part
         parts.append(total)
     rows = []
     for g in range(2 * MERGE):
-        whole = jnp.concatenate([part[:, g * HALF : (g + 1) * HALF] for part in parts], axis=1)
+        whole = jnp.concatenate([part[:, g * RUN : (g + 1) * RUN] for part in parts], axis=1)
         high = whole.astype(BF16)
         rows += [high, (whole - high.astype(F32)).astype(BF16)]
     ordered = jnp.dot(
@@ -234,15 +234,16 @@
 
 
 def column_order():
-    lane = lax.broadcasted_iota(jnp.int32, (SIDE * HALF, HALF // PART_PAD * IN_OWN), 0)
+    lane = lax.broadcasted_iota(jnp.int32, (2 * RUN, 2 * RUN), 0)
     col = lax.broadcasted_iota(jnp.int32, lane.shape, 1)
-    place, prompt, row = lane // HALF, lane % HALF // PART_PAD, lane % PART_PAD
-    return ((prompt * IN_OWN + place * PART + row == col) & (row < PART)).astype(BF16)
+    side, prompt, row = lane // RUN, lane % RUN // PART, lane % PART
+    return (prompt * IN_OWN + side * PART + row == col).astype(BF16)
 
 
 def per_device(row_grads, used_ids, used_count, pre_act, patches, ln_gain, w_fc2, w_fc1):
-    w1_part = exchange(call(split_kernel, (SIDE, PART_PAD, HID_OWN), [VMEM])(w_fc1), x_groups())
-    weights = call(weights_kernel, (W_ROWS, 256), [VMEM] * 2)(w_fc2, w1_part)
+    odd = lax.axis_index("rollout") % 2 == 1
+    theirs = swap(jnp.where(odd, w_fc1[:PART], w_fc1[PART:]))
+    weights = call(weights_kernel, (W_ROWS, 256), [VMEM] * 3)(w_fc2, w_fc1, theirs)
     weights = lax.all_gather(weights, "prompt", axis=0, tiled=False)
 
     outgoing = call(
@@ -256,26 +257,25 @@
 
     act = call(
         act_kernel,
-        (SIDE, ROWS, HID_OWN),
-        [HBM] + [VMEM] * 8,
+        (ROWS, HID_OWN),
+        [ANY] + [VMEM] * 8,
         flops=1 << 31,
         moved=12 << 20,
-        vmem=24,
+        vmem=50,
         scratch=[pltpu.VMEM((HID_OWN, D_LLM), BF16), pltpu.SemaphoreType.DMA((ROLLOUTS, 2))],
     )(weights, line, a1, a2, b1, b2, a3, b3, gelu_slope(pre_act.astype(F32)))
-    act_line = exchange(act, x_groups())
     partial = call(
         upstream_kernel,
-        (ROLLOUTS, OWN, IN_PAD),
-        [HBM, VMEM],
+        (ROLLOUTS, OWN, IN_PART),
+        [ANY, VMEM, VMEM],
         flops=5 << 28,
         moved=6 << 20,
-        vmem=24,
+        vmem=56,
         scratch=[
             pltpu.VMEM((PROMPTS, W_ROWS - HID_OWN, 256), BF16),
             pltpu.SemaphoreType.DMA((MERGE,)),
         ],
-    )(weights, act_line)
+    )(weights, act, swap(act))
     return call(norm_kernel, (OWN, HID), [VMEM] * 4)(
         exchange_all(partial), column_order(), patches, ln_gain.reshape(1, VIT)
     )

time: 175 us -> 172 us (0.983)
  the two profiles are of different devices: /device:TPU:6 before, /device:TPU:32 now
where the time goes in v5:
time: 172 us; the launch traced here: 171 us
  waiting for transfers between devices  57.9 us (34%)
  blocking collectives  39.2 us (23%)
  starting transfers between devices  34.7 us (20%)
  Pallas kernels  18.2 us (11%)
  between operations  14.3 us (8%)
  local copies, waits for them, and re-layouts  4.65 us (3%)
  other arithmetic  2.51 us (1%)
    all_to_all x1, waiting for transfers between devices, exchange_all(): lax.all_to_all(blocks, 'rollout', split_axis=0, concat_axis=0, tiled=True)  27.5 us
    all_to_all x1, blocking collectives, exchange_all(): lax.all_to_all(blocks, 'rollout', split_axis=0, concat_axis=0, tiled=True)  23.1 us
    ppermute x6, starting transfers between devices, shift(): return lax.ppermute(value, AXES, pairs)  21.1 us
    all_to_all x1, blocking collectives, exchange(): lax.all_to_all(blocks, AXES, split_axis=0, concat_axis=0, axis_index_grou...  16.1 us
    ppermute x6, waiting for transfers between devices, shift(): return lax.ppermute(value, AXES, pairs)  12 us
    ppermute x2, waiting for transfers between devices, swap(): return lax.ppermute(value, 'rollout', [(r, r ^ 1) for r in range(ROLLOUTS)])  10.6 us
    pallas_call x1, Pallas kernels, per_device(): call(act_kernel, (ROWS, HID_OWN), [ANY] + [VMEM] * 8, flops=1 << 31, move...  7.95 us
    all_gather x1, waiting for transfers between devices, per_device(): weights = lax.all_gather(weights, 'prompt', axis=0, tiled=False)  7.85 us
  transfers between devices with their start and end apart: 10, of which 9 were waited for; matrix products, arithmetic and copies ran while one was open for 2% of the time, Pallas kernels for 0%

profile of v5, /device:TPU:32, one launch (start us, length us, event | category | flops | bytes accessed | tf_op | source)
XLA Modules:
  0.0 171.4 jit_solution(3395590083755921020)
XLA Ops:
  6.5 0.9 slice_select_fusion
  7.5 3.4 %collective-permute-start = (bf16[80,320]{1,0:T(8,128)(2,1)S(1)}, bf16[80,320]{1,0:T(8,128)(2,1)S(1)}, u32[]{:S(2)}, u32[]{:S(2)}) collective-permute-start(bf16[80,320]{1,0:T(8,128)(2,1)S(1)} %slice_select_fusion), channel_id=1, source_target_pairs={{0,1},{1,0},{2,3},{3,2},{4,5},{5,4},{6,7},{7,6},{8,9},{9,8},{10,11... | collective-permute-start | bytes 153608 | tf_op jit(solution)/shard_map/ppermute | solution.py:75
  10.9 2.7 %collective-permute-done.theirs_ref = bf16[80,320]{1,0:T(8,128)(2,1)S(1)} collective-permute-done((bf16[80,320]{1,0:T(8,128)(2,1)S(1)}, bf16[80,320]{1,0:T(8,128)(2,1)S(1)}, u32[]{:S(2)}, u32[]{:S(2)}) %collective-permute-start) | collective-permute-done | bytes 51232 | tf_op jit(solution)/shard_map/ppermute | solution.py:75
  13.6 0.9 copy-done.2
  14.5 0.9 copy-done.4
  15.4 0.8 shard_map.82
  16.9 0.6 copy-done.5
  17.6 23.1 %all_to_all.15.recv_ref = bf16[16,64,512]{2,1,0:T(8,128)(2,1)S(1)} all-to-all(bf16[16,64,512]{2,1,0:T(8,128)(2,1)S(1)} %shard_map.83), channel_id=1, replica_groups=mesh['prompt'=32,'rollout'=16] {'rollout'}, dimensions={0} | all-to-all | bytes 2097152 | tf_op jit(solution)/shard_map/all_to_all | solution.py:64
  40.7 0.6 shard_map.84
  41.4 16.1 %all_to_all.16.refs_0_ = bf16[4,384,512]{2,1,0:T(8,128)(2,1)S(1)} all-to-all(bf16[4,384,512]{2,1,0:T(8,128)(2,1)S(1)} %shard_map.84), channel_id=1, replica_groups={{0,1,2,3},{4,5,6,7},{8,9,10,11},{12,13,14,15},{16,20,24,28},{17,21,25,2..., dimensions={0} | all-to-all | bytes 3145728 | tf_op jit(solution)/shard_map/all_to_all | solution.py:58
  57.5 1.3 fusion.22
  58.8 1.9 %collective-permute-start.1 = (bf16[2,384,512]{2,1,0:T(8,128)(2,1)}, bf16[2,384,512]{2,1,0:T(8,128)(2,1)S(1)}, u32[]{:S(2)}, u32[]{:S(2)}) collective-permute-start(bf16[2,384,512]{2,1,0:T(8,128)(2,1)} %get-tuple-element.6), channel_id=1, source_target_pairs={{0,4},{4,8},{8,12},{12,0},{1,5},{5,9},{9,13},{13,1},{2,6},{6,10},{... | collective-permute-start | bytes 2359304 | tf_op jit(solution)/shard_map/ppermute | solution.py:71
  60.7 5.1 %collective-permute-start.3 = (bf16[2,384,512]{2,1,0:T(8,128)(2,1)}, bf16[2,384,512]{2,1,0:T(8,128)(2,1)S(1)}, u32[]{:S(2)}, u32[]{:S(2)}) collective-permute-start(bf16[2,384,512]{2,1,0:T(8,128)(2,1)} %get-tuple-element.5), channel_id=1, source_target_pairs={{0,12},{4,0},{8,4},{12,8},{1,13},{5,1},{9,5},{13,9},{2,14},{6,2},{... | collective-permute-start | bytes 2359304 | tf_op jit(solution)/shard_map/ppermute | solution.py:71
  65.8 1.9 %collective-permute-start.2 = (bf16[2,384,512]{2,1,0:T(8,128)(2,1)}, bf16[2,384,512]{2,1,0:T(8,128)(2,1)S(1)}, u32[]{:S(2)}, u32[]{:S(2)}) collective-permute-start(bf16[2,384,512]{2,1,0:T(8,128)(2,1)} %get-tuple-element.5), channel_id=1, source_target_pairs={{0,4},{4,8},{8,12},{12,0},{1,5},{5,9},{9,13},{13,1},{2,6},{6,10},{... | collective-permute-start | bytes 2359304 | tf_op jit(solution)/shard_map/ppermute | solution.py:71
  67.8 5.1 %collective-permute-start.4 = (bf16[2,384,512]{2,1,0:T(8,128)(2,1)}, bf16[2,384,512]{2,1,0:T(8,128)(2,1)}, u32[]{:S(2)}, u32[]{:S(2)}) collective-permute-start(bf16[2,384,512]{2,1,0:T(8,128)(2,1)} %get-tuple-element.6), channel_id=1, source_target_pairs={{0,12},{4,0},{8,4},{12,8},{1,13},{5,1},{9,5},{13,9},{2,14},{6,2},{... | collective-permute-start | bytes 2359304 | tf_op jit(solution)/shard_map/ppermute | solution.py:71
  72.9 1.2 collective-permute-done.1.refs_1_
  74.1 1.9 %collective-permute-start.5 = (bf16[2,384,512]{2,1,0:T(8,128)(2,1)S(1)}, bf16[2,384,512]{2,1,0:T(8,128)(2,1)}, u32[]{:S(2)}, u32[]{:S(2)}) collective-permute-start(bf16[2,384,512]{2,1,0:T(8,128)(2,1)S(1)} %collective-permute-done.1.refs_1_), channel_id=1, source_target_pairs={{0,4},{4,8},{8,12},{12,0},{1,5},{5,9},{9,13},{13,1},{2,6},{6,10},{... | collective-permute-start | bytes 2359304 | tf_op jit(solution)/shard_map/ppermute | solution.py:71
  76.0 5.1 %collective-permute-start.6 = (bf16[2,384,512]{2,1,0:T(8,128)(2,1)S(1)}, bf16[2,384,512]{2,1,0:T(8,128)(2,1)}, u32[]{:S(2)}, u32[]{:S(2)}) collective-permute-start(bf16[2,384,512]{2,1,0:T(8,128)(2,1)S(1)} %collective-permute-done.3.refs_3_), channel_id=1, source_target_pairs={{0,12},{4,0},{8,4},{12,8},{1,13},{5,1},{9,5},{13,9},{2,14},{6,2},{... | collective-permute-start | bytes 2359304 | tf_op jit(solution)/shard_map/ppermute | solution.py:71
  81.6 0.9 collective-permute-done.2.refs_2_
  82.5 1.6 collective-permute-done.4.refs_4_
  84.1 7.0 %collective-permute-done.5.refs_5_ = bf16[2,384,512]{2,1,0:T(8,128)(2,1)} collective-permute-done((bf16[2,384,512]{2,1,0:T(8,128)(2,1)S(1)}, bf16[2,384,512]{2,1,0:T(8,128)(2,1)}, u32[]{:S(2)}, u32[]{:S(2)}) %collective-permute-start.5) | collective-permute-done | bytes 786464 | tf_op jit(solution)/shard_map/ppermute | solution.py:71
  91.0 1.4 collective-permute-done.6.refs_6_
  92.4 7.8 %all-gather.3.cloned.1.call-done = bf16[16896,256]{1,0:T(8,128)(2,1)} async-done(((bf16[528,256]{1,0:T(8,128)(2,1)}), bf16[16896,256]{1,0:T(8,128)(2,1)}) %all-gather.3.cloned.1.call-update) | async-done | bytes 8650768 | tf_op jit(solution)/shard_map/all_gather | solution.py:247
  100.2 8.0 %shard_map.85.mine_ref = bf16[384,320]{1,0:T(8,128)(2,1)S(1)} custom-call(bf16[32,528,256]{2,1,0:T(8,128)(2,1)} %bitcast.5, bf16[4,384,512]{2,1,0:T(8,128)(2,1)} %copy-done.6, bf16[2,384,512]{2,1,0:T(8,128)(2,1)S(1)} %collective-permute-done.1.refs_1_, bf16[2,384,512]{2,1,0:T(8,128)(2,1)S(1)} %collective-permute-done.2.refs_2_, ...), custom_call_target="tpu_custom_call" | custom-call | flops 2147483648 | bytes 12582912 | tf_op jit(solution)/shard_map/pallas_call | solution.py:258
  108.2 3.2 %collective-permute-start.7 = (bf16[384,320]{1,0:T(8,128)(2,1)S(1)}, bf16[384,320]{1,0:T(8,128)(2,1)S(1)}, u32[]{:S(2)}, u32[]{:S(2)}) collective-permute-start(bf16[384,320]{1,0:T(8,128)(2,1)S(1)} %shard_map.85.mine_ref), channel_id=1, source_target_pairs={{0,1},{1,0},{2,3},{3,2},{4,5},{5,4},{6,7},{7,6},{8,9},{9,8},{10,11... | collective-permute-start | bytes 737288 | tf_op jit(solution)/shard_map/ppermute | solution.py:75
  111.4 7.9 %collective-permute-done.7.theirs_ref = bf16[384,320]{1,0:T(8,128)(2,1)S(1)} collective-permute-done((bf16[384,320]{1,0:T(8,128)(2,1)S(1)}, bf16[384,320]{1,0:T(8,128)(2,1)S(1)}, u32[]{:S(2)}, u32[]{:S(2)}) %collective-permute-start.7) | collective-permute-done | bytes 245792 | tf_op jit(solution)/shard_map/ppermute | solution.py:75
  119.3 0.7 copy-done.7
  120.0 7.2 %shard_map.86 = bf16[16,24,2560]{2,1,0:T(8,128)(2,1)} custom-call(bf16[32,528,256]{2,1,0:T(8,128)(2,1)} %bitcast.6, bf16[384,320]{1,0:T(8,128)(2,1)} %copy-done, bf16[384,320]{1,0:T(8,128)(2,1)} %copy-done.7), custom_call_target="tpu_custom_call" | custom-call | flops 1342177280 | bytes 6291456 | tf_op jit(solution)/shard_map/pallas_call | solution.py:267
  127.2 7.0 %all-to-all-start.2 = ((bf16[16,24,2560]{2,1,0:T(8,128)(2,1)}), bf16[16,24,2560]{2,1,0:T(8,128)(2,1)S(1)}, u32[]{:S(2)}, u32[]{:S(2)}) async-start(bf16[16,24,2560]{2,1,0:T(8,128)(2,1)} %shard_map.86), calls=%async_computation.2 | async-start | bytes 3932160 | tf_op jit(solution)/shard_map/all_to_all | solution.py:64
  134.2 1.3 fusion.6.order_ref
  135.5 27.5 %all-to-all-done.2.recv_ref = bf16[16,24,2560]{2,1,0:T(8,128)(2,1)S(1)} async-done(((bf16[16,24,2560]{2,1,0:T(8,128)(2,1)}), bf16[16,24,2560]{2,1,0:T(8,128)(2,1)S(1)}, u32[]{:S(2)}, u32[]{:S(2)}) %all-to-all-start.2) | async-done | bytes 1966112 | tf_op jit(solution)/shard_map/all_to_all | solution.py:64
  163.0 1.6 shard_map.87
  (28 shorter events, 0.6 us)
Async XLA Ops:
  6.5 10.4 %copy-start.1 = (bf16[1,1,50,8192]{3,2,1,0:T(8,128)(2,1)S(1)}, bf16[1,1,50,8192]{3,2,1,0:T(8,128)(2,1)}, u32[]{:S(2)}) copy-start(bf16[1,1,50,8192]{3,2,1,0:T(8,128)(2,1)} %param.8) | copy-start | bytes 2457604
  6.5 93.7 %all-gather.3.cloned.1.call-start = ((), (), s32[]{:S(2)}) async-start(), calls=%async_computation.3 | async-start | bytes 8921088 | tf_op jit(solution)/shard_map/all_gather | solution.py:247
  7.5 6.1 %collective-permute-start = (bf16[80,320]{1,0:T(8,128)(2,1)S(1)}, bf16[80,320]{1,0:T(8,128)(2,1)S(1)}, u32[]{:S(2)}, u32[]{:S(2)}) collective-permute-start(bf16[80,320]{1,0:T(8,128)(2,1)S(1)} %slice_select_fusion), channel_id=1, source_target_pairs={{0,1},{1,0},{2,3},{3,2},{4,5},{5,4},{6,7},{7,6},{8,9},{9,8},{10,11... | collective-permute-start | bytes 153608 | tf_op jit(solution)/shard_map/ppermute | solution.py:75
  13.6 0.9 copy-start.2
  14.5 0.9 copy-start.4
  16.9 0.7 copy-start.5
  57.5 18.5 %copy-start.6 = (bf16[4,384,512]{2,1,0:T(8,128)(2,1)}, bf16[4,384,512]{2,1,0:T(8,128)(2,1)S(1)}, u32[]{:S(2)}) copy-start(bf16[4,384,512]{2,1,0:T(8,128)(2,1)S(1)} %all_to_all.16.refs_0_) | copy-start | bytes 4718596
  57.5 23.6 %copy-start.8 = (bf16[384,320]{0,1:T(8,128)(2,1)S(1)}, bf16[384,320]{0,1:T(8,128)(2,1)}, u32[]{:S(2)}) copy-start(bf16[384,320]{0,1:T(8,128)(2,1)} %param.11) | copy-start | bytes 737284
  58.8 15.3 %collective-permute-start.1 = (bf16[2,384,512]{2,1,0:T(8,128)(2,1)}, bf16[2,384,512]{2,1,0:T(8,128)(2,1)S(1)}, u32[]{:S(2)}, u32[]{:S(2)}) collective-permute-start(bf16[2,384,512]{2,1,0:T(8,128)(2,1)} %get-tuple-element.6), channel_id=1, source_target_pairs={{0,4},{4,8},{8,12},{12,0},{1,5},{5,9},{9,13},{13,1},{2,6},{6,10},{... | collective-permute-start | bytes 2359304 | tf_op jit(solution)/shard_map/ppermute | solution.py:71
  60.7 15.3 %collective-permute-start.3 = (bf16[2,384,512]{2,1,0:T(8,128)(2,1)}, bf16[2,384,512]{2,1,0:T(8,128)(2,1)S(1)}, u32[]{:S(2)}, u32[]{:S(2)}) collective-permute-start(bf16[2,384,512]{2,1,0:T(8,128)(2,1)} %get-tuple-element.5), channel_id=1, source_target_pairs={{0,12},{4,0},{8,4},{12,8},{1,13},{5,1},{9,5},{13,9},{2,14},{6,2},{... | collective-permute-start | bytes 2359304 | tf_op jit(solution)/shard_map/ppermute | solution.py:71
  65.8 16.7 %collective-permute-start.2 = (bf16[2,384,512]{2,1,0:T(8,128)(2,1)}, bf16[2,384,512]{2,1,0:T(8,128)(2,1)S(1)}, u32[]{:S(2)}, u32[]{:S(2)}) collective-permute-start(bf16[2,384,512]{2,1,0:T(8,128)(2,1)} %get-tuple-element.5), channel_id=1, source_target_pairs={{0,4},{4,8},{8,12},{12,0},{1,5},{5,9},{9,13},{13,1},{2,6},{6,10},{... | collective-permute-start | bytes 2359304 | tf_op jit(solution)/shard_map/ppermute | solution.py:71
  67.8 16.3 %collective-permute-start.4 = (bf16[2,384,512]{2,1,0:T(8,128)(2,1)}, bf16[2,384,512]{2,1,0:T(8,128)(2,1)}, u32[]{:S(2)}, u32[]{:S(2)}) collective-permute-start(bf16[2,384,512]{2,1,0:T(8,128)(2,1)} %get-tuple-element.6), channel_id=1, source_target_pairs={{0,12},{4,0},{8,4},{12,8},{1,13},{5,1},{9,5},{13,9},{2,14},{6,2},{... | collective-permute-start | bytes 2359304 | tf_op jit(solution)/shard_map/ppermute | solution.py:71
  74.1 17.0 %collective-permute-start.5 = (bf16[2,384,512]{2,1,0:T(8,128)(2,1)S(1)}, bf16[2,384,512]{2,1,0:T(8,128)(2,1)}, u32[]{:S(2)}, u32[]{:S(2)}) collective-permute-start(bf16[2,384,512]{2,1,0:T(8,128)(2,1)S(1)} %collective-permute-done.1.refs_1_), channel_id=1, source_target_pairs={{0,4},{4,8},{8,12},{12,0},{1,5},{5,9},{9,13},{13,1},{2,6},{6,10},{... | collective-permute-start | bytes 2359304 | tf_op jit(solution)/shard_map/ppermute | solution.py:71
  76.0 16.4 %collective-permute-start.6 = (bf16[2,384,512]{2,1,0:T(8,128)(2,1)S(1)}, bf16[2,384,512]{2,1,0:T(8,128)(2,1)}, u32[]{:S(2)}, u32[]{:S(2)}) collective-permute-start(bf16[2,384,512]{2,1,0:T(8,128)(2,1)S(1)} %collective-permute-done.3.refs_3_), channel_id=1, source_target_pairs={{0,12},{4,0},{8,4},{12,8},{1,13},{5,1},{9,5},{13,9},{2,14},{6,2},{... | collective-permute-start | bytes 2359304 | tf_op jit(solution)/shard_map/ppermute | solution.py:71
  108.2 11.1 %copy-start = (bf16[384,320]{1,0:T(8,128)(2,1)}, bf16[384,320]{1,0:T(8,128)(2,1)S(1)}, u32[]{:S(2)}) copy-start(bf16[384,320]{1,0:T(8,128)(2,1)S(1)} %shard_map.85.mine_ref) | copy-start | bytes 737284
  108.2 11.1 %collective-permute-start.7 = (bf16[384,320]{1,0:T(8,128)(2,1)S(1)}, bf16[384,320]{1,0:T(8,128)(2,1)S(1)}, u32[]{:S(2)}, u32[]{:S(2)}) collective-permute-start(bf16[384,320]{1,0:T(8,128)(2,1)S(1)} %shard_map.85.mine_ref), channel_id=1, source_target_pairs={{0,1},{1,0},{2,3},{3,2},{4,5},{5,4},{6,7},{7,6},{8,9},{9,8},{10,11... | collective-permute-start | bytes 737288 | tf_op jit(solution)/shard_map/ppermute | solution.py:75
  119.3 0.7 copy-start.7
  127.1 7.0 %copy-start.9 = (f32[1280]{0:T(1024)S(1)}, f32[1280]{0:T(1024)}, u32[]{:S(2)}) copy-start(f32[1280]{0:T(1024)} %param.13) | copy-start | bytes 15364
  127.2 35.9 %copy-start.3 = (bf16[24,5120]{1,0:T(8,128)(2,1)S(1)}, bf16[24,5120]{1,0:T(8,128)(2,1)}, u32[]{:S(2)}) copy-start(bf16[24,5120]{1,0:T(8,128)(2,1)} %patches_ref.1) | copy-start | bytes 737284
  127.2 35.8 %all-to-all-start.2 = ((bf16[16,24,2560]{2,1,0:T(8,128)(2,1)}), bf16[16,24,2560]{2,1,0:T(8,128)(2,1)S(1)}, u32[]{:S(2)}, u32[]{:S(2)}) async-start(bf16[16,24,2560]{2,1,0:T(8,128)(2,1)} %shard_map.86), calls=%async_computation.2 | async-start | bytes 3932160 | tf_op jit(solution)/shard_map/all_to_all | solution.py:64
Sparse Core Ops, SparseCore 0:
  16.4 83.8 all-gather.2

commit v6 on v2

--- a/solution.py
+++ b/solution.py
@@ -116,91 +116,85 @@
 
 def start_w1(w_ref, w1, sems):
     base = HID_OWN + IN_OWN
-    copies = [
-        pltpu.make_async_copy(w_ref.at[:, HID_OWN:base], w1.at[:, :, 0:256], sems.at[0]),
-        pltpu.make_async_copy(w_ref.at[:, base:W_ROWS, 0:128], w1.at[:, 0:TAIL, 256:384], sems.at[1]),
-        pltpu.make_async_copy(w_ref.at[:, base:W_ROWS, 128:256], w1.at[:, TAIL:IN_OWN, 256:384], sems.at[2]),
-    ]
-    for copy in copies:
-        copy.start()
-    return copies
-
-
-def w1_chunk(w1, g, prompts):
-    return w1[prompts * g : prompts * (g + 1)].reshape(prompts * IN_OWN, 384)[:, :HID_OWN]
-
-
-GATHERED = ((0, (0, 1, 2, 3), 0), (1, (0, 1), 3), (2, (2, 3), 3), (3, (2, 3), 1), (4, (0, 1), 1), (5, (0, 1), 2), (6, (2, 3), 2))
+    quarters = []
+    for q in range(SIDE):
+        copies = [
+            pltpu.make_async_copy(w_ref.at[q, :, :, HID_OWN:base], w1.at[q, :, :, :, 0:256], sems.at[q, 0]),
+            pltpu.make_async_copy(
+                w_ref.at[q, :, :, base:W_ROWS, 0:128], w1.at[q, :, :, 0:TAIL, 256:384], sems.at[q, 1]
+            ),
+            pltpu.make_async_copy(
+                w_ref.at[q, :, :, base:W_ROWS, 128:256], w1.at[q, :, :, TAIL:IN_OWN, 256:384], sems.at[q, 2]
+            ),
+        ]
+        for copy in copies:
+            copy.start()
+        quarters.append(copies)
+    return quarters
+
+
+def w1_chunks(w1, quarters):
+    for q in range(SIDE):
+        for copy in quarters[q]:
+            copy.wait()
+        for h in range(2):
+            rows = w1[q, 2 * h : 2 * h + 2].reshape(4 * IN_OWN, 384)[:, :HID_OWN]
+            at = (2 * q + h) * 4 * IN_OWN
+            yield slice(at, at + 4 * IN_OWN), rows
+
+
+GATHERED = (
+    (0, ((0, 0), (0, 1), (0, 2), (0, 3))),
+    (3, ((1, 0), (1, 1), (2, 0), (2, 1))),
+    (1, ((4, 0), (4, 1), (3, 0), (3, 1))),
+    (2, ((5, 0), (5, 1), (6, 0), (6, 1))),
+)
 
 
 def act_kernel(w_ref, *refs):
-    sums, (slope_ref, act_ref, low_ref, high_ref, w2, w1, sems2, sems1) = refs[:7], refs[7:]
+    sums, (slope_ref, act_ref, far_ref, w2, w1, sems2, sems1) = refs[:7], refs[7:]
     even, first, second = place_in_plane()
-    slots, copies = [], []
-    for operand, places, offset in GATHERED:
-        for n, k in enumerate(places):
-            s = lax.rem(second + offset, SIDE)
-            block = jnp.where(even, s * SIDE + k, k * SIDE + s)
-            i = len(slots)
-            pair = [
-                pltpu.make_async_copy(
-                    w_ref.at[2 * block + h, 0:HID_OWN],
-                    w2.at[:, pl.ds((2 * i + h) * W2_COLS, W2_COLS)],
-                    sems2.at[i, h],
-                )
-                for h in range(2)
-            ]
-            for copy in pair:
-                copy.start()
-            copies.append(pair)
-            slots.append((sums[operand], n))
-    late = start_w1(w_ref, w1, sems1)
+    copies = []
+    for n, (offset, _) in enumerate(GATHERED):
+        other = lax.rem(second + offset, SIDE)
+        by_row = pltpu.make_async_copy(w_ref.at[other, :, :, 0:HID_OWN], w2.at[n], sems2.at[n])
+        by_col = pltpu.make_async_copy(w_ref.at[:, other, :, 0:HID_OWN], w2.at[n], sems2.at[n])
+        pl.when(even)(by_row.start)
+        pl.when(jnp.logical_not(even))(by_col.start)
+        copies.append(by_row)
+    quarters = start_w1(w_ref, w1, sems1)
     hidden = None
-    for i, (ref, n) in enumerate(slots):
-        for copy in copies[i]:
-            copy.wait()
-        part = dot_t(ref[n], w2[:, i * COLS : (i + 1) * COLS])
-        hidden = part if hidden is None else hidden + part
+    for n, (_, blocks) in enumerate(GATHERED):
+        copies[n].wait()
+        for k, (operand, index) in enumerate(blocks):
+            block = sums[operand][index]
+            part = dot_t(block[:, :W2_COLS], w2[n, k, 0]) + dot_t(block[:, W2_COLS:], w2[n, k, 1])
+            hidden = part if hidden is None else hidden + part
     act_ref[...] = (hidden * slope_ref[...]).astype(BF16)
     far = lax.rem(first + 2, SIDE)
     rows = act_ref[pl.ds(pl.multiple_of(far * 96, 96), 96), :]
-    for copy in late:
-        copy.wait()
-    for g in range(8):
-        part = dot_t(rows, w1_chunk(w1, g, 4)).astype(BF16)
-        cols = slice(640 * g, 640 * (g + 1))
-        low_ref[:, cols] = part[:48]
-        high_ref[:, cols] = part[48:]
-
-
-def rest_kernel(w_ref, act_ref, right_low, right_high, left_low, left_high, own_ref, w1, sems1):
+    for cols, w in w1_chunks(w1, quarters):
+        far_ref[:, cols] = dot_t(rows, w).astype(BF16)
+
+
+def rest_kernel(w_ref, act_ref, right_ref, left_ref, own_ref, w1, sems1):
     _, first, _ = place_in_plane()
-    late = start_w1(w_ref, w1, sems1)
+    quarters = start_w1(w_ref, w1, sems1)
     blocks = [
         act_ref[pl.ds(pl.multiple_of(lax.rem(first + by, SIDE) * 96, 96), 96), :] for by in (1, 3, 0)
     ]
     rows = jnp.concatenate(blocks, axis=0)
-    for copy in late:
-        copy.wait()
-    for g in range(8):
-        part = dot_t(rows, w1_chunk(w1, g, 4)).astype(BF16)
-        cols = slice(640 * g, 640 * (g + 1))
-        right_low[:, cols] = part[0:48]
-        right_high[:, cols] = part[48:96]
-        left_low[:, cols] = part[96:144]
-        left_high[:, cols] = part[144:192]
+    for cols, w in w1_chunks(w1, quarters):
+        part = dot_t(rows, w).astype(BF16)
+        right_ref[:, cols] = part[0:96]
+        left_ref[:, cols] = part[96:192]
         own_ref[:, cols] = part[192:288]
 
 
-def pair_kernel(a_ref, b_ref, out_ref):
-    out_ref[...] = (a_ref[...].astype(F32) + b_ref[...].astype(F32)).astype(BF16)
-
-
-def join_kernel(own_ref, low_a, low_b, high_a, high_b, out_ref):
-    low = own_ref[0:48].astype(F32) + low_a[...].astype(F32) + low_b[...].astype(F32)
-    high = own_ref[48:96].astype(F32) + high_a[...].astype(F32) + high_b[...].astype(F32)
-    out_ref[0:48] = low.astype(BF16)
-    out_ref[48:96] = high.astype(BF16)
+def join_kernel(own_ref, a_ref, b_ref, c_ref, out_ref):
+    total = own_ref[...].astype(F32) + a_ref[...].astype(F32)
+    total = total + b_ref[...].astype(F32) + c_ref[...].astype(F32)
+    out_ref[...] = total.astype(BF16)
 
 
 def norm_kernel(recv_ref, patches_ref, gain_ref, out_ref):
@@ -254,36 +248,30 @@
     even = lax.axis_index("prompt") % 2 == 0
     slope = gelu_slope(pre_act.astype(F32)).reshape(SIDE, SIDE, OWN, HID_OWN)
     slope = jnp.where(even, slope.transpose(1, 0, 2, 3), slope).reshape(ROWS, HID_OWN)
-    w1_scratch = [pltpu.VMEM((PROMPTS, IN_OWN, 384), BF16), pltpu.SemaphoreType.DMA((3,))]
-    act, far_low, far_high = call(
+    weights = weights.reshape(SIDE, SIDE, 2, W_ROWS, 256)
+    w1_scratch = [pltpu.VMEM((SIDE, SIDE, 2, IN_OWN, 384), BF16), pltpu.SemaphoreType.DMA((SIDE, 3))]
+    act, far = call(
         act_kernel,
-        ((ROWS, HID_OWN), (48, HID), (48, HID)),
+        ((ROWS, HID_OWN), (96, HID)),
         [ANY] + [VMEM] * 8,
         flops=5 << 29,
         moved=12 << 20,
-        vmem=30,
+        vmem=50,
         scratch=[
-            pltpu.VMEM((HID_OWN, D_LLM), BF16),
+            pltpu.VMEM((SIDE, SIDE, 2, HID_OWN, W2_COLS), BF16),
             w1_scratch[0],
-            pltpu.SemaphoreType.DMA((ROLLOUTS, 2)),
+            pltpu.SemaphoreType.DMA((SIDE,)),
             w1_scratch[1],
         ],
     )(weights, line, a1, a2, b1, b2, a3, b3, slope)
 
-    via_right, via_left = shift(far_low, 0, 1), shift(far_high, 0, -1)
-    right_low, right_high, left_low, left_high, own = call(
-        rest_kernel,
-        ((48, HID),) * 4 + ((96, HID),),
-        [ANY, VMEM],
-        flops=1 << 30,
-        moved=8 << 20,
-        vmem=20,
-        scratch=w1_scratch,
+    from_far = shift(far, 0, 2)
+    right, left, own = call(
+        rest_kernel, ((96, HID),) * 3, [ANY, VMEM], flops=1 << 30, moved=8 << 20, vmem=54, scratch=w1_scratch
     )(weights, act)
-    high_a, low_b = shift(right_high, 0, 1), shift(left_low, 0, -1)
-    pair = call(pair_kernel, (48, HID), [VMEM] * 2)
-    low_a, high_b = shift(pair(right_low, via_right), 0, 1), shift(pair(left_high, via_left), 0, -1)
-    halfway = call(join_kernel, (96, HID), [VMEM] * 5)(own, low_a, low_b, high_a, high_b)
+    right, left, from_far = lax.optimization_barrier((right, left, from_far))
+    from_left, from_right = shift(right, 0, 1), shift(left, 0, -1)
+    halfway = call(join_kernel, (96, HID), [VMEM] * 4)(own, from_far, from_left, from_right)
     last = exchange(halfway.reshape(SIDE, OWN, HID), 1)
     return call(norm_kernel, (OWN, HID), [VMEM] * 3)(last, patches, ln_gain.reshape(1, VIT))
 

time: 165 us -> 169 us (1.024); the launches traced: 162 us -> 168 us
  waiting for transfers between devices: 36.8 us -> 52.5 us
  starting transfers between devices: 47.1 us -> 34.4 us
  Pallas kernels: 16 us -> 20.3 us
    ppermute x12 -> x9, waiting for transfers between devices: 18.2 us -> 33.8 us  [shift(): return lax.ppermute(value, AXES, pairs)]
    ppermute x12 -> x9, starting transfers between devices: 42.4 us -> 30.1 us  [shift(): return lax.ppermute(value, AXES, pairs)]
    pallas_call x2, Pallas kernels: 12 us -> 16.4 us  [the longest x1 9.95 us: per_device(): call(act_kernel, ((ROWS, HID_OWN), (96, HID)), [ANY] + [VMEM] * 8, flops=...]
    unnamed x19 -> x21, local copies, waits for them, and re-layouts: 7.48 us -> 6.18 us
    pallas_call x7 -> x5, Pallas kernels: 4.04 us -> 3.93 us  [call(): return (lambda *args: run(*args)[0]) if one else run]
  transfers between devices with their start and end apart: 14 -> 11, of which waited for: 9 -> 10; matrix products, arithmetic and copies ran while one was open for 1% -> 1% of each run, Pallas kernels for 2% -> 4%
where the time goes in v6:
time: 169 us; the launch traced here: 168 us
  waiting for transfers between devices  52.5 us (31%)
  blocking collectives  38.8 us (23%)
  starting transfers between devices  34.4 us (20%)
  Pallas kernels  20.3 us (12%)
  between operations  14.2 us (8%)
  local copies, waits for them, and re-layouts  7.46 us (4%)
    ppermute x9, waiting for transfers between devices, shift(): return lax.ppermute(value, AXES, pairs)  33.8 us
    ppermute x9, starting transfers between devices, shift(): return lax.ppermute(value, AXES, pairs)  30.1 us
    all_to_all x1, blocking collectives, per_device(): lax.all_to_all(outgoing, 'rollout', split_axis=0, concat_axis=0, tiled=True)  21.7 us
    all_to_all x1, blocking collectives, exchange(): lax.all_to_all(blocks, AXES, split_axis=0, concat_axis=0, axis_index_grou...  17.1 us
    all_to_all x1, waiting for transfers between devices, exchange(): lax.all_to_all(blocks, AXES, split_axis=0, concat_axis=0, axis_index_grou...  10.5 us
    pallas_call x1, Pallas kernels, per_device(): call(act_kernel, ((ROWS, HID_OWN), (96, HID)), [ANY] + [VMEM] * 8, flops=...  9.95 us
    all_gather x1, waiting for transfers between devices, per_device(): weights = lax.all_gather(weights, 'prompt', axis=0, tiled=False)  8.18 us
    pallas_call x1, Pallas kernels, per_device(): call(rest_kernel, ((96, HID),) * 3, [ANY, VMEM], flops=1 << 30, moved=8 <...  6.46 us
  transfers between devices with their start and end apart: 11, of which 10 were waited for; matrix products, arithmetic and copies ran while one was open for 1% of the time, Pallas kernels for 4%

profile of v6, /device:TPU:6, one launch (start us, length us, event | category | flops | bytes accessed | tf_op | source)
XLA Modules:
  0.0 168.0 jit_solution(7205052150913725980)
XLA Ops:
  6.5 0.9 copy-done.4
  7.5 0.9 copy-done.5
  8.4 0.7 shard_map.82
  9.8 1.2 copy-done.1
  11.7 21.7 %all_to_all.15.recv_ref = bf16[16,64,512]{2,1,0:T(8,128)(2,1)S(1)} all-to-all(bf16[16,64,512]{2,1,0:T(8,128)(2,1)S(1)} %shard_map.83), channel_id=1, replica_groups=mesh['prompt'=32,'rollout'=16] {'rollout'}, dimensions={0} | all-to-all | bytes 2097152 | tf_op jit(solution)/shard_map/all_to_all | solution.py:241
  34.1 17.1 %all_to_all.16.refs_0_ = bf16[4,384,512]{2,1,0:T(8,128)(2,1)S(1)} all-to-all(bf16[4,384,512]{2,1,0:T(8,128)(2,1)S(1)} %shard_map.84), channel_id=1, replica_groups={{0,1,2,3},{4,5,6,7},{8,9,10,11},{12,13,14,15},{16,20,24,28},{17,21,25,2..., dimensions={0} | all-to-all | bytes 3145728 | tf_op jit(solution)/shard_map/all_to_all | solution.py:52
  51.1 1.3 fusion.6
  52.8 1.9 %collective-permute-start = (bf16[2,384,512]{2,1,0:T(8,128)(2,1)}, bf16[2,384,512]{2,1,0:T(8,128)(2,1)S(1)}, u32[]{:S(2)}, u32[]{:S(2)}) collective-permute-start(bf16[2,384,512]{2,1,0:T(8,128)(2,1)} %get-tuple-element.22), channel_id=1, source_target_pairs={{0,4},{4,8},{8,12},{12,0},{1,5},{5,9},{9,13},{13,1},{2,6},{6,10},{... | collective-permute-start | bytes 2359304 | tf_op jit(solution)/shard_map/ppermute | solution.py:61
  54.7 5.1 %collective-permute-start.2 = (bf16[2,384,512]{2,1,0:T(8,128)(2,1)}, bf16[2,384,512]{2,1,0:T(8,128)(2,1)S(1)}, u32[]{:S(2)}, u32[]{:S(2)}) collective-permute-start(bf16[2,384,512]{2,1,0:T(8,128)(2,1)} %get-tuple-element.21), channel_id=1, source_target_pairs={{0,12},{4,0},{8,4},{12,8},{1,13},{5,1},{9,5},{13,9},{2,14},{6,2},{... | collective-permute-start | bytes 2359304 | tf_op jit(solution)/shard_map/ppermute | solution.py:61
  59.9 1.9 %collective-permute-start.1 = (bf16[2,384,512]{2,1,0:T(8,128)(2,1)}, bf16[2,384,512]{2,1,0:T(8,128)(2,1)S(1)}, u32[]{:S(2)}, u32[]{:S(2)}) collective-permute-start(bf16[2,384,512]{2,1,0:T(8,128)(2,1)} %get-tuple-element.21), channel_id=1, source_target_pairs={{0,4},{4,8},{8,12},{12,0},{1,5},{5,9},{9,13},{13,1},{2,6},{6,10},{... | collective-permute-start | bytes 2359304 | tf_op jit(solution)/shard_map/ppermute | solution.py:61
  61.8 5.1 %collective-permute-start.3 = (bf16[2,384,512]{2,1,0:T(8,128)(2,1)}, bf16[2,384,512]{2,1,0:T(8,128)(2,1)}, u32[]{:S(2)}, u32[]{:S(2)}) collective-permute-start(bf16[2,384,512]{2,1,0:T(8,128)(2,1)} %get-tuple-element.22), channel_id=1, source_target_pairs={{0,12},{4,0},{8,4},{12,8},{1,13},{5,1},{9,5},{13,9},{2,14},{6,2},{... | collective-permute-start | bytes 2359304 | tf_op jit(solution)/shard_map/ppermute | solution.py:61
  66.9 1.2 collective-permute-done.refs_1_
  68.1 1.9 %collective-permute-start.4 = (bf16[2,384,512]{2,1,0:T(8,128)(2,1)S(1)}, bf16[2,384,512]{2,1,0:T(8,128)(2,1)}, u32[]{:S(2)}, u32[]{:S(2)}) collective-permute-start(bf16[2,384,512]{2,1,0:T(8,128)(2,1)S(1)} %collective-permute-done.refs_1_), channel_id=1, source_target_pairs={{0,4},{4,8},{8,12},{12,0},{1,5},{5,9},{9,13},{13,1},{2,6},{6,10},{... | collective-permute-start | bytes 2359304 | tf_op jit(solution)/shard_map/ppermute | solution.py:61
  70.0 5.1 %collective-permute-start.5 = (bf16[2,384,512]{2,1,0:T(8,128)(2,1)S(1)}, bf16[2,384,512]{2,1,0:T(8,128)(2,1)}, u32[]{:S(2)}, u32[]{:S(2)}) collective-permute-start(bf16[2,384,512]{2,1,0:T(8,128)(2,1)S(1)} %collective-permute-done.2.refs_3_), channel_id=1, source_target_pairs={{0,12},{4,0},{8,4},{12,8},{1,13},{5,1},{9,5},{13,9},{2,14},{6,2},{... | collective-permute-start | bytes 2359304 | tf_op jit(solution)/shard_map/ppermute | solution.py:61
  75.7 0.8 collective-permute-done.1.refs_2_
  76.5 1.6 collective-permute-done.3.refs_4_
  78.1 7.0 %collective-permute-done.4.refs_5_ = bf16[2,384,512]{2,1,0:T(8,128)(2,1)} collective-permute-done((bf16[2,384,512]{2,1,0:T(8,128)(2,1)S(1)}, bf16[2,384,512]{2,1,0:T(8,128)(2,1)}, u32[]{:S(2)}, u32[]{:S(2)}) %collective-permute-start.4) | collective-permute-done | bytes 786464 | tf_op jit(solution)/shard_map/ppermute | solution.py:61
  85.1 1.4 collective-permute-done.5.refs_6_
  86.4 8.2 %all-gather.3.cloned.1.call-done = bf16[17920,256]{1,0:T(8,128)(2,1)} async-done(((bf16[560,256]{1,0:T(8,128)(2,1)}), bf16[17920,256]{1,0:T(8,128)(2,1)}) %all-gather.3.cloned.1.call-update) | async-done | bytes 9175056 | tf_op jit(solution)/shard_map/all_gather | solution.py:236
  94.6 9.9 %shard_map.85 = (bf16[384,320]{1,0:T(8,128)(2,1)S(1)}, bf16[96,5120]{1,0:T(8,128)(2,1)}) custom-call(bf16[4,4,2,560,256]{4,3,2,1,0:T(8,128)(2,1)} %bitcast.11, bf16[4,384,512]{2,1,0:T(8,128)(2,1)} %copy-done.7, bf16[2,384,512]{2,1,0:T(8,128)(2,1)S(1)} %collective-permute-done.refs_1_, bf16[2,384,512]{2,1,0:T(8,128)(2,1)S(1)} %collective-permute-done.1.refs_2_, ...), custom_call_target="tpu_custom_call" | custom-call | flops 2684354560 | bytes 12582912 | tf_op jit(solution)/shard_map/pallas_call | solution.py:253
  105.3 3.2 %collective-permute-start.6 = (bf16[96,5120]{1,0:T(8,128)(2,1)}, bf16[96,5120]{1,0:T(8,128)(2,1)S(1)}, u32[]{:S(2)}, u32[]{:S(2)}) collective-permute-start(bf16[96,5120]{1,0:T(8,128)(2,1)} %get-tuple-element.17), channel_id=1, source_target_pairs={{0,2},{1,3},{2,0},{3,1},{4,6},{5,7},{6,4},{7,5},{8,10},{9,11},{10,... | collective-permute-start | bytes 2949128 | tf_op jit(solution)/shard_map/ppermute | solution.py:61
  108.4 6.5 %shard_map.86 = (bf16[96,5120]{1,0:T(8,128)(2,1)}, bf16[96,5120]{1,0:T(8,128)(2,1)}, bf16[96,5120]{1,0:T(8,128)(2,1)}) custom-call(bf16[4,4,2,560,256]{4,3,2,1,0:T(8,128)(2,1)} %bitcast.12, bf16[384,320]{1,0:T(8,128)(2,1)} %copy-done.2), custom_call_target="tpu_custom_call" | custom-call | flops 1073741824 | bytes 8388608 | tf_op jit(solution)/shard_map/pallas_call | solution.py:269
  114.9 8.1 %collective-permute-done.6.a_ref = bf16[96,5120]{1,0:T(8,128)(2,1)S(1)} collective-permute-done((bf16[96,5120]{1,0:T(8,128)(2,1)}, bf16[96,5120]{1,0:T(8,128)(2,1)S(1)}, u32[]{:S(2)}, u32[]{:S(2)}) %collective-permute-start.6) | collective-permute-done | bytes 983072 | tf_op jit(solution)/shard_map/ppermute | solution.py:61
  123.0 2.3 %collective-permute-start.7 = (bf16[96,5120]{1,0:T(8,128)(2,1)}, bf16[96,5120]{1,0:T(8,128)(2,1)S(1)}, u32[]{:S(2)}, u32[]{:S(2)}) collective-permute-start(bf16[96,5120]{1,0:T(8,128)(2,1)} %get-tuple-element.19), channel_id=1, source_target_pairs={{0,1},{1,2},{2,3},{3,0},{4,5},{5,6},{6,7},{7,4},{8,9},{9,10},{10,1... | collective-permute-start | bytes 2949128 | tf_op jit(solution)/shard_map/ppermute | solution.py:61
  125.3 3.5 %collective-permute-start.8 = (bf16[96,5120]{1,0:T(8,128)(2,1)}, bf16[96,5120]{1,0:T(8,128)(2,1)S(1)}, u32[]{:S(2)}, u32[]{:S(2)}) collective-permute-start(bf16[96,5120]{1,0:T(8,128)(2,1)} %get-tuple-element.20), channel_id=1, source_target_pairs={{0,3},{1,0},{2,1},{3,2},{4,7},{5,4},{6,5},{7,6},{8,11},{9,8},{10,9... | collective-permute-start | bytes 2949128 | tf_op jit(solution)/shard_map/ppermute | solution.py:61
  128.8 10.3 %collective-permute-done.7.b_ref = bf16[96,5120]{1,0:T(8,128)(2,1)S(1)} collective-permute-done((bf16[96,5120]{1,0:T(8,128)(2,1)}, bf16[96,5120]{1,0:T(8,128)(2,1)S(1)}, u32[]{:S(2)}, u32[]{:S(2)}) %collective-permute-start.7) | collective-permute-done | bytes 983072 | tf_op jit(solution)/shard_map/ppermute | solution.py:61
  139.2 3.5 %collective-permute-done.8.c_ref = bf16[96,5120]{1,0:T(8,128)(2,1)S(1)} collective-permute-done((bf16[96,5120]{1,0:T(8,128)(2,1)}, bf16[96,5120]{1,0:T(8,128)(2,1)S(1)}, u32[]{:S(2)}, u32[]{:S(2)}) %collective-permute-start.8) | collective-permute-done | bytes 983072 | tf_op jit(solution)/shard_map/ppermute | solution.py:61
  142.7 1.2 copy-done
  143.9 1.5 shard_map.87
  145.4 4.2 %all-to-all-start.2 = ((bf16[4,24,5120]{2,1,0:T(8,128)(2,1)}), bf16[4,24,5120]{2,1,0:T(8,128)(2,1)S(1)}, u32[]{:S(2)}, u32[]{:S(2)}) async-start(bf16[4,24,5120]{2,1,0:T(8,128)(2,1)} %bitcast.6), calls=%async_computation.2 | async-start | bytes 1966080 | tf_op jit(solution)/shard_map/all_to_all | solution.py:52
  149.6 10.5 %all-to-all-done.2.recv_ref = bf16[4,24,5120]{2,1,0:T(8,128)(2,1)S(1)} async-done(((bf16[4,24,5120]{2,1,0:T(8,128)(2,1)}), bf16[4,24,5120]{2,1,0:T(8,128)(2,1)S(1)}, u32[]{:S(2)}, u32[]{:S(2)}) %all-to-all-start.2) | async-done | bytes 983072 | tf_op jit(solution)/shard_map/all_to_all | solution.py:52
  160.2 1.0 shard_map.88
  (25 shorter events, 3.0 us)
Async XLA Ops:
  6.5 88.1 %all-gather.3.cloned.1.call-start = ((), (), s32[]{:S(2)}) async-start(), calls=%async_computation.3 | async-start | bytes 9461760 | tf_op jit(solution)/shard_map/all_gather | solution.py:236
  6.5 0.9 copy-start.4
  7.5 0.9 copy-start.5
  9.8 1.2 copy-start.1
  11.0 0.7 copy-start.6
  51.1 1.7 copy-start.7
  51.1 24.0 %copy-start.8 = (bf16[384,320]{0,1:T(8,128)(2,1)S(1)}, bf16[384,320]{0,1:T(8,128)(2,1)}, u32[]{:S(2)}) copy-start(bf16[384,320]{0,1:T(8,128)(2,1)} %param.11) | copy-start | bytes 737284
  52.8 15.3 %collective-permute-start = (bf16[2,384,512]{2,1,0:T(8,128)(2,1)}, bf16[2,384,512]{2,1,0:T(8,128)(2,1)S(1)}, u32[]{:S(2)}, u32[]{:S(2)}) collective-permute-start(bf16[2,384,512]{2,1,0:T(8,128)(2,1)} %get-tuple-element.22), channel_id=1, source_target_pairs={{0,4},{4,8},{8,12},{12,0},{1,5},{5,9},{9,13},{13,1},{2,6},{6,10},{... | collective-permute-start | bytes 2359304 | tf_op jit(solution)/shard_map/ppermute | solution.py:61
  54.7 15.3 %collective-permute-start.2 = (bf16[2,384,512]{2,1,0:T(8,128)(2,1)}, bf16[2,384,512]{2,1,0:T(8,128)(2,1)S(1)}, u32[]{:S(2)}, u32[]{:S(2)}) collective-permute-start(bf16[2,384,512]{2,1,0:T(8,128)(2,1)} %get-tuple-element.21), channel_id=1, source_target_pairs={{0,12},{4,0},{8,4},{12,8},{1,13},{5,1},{9,5},{13,9},{2,14},{6,2},{... | collective-permute-start | bytes 2359304 | tf_op jit(solution)/shard_map/ppermute | solution.py:61
  59.9 16.7 %collective-permute-start.1 = (bf16[2,384,512]{2,1,0:T(8,128)(2,1)}, bf16[2,384,512]{2,1,0:T(8,128)(2,1)S(1)}, u32[]{:S(2)}, u32[]{:S(2)}) collective-permute-start(bf16[2,384,512]{2,1,0:T(8,128)(2,1)} %get-tuple-element.21), channel_id=1, source_target_pairs={{0,4},{4,8},{8,12},{12,0},{1,5},{5,9},{9,13},{13,1},{2,6},{6,10},{... | collective-permute-start | bytes 2359304 | tf_op jit(solution)/shard_map/ppermute | solution.py:61
  61.8 16.3 %collective-permute-start.3 = (bf16[2,384,512]{2,1,0:T(8,128)(2,1)}, bf16[2,384,512]{2,1,0:T(8,128)(2,1)}, u32[]{:S(2)}, u32[]{:S(2)}) collective-permute-start(bf16[2,384,512]{2,1,0:T(8,128)(2,1)} %get-tuple-element.22), channel_id=1, source_target_pairs={{0,12},{4,0},{8,4},{12,8},{1,13},{5,1},{9,5},{13,9},{2,14},{6,2},{... | collective-permute-start | bytes 2359304 | tf_op jit(solution)/shard_map/ppermute | solution.py:61
  68.1 17.0 %collective-permute-start.4 = (bf16[2,384,512]{2,1,0:T(8,128)(2,1)S(1)}, bf16[2,384,512]{2,1,0:T(8,128)(2,1)}, u32[]{:S(2)}, u32[]{:S(2)}) collective-permute-start(bf16[2,384,512]{2,1,0:T(8,128)(2,1)S(1)} %collective-permute-done.refs_1_), channel_id=1, source_target_pairs={{0,4},{4,8},{8,12},{12,0},{1,5},{5,9},{9,13},{13,1},{2,6},{6,10},{... | collective-permute-start | bytes 2359304 | tf_op jit(solution)/shard_map/ppermute | solution.py:61
  70.0 16.4 %collective-permute-start.5 = (bf16[2,384,512]{2,1,0:T(8,128)(2,1)S(1)}, bf16[2,384,512]{2,1,0:T(8,128)(2,1)}, u32[]{:S(2)}, u32[]{:S(2)}) collective-permute-start(bf16[2,384,512]{2,1,0:T(8,128)(2,1)S(1)} %collective-permute-done.2.refs_3_), channel_id=1, source_target_pairs={{0,12},{4,0},{8,4},{12,8},{1,13},{5,1},{9,5},{13,9},{2,14},{6,2},{... | collective-permute-start | bytes 2359304 | tf_op jit(solution)/shard_map/ppermute | solution.py:61
  104.5 0.7 copy-start.2
  105.3 17.7 %collective-permute-start.6 = (bf16[96,5120]{1,0:T(8,128)(2,1)}, bf16[96,5120]{1,0:T(8,128)(2,1)S(1)}, u32[]{:S(2)}, u32[]{:S(2)}) collective-permute-start(bf16[96,5120]{1,0:T(8,128)(2,1)} %get-tuple-element.17), channel_id=1, source_target_pairs={{0,2},{1,3},{2,0},{3,1},{4,6},{5,7},{6,4},{7,5},{8,10},{9,11},{10,... | collective-permute-start | bytes 2949128 | tf_op jit(solution)/shard_map/ppermute | solution.py:61
  123.0 16.2 %collective-permute-start.7 = (bf16[96,5120]{1,0:T(8,128)(2,1)}, bf16[96,5120]{1,0:T(8,128)(2,1)S(1)}, u32[]{:S(2)}, u32[]{:S(2)}) collective-permute-start(bf16[96,5120]{1,0:T(8,128)(2,1)} %get-tuple-element.19), channel_id=1, source_target_pairs={{0,1},{1,2},{2,3},{3,0},{4,5},{5,6},{6,7},{7,4},{8,9},{9,10},{10,1... | collective-permute-start | bytes 2949128 | tf_op jit(solution)/shard_map/ppermute | solution.py:61
  125.3 17.4 %collective-permute-start.8 = (bf16[96,5120]{1,0:T(8,128)(2,1)}, bf16[96,5120]{1,0:T(8,128)(2,1)S(1)}, u32[]{:S(2)}, u32[]{:S(2)}) collective-permute-start(bf16[96,5120]{1,0:T(8,128)(2,1)} %get-tuple-element.20), channel_id=1, source_target_pairs={{0,3},{1,0},{2,1},{3,2},{4,7},{5,4},{6,5},{7,6},{8,11},{9,8},{10,9... | collective-permute-start | bytes 2949128 | tf_op jit(solution)/shard_map/ppermute | solution.py:61
  142.7 1.2 copy-start
  145.4 4.3 %copy-start.9 = (f32[1280]{0:T(1024)S(1)}, f32[1280]{0:T(1024)}, u32[]{:S(2)}) copy-start(f32[1280]{0:T(1024)} %param.13) | copy-start | bytes 15364
  145.4 14.8 %copy-start.3 = (bf16[24,5120]{1,0:T(8,128)(2,1)S(1)}, bf16[24,5120]{1,0:T(8,128)(2,1)}, u32[]{:S(2)}) copy-start(bf16[24,5120]{1,0:T(8,128)(2,1)} %patches_ref.1) | copy-start | bytes 737284
  145.4 14.8 %all-to-all-start.2 = ((bf16[4,24,5120]{2,1,0:T(8,128)(2,1)}), bf16[4,24,5120]{2,1,0:T(8,128)(2,1)S(1)}, u32[]{:S(2)}, u32[]{:S(2)}) async-start(bf16[4,24,5120]{2,1,0:T(8,128)(2,1)} %bitcast.6), calls=%async_computation.2 | async-start | bytes 1966080 | tf_op jit(solution)/shard_map/all_to_all | solution.py:52
Sparse Core Ops, SparseCore 0:
  9.5 85.0 all-gather.2

commit v7 on v4

--- a/solution.py
+++ b/solution.py
@@ -113,58 +113,62 @@
         out_ref[k] = value
 
 
-def start_w1(w_ref, w1, sems):
+GATHERED = (
+    (0, ((0, 0),)),
+    (3, ((1, 0), (2, 2))),
+    (1, ((4, 0), (3, 2))),
+    (2, ((5, 0), (6, 2))),
+)
+
+
+def mlp_kernel(w_ref, *refs):
+    sums, (slope_ref, out_ref, s, w2, w1, w1_tail, out, sems2, sems1, out_sems) = refs[:7], refs[7:]
+    even, second = place_in_plane()
     base = HID_OWN + IN_OWN
-    copies = [
-        pltpu.make_async_copy(w_ref.at[:, HID_OWN:base], w1.at[:, :, 0:256], sems.at[0]),
-        pltpu.make_async_copy(w_ref.at[:, base:W_ROWS, 0:128], w1.at[:, 0:TAIL, 256:384], sems.at[1]),
-        pltpu.make_async_copy(w_ref.at[:, base:W_ROWS, 128:256], w1.at[:, TAIL:IN_OWN, 256:384], sems.at[2]),
-    ]
-    for copy in copies:
-        copy.start()
-    return copies
-
-
-def w1_chunk(w1, g, prompts):
-    return w1[prompts * g : prompts * (g + 1)].reshape(prompts * IN_OWN, 384)[:, :HID_OWN]
-
-
-GATHERED = ((0, (0, 1, 2, 3), 0), (1, (0, 1), 3), (2, (2, 3), 3), (3, (2, 3), 1), (4, (0, 1), 1), (5, (0, 1), 2), (6, (2, 3), 2))
-
-
-def mlp_kernel(w_ref, *refs):
-    sums, (slope_ref, out_ref, w2, w1, sems2, sems1) = refs[:7], refs[7:]
-    even, second = place_in_plane()
-    slots, copies = [], []
-    for operand, places, offset in GATHERED:
-        for n, k in enumerate(places):
-            s = lax.rem(second + offset, SIDE)
-            block = jnp.where(even, s * SIDE + k, k * SIDE + s)
-            i = len(slots)
-            pair = [
-                pltpu.make_async_copy(
-                    w_ref.at[2 * block + h, 0:HID_OWN],
-                    w2.at[:, pl.ds((2 * i + h) * W2_COLS, W2_COLS)],
-                    sems2.at[i, h],
-                )
-                for h in range(2)
-            ]
-            for copy in pair:
-                copy.start()
-            copies.append(pair)
-            slots.append((sums[operand], n))
-    late = start_w1(w_ref, w1, sems1)
+    copies, late = [], []
+    for n, (offset, parts) in enumerate(GATHERED):
+        other = lax.rem(second + offset, SIDE)
+        by_row = pltpu.make_async_copy(w_ref.at[other, :, :, 0:HID_OWN], w2.at[n], sems2.at[n, 0])
+        by_col = pltpu.make_async_copy(w_ref.at[:, other, :, 0:HID_OWN], w2.at[n], sems2.at[n, 0])
+        pl.when(even)(by_row.start)
+        pl.when(jnp.logical_not(even))(by_col.start)
+        group = [by_row]
+        for h, (operand, k) in enumerate(parts):
+            count = SIDE // len(parts)
+            copy = pltpu.make_async_copy(sums[operand], s.at[n, k : k + count], sems2.at[n, h + 1])
+            copy.start()
+            group.append(copy)
+        copies.append(group)
+    for q in range(SIDE):
+        pair = [
+            pltpu.make_async_copy(w_ref.at[q, :, :, HID_OWN:base], w1.at[q], sems1.at[q, 0]),
+            pltpu.make_async_copy(w_ref.at[q, :, :, base:W_ROWS], w1_tail.at[q], sems1.at[q, 1]),
+        ]
+        for copy in pair:
+            copy.start()
+        late.append(pair)
     hidden = None
-    for i, (ref, n) in enumerate(slots):
-        for copy in copies[i]:
+    for n in range(SIDE):
+        for copy in copies[n]:
             copy.wait()
-        part = dot_t(ref[n], w2[:, i * COLS : (i + 1) * COLS])
-        hidden = part if hidden is None else hidden + part
+        for k in range(SIDE):
+            block = s[n, k]
+            part = dot_t(block[:, :W2_COLS], w2[n, k, 0]) + dot_t(block[:, W2_COLS:], w2[n, k, 1])
+            hidden = part if hidden is None else hidden + part
     act = (hidden * slope_ref[...]).astype(BF16)
-    for copy in late:
+    width, done = HID // SIDE, []
+    for q in range(SIDE):
+        for copy in late[q]:
+            copy.wait()
+        fold = w1_tail[q]
+        tail = jnp.concatenate([fold[..., 0:128], fold[..., 128:256]], axis=2).reshape(width, 128)
+        part = dot_t(act[:, 0:256], w1[q].reshape(width, 256)) + dot_t(act[:, 256:], tail[:, 0:64])
+        cols = pl.ds(width * q, width)
+        out[:, cols] = part.astype(BF16)
+        done.append(pltpu.make_async_copy(out.at[:, cols], out_ref.at[:, cols], out_sems.at[q]))
+        done[q].start()
+    for copy in done:
         copy.wait()
-    for g in range(8):
-        out_ref[:, 640 * g : 640 * (g + 1)] = dot_t(act, w1_chunk(w1, g, 4)).astype(BF16)
 
 
 def add_kernel(recv_ref, out_ref):
@@ -222,19 +226,24 @@
     even = lax.axis_index("prompt") % 2 == 0
     slope = gelu_slope(pre_act.astype(F32)).reshape(SIDE, SIDE, OWN, HID_OWN)
     slope = jnp.where(even, slope.transpose(1, 0, 2, 3), slope).reshape(ROWS, HID_OWN)
-    partial = call(
+    weights = weights.reshape(SIDE, SIDE, 2, W_ROWS, 256)
+    partial = pl.pallas_call(
         mlp_kernel,
-        (ROWS, HID),
-        [ANY] + [VMEM] * 8,
-        flops=3 << 30,
-        moved=16 << 20,
-        vmem=50,
-        scratch=[
-            pltpu.VMEM((HID_OWN, D_LLM), BF16),
-            pltpu.VMEM((PROMPTS, IN_OWN, 384), BF16),
-            pltpu.SemaphoreType.DMA((ROLLOUTS, 2)),
-            pltpu.SemaphoreType.DMA((3,)),
+        out_shape=jax.ShapeDtypeStruct((ROWS, HID), BF16),
+        in_specs=[ANY] * 8 + [VMEM],
+        out_specs=ANY,
+        scratch_shapes=[
+            pltpu.VMEM((SIDE, SIDE, ROWS, COLS), BF16),
+            pltpu.VMEM((SIDE, SIDE, 2, HID_OWN, W2_COLS), BF16),
+            pltpu.VMEM((SIDE, SIDE, 2, IN_OWN, 256), BF16),
+            pltpu.VMEM((SIDE, SIDE, 2, TAIL, 256), BF16),
+            pltpu.VMEM((ROWS, HID), BF16),
+            pltpu.SemaphoreType.DMA((SIDE, 3)),
+            pltpu.SemaphoreType.DMA((SIDE, 2)),
+            pltpu.SemaphoreType.DMA((SIDE,)),
         ],
+        cost_estimate=pl.CostEstimate(flops=3 << 30, bytes_accessed=16 << 20, transcendentals=0),
+        compiler_params=pltpu.CompilerParams(vmem_limit_bytes=50 << 20),
     )(weights, line, a1, a2, b1, b2, a3, b3, slope)
 
     halfway = exchange(partial.reshape(SIDE, SIDE * OWN, HID), 0)

time: 162 us -> 159 us (0.981)
  Pallas kernels: 16.4 us -> 13.9 us
    pallas_call x1, Pallas kernels: 12.5 us -> 9.99 us  [per_device(): pl.pallas_call(mlp_kernel, out_shape=jax.ShapeDtypeStruct((ROWS, HID), BF...]
where the time goes in v7:
time: 159 us; the launch traced here: 158 us
  blocking collectives  67.6 us (43%)
  waiting for transfers between devices  30.8 us (19%)
  starting transfers between devices  25.7 us (16%)
  between operations  14.2 us (9%)
  Pallas kernels  13.9 us (9%)
  local copies, waits for them, and re-layouts  5.24 us (3%)
    all_to_all x2, blocking collectives, exchange(): lax.all_to_all(blocks, AXES, split_axis=0, concat_axis=0, axis_index_grou...  45.9 us
    all_to_all x1, blocking collectives, per_device(): lax.all_to_all(outgoing, 'rollout', split_axis=0, concat_axis=0, tiled=True)  21.7 us
    ppermute x6, starting transfers between devices, shift(): return lax.ppermute(value, AXES, pairs)  21.1 us
    ppermute x6, waiting for transfers between devices, shift(): return lax.ppermute(value, AXES, pairs)  11.9 us
    all_to_all x1, waiting for transfers between devices, exchange(): lax.all_to_all(blocks, AXES, split_axis=0, concat_axis=0, axis_index_grou...  10.5 us
    pallas_call x1, Pallas kernels, per_device(): pl.pallas_call(mlp_kernel, out_shape=jax.ShapeDtypeStruct((ROWS, HID), BF...  9.99 us
    all_gather x1, waiting for transfers between devices, per_device(): weights = lax.all_gather(weights, 'prompt', axis=0, tiled=False)  8.41 us
    all_to_all x1, starting transfers between devices, exchange(): lax.all_to_all(blocks, AXES, split_axis=0, concat_axis=0, axis_index_grou...  4.54 us
  transfers between devices with their start and end apart: 8, of which 7 were waited for; matrix products, arithmetic and copies ran while one was open for 1% of the time, Pallas kernels for 0%

profile of v7, /device:TPU:6, one launch (start us, length us, event | category | flops | bytes accessed | tf_op | source)
XLA Modules:
  0.0 157.7 jit_solution(9150902846047551474)
XLA Ops:
  6.5 0.9 copy-done.2
  7.5 0.9 copy-done.3
  8.4 0.7 shard_map.82
  9.1 0.0 all-gather.3.cloned.1.call-update
  9.8 0.0 copy-start
  9.8 1.2 copy-done
  11.0 0.7 copy-done.4
  11.6 0.1 shard_map.83
  11.7 21.7 %all_to_all.20.recv_ref = bf16[16,64,512]{2,1,0:T(8,128)(2,1)S(1)} all-to-all(bf16[16,64,512]{2,1,0:T(8,128)(2,1)S(1)} %shard_map.83), channel_id=1, replica_groups=mesh['prompt'=32,'rollout'=16] {'rollout'}, dimensions={0} | all-to-all | bytes 2097152 | tf_op jit(solution)/shard_map/all_to_all | solution.py:219
  33.4 0.6 shard_map.84
  34.1 17.1 %all_to_all.21.refs_0_ = bf16[4,384,512]{2,1,0:T(8,128)(2,1)S(1)} all-to-all(bf16[4,384,512]{2,1,0:T(8,128)(2,1)S(1)} %shard_map.84), channel_id=1, replica_groups={{0,1,2,3},{4,5,6,7},{8,9,10,11},{12,13,14,15},{16,20,24,28},{17,21,25,2..., dimensions={0} | all-to-all | bytes 3145728 | tf_op jit(solution)/shard_map/all_to_all | solution.py:52
  51.1 1.4 fusion.6
  52.5 1.9 %collective-permute-start = (bf16[2,384,512]{2,1,0:T(8,128)(2,1)}, bf16[2,384,512]{2,1,0:T(8,128)(2,1)S(1)}, u32[]{:S(2)}, u32[]{:S(2)}) collective-permute-start(bf16[2,384,512]{2,1,0:T(8,128)(2,1)} %get-tuple-element.6), channel_id=1, source_target_pairs={{0,4},{4,8},{8,12},{12,0},{1,5},{5,9},{9,13},{13,1},{2,6},{6,10},{... | collective-permute-start | bytes 2359304 | tf_op jit(solution)/shard_map/ppermute | solution.py:61
  54.4 5.1 %collective-permute-start.2 = (bf16[2,384,512]{2,1,0:T(8,128)(2,1)}, bf16[2,384,512]{2,1,0:T(8,128)(2,1)S(1)}, u32[]{:S(2)}, u32[]{:S(2)}) collective-permute-start(bf16[2,384,512]{2,1,0:T(8,128)(2,1)} %get-tuple-element.5), channel_id=1, source_target_pairs={{0,12},{4,0},{8,4},{12,8},{1,13},{5,1},{9,5},{13,9},{2,14},{6,2},{... | collective-permute-start | bytes 2359304 | tf_op jit(solution)/shard_map/ppermute | solution.py:61
  59.5 1.9 %collective-permute-start.1 = (bf16[2,384,512]{2,1,0:T(8,128)(2,1)}, bf16[2,384,512]{2,1,0:T(8,128)(2,1)S(1)}, u32[]{:S(2)}, u32[]{:S(2)}) collective-permute-start(bf16[2,384,512]{2,1,0:T(8,128)(2,1)} %get-tuple-element.5), channel_id=1, source_target_pairs={{0,4},{4,8},{8,12},{12,0},{1,5},{5,9},{9,13},{13,1},{2,6},{6,10},{... | collective-permute-start | bytes 2359304 | tf_op jit(solution)/shard_map/ppermute | solution.py:61
  61.5 5.1 %collective-permute-start.3 = (bf16[2,384,512]{2,1,0:T(8,128)(2,1)}, bf16[2,384,512]{2,1,0:T(8,128)(2,1)}, u32[]{:S(2)}, u32[]{:S(2)}) collective-permute-start(bf16[2,384,512]{2,1,0:T(8,128)(2,1)} %get-tuple-element.6), channel_id=1, source_target_pairs={{0,12},{4,0},{8,4},{12,8},{1,13},{5,1},{9,5},{13,9},{2,14},{6,2},{... | collective-permute-start | bytes 2359304 | tf_op jit(solution)/shard_map/ppermute | solution.py:61
  66.6 1.2 collective-permute-done.refs_1_
  67.8 1.9 %collective-permute-start.4 = (bf16[2,384,512]{2,1,0:T(8,128)(2,1)S(1)}, bf16[2,384,512]{2,1,0:T(8,128)(2,1)}, u32[]{:S(2)}, u32[]{:S(2)}) collective-permute-start(bf16[2,384,512]{2,1,0:T(8,128)(2,1)S(1)} %collective-permute-done.refs_1_), channel_id=1, source_target_pairs={{0,4},{4,8},{8,12},{12,0},{1,5},{5,9},{9,13},{13,1},{2,6},{6,10},{... | collective-permute-start | bytes 2359304 | tf_op jit(solution)/shard_map/ppermute | solution.py:61
  69.7 5.1 %collective-permute-start.5 = (bf16[2,384,512]{2,1,0:T(8,128)(2,1)S(1)}, bf16[2,384,512]{2,1,0:T(8,128)(2,1)}, u32[]{:S(2)}, u32[]{:S(2)}) collective-permute-start(bf16[2,384,512]{2,1,0:T(8,128)(2,1)S(1)} %collective-permute-done.2.refs_3_), channel_id=1, source_target_pairs={{0,12},{4,0},{8,4},{12,8},{1,13},{5,1},{9,5},{13,9},{2,14},{6,2},{... | collective-permute-start | bytes 2359304 | tf_op jit(solution)/shard_map/ppermute | solution.py:61
  74.9 0.2 copy.11
  75.1 0.2 fusion.3
  75.4 0.8 collective-permute-done.1.refs_2_
  76.2 1.6 collective-permute-done.3.refs_4_
  77.8 7.0 %collective-permute-done.4.refs_5_ = bf16[2,384,512]{2,1,0:T(8,128)(2,1)} collective-permute-done((bf16[2,384,512]{2,1,0:T(8,128)(2,1)S(1)}, bf16[2,384,512]{2,1,0:T(8,128)(2,1)}, u32[]{:S(2)}, u32[]{:S(2)}) %collective-permute-start.4) | collective-permute-done | bytes 786464 | tf_op jit(solution)/shard_map/ppermute | solution.py:61
  84.7 1.4 collective-permute-done.5.refs_6_
  86.1 8.4 %all-gather.3.cloned.1.call-done = bf16[17920,256]{1,0:T(8,128)(2,1)} async-done(((bf16[560,256]{1,0:T(8,128)(2,1)}), bf16[17920,256]{1,0:T(8,128)(2,1)}) %all-gather.3.cloned.1.call-update) | async-done | bytes 9175056 | tf_op jit(solution)/shard_map/all_gather | solution.py:214
  94.5 10.0 %shard_map.85 = bf16[384,5120]{1,0:T(8,128)(2,1)} custom-call(bf16[4,4,2,560,256]{4,3,2,1,0:T(8,128)(2,1)} %bitcast.13, bf16[4,384,512]{2,1,0:T(8,128)(2,1)} %copy-done.5, bf16[2,384,512]{2,1,0:T(8,128)(2,1)S(1)} %collective-permute-done.refs_1_, bf16[2,384,512]{2,1,0:T(8,128)(2,1)S(1)} %collective-permute-done.1.refs_2_, ...), custom_call_target="tpu_custom_call" | custom-call | flops 3221225472 | bytes 16777216 | tf_op jit(solution)/shard_map/pallas_call | solution.py:230
  104.5 28.8 %all_to_all.22.recv_ref = bf16[4,96,5120]{2,1,0:T(8,128)(2,1)S(1)} all-to-all(bf16[4,96,5120]{2,1,0:T(8,128)(2,1)} %bitcast.12), channel_id=1, replica_groups={{0,1,2,3},{4,5,6,7},{8,9,10,11},{12,13,14,15},{16,20,24,28},{17,21,25,2..., dimensions={0} | all-to-all | bytes 7864320 | tf_op jit(solution)/shard_map/all_to_all | solution.py:52
  133.3 1.4 shard_map.86
  134.7 4.5 %all-to-all-start.3 = ((bf16[4,24,5120]{2,1,0:T(8,128)(2,1)}), bf16[4,24,5120]{2,1,0:T(8,128)(2,1)S(1)}, u32[]{:S(2)}, u32[]{:S(2)}) async-start(bf16[4,24,5120]{2,1,0:T(8,128)(2,1)} %bitcast.7), calls=%async_computation.3 | async-start | bytes 1966080 | tf_op jit(solution)/shard_map/all_to_all | solution.py:52
  139.3 10.5 %all-to-all-done.3.recv_ref = bf16[4,24,5120]{2,1,0:T(8,128)(2,1)S(1)} async-done(((bf16[4,24,5120]{2,1,0:T(8,128)(2,1)}), bf16[4,24,5120]{2,1,0:T(8,128)(2,1)S(1)}, u32[]{:S(2)}, u32[]{:S(2)}) %all-to-all-start.3) | async-done | bytes 983072 | tf_op jit(solution)/shard_map/all_to_all | solution.py:52
  149.8 1.0 shard_map.87
  (15 shorter events, 0.1 us)
Async XLA Ops:
  6.5 88.0 %all-gather.3.cloned.1.call-start = ((), (), s32[]{:S(2)}) async-start(), calls=%async_computation.4 | async-start | bytes 9461760 | tf_op jit(solution)/shard_map/all_gather | solution.py:214
  6.5 0.9 copy-start.2
  7.5 0.9 copy-start.3
  9.8 1.2 copy-start
  10.9 0.7 copy-start.4
  33.4 41.4 %copy-start.6 = (bf16[384,320]{0,1:T(8,128)(2,1)S(1)}, bf16[384,320]{0,1:T(8,128)(2,1)}, u32[]{:S(2)}) copy-start(bf16[384,320]{0,1:T(8,128)(2,1)} %param.11) | copy-start | bytes 737284
  51.1 18.6 %copy-start.5 = (bf16[4,384,512]{2,1,0:T(8,128)(2,1)}, bf16[4,384,512]{2,1,0:T(8,128)(2,1)S(1)}, u32[]{:S(2)}) copy-start(bf16[4,384,512]{2,1,0:T(8,128)(2,1)S(1)} %all_to_all.21.refs_0_) | copy-start | bytes 4718596
  52.5 15.3 %collective-permute-start = (bf16[2,384,512]{2,1,0:T(8,128)(2,1)}, bf16[2,384,512]{2,1,0:T(8,128)(2,1)S(1)}, u32[]{:S(2)}, u32[]{:S(2)}) collective-permute-start(bf16[2,384,512]{2,1,0:T(8,128)(2,1)} %get-tuple-element.6), channel_id=1, source_target_pairs={{0,4},{4,8},{8,12},{12,0},{1,5},{5,9},{9,13},{13,1},{2,6},{6,10},{... | collective-permute-start | bytes 2359304 | tf_op jit(solution)/shard_map/ppermute | solution.py:61
  54.4 15.3 %collective-permute-start.2 = (bf16[2,384,512]{2,1,0:T(8,128)(2,1)}, bf16[2,384,512]{2,1,0:T(8,128)(2,1)S(1)}, u32[]{:S(2)}, u32[]{:S(2)}) collective-permute-start(bf16[2,384,512]{2,1,0:T(8,128)(2,1)} %get-tuple-element.5), channel_id=1, source_target_pairs={{0,12},{4,0},{8,4},{12,8},{1,13},{5,1},{9,5},{13,9},{2,14},{6,2},{... | collective-permute-start | bytes 2359304 | tf_op jit(solution)/shard_map/ppermute | solution.py:61
  59.5 16.7 %collective-permute-start.1 = (bf16[2,384,512]{2,1,0:T(8,128)(2,1)}, bf16[2,384,512]{2,1,0:T(8,128)(2,1)S(1)}, u32[]{:S(2)}, u32[]{:S(2)}) collective-permute-start(bf16[2,384,512]{2,1,0:T(8,128)(2,1)} %get-tuple-element.5), channel_id=1, source_target_pairs={{0,4},{4,8},{8,12},{12,0},{1,5},{5,9},{9,13},{13,1},{2,6},{6,10},{... | collective-permute-start | bytes 2359304 | tf_op jit(solution)/shard_map/ppermute | solution.py:61
  61.5 16.3 %collective-permute-start.3 = (bf16[2,384,512]{2,1,0:T(8,128)(2,1)}, bf16[2,384,512]{2,1,0:T(8,128)(2,1)}, u32[]{:S(2)}, u32[]{:S(2)}) collective-permute-start(bf16[2,384,512]{2,1,0:T(8,128)(2,1)} %get-tuple-element.6), channel_id=1, source_target_pairs={{0,12},{4,0},{8,4},{12,8},{1,13},{5,1},{9,5},{13,9},{2,14},{6,2},{... | collective-permute-start | bytes 2359304 | tf_op jit(solution)/shard_map/ppermute | solution.py:61
  67.8 17.0 %collective-permute-start.4 = (bf16[2,384,512]{2,1,0:T(8,128)(2,1)S(1)}, bf16[2,384,512]{2,1,0:T(8,128)(2,1)}, u32[]{:S(2)}, u32[]{:S(2)}) collective-permute-start(bf16[2,384,512]{2,1,0:T(8,128)(2,1)S(1)} %collective-permute-done.refs_1_), channel_id=1, source_target_pairs={{0,4},{4,8},{8,12},{12,0},{1,5},{5,9},{9,13},{13,1},{2,6},{6,10},{... | collective-permute-start | bytes 2359304 | tf_op jit(solution)/shard_map/ppermute | solution.py:61
  69.7 16.4 %collective-permute-start.5 = (bf16[2,384,512]{2,1,0:T(8,128)(2,1)S(1)}, bf16[2,384,512]{2,1,0:T(8,128)(2,1)}, u32[]{:S(2)}, u32[]{:S(2)}) collective-permute-start(bf16[2,384,512]{2,1,0:T(8,128)(2,1)S(1)} %collective-permute-done.2.refs_3_), channel_id=1, source_target_pairs={{0,12},{4,0},{8,4},{12,8},{1,13},{5,1},{9,5},{13,9},{2,14},{6,2},{... | collective-permute-start | bytes 2359304 | tf_op jit(solution)/shard_map/ppermute | solution.py:61
  133.3 6.0 %copy-start.7 = (f32[1280]{0:T(1024)S(1)}, f32[1280]{0:T(1024)}, u32[]{:S(2)}) copy-start(f32[1280]{0:T(1024)} %param.13) | copy-start | bytes 15364
  133.3 16.5 %copy-start.1 = (bf16[24,5120]{1,0:T(8,128)(2,1)S(1)}, bf16[24,5120]{1,0:T(8,128)(2,1)}, u32[]{:S(2)}) copy-start(bf16[24,5120]{1,0:T(8,128)(2,1)} %patches_ref.1) | copy-start | bytes 737284
  134.7 15.1 %all-to-all-start.3 = ((bf16[4,24,5120]{2,1,0:T(8,128)(2,1)}), bf16[4,24,5120]{2,1,0:T(8,128)(2,1)S(1)}, u32[]{:S(2)}, u32[]{:S(2)}) async-start(bf16[4,24,5120]{2,1,0:T(8,128)(2,1)} %bitcast.7), calls=%async_computation.3 | async-start | bytes 1966080 | tf_op jit(solution)/shard_map/all_to_all | solution.py:52
Sparse Core Ops, SparseCore 0:
  9.5 84.9 all-gather.2

commit v8 on v7

--- a/solution.py
+++ b/solution.py
@@ -122,7 +122,7 @@
 
 
 def mlp_kernel(w_ref, *refs):
-    sums, (slope_ref, out_ref, s, w2, w1, w1_tail, out, sems2, sems1, out_sems) = refs[:7], refs[7:]
+    sums, (slope_ref, out_ref, s, w2, w1, w1_tail, sems2, sems1) = refs[:7], refs[7:]
     even, second = place_in_plane()
     base = HID_OWN + IN_OWN
     copies, late = [], []
@@ -156,19 +156,14 @@
             part = dot_t(block[:, :W2_COLS], w2[n, k, 0]) + dot_t(block[:, W2_COLS:], w2[n, k, 1])
             hidden = part if hidden is None else hidden + part
     act = (hidden * slope_ref[...]).astype(BF16)
-    width, done = HID // SIDE, []
+    width = HID // SIDE
     for q in range(SIDE):
         for copy in late[q]:
             copy.wait()
         fold = w1_tail[q]
         tail = jnp.concatenate([fold[..., 0:128], fold[..., 128:256]], axis=2).reshape(width, 128)
         part = dot_t(act[:, 0:256], w1[q].reshape(width, 256)) + dot_t(act[:, 256:], tail[:, 0:64])
-        cols = pl.ds(width * q, width)
-        out[:, cols] = part.astype(BF16)
-        done.append(pltpu.make_async_copy(out.at[:, cols], out_ref.at[:, cols], out_sems.at[q]))
-        done[q].start()
-    for copy in done:
-        copy.wait()
+        out_ref[:, width * q : width * (q + 1)] = part.astype(BF16)
 
 
 def add_kernel(recv_ref, out_ref):
@@ -197,10 +192,10 @@
 ANY = pl.BlockSpec(memory_space=pl.ANY)
 
 
-def call(kernel, shape, in_specs, flops=0, moved=0, vmem=16, scratch=()):
+def call(kernel, shape, in_specs, flops=0, moved=0, vmem=16, scratch=(), fast=False):
     return pl.pallas_call(
         kernel,
-        out_shape=jax.ShapeDtypeStruct(shape, BF16),
+        out_shape=pltpu.VMEM(shape, BF16) if fast else jax.ShapeDtypeStruct(shape, BF16),
         in_specs=in_specs,
         out_specs=VMEM,
         scratch_shapes=list(scratch),
@@ -229,25 +224,23 @@
     weights = weights.reshape(SIDE, SIDE, 2, W_ROWS, 256)
     partial = pl.pallas_call(
         mlp_kernel,
-        out_shape=jax.ShapeDtypeStruct((ROWS, HID), BF16),
+        out_shape=pltpu.VMEM((ROWS, HID), BF16),
         in_specs=[ANY] * 8 + [VMEM],
-        out_specs=ANY,
+        out_specs=VMEM,
         scratch_shapes=[
             pltpu.VMEM((SIDE, SIDE, ROWS, COLS), BF16),
             pltpu.VMEM((SIDE, SIDE, 2, HID_OWN, W2_COLS), BF16),
             pltpu.VMEM((SIDE, SIDE, 2, IN_OWN, 256), BF16),
             pltpu.VMEM((SIDE, SIDE, 2, TAIL, 256), BF16),
-            pltpu.VMEM((ROWS, HID), BF16),
             pltpu.SemaphoreType.DMA((SIDE, 3)),
             pltpu.SemaphoreType.DMA((SIDE, 2)),
-            pltpu.SemaphoreType.DMA((SIDE,)),
         ],
         cost_estimate=pl.CostEstimate(flops=3 << 30, bytes_accessed=16 << 20, transcendentals=0),
-        compiler_params=pltpu.CompilerParams(vmem_limit_bytes=50 << 20),
-    )(weights, line, a1, a2, b1, b2, a3, b3, slope)
+        compiler_params=pltpu.CompilerParams(vmem_limit_bytes=24 << 20),
+    )(pltpu.with_memory_space_constraint(weights, pltpu.HBM), line, a1, a2, b1, b2, a3, b3, slope)
 
     halfway = exchange(partial.reshape(SIDE, SIDE * OWN, HID), 0)
-    halfway = call(add_kernel, (SIDE * OWN, HID), [VMEM], moved=5 << 20)(halfway)
+    halfway = call(add_kernel, (SIDE * OWN, HID), [VMEM], moved=5 << 20, fast=True)(halfway)
     last = exchange(halfway.reshape(SIDE, OWN, HID), 1)
     return call(norm_kernel, (OWN, HID), [VMEM] * 3)(last, patches, ln_gain.reshape(1, VIT))
 

time: 159 us -> 158 us (level)
    unnamed x17 -> x15, local copies, waits for them, and re-layouts: 3.88 us -> 3.87 us
where the time goes in v8:
time: 158 us; the launch traced here: 156 us
  blocking collectives  67.5 us (43%)
  waiting for transfers between devices  30.8 us (19%)
  starting transfers between devices  25.6 us (16%)
  between operations  14.2 us (9%)
  Pallas kernels  12.9 us (8%)
  local copies, waits for them, and re-layouts  5.13 us (3%)
    all_to_all x2, blocking collectives, exchange(): lax.all_to_all(blocks, AXES, split_axis=0, concat_axis=0, axis_index_grou...  45.8 us
    all_to_all x1, blocking collectives, per_device(): lax.all_to_all(outgoing, 'rollout', split_axis=0, concat_axis=0, tiled=True)  21.7 us
    ppermute x6, starting transfers between devices, shift(): return lax.ppermute(value, AXES, pairs)  21.2 us
    ppermute x6, waiting for transfers between devices, shift(): return lax.ppermute(value, AXES, pairs)  11.9 us
    all_to_all x1, waiting for transfers between devices, exchange(): lax.all_to_all(blocks, AXES, split_axis=0, concat_axis=0, axis_index_grou...  10.5 us
    pallas_call x1, Pallas kernels, per_device(): pl.pallas_call(mlp_kernel, out_shape=pltpu.VMEM((ROWS, HID), BF16), in_sp...  8.96 us
    all_gather x1, waiting for transfers between devices, per_device(): weights = lax.all_gather(weights, 'prompt', axis=0, tiled=False)  8.41 us
    all_to_all x1, starting transfers between devices, exchange(): lax.all_to_all(blocks, AXES, split_axis=0, concat_axis=0, axis_index_grou...  4.37 us
  transfers between devices with their start and end apart: 8, of which 7 were waited for; matrix products, arithmetic and copies ran while one was open for 1% of the time, Pallas kernels for 0%

profile of v8, /device:TPU:6, one launch (start us, length us, event | category | flops | bytes accessed | tf_op | source)
XLA Modules:
  0.0 156.4 jit_solution(11088219433298664956)
XLA Ops:
  6.5 0.9 copy-done.2
  7.5 0.9 copy-done.3
  8.4 0.7 shard_map.82
  9.1 0.0 all-gather.3.cloned.1.call-update
  9.8 0.0 copy-start
  9.8 1.2 copy-done
  10.9 0.7 copy-done.4
  11.6 0.1 shard_map.83
  11.7 21.7 %all_to_all.20.recv_ref = bf16[16,64,512]{2,1,0:T(8,128)(2,1)S(1)} all-to-all(bf16[16,64,512]{2,1,0:T(8,128)(2,1)S(1)} %shard_map.83), channel_id=1, replica_groups=mesh['prompt'=32,'rollout'=16] {'rollout'}, dimensions={0} | all-to-all | bytes 2097152 | tf_op jit(solution)/shard_map/all_to_all | solution.py:214
  33.4 0.6 shard_map.84
  34.1 17.1 %all_to_all.21.refs_0_ = bf16[4,384,512]{2,1,0:T(8,128)(2,1)S(1)} all-to-all(bf16[4,384,512]{2,1,0:T(8,128)(2,1)S(1)} %shard_map.84), channel_id=1, replica_groups={{0,1,2,3},{4,5,6,7},{8,9,10,11},{12,13,14,15},{16,20,24,28},{17,21,25,2..., dimensions={0} | all-to-all | bytes 3145728 | tf_op jit(solution)/shard_map/all_to_all | solution.py:52
  51.1 1.2 fusion.6
  52.4 1.9 %collective-permute-start = (bf16[2,384,512]{2,1,0:T(8,128)(2,1)}, bf16[2,384,512]{2,1,0:T(8,128)(2,1)S(1)}, u32[]{:S(2)}, u32[]{:S(2)}) collective-permute-start(bf16[2,384,512]{2,1,0:T(8,128)(2,1)} %get-tuple-element.6), channel_id=1, source_target_pairs={{0,4},{4,8},{8,12},{12,0},{1,5},{5,9},{9,13},{13,1},{2,6},{6,10},{... | collective-permute-start | bytes 2359304 | tf_op jit(solution)/shard_map/ppermute | solution.py:61
  54.3 5.1 %collective-permute-start.2 = (bf16[2,384,512]{2,1,0:T(8,128)(2,1)}, bf16[2,384,512]{2,1,0:T(8,128)(2,1)}, u32[]{:S(2)}, u32[]{:S(2)}) collective-permute-start(bf16[2,384,512]{2,1,0:T(8,128)(2,1)} %get-tuple-element.5), channel_id=1, source_target_pairs={{0,12},{4,0},{8,4},{12,8},{1,13},{5,1},{9,5},{13,9},{2,14},{6,2},{... | collective-permute-start | bytes 2359304 | tf_op jit(solution)/shard_map/ppermute | solution.py:61
  59.4 1.9 %collective-permute-start.1 = (bf16[2,384,512]{2,1,0:T(8,128)(2,1)}, bf16[2,384,512]{2,1,0:T(8,128)(2,1)}, u32[]{:S(2)}, u32[]{:S(2)}) collective-permute-start(bf16[2,384,512]{2,1,0:T(8,128)(2,1)} %get-tuple-element.5), channel_id=1, source_target_pairs={{0,4},{4,8},{8,12},{12,0},{1,5},{5,9},{9,13},{13,1},{2,6},{6,10},{... | collective-permute-start | bytes 2359304 | tf_op jit(solution)/shard_map/ppermute | solution.py:61
  61.4 5.1 %collective-permute-start.3 = (bf16[2,384,512]{2,1,0:T(8,128)(2,1)}, bf16[2,384,512]{2,1,0:T(8,128)(2,1)}, u32[]{:S(2)}, u32[]{:S(2)}) collective-permute-start(bf16[2,384,512]{2,1,0:T(8,128)(2,1)} %get-tuple-element.6), channel_id=1, source_target_pairs={{0,12},{4,0},{8,4},{12,8},{1,13},{5,1},{9,5},{13,9},{2,14},{6,2},{... | collective-permute-start | bytes 2359304 | tf_op jit(solution)/shard_map/ppermute | solution.py:61
  66.5 1.2 collective-permute-done.refs_1_
  67.7 1.9 %collective-permute-start.4 = (bf16[2,384,512]{2,1,0:T(8,128)(2,1)S(1)}, bf16[2,384,512]{2,1,0:T(8,128)(2,1)}, u32[]{:S(2)}, u32[]{:S(2)}) collective-permute-start(bf16[2,384,512]{2,1,0:T(8,128)(2,1)S(1)} %collective-permute-done.refs_1_), channel_id=1, source_target_pairs={{0,4},{4,8},{8,12},{12,0},{1,5},{5,9},{9,13},{13,1},{2,6},{6,10},{... | collective-permute-start | bytes 2359304 | tf_op jit(solution)/shard_map/ppermute | solution.py:61
  69.6 5.2 %collective-permute-start.5 = (bf16[2,384,512]{2,1,0:T(8,128)(2,1)}, bf16[2,384,512]{2,1,0:T(8,128)(2,1)}, u32[]{:S(2)}, u32[]{:S(2)}) collective-permute-start(bf16[2,384,512]{2,1,0:T(8,128)(2,1)} %collective-permute-done.2.refs_3_), channel_id=1, source_target_pairs={{0,12},{4,0},{8,4},{12,8},{1,13},{5,1},{9,5},{13,9},{2,14},{6,2},{... | collective-permute-start | bytes 2359304 | tf_op jit(solution)/shard_map/ppermute | solution.py:61
  74.9 0.2 copy.11
  75.1 0.2 fusion.3
  75.4 0.8 collective-permute-done.1.refs_2_
  76.2 1.5 collective-permute-done.3.refs_4_
  77.7 7.0 %collective-permute-done.4.refs_5_ = bf16[2,384,512]{2,1,0:T(8,128)(2,1)} collective-permute-done((bf16[2,384,512]{2,1,0:T(8,128)(2,1)S(1)}, bf16[2,384,512]{2,1,0:T(8,128)(2,1)}, u32[]{:S(2)}, u32[]{:S(2)}) %collective-permute-start.4) | collective-permute-done | bytes 786464 | tf_op jit(solution)/shard_map/ppermute | solution.py:61
  84.6 1.5 collective-permute-done.5.refs_6_
  86.1 8.4 %all-gather.3.cloned.1.call-done = bf16[17920,256]{1,0:T(8,128)(2,1)} async-done(((bf16[560,256]{1,0:T(8,128)(2,1)}), bf16[17920,256]{1,0:T(8,128)(2,1)}) %all-gather.3.cloned.1.call-update) | async-done | bytes 9175056 | tf_op jit(solution)/shard_map/all_gather | solution.py:209
  94.5 9.0 %shard_map.85 = bf16[384,5120]{1,0:T(8,128)(2,1)S(1)} custom-call(bf16[4,4,2,560,256]{4,3,2,1,0:T(8,128)(2,1)} %bitcast.13, bf16[4,384,512]{2,1,0:T(8,128)(2,1)S(1)} %all_to_all.21.refs_0_, bf16[2,384,512]{2,1,0:T(8,128)(2,1)S(1)} %collective-permute-done.refs_1_, bf16[2,384,512]{2,1,0:T(8,128)(2,1)} %collective-permute-done.1.refs_2_, ...), custom_call_target="tpu_custom_call" | custom-call | flops 3221225472 | bytes 16777216 | tf_op jit(solution)/shard_map/pallas_call | solution.py:225
  103.5 28.7 %all_to_all.22.recv_ref = bf16[4,96,5120]{2,1,0:T(8,128)(2,1)S(1)} all-to-all(bf16[4,96,5120]{2,1,0:T(8,128)(2,1)S(1)} %bitcast.9), channel_id=1, replica_groups={{0,1,2,3},{4,5,6,7},{8,9,10,11},{12,13,14,15},{16,20,24,28},{17,21,25,2..., dimensions={0} | all-to-all | bytes 7864320 | tf_op jit(solution)/shard_map/all_to_all | solution.py:52
  132.2 1.4 shard_map.86
  133.6 4.4 %all-to-all-start.3 = ((bf16[4,24,5120]{2,1,0:T(8,128)(2,1)}), bf16[4,24,5120]{2,1,0:T(8,128)(2,1)S(1)}, u32[]{:S(2)}, u32[]{:S(2)}) async-start(bf16[4,24,5120]{2,1,0:T(8,128)(2,1)} %bitcast.7), calls=%async_computation.3 | async-start | bytes 1966080 | tf_op jit(solution)/shard_map/all_to_all | solution.py:52
  138.0 10.5 %all-to-all-done.3.recv_ref = bf16[4,24,5120]{2,1,0:T(8,128)(2,1)S(1)} async-done(((bf16[4,24,5120]{2,1,0:T(8,128)(2,1)}), bf16[4,24,5120]{2,1,0:T(8,128)(2,1)S(1)}, u32[]{:S(2)}, u32[]{:S(2)}) %all-to-all-start.3) | async-done | bytes 983072 | tf_op jit(solution)/shard_map/all_to_all | solution.py:52
  148.6 1.0 shard_map.87
  (13 shorter events, 0.1 us)
Async XLA Ops:
  6.5 88.0 %all-gather.3.cloned.1.call-start = ((), (), s32[]{:S(2)}) async-start(), calls=%async_computation.4 | async-start | bytes 9461760 | tf_op jit(solution)/shard_map/all_gather | solution.py:209
  6.5 0.9 copy-start.2
  7.5 0.9 copy-start.3
  9.8 1.2 copy-start
  10.9 0.7 copy-start.4
  33.4 41.4 %copy-start.5 = (bf16[384,320]{0,1:T(8,128)(2,1)S(1)}, bf16[384,320]{0,1:T(8,128)(2,1)}, u32[]{:S(2)}) copy-start(bf16[384,320]{0,1:T(8,128)(2,1)} %param.11) | copy-start | bytes 737284
  52.4 15.3 %collective-permute-start = (bf16[2,384,512]{2,1,0:T(8,128)(2,1)}, bf16[2,384,512]{2,1,0:T(8,128)(2,1)S(1)}, u32[]{:S(2)}, u32[]{:S(2)}) collective-permute-start(bf16[2,384,512]{2,1,0:T(8,128)(2,1)} %get-tuple-element.6), channel_id=1, source_target_pairs={{0,4},{4,8},{8,12},{12,0},{1,5},{5,9},{9,13},{13,1},{2,6},{6,10},{... | collective-permute-start | bytes 2359304 | tf_op jit(solution)/shard_map/ppermute | solution.py:61
  54.3 15.3 %collective-permute-start.2 = (bf16[2,384,512]{2,1,0:T(8,128)(2,1)}, bf16[2,384,512]{2,1,0:T(8,128)(2,1)}, u32[]{:S(2)}, u32[]{:S(2)}) collective-permute-start(bf16[2,384,512]{2,1,0:T(8,128)(2,1)} %get-tuple-element.5), channel_id=1, source_target_pairs={{0,12},{4,0},{8,4},{12,8},{1,13},{5,1},{9,5},{13,9},{2,14},{6,2},{... | collective-permute-start | bytes 2359304 | tf_op jit(solution)/shard_map/ppermute | solution.py:61
  59.4 16.8 %collective-permute-start.1 = (bf16[2,384,512]{2,1,0:T(8,128)(2,1)}, bf16[2,384,512]{2,1,0:T(8,128)(2,1)}, u32[]{:S(2)}, u32[]{:S(2)}) collective-permute-start(bf16[2,384,512]{2,1,0:T(8,128)(2,1)} %get-tuple-element.5), channel_id=1, source_target_pairs={{0,4},{4,8},{8,12},{12,0},{1,5},{5,9},{9,13},{13,1},{2,6},{6,10},{... | collective-permute-start | bytes 2359304 | tf_op jit(solution)/shard_map/ppermute | solution.py:61
  61.4 16.3 %collective-permute-start.3 = (bf16[2,384,512]{2,1,0:T(8,128)(2,1)}, bf16[2,384,512]{2,1,0:T(8,128)(2,1)}, u32[]{:S(2)}, u32[]{:S(2)}) collective-permute-start(bf16[2,384,512]{2,1,0:T(8,128)(2,1)} %get-tuple-element.6), channel_id=1, source_target_pairs={{0,12},{4,0},{8,4},{12,8},{1,13},{5,1},{9,5},{13,9},{2,14},{6,2},{... | collective-permute-start | bytes 2359304 | tf_op jit(solution)/shard_map/ppermute | solution.py:61
  67.7 17.0 %collective-permute-start.4 = (bf16[2,384,512]{2,1,0:T(8,128)(2,1)S(1)}, bf16[2,384,512]{2,1,0:T(8,128)(2,1)}, u32[]{:S(2)}, u32[]{:S(2)}) collective-permute-start(bf16[2,384,512]{2,1,0:T(8,128)(2,1)S(1)} %collective-permute-done.refs_1_), channel_id=1, source_target_pairs={{0,4},{4,8},{8,12},{12,0},{1,5},{5,9},{9,13},{13,1},{2,6},{6,10},{... | collective-permute-start | bytes 2359304 | tf_op jit(solution)/shard_map/ppermute | solution.py:61
  69.6 16.5 %collective-permute-start.5 = (bf16[2,384,512]{2,1,0:T(8,128)(2,1)}, bf16[2,384,512]{2,1,0:T(8,128)(2,1)}, u32[]{:S(2)}, u32[]{:S(2)}) collective-permute-start(bf16[2,384,512]{2,1,0:T(8,128)(2,1)} %collective-permute-done.2.refs_3_), channel_id=1, source_target_pairs={{0,12},{4,0},{8,4},{12,8},{1,13},{5,1},{9,5},{13,9},{2,14},{6,2},{... | collective-permute-start | bytes 2359304 | tf_op jit(solution)/shard_map/ppermute | solution.py:61
  132.2 5.8 %copy-start.6 = (f32[1280]{0:T(1024)S(1)}, f32[1280]{0:T(1024)}, u32[]{:S(2)}) copy-start(f32[1280]{0:T(1024)} %param.13) | copy-start | bytes 15364
  132.2 16.4 %copy-start.1 = (bf16[24,5120]{1,0:T(8,128)(2,1)S(1)}, bf16[24,5120]{1,0:T(8,128)(2,1)}, u32[]{:S(2)}) copy-start(bf16[24,5120]{1,0:T(8,128)(2,1)} %patches_ref.1) | copy-start | bytes 737284
  133.6 14.9 %all-to-all-start.3 = ((bf16[4,24,5120]{2,1,0:T(8,128)(2,1)}), bf16[4,24,5120]{2,1,0:T(8,128)(2,1)S(1)}, u32[]{:S(2)}, u32[]{:S(2)}) async-start(bf16[4,24,5120]{2,1,0:T(8,128)(2,1)} %bitcast.7), calls=%async_computation.3 | async-start | bytes 1966080 | tf_op jit(solution)/shard_map/all_to_all | solution.py:52
Sparse Core Ops, SparseCore 0:
  9.5 84.9 all-gather.2

commit v9 on v8

--- a/solution.py
+++ b/solution.py
@@ -153,9 +153,9 @@
             copy.wait()
         for k in range(SIDE):
             block = s[n, k]
-            part = dot_t(block[:, :W2_COLS], w2[n, k, 0]) + dot_t(block[:, W2_COLS:], w2[n, k, 1])
+            part = dot_t(w2[n, k, 0], block[:, :W2_COLS]) + dot_t(w2[n, k, 1], block[:, W2_COLS:])
             hidden = part if hidden is None else hidden + part
-    act = (hidden * slope_ref[...]).astype(BF16)
+    act = (hidden.T * slope_ref[...]).astype(BF16)
     width = HID // SIDE
     for q in range(SIDE):
         for copy in late[q]:
@@ -173,14 +173,22 @@
     out_ref[...] = total.astype(BF16)
 
 
-def norm_kernel(recv_ref, patches_ref, gain_ref, out_ref):
+def norm_kernel(recv_ref, patches_hbm, gain_hbm, out_ref, patches_ref, gain_ref, sems):
+    copies = [
+        pltpu.make_async_copy(patches_hbm, patches_ref, sems.at[0]),
+        pltpu.make_async_copy(gain_hbm, gain_ref, sems.at[1]),
+    ]
+    for copy in copies:
+        copy.start()
+    for copy in copies:
+        copy.wait()
     for m in range(MERGE):
         cols = slice(m * VIT, (m + 1) * VIT)
         upstream = recv_ref[0, :, cols].astype(F32)
         for k in range(1, SIDE):
             upstream = upstream + recv_ref[k, :, cols].astype(F32)
         inputs = patches_ref[:, cols].astype(F32)
-        scaled = upstream * gain_ref[...]
+        scaled = upstream * gain_ref[...][None]
         inverse = lax.rsqrt(jnp.mean(inputs * inputs, axis=-1, keepdims=True) + 1e-06)
         inner = jnp.mean(scaled * inputs, axis=-1, keepdims=True)
         result = inverse * scaled - inputs * inverse * inverse * inverse * inner
@@ -202,6 +210,10 @@
         cost_estimate=pl.CostEstimate(flops=flops, bytes_accessed=moved, transcendentals=0),
         compiler_params=pltpu.CompilerParams(vmem_limit_bytes=vmem << 20),
     )
+
+
+def pinned(value):
+    return pltpu.with_memory_space_constraint(value, pltpu.HBM)
 
 
 def per_device(row_grads, used_ids, used_count, pre_act, patches, ln_gain, w_fc2, w_fc1):
@@ -237,12 +249,21 @@
         ],
         cost_estimate=pl.CostEstimate(flops=3 << 30, bytes_accessed=16 << 20, transcendentals=0),
         compiler_params=pltpu.CompilerParams(vmem_limit_bytes=24 << 20),
-    )(pltpu.with_memory_space_constraint(weights, pltpu.HBM), line, a1, a2, b1, b2, a3, b3, slope)
+    )(pinned(weights), line, a1, a2, b1, b2, a3, b3, slope)
 
     halfway = exchange(partial.reshape(SIDE, SIDE * OWN, HID), 0)
     halfway = call(add_kernel, (SIDE * OWN, HID), [VMEM], moved=5 << 20, fast=True)(halfway)
     last = exchange(halfway.reshape(SIDE, OWN, HID), 1)
-    return call(norm_kernel, (OWN, HID), [VMEM] * 3)(last, patches, ln_gain.reshape(1, VIT))
+    return call(
+        norm_kernel,
+        (OWN, HID),
+        [VMEM, ANY, ANY],
+        scratch=[
+            pltpu.VMEM((OWN, HID), BF16),
+            pltpu.VMEM((VIT,), F32),
+            pltpu.SemaphoreType.DMA((2,)),
+        ],
+    )(last, pinned(patches), pinned(ln_gain))
 
 
 def solution(mesh):

time: 158 us -> 157 us (level)
  blocking collectives: 67.5 us -> 82.2 us
  waiting for transfers between devices: 30.8 us -> 22.7 us
  starting transfers between devices: 25.6 us -> 18.7 us
    all_to_all x2 -> x3, blocking collectives: 45.8 us -> 60.5 us  [exchange(): lax.all_to_all(blocks, AXES, split_axis=0, concat_axis=0, axis_index_grou...]
    all_to_all x1 -> x0, waiting for transfers between devices: 10.5 us -> none  [exchange(): lax.all_to_all(blocks, AXES, split_axis=0, concat_axis=0, axis_index_grou...]
    all_to_all x1 -> x0, starting transfers between devices: 4.37 us -> none  [exchange(): lax.all_to_all(blocks, AXES, split_axis=0, concat_axis=0, axis_index_grou...]
    ppermute x6, waiting for transfers between devices: 11.9 us -> 15.5 us  [shift(): return lax.ppermute(value, AXES, pairs)]
    ppermute x6, starting transfers between devices: 21.2 us -> 18.7 us  [shift(): return lax.ppermute(value, AXES, pairs)]
    unnamed x15 -> x11, local copies, waits for them, and re-layouts: 3.87 us -> 3.87 us
  transfers between devices with their start and end apart: 8 -> 7, of which waited for: 7 -> 6; matrix products, arithmetic and copies ran while one was open for 1% -> 1% of each run, Pallas kernels for 0% -> 0%
where the time goes in v9:
time: 157 us; the launch traced here: 156 us
  blocking collectives  82.2 us (52%)
  waiting for transfers between devices  22.7 us (14%)
  starting transfers between devices  18.7 us (12%)
  between operations  14.2 us (9%)
  Pallas kernels  12.9 us (8%)
  local copies, waits for them, and re-layouts  5.13 us (3%)
    all_to_all x3, blocking collectives, exchange(): lax.all_to_all(blocks, AXES, split_axis=0, concat_axis=0, axis_index_grou...  60.5 us
    all_to_all x1, blocking collectives, per_device(): lax.all_to_all(outgoing, 'rollout', split_axis=0, concat_axis=0, tiled=True)  21.7 us
    ppermute x6, starting transfers between devices, shift(): return lax.ppermute(value, AXES, pairs)  18.7 us
    ppermute x6, waiting for transfers between devices, shift(): return lax.ppermute(value, AXES, pairs)  15.5 us
    pallas_call x1, Pallas kernels, per_device(): pl.pallas_call(mlp_kernel, out_shape=pltpu.VMEM((ROWS, HID), BF16), in_sp...  8.94 us
    all_gather x1, waiting for transfers between devices, per_device(): weights = lax.all_gather(weights, 'prompt', axis=0, tiled=False)  7.17 us
    unnamed x11, local copies, waits for them, and re-layouts  3.87 us
  transfers between devices with their start and end apart: 7, of which 6 were waited for; matrix products, arithmetic and copies ran while one was open for 1% of the time, Pallas kernels for 0%

profile of v9, /device:TPU:6, one launch (start us, length us, event | category | flops | bytes accessed | tf_op | source)
XLA Modules:
  0.0 156.1 jit_solution(10139008793981382797)
XLA Ops:
  6.5 0.9 copy-done.1
  7.5 0.9 copy-done.2
  8.4 0.8 shard_map.82
  9.1 0.0 all-gather.3.cloned.1.call-update
  9.8 0.0 copy-start
  9.8 1.2 copy-done
  11.0 0.7 copy-done.3
  11.6 0.1 shard_map.83
  11.7 21.7 %all_to_all.20.recv_ref = bf16[16,64,512]{2,1,0:T(8,128)(2,1)S(1)} all-to-all(bf16[16,64,512]{2,1,0:T(8,128)(2,1)S(1)} %shard_map.83), channel_id=1, replica_groups=mesh['prompt'=32,'rollout'=16] {'rollout'}, dimensions={0} | all-to-all | bytes 2097152 | tf_op jit(solution)/shard_map/all_to_all | solution.py:226
  33.5 0.6 shard_map.84
  34.1 17.1 %all_to_all.21.refs_0_ = bf16[4,384,512]{2,1,0:T(8,128)(2,1)S(1)} all-to-all(bf16[4,384,512]{2,1,0:T(8,128)(2,1)S(1)} %shard_map.84), channel_id=1, replica_groups={{0,1,2,3},{4,5,6,7},{8,9,10,11},{12,13,14,15},{16,20,24,28},{17,21,25,2..., dimensions={0} | all-to-all | bytes 3145728 | tf_op jit(solution)/shard_map/all_to_all | solution.py:52
  51.1 1.3 fusion.6
  52.4 2.6 %collective-permute-start.2 = (bf16[2,384,512]{2,1,0:T(8,128)(2,1)}, bf16[2,384,512]{2,1,0:T(8,128)(2,1)S(1)}, u32[]{:S(2)}, u32[]{:S(2)}) collective-permute-start(bf16[2,384,512]{2,1,0:T(8,128)(2,1)} %get-tuple-element.5), channel_id=1, source_target_pairs={{0,12},{4,0},{8,4},{12,8},{1,13},{5,1},{9,5},{13,9},{2,14},{6,2},{... | collective-permute-start | bytes 2359304 | tf_op jit(solution)/shard_map/ppermute | solution.py:61
  55.0 3.3 %collective-permute-start = (bf16[2,384,512]{2,1,0:T(8,128)(2,1)}, bf16[2,384,512]{2,1,0:T(8,128)(2,1)}, u32[]{:S(2)}, u32[]{:S(2)}) collective-permute-start(bf16[2,384,512]{2,1,0:T(8,128)(2,1)} %get-tuple-element.6), channel_id=1, source_target_pairs={{0,4},{4,8},{8,12},{12,0},{1,5},{5,9},{9,13},{13,1},{2,6},{6,10},{... | collective-permute-start | bytes 2359304 | tf_op jit(solution)/shard_map/ppermute | solution.py:61
  58.3 1.9 %collective-permute-start.1 = (bf16[2,384,512]{2,1,0:T(8,128)(2,1)}, bf16[2,384,512]{2,1,0:T(8,128)(2,1)}, u32[]{:S(2)}, u32[]{:S(2)}) collective-permute-start(bf16[2,384,512]{2,1,0:T(8,128)(2,1)} %get-tuple-element.5), channel_id=1, source_target_pairs={{0,4},{4,8},{8,12},{12,0},{1,5},{5,9},{9,13},{13,1},{2,6},{6,10},{... | collective-permute-start | bytes 2359304 | tf_op jit(solution)/shard_map/ppermute | solution.py:61
  60.2 5.1 %collective-permute-start.3 = (bf16[2,384,512]{2,1,0:T(8,128)(2,1)}, bf16[2,384,512]{2,1,0:T(8,128)(2,1)}, u32[]{:S(2)}, u32[]{:S(2)}) collective-permute-start(bf16[2,384,512]{2,1,0:T(8,128)(2,1)} %get-tuple-element.6), channel_id=1, source_target_pairs={{0,12},{4,0},{8,4},{12,8},{1,13},{5,1},{9,5},{13,9},{2,14},{6,2},{... | collective-permute-start | bytes 2359304 | tf_op jit(solution)/shard_map/ppermute | solution.py:61
  65.3 1.2 collective-permute-done.2.refs_3_
  66.5 3.8 %collective-permute-start.5 = (bf16[2,384,512]{2,1,0:T(8,128)(2,1)S(1)}, bf16[2,384,512]{2,1,0:T(8,128)(2,1)}, u32[]{:S(2)}, u32[]{:S(2)}) collective-permute-start(bf16[2,384,512]{2,1,0:T(8,128)(2,1)S(1)} %collective-permute-done.2.refs_3_), channel_id=1, source_target_pairs={{0,12},{4,0},{8,4},{12,8},{1,13},{5,1},{9,5},{13,9},{2,14},{6,2},{... | collective-permute-start | bytes 2359304 | tf_op jit(solution)/shard_map/ppermute | solution.py:61
  70.3 0.1 collective-permute-done.refs_1_
  70.4 2.0 %collective-permute-start.4 = (bf16[2,384,512]{2,1,0:T(8,128)(2,1)}, bf16[2,384,512]{2,1,0:T(8,128)(2,1)}, u32[]{:S(2)}, u32[]{:S(2)}) collective-permute-start(bf16[2,384,512]{2,1,0:T(8,128)(2,1)} %collective-permute-done.refs_1_), channel_id=1, source_target_pairs={{0,4},{4,8},{8,12},{12,0},{1,5},{5,9},{9,13},{13,1},{2,6},{6,10},{... | collective-permute-start | bytes 2359304 | tf_op jit(solution)/shard_map/ppermute | solution.py:61
  72.5 0.2 copy.11
  72.7 0.2 fusion.3
  73.0 5.8 %collective-permute-done.1.refs_2_ = bf16[2,384,512]{2,1,0:T(8,128)(2,1)} collective-permute-done((bf16[2,384,512]{2,1,0:T(8,128)(2,1)}, bf16[2,384,512]{2,1,0:T(8,128)(2,1)}, u32[]{:S(2)}, u32[]{:S(2)}) %collective-permute-start.1) | collective-permute-done | bytes 786464 | tf_op jit(solution)/shard_map/ppermute | solution.py:61
  78.8 0.0 collective-permute-done.3.refs_4_
  78.8 4.6 %collective-permute-done.5.refs_6_ = bf16[2,384,512]{2,1,0:T(8,128)(2,1)} collective-permute-done((bf16[2,384,512]{2,1,0:T(8,128)(2,1)S(1)}, bf16[2,384,512]{2,1,0:T(8,128)(2,1)}, u32[]{:S(2)}, u32[]{:S(2)}) %collective-permute-start.5) | collective-permute-done | bytes 786464 | tf_op jit(solution)/shard_map/ppermute | solution.py:61
  83.5 3.8 %collective-permute-done.4.refs_5_ = bf16[2,384,512]{2,1,0:T(8,128)(2,1)} collective-permute-done((bf16[2,384,512]{2,1,0:T(8,128)(2,1)}, bf16[2,384,512]{2,1,0:T(8,128)(2,1)}, u32[]{:S(2)}, u32[]{:S(2)}) %collective-permute-start.4) | collective-permute-done | bytes 786464 | tf_op jit(solution)/shard_map/ppermute | solution.py:61
  87.2 7.2 %all-gather.3.cloned.1.call-done = bf16[17920,256]{1,0:T(8,128)(2,1)} async-done(((bf16[560,256]{1,0:T(8,128)(2,1)}), bf16[17920,256]{1,0:T(8,128)(2,1)}) %all-gather.3.cloned.1.call-update) | async-done | bytes 9175056 | tf_op jit(solution)/shard_map/all_gather | solution.py:221
  94.4 8.9 %shard_map.85 = bf16[384,5120]{1,0:T(8,128)(2,1)S(1)} custom-call(bf16[4,4,2,560,256]{4,3,2,1,0:T(8,128)(2,1)} %bitcast.14, bf16[4,384,512]{2,1,0:T(8,128)(2,1)S(1)} %all_to_all.21.refs_0_, bf16[2,384,512]{2,1,0:T(8,128)(2,1)} %collective-permute-done.refs_1_, bf16[2,384,512]{2,1,0:T(8,128)(2,1)} %collective-permute-done.1.refs_2_, ...), custom_call_target="tpu_custom_call" | custom-call | flops 3221225472 | bytes 16777216 | tf_op jit(solution)/shard_map/pallas_call | solution.py:237
  103.4 28.9 %all_to_all.22.recv_ref = bf16[4,96,5120]{2,1,0:T(8,128)(2,1)S(1)} all-to-all(bf16[4,96,5120]{2,1,0:T(8,128)(2,1)S(1)} %bitcast.9), channel_id=1, replica_groups={{0,1,2,3},{4,5,6,7},{8,9,10,11},{12,13,14,15},{16,20,24,28},{17,21,25,2..., dimensions={0} | all-to-all | bytes 7864320 | tf_op jit(solution)/shard_map/all_to_all | solution.py:52
  132.2 0.5 shard_map.86
  132.7 14.5 %all_to_all.23.recv_ref = bf16[4,24,5120]{2,1,0:T(8,128)(2,1)S(1)} all-to-all(bf16[4,24,5120]{2,1,0:T(8,128)(2,1)S(1)} %bitcast.10), channel_id=1, replica_groups={{0,4,8,12},{1,5,9,13},{2,6,10,14},{3,7,11,15},{16,17,18,19},{20,21,22,2..., dimensions={0} | all-to-all | bytes 1966080 | tf_op jit(solution)/shard_map/all_to_all | solution.py:52
  147.2 2.0 %shard_map.87 = bf16[24,5120]{1,0:T(8,128)(2,1)} custom-call(bf16[4,24,5120]{2,1,0:T(8,128)(2,1)S(1)} %all_to_all.23.recv_ref, bf16[24,5120]{1,0:T(8,128)(2,1)} %patches_hbm.1, f32[1280]{0:T(1024)} %gain_hbm.1), custom_call_target="tpu_custom_call" | custom-call | tf_op jit(solution)/shard_map/pallas_call | solution.py:257
  (7 shorter events, 0.1 us)
Async XLA Ops:
  6.5 87.9 %all-gather.3.cloned.1.call-start = ((), (), s32[]{:S(2)}) async-start(), calls=%async_computation.4 | async-start | bytes 9461760 | tf_op jit(solution)/shard_map/all_gather | solution.py:221
  6.5 0.9 copy-start.1
  7.5 0.9 copy-start.2
  9.8 1.2 copy-start
  11.0 0.7 copy-start.3
  33.5 39.0 %copy-start.4 = (bf16[384,320]{0,1:T(8,128)(2,1)S(1)}, bf16[384,320]{0,1:T(8,128)(2,1)}, u32[]{:S(2)}) copy-start(bf16[384,320]{0,1:T(8,128)(2,1)} %param.11) | copy-start | bytes 737284
  52.4 14.1 %collective-permute-start.2 = (bf16[2,384,512]{2,1,0:T(8,128)(2,1)}, bf16[2,384,512]{2,1,0:T(8,128)(2,1)S(1)}, u32[]{:S(2)}, u32[]{:S(2)}) collective-permute-start(bf16[2,384,512]{2,1,0:T(8,128)(2,1)} %get-tuple-element.5), channel_id=1, source_target_pairs={{0,12},{4,0},{8,4},{12,8},{1,13},{5,1},{9,5},{13,9},{2,14},{6,2},{... | collective-permute-start | bytes 2359304 | tf_op jit(solution)/shard_map/ppermute | solution.py:61
  55.0 15.4 %collective-permute-start = (bf16[2,384,512]{2,1,0:T(8,128)(2,1)}, bf16[2,384,512]{2,1,0:T(8,128)(2,1)}, u32[]{:S(2)}, u32[]{:S(2)}) collective-permute-start(bf16[2,384,512]{2,1,0:T(8,128)(2,1)} %get-tuple-element.6), channel_id=1, source_target_pairs={{0,4},{4,8},{8,12},{12,0},{1,5},{5,9},{9,13},{13,1},{2,6},{6,10},{... | collective-permute-start | bytes 2359304 | tf_op jit(solution)/shard_map/ppermute | solution.py:61
  58.3 20.6 %collective-permute-start.1 = (bf16[2,384,512]{2,1,0:T(8,128)(2,1)}, bf16[2,384,512]{2,1,0:T(8,128)(2,1)}, u32[]{:S(2)}, u32[]{:S(2)}) collective-permute-start(bf16[2,384,512]{2,1,0:T(8,128)(2,1)} %get-tuple-element.5), channel_id=1, source_target_pairs={{0,4},{4,8},{8,12},{12,0},{1,5},{5,9},{9,13},{13,1},{2,6},{6,10},{... | collective-permute-start | bytes 2359304 | tf_op jit(solution)/shard_map/ppermute | solution.py:61
  60.2 18.6 %collective-permute-start.3 = (bf16[2,384,512]{2,1,0:T(8,128)(2,1)}, bf16[2,384,512]{2,1,0:T(8,128)(2,1)}, u32[]{:S(2)}, u32[]{:S(2)}) collective-permute-start(bf16[2,384,512]{2,1,0:T(8,128)(2,1)} %get-tuple-element.6), channel_id=1, source_target_pairs={{0,12},{4,0},{8,4},{12,8},{1,13},{5,1},{9,5},{13,9},{2,14},{6,2},{... | collective-permute-start | bytes 2359304 | tf_op jit(solution)/shard_map/ppermute | solution.py:61
  66.5 17.0 %collective-permute-start.5 = (bf16[2,384,512]{2,1,0:T(8,128)(2,1)S(1)}, bf16[2,384,512]{2,1,0:T(8,128)(2,1)}, u32[]{:S(2)}, u32[]{:S(2)}) collective-permute-start(bf16[2,384,512]{2,1,0:T(8,128)(2,1)S(1)} %collective-permute-done.2.refs_3_), channel_id=1, source_target_pairs={{0,12},{4,0},{8,4},{12,8},{1,13},{5,1},{9,5},{13,9},{2,14},{6,2},{... | collective-permute-start | bytes 2359304 | tf_op jit(solution)/shard_map/ppermute | solution.py:61
  70.4 16.9 %collective-permute-start.4 = (bf16[2,384,512]{2,1,0:T(8,128)(2,1)}, bf16[2,384,512]{2,1,0:T(8,128)(2,1)}, u32[]{:S(2)}, u32[]{:S(2)}) collective-permute-start(bf16[2,384,512]{2,1,0:T(8,128)(2,1)} %collective-permute-done.refs_1_), channel_id=1, source_target_pairs={{0,4},{4,8},{8,12},{12,0},{1,5},{5,9},{9,13},{13,1},{2,6},{6,10},{... | collective-permute-start | bytes 2359304 | tf_op jit(solution)/shard_map/ppermute | solution.py:61
Sparse Core Ops, SparseCore 0:
  9.5 84.8 all-gather.2

commit v10 on v9

--- a/solution.py
+++ b/solution.py
@@ -67,16 +67,21 @@
     return even, jnp.where(even, rollout // SIDE, rollout % SIDE)
 
 
-def weights_kernel(w2_ref, w1_ref, out_ref):
-    out_ref[0:HID_OWN, :] = w2_ref[...]
-    out_ref[HID_OWN : HID_OWN + IN_OWN, :] = w1_ref[:, 0:256]
+def pack_kernel(count_ref, ids_ref, grads_ref, w2_ref, w1_ref, out_ref, weights_ref, weights, w1, meta, sems):
     base = HID_OWN + IN_OWN
-    out_ref[base:W_ROWS, :] = jnp.zeros((TAIL, 256), BF16)
-    out_ref[base:W_ROWS, 0:64] = w1_ref[0:TAIL, 256:320]
-    out_ref[base:W_ROWS, 128:192] = w1_ref[TAIL:IN_OWN, 256:320]
-
-
-def pack_kernel(count_ref, ids_ref, grads_ref, out_ref, meta):
+    from_w2 = pltpu.make_async_copy(w2_ref, weights.at[0:HID_OWN], sems.at[0])
+    from_w1 = pltpu.make_async_copy(w1_ref, w1, sems.at[1])
+    from_w2.start()
+    from_w1.start()
+    from_w1.wait()
+    weights[HID_OWN:base, :] = w1[:, 0:256]
+    weights[base:W_ROWS, :] = jnp.zeros((TAIL, 256), BF16)
+    weights[base:W_ROWS, 0:64] = w1[0:TAIL, 256:320]
+    weights[base:W_ROWS, 128:192] = w1[TAIL:IN_OWN, 256:320]
+    from_w2.wait()
+    to_weights = pltpu.make_async_copy(weights, weights_ref, sems.at[2])
+    to_weights.start()
+
     even, _ = place_in_plane()
     ids = ids_ref[...]
     owner = (ids * 2731) >> 16
@@ -94,6 +99,7 @@
         out_ref[k, 0:48, :] = grads_ref[0:48, cols]
         two = jnp.concatenate([grads_ref[48:SLOTS, cols].astype(F32), zeros[0:6]], axis=0)
         out_ref[k, 48:64, :] = jnp.concatenate([two + codes, zeros], axis=0).astype(BF16)
+    to_weights.wait()
 
 
 def sum_kernel(recv_ref, out_ref):
@@ -180,15 +186,20 @@
     ]
     for copy in copies:
         copy.start()
-    for copy in copies:
-        copy.wait()
+    sums = []
     for m in range(MERGE):
         cols = slice(m * VIT, (m + 1) * VIT)
         upstream = recv_ref[0, :, cols].astype(F32)
         for k in range(1, SIDE):
             upstream = upstream + recv_ref[k, :, cols].astype(F32)
+        sums.append(upstream)
+    for copy in copies:
+        copy.wait()
+    gain = gain_ref[...][None]
+    for m in range(MERGE):
+        cols = slice(m * VIT, (m + 1) * VIT)
         inputs = patches_ref[:, cols].astype(F32)
-        scaled = upstream * gain_ref[...][None]
+        scaled = sums[m] * gain
         inverse = lax.rsqrt(jnp.mean(inputs * inputs, axis=-1, keepdims=True) + 1e-06)
         inner = jnp.mean(scaled * inputs, axis=-1, keepdims=True)
         result = inverse * scaled - inputs * inverse * inverse * inverse * inner
@@ -217,12 +228,25 @@
 
 
 def per_device(row_grads, used_ids, used_count, pre_act, patches, ln_gain, w_fc2, w_fc1):
-    weights = call(weights_kernel, (W_ROWS, 256), [VMEM] * 2)(w_fc2, w_fc1)
-    weights = lax.all_gather(weights, "prompt", axis=0, tiled=False)
-
-    outgoing = call(
-        pack_kernel, (ROLLOUTS, PAD_SLOTS, COLS), [SMEM, VMEM, VMEM], scratch=[pltpu.VMEM((8, COLS), F32)]
-    )(used_count, used_ids[0], row_grads[0, 0])
+    outgoing, weights = pl.pallas_call(
+        pack_kernel,
+        out_shape=[
+            jax.ShapeDtypeStruct((ROLLOUTS, PAD_SLOTS, COLS), BF16),
+            jax.ShapeDtypeStruct((W_ROWS, 256), BF16),
+        ],
+        in_specs=[SMEM, VMEM, VMEM, ANY, ANY],
+        out_specs=[VMEM, ANY],
+        scratch_shapes=[
+            pltpu.VMEM((W_ROWS, 256), BF16),
+            pltpu.VMEM((IN_OWN, HID_OWN), BF16),
+            pltpu.VMEM((8, COLS), F32),
+            pltpu.SemaphoreType.DMA((3,)),
+        ],
+        compiler_params=pltpu.CompilerParams(vmem_limit_bytes=16 << 20),
+    )(used_count, used_ids[0], row_grads[0, 0], pinned(w_fc2), pinned(w_fc1))
+    groups = [[p * ROLLOUTS + r for p in range(PROMPTS)] for r in range(ROLLOUTS)]
+    weights = lax.all_gather(weights, AXES, axis=0, tiled=False, axis_index_groups=groups)
+
     received = lax.all_to_all(outgoing, "rollout", split_axis=0, concat_axis=0, tiled=True)
     summed = call(sum_kernel, (SIDE, ROWS, COLS), [VMEM])(received)
     line = exchange(summed, 0)

time: 157 us -> 159 us (1.013)
  waiting for transfers between devices: 22.7 us -> 25.1 us
  local copies, waits for them, and re-layouts: 5.13 us -> 3.32 us
    all_gather x1, waiting for transfers between devices: 7.17 us -> 9.54 us  [per_device(): lax.all_gather(weights, AXES, axis=0, tiled=False, axis_index_groups=groups)]
    unnamed x11 -> x7, local copies, waits for them, and re-layouts: 3.87 us -> 2.05 us
where the time goes in v10:
time: 159 us; the launch traced here: 158 us
  blocking collectives  82.3 us (52%)
  waiting for transfers between devices  25.1 us (16%)
  starting transfers between devices  18.7 us (12%)
  between operations  14.2 us (9%)
  Pallas kernels  13.7 us (9%)
  local copies, waits for them, and re-layouts  3.32 us (2%)
    all_to_all x3, blocking collectives, exchange(): lax.all_to_all(blocks, AXES, split_axis=0, concat_axis=0, axis_index_grou...  60.6 us
    all_to_all x1, blocking collectives, per_device(): lax.all_to_all(outgoing, 'rollout', split_axis=0, concat_axis=0, tiled=True)  21.8 us
    ppermute x6, starting transfers between devices, shift(): return lax.ppermute(value, AXES, pairs)  18.7 us
    ppermute x6, waiting for transfers between devices, shift(): return lax.ppermute(value, AXES, pairs)  15.6 us
    all_gather x1, waiting for transfers between devices, per_device(): lax.all_gather(weights, AXES, axis=0, tiled=False, axis_index_groups=groups)  9.54 us
    pallas_call x1, Pallas kernels, per_device(): pl.pallas_call(mlp_kernel, out_shape=pltpu.VMEM((ROWS, HID), BF16), in_sp...  8.94 us
  transfers between devices with their start and end apart: 7, of which 6 were waited for; matrix products, arithmetic and copies ran while one was open for 1% of the time, Pallas kernels for 0%

profile of v10, /device:TPU:6, one launch (start us, length us, event | category | flops | bytes accessed | tf_op | source)
XLA Modules:
  0.0 157.6 jit_solution(13547864219722439651)
XLA Ops:
  6.5 0.0 all-gather.3.cloned.1.call-start
  7.2 0.0 copy-start
  7.2 1.2 copy-done
  8.4 0.0 copy-start.1
  8.4 0.7 copy-done.1
  9.0 1.8 %shard_map.82 = (bf16[16,64,512]{2,1,0:T(8,128)(2,1)S(1)}, bf16[560,256]{1,0:T(8,128)(2,1)}) custom-call(s32[1,1]{1,0:T(1,128)S(6)} %copy.14.count_ref, s32[1,50]{1,0:T(1,128)S(1)} %bitcast.13, bf16[50,8192]{1,0:T(8,128)(2,1)S(1)} %bitcast.12, bf16[320,256]{1,0:T(8,128)(2,1)} %w2_ref.1, bf16[160,320]{1,0:T(8,128)(2,1)} %w1_ref.1), custom_call_target="tpu_custom_call" | custom-call | tf_op jit(solution)/shard_map/pallas_call | solution.py:231
  10.8 0.0 all-gather.3.cloned.1.call-update
  10.8 21.8 %all_to_all.20.recv_ref = bf16[16,64,512]{2,1,0:T(8,128)(2,1)S(1)} all-to-all(bf16[16,64,512]{2,1,0:T(8,128)(2,1)S(1)} %get-tuple-element.8), channel_id=1, replica_groups=mesh['prompt'=32,'rollout'=16] {'rollout'}, dimensions={0} | all-to-all | bytes 2097152 | tf_op jit(solution)/shard_map/all_to_all | solution.py:250
  32.6 0.6 shard_map.83
  33.2 17.1 %all_to_all.21.refs_0_ = bf16[4,384,512]{2,1,0:T(8,128)(2,1)S(1)} all-to-all(bf16[4,384,512]{2,1,0:T(8,128)(2,1)S(1)} %shard_map.83), channel_id=1, replica_groups={{0,1,2,3},{4,5,6,7},{8,9,10,11},{12,13,14,15},{16,20,24,28},{17,21,25,2..., dimensions={0} | all-to-all | bytes 3145728 | tf_op jit(solution)/shard_map/all_to_all | solution.py:52
  50.3 1.3 fusion.6
  51.5 2.6 %collective-permute-start.2 = (bf16[2,384,512]{2,1,0:T(8,128)(2,1)}, bf16[2,384,512]{2,1,0:T(8,128)(2,1)S(1)}, u32[]{:S(2)}, u32[]{:S(2)}) collective-permute-start(bf16[2,384,512]{2,1,0:T(8,128)(2,1)} %get-tuple-element.9), channel_id=1, source_target_pairs={{0,12},{4,0},{8,4},{12,8},{1,13},{5,1},{9,5},{13,9},{2,14},{6,2},{... | collective-permute-start | bytes 2359304 | tf_op jit(solution)/shard_map/ppermute | solution.py:61
  54.1 3.3 %collective-permute-start = (bf16[2,384,512]{2,1,0:T(8,128)(2,1)}, bf16[2,384,512]{2,1,0:T(8,128)(2,1)}, u32[]{:S(2)}, u32[]{:S(2)}) collective-permute-start(bf16[2,384,512]{2,1,0:T(8,128)(2,1)} %get-tuple-element.10), channel_id=1, source_target_pairs={{0,4},{4,8},{8,12},{12,0},{1,5},{5,9},{9,13},{13,1},{2,6},{6,10},{... | collective-permute-start | bytes 2359304 | tf_op jit(solution)/shard_map/ppermute | solution.py:61
  57.4 1.9 %collective-permute-start.1 = (bf16[2,384,512]{2,1,0:T(8,128)(2,1)}, bf16[2,384,512]{2,1,0:T(8,128)(2,1)}, u32[]{:S(2)}, u32[]{:S(2)}) collective-permute-start(bf16[2,384,512]{2,1,0:T(8,128)(2,1)} %get-tuple-element.9), channel_id=1, source_target_pairs={{0,4},{4,8},{8,12},{12,0},{1,5},{5,9},{9,13},{13,1},{2,6},{6,10},{... | collective-permute-start | bytes 2359304 | tf_op jit(solution)/shard_map/ppermute | solution.py:61
  59.3 5.1 %collective-permute-start.3 = (bf16[2,384,512]{2,1,0:T(8,128)(2,1)}, bf16[2,384,512]{2,1,0:T(8,128)(2,1)}, u32[]{:S(2)}, u32[]{:S(2)}) collective-permute-start(bf16[2,384,512]{2,1,0:T(8,128)(2,1)} %get-tuple-element.10), channel_id=1, source_target_pairs={{0,12},{4,0},{8,4},{12,8},{1,13},{5,1},{9,5},{13,9},{2,14},{6,2},{... | collective-permute-start | bytes 2359304 | tf_op jit(solution)/shard_map/ppermute | solution.py:61
  64.4 1.2 collective-permute-done.2.refs_3_
  65.6 3.8 %collective-permute-start.5 = (bf16[2,384,512]{2,1,0:T(8,128)(2,1)S(1)}, bf16[2,384,512]{2,1,0:T(8,128)(2,1)}, u32[]{:S(2)}, u32[]{:S(2)}) collective-permute-start(bf16[2,384,512]{2,1,0:T(8,128)(2,1)S(1)} %collective-permute-done.2.refs_3_), channel_id=1, source_target_pairs={{0,12},{4,0},{8,4},{12,8},{1,13},{5,1},{9,5},{13,9},{2,14},{6,2},{... | collective-permute-start | bytes 2359304 | tf_op jit(solution)/shard_map/ppermute | solution.py:61
  69.4 0.1 collective-permute-done.refs_1_
  69.5 2.0 %collective-permute-start.4 = (bf16[2,384,512]{2,1,0:T(8,128)(2,1)}, bf16[2,384,512]{2,1,0:T(8,128)(2,1)}, u32[]{:S(2)}, u32[]{:S(2)}) collective-permute-start(bf16[2,384,512]{2,1,0:T(8,128)(2,1)} %collective-permute-done.refs_1_), channel_id=1, source_target_pairs={{0,4},{4,8},{8,12},{12,0},{1,5},{5,9},{9,13},{13,1},{2,6},{6,10},{... | collective-permute-start | bytes 2359304 | tf_op jit(solution)/shard_map/ppermute | solution.py:61
  71.6 0.0 copy-done.2
  71.6 0.2 copy.11
  71.8 0.2 fusion.3
  72.1 5.8 %collective-permute-done.1.refs_2_ = bf16[2,384,512]{2,1,0:T(8,128)(2,1)} collective-permute-done((bf16[2,384,512]{2,1,0:T(8,128)(2,1)}, bf16[2,384,512]{2,1,0:T(8,128)(2,1)}, u32[]{:S(2)}, u32[]{:S(2)}) %collective-permute-start.1) | collective-permute-done | bytes 786464 | tf_op jit(solution)/shard_map/ppermute | solution.py:61
  77.9 0.0 collective-permute-done.3.refs_4_
  78.0 4.6 %collective-permute-done.5.refs_6_ = bf16[2,384,512]{2,1,0:T(8,128)(2,1)} collective-permute-done((bf16[2,384,512]{2,1,0:T(8,128)(2,1)S(1)}, bf16[2,384,512]{2,1,0:T(8,128)(2,1)}, u32[]{:S(2)}, u32[]{:S(2)}) %collective-permute-start.5) | collective-permute-done | bytes 786464 | tf_op jit(solution)/shard_map/ppermute | solution.py:61
  82.6 3.8 %collective-permute-done.4.refs_5_ = bf16[2,384,512]{2,1,0:T(8,128)(2,1)} collective-permute-done((bf16[2,384,512]{2,1,0:T(8,128)(2,1)}, bf16[2,384,512]{2,1,0:T(8,128)(2,1)}, u32[]{:S(2)}, u32[]{:S(2)}) %collective-permute-start.4) | collective-permute-done | bytes 786464 | tf_op jit(solution)/shard_map/ppermute | solution.py:61
  86.4 9.5 %all-gather.3.cloned.1.call-done = bf16[17920,256]{1,0:T(8,128)(2,1)} async-done(((bf16[560,256]{1,0:T(8,128)(2,1)}), bf16[17920,256]{1,0:T(8,128)(2,1)}) %all-gather.3.cloned.1.call-update) | async-done | bytes 9175056 | tf_op jit(solution)/shard_map/all_gather | solution.py:248
  95.9 8.9 %shard_map.84 = bf16[384,5120]{1,0:T(8,128)(2,1)S(1)} custom-call(bf16[4,4,2,560,256]{4,3,2,1,0:T(8,128)(2,1)} %bitcast.14, bf16[4,384,512]{2,1,0:T(8,128)(2,1)S(1)} %all_to_all.21.refs_0_, bf16[2,384,512]{2,1,0:T(8,128)(2,1)} %collective-permute-done.refs_1_, bf16[2,384,512]{2,1,0:T(8,128)(2,1)} %collective-permute-done.1.refs_2_, ...), custom_call_target="tpu_custom_call" | custom-call | flops 3221225472 | bytes 16777216 | tf_op jit(solution)/shard_map/pallas_call | solution.py:261
  104.9 28.7 %all_to_all.22.recv_ref = bf16[4,96,5120]{2,1,0:T(8,128)(2,1)S(1)} all-to-all(bf16[4,96,5120]{2,1,0:T(8,128)(2,1)S(1)} %bitcast.9), channel_id=1, replica_groups={{0,1,2,3},{4,5,6,7},{8,9,10,11},{12,13,14,15},{16,20,24,28},{17,21,25,2..., dimensions={0} | all-to-all | bytes 7864320 | tf_op jit(solution)/shard_map/all_to_all | solution.py:52
  133.6 0.5 shard_map.85
  134.1 14.8 %all_to_all.23.recv_ref = bf16[4,24,5120]{2,1,0:T(8,128)(2,1)S(1)} all-to-all(bf16[4,24,5120]{2,1,0:T(8,128)(2,1)S(1)} %bitcast.10), channel_id=1, replica_groups={{0,4,8,12},{1,5,9,13},{2,6,10,14},{3,7,11,15},{16,17,18,19},{20,21,22,2..., dimensions={0} | all-to-all | bytes 1966080 | tf_op jit(solution)/shard_map/all_to_all | solution.py:52
  148.9 1.9 %shard_map.86 = bf16[24,5120]{1,0:T(8,128)(2,1)} custom-call(bf16[4,24,5120]{2,1,0:T(8,128)(2,1)S(1)} %all_to_all.23.recv_ref, bf16[24,5120]{1,0:T(8,128)(2,1)} %patches_hbm.1, f32[1280]{0:T(1024)} %gain_hbm.1), custom_call_target="tpu_custom_call" | custom-call | tf_op jit(solution)/shard_map/pallas_call | solution.py:281
  (2 shorter events, 0.0 us)
Async XLA Ops:
  6.5 89.4 %all-gather.3.cloned.1.call-start = ((), (), s32[]{:S(2)}) async-start(), calls=%async_computation.4 | async-start | bytes 9461760 | tf_op jit(solution)/shard_map/all_gather | solution.py:248
  7.2 1.2 copy-start
  8.4 0.7 copy-start.1
  32.6 39.0 %copy-start.2 = (bf16[384,320]{0,1:T(8,128)(2,1)S(1)}, bf16[384,320]{0,1:T(8,128)(2,1)}, u32[]{:S(2)}) copy-start(bf16[384,320]{0,1:T(8,128)(2,1)} %param.11) | copy-start | bytes 737284
  51.5 14.1 %collective-permute-start.2 = (bf16[2,384,512]{2,1,0:T(8,128)(2,1)}, bf16[2,384,512]{2,1,0:T(8,128)(2,1)S(1)}, u32[]{:S(2)}, u32[]{:S(2)}) collective-permute-start(bf16[2,384,512]{2,1,0:T(8,128)(2,1)} %get-tuple-element.9), channel_id=1, source_target_pairs={{0,12},{4,0},{8,4},{12,8},{1,13},{5,1},{9,5},{13,9},{2,14},{6,2},{... | collective-permute-start | bytes 2359304 | tf_op jit(solution)/shard_map/ppermute | solution.py:61
  54.1 15.4 %collective-permute-start = (bf16[2,384,512]{2,1,0:T(8,128)(2,1)}, bf16[2,384,512]{2,1,0:T(8,128)(2,1)}, u32[]{:S(2)}, u32[]{:S(2)}) collective-permute-start(bf16[2,384,512]{2,1,0:T(8,128)(2,1)} %get-tuple-element.10), channel_id=1, source_target_pairs={{0,4},{4,8},{8,12},{12,0},{1,5},{5,9},{9,13},{13,1},{2,6},{6,10},{... | collective-permute-start | bytes 2359304 | tf_op jit(solution)/shard_map/ppermute | solution.py:61
  57.4 20.6 %collective-permute-start.1 = (bf16[2,384,512]{2,1,0:T(8,128)(2,1)}, bf16[2,384,512]{2,1,0:T(8,128)(2,1)}, u32[]{:S(2)}, u32[]{:S(2)}) collective-permute-start(bf16[2,384,512]{2,1,0:T(8,128)(2,1)} %get-tuple-element.9), channel_id=1, source_target_pairs={{0,4},{4,8},{8,12},{12,0},{1,5},{5,9},{9,13},{13,1},{2,6},{6,10},{... | collective-permute-start | bytes 2359304 | tf_op jit(solution)/shard_map/ppermute | solution.py:61
  59.3 18.6 %collective-permute-start.3 = (bf16[2,384,512]{2,1,0:T(8,128)(2,1)}, bf16[2,384,512]{2,1,0:T(8,128)(2,1)}, u32[]{:S(2)}, u32[]{:S(2)}) collective-permute-start(bf16[2,384,512]{2,1,0:T(8,128)(2,1)} %get-tuple-element.10), channel_id=1, source_target_pairs={{0,12},{4,0},{8,4},{12,8},{1,13},{5,1},{9,5},{13,9},{2,14},{6,2},{... | collective-permute-start | bytes 2359304 | tf_op jit(solution)/shard_map/ppermute | solution.py:61
  65.6 17.0 %collective-permute-start.5 = (bf16[2,384,512]{2,1,0:T(8,128)(2,1)S(1)}, bf16[2,384,512]{2,1,0:T(8,128)(2,1)}, u32[]{:S(2)}, u32[]{:S(2)}) collective-permute-start(bf16[2,384,512]{2,1,0:T(8,128)(2,1)S(1)} %collective-permute-done.2.refs_3_), channel_id=1, source_target_pairs={{0,12},{4,0},{8,4},{12,8},{1,13},{5,1},{9,5},{13,9},{2,14},{6,2},{... | collective-permute-start | bytes 2359304 | tf_op jit(solution)/shard_map/ppermute | solution.py:61
  69.5 16.9 %collective-permute-start.4 = (bf16[2,384,512]{2,1,0:T(8,128)(2,1)}, bf16[2,384,512]{2,1,0:T(8,128)(2,1)}, u32[]{:S(2)}, u32[]{:S(2)}) collective-permute-start(bf16[2,384,512]{2,1,0:T(8,128)(2,1)} %collective-permute-done.refs_1_), channel_id=1, source_target_pairs={{0,4},{4,8},{8,12},{12,0},{1,5},{5,9},{9,13},{13,1},{2,6},{6,10},{... | collective-permute-start | bytes 2359304 | tf_op jit(solution)/shard_map/ppermute | solution.py:61
Sparse Core Ops, SparseCore 0:
  10.9 84.9 all-gather.2

commit v11 on v9

--- a/solution.py
+++ b/solution.py
@@ -20,7 +20,8 @@
 HID_OWN = HID // ROLLOUTS
 IN_OWN = HID // PROMPTS
 W2_COLS = D_LLM // PROMPTS
-TAIL = IN_OWN // 2
+RUNS = (48, 48, 32, 32)
+TAIL = 48
 W_ROWS = HID_OWN + IN_OWN + TAIL
 AXES = ("prompt", "rollout")
 F32 = jnp.float32
@@ -67,13 +68,23 @@
     return even, jnp.where(even, rollout // SIDE, rollout % SIDE)
 
 
-def weights_kernel(w2_ref, w1_ref, out_ref):
-    out_ref[0:HID_OWN, :] = w2_ref[...]
-    out_ref[HID_OWN : HID_OWN + IN_OWN, :] = w1_ref[:, 0:256]
+def weights_kernel(w2_ref, w1_ref, out_ref, block, w1, sems):
     base = HID_OWN + IN_OWN
-    out_ref[base:W_ROWS, :] = jnp.zeros((TAIL, 256), BF16)
-    out_ref[base:W_ROWS, 0:64] = w1_ref[0:TAIL, 256:320]
-    out_ref[base:W_ROWS, 128:192] = w1_ref[TAIL:IN_OWN, 256:320]
+    from_w2 = pltpu.make_async_copy(w2_ref, block.at[0:HID_OWN], sems.at[0])
+    from_w1 = pltpu.make_async_copy(w1_ref, w1, sems.at[1])
+    from_w2.start()
+    from_w1.start()
+    block[base:W_ROWS, :] = jnp.zeros((TAIL, 256), BF16)
+    from_w1.wait()
+    block[HID_OWN:base, :] = w1[:, 0:256]
+    at = 0
+    for n, rows in enumerate(RUNS):
+        block[base : base + rows, 64 * n : 64 * n + 64] = w1[at : at + rows, 256:HID_OWN]
+        at += rows
+    from_w2.wait()
+    to_out = pltpu.make_async_copy(block, out_ref, sems.at[2])
+    to_out.start()
+    to_out.wait()
 
 
 def pack_kernel(count_ref, ids_ref, grads_ref, out_ref, meta):
@@ -161,8 +172,9 @@
         for copy in late[q]:
             copy.wait()
         fold = w1_tail[q]
-        tail = jnp.concatenate([fold[..., 0:128], fold[..., 128:256]], axis=2).reshape(width, 128)
-        part = dot_t(act[:, 0:256], w1[q].reshape(width, 256)) + dot_t(act[:, 256:], tail[:, 0:64])
+        runs = [fold[:, :, :rows, 64 * n : 64 * n + 64] for n, rows in enumerate(RUNS)]
+        tail = jnp.concatenate(runs, axis=2).reshape(width, 64)
+        part = dot_t(act[:, 0:256], w1[q].reshape(width, 256)) + dot_t(act[:, 256:], tail)
         out_ref[:, width * q : width * (q + 1)] = part.astype(BF16)
 
 
@@ -180,15 +192,20 @@
     ]
     for copy in copies:
         copy.start()
-    for copy in copies:
-        copy.wait()
+    sums = []
     for m in range(MERGE):
         cols = slice(m * VIT, (m + 1) * VIT)
         upstream = recv_ref[0, :, cols].astype(F32)
         for k in range(1, SIDE):
             upstream = upstream + recv_ref[k, :, cols].astype(F32)
+        sums.append(upstream)
+    for copy in copies:
+        copy.wait()
+    gain = gain_ref[...][None]
+    for m in range(MERGE):
+        cols = slice(m * VIT, (m + 1) * VIT)
         inputs = patches_ref[:, cols].astype(F32)
-        scaled = upstream * gain_ref[...][None]
+        scaled = sums[m] * gain
         inverse = lax.rsqrt(jnp.mean(inputs * inputs, axis=-1, keepdims=True) + 1e-06)
         inner = jnp.mean(scaled * inputs, axis=-1, keepdims=True)
         result = inverse * scaled - inputs * inverse * inverse * inverse * inner
@@ -200,12 +217,12 @@
 ANY = pl.BlockSpec(memory_space=pl.ANY)
 
 
-def call(kernel, shape, in_specs, flops=0, moved=0, vmem=16, scratch=(), fast=False):
+def call(kernel, shape, in_specs, flops=0, moved=0, vmem=16, scratch=(), fast=False, out_spec=VMEM):
     return pl.pallas_call(
         kernel,
         out_shape=pltpu.VMEM(shape, BF16) if fast else jax.ShapeDtypeStruct(shape, BF16),
         in_specs=in_specs,
-        out_specs=VMEM,
+        out_specs=out_spec,
         scratch_shapes=list(scratch),
         cost_estimate=pl.CostEstimate(flops=flops, bytes_accessed=moved, transcendentals=0),
         compiler_params=pltpu.CompilerParams(vmem_limit_bytes=vmem << 20),
@@ -217,7 +234,17 @@
 
 
 def per_device(row_grads, used_ids, used_count, pre_act, patches, ln_gain, w_fc2, w_fc1):
-    weights = call(weights_kernel, (W_ROWS, 256), [VMEM] * 2)(w_fc2, w_fc1)
+    weights = call(
+        weights_kernel,
+        (W_ROWS, 256),
+        [ANY, ANY],
+        out_spec=ANY,
+        scratch=[
+            pltpu.VMEM((W_ROWS, 256), BF16),
+            pltpu.VMEM((IN_OWN, HID_OWN), BF16),
+            pltpu.SemaphoreType.DMA((3,)),
+        ],
+    )(pinned(w_fc2), pinned(w_fc1))
     weights = lax.all_gather(weights, "prompt", axis=0, tiled=False)
 
     outgoing = call(

time: 157 us -> 157 us (level)
  local copies, waits for them, and re-layouts: 5.13 us -> 3.32 us
    unnamed x11 -> x7, local copies, waits for them, and re-layouts: 3.87 us -> 2.05 us
where the time goes in v11:
time: 157 us; the launch traced here: 156 us
  blocking collectives  82.3 us (52%)
  waiting for transfers between devices  23 us (15%)
  starting transfers between devices  18.7 us (12%)
  between operations  14.2 us (9%)
  Pallas kernels  13.9 us (9%)
  local copies, waits for them, and re-layouts  3.32 us (2%)
    all_to_all x3, blocking collectives, exchange(): lax.all_to_all(blocks, AXES, split_axis=0, concat_axis=0, axis_index_grou...  60.6 us
    all_to_all x1, blocking collectives, per_device(): lax.all_to_all(outgoing, 'rollout', split_axis=0, concat_axis=0, tiled=True)  21.7 us
    ppermute x6, starting transfers between devices, shift(): return lax.ppermute(value, AXES, pairs)  18.7 us
    ppermute x6, waiting for transfers between devices, shift(): return lax.ppermute(value, AXES, pairs)  15.5 us
    pallas_call x1, Pallas kernels, per_device(): pl.pallas_call(mlp_kernel, out_shape=pltpu.VMEM((ROWS, HID), BF16), in_sp...  9.07 us
    all_gather x1, waiting for transfers between devices, per_device(): weights = lax.all_gather(weights, 'prompt', axis=0, tiled=False)  7.49 us
  transfers between devices with their start and end apart: 7, of which 6 were waited for; matrix products, arithmetic and copies ran while one was open for 1% of the time, Pallas kernels for 0%

profile of v11, /device:TPU:6, one launch (start us, length us, event | category | flops | bytes accessed | tf_op | source)
XLA Modules:
  0.0 155.8 jit_solution(4456972166519256715)
XLA Ops:
  6.5 0.0 all-gather.3.cloned.1.call-start
  6.5 1.8 %shard_map.82 = bf16[528,256]{1,0:T(8,128)(2,1)} custom-call(bf16[320,256]{1,0:T(8,128)(2,1)} %w2_ref.1, bf16[160,320]{1,0:T(8,128)(2,1)} %w1_ref.1), custom_call_target="tpu_custom_call" | custom-call | tf_op jit(solution)/shard_map/pallas_call | solution.py:237
  8.3 0.0 all-gather.3.cloned.1.call-update
  9.0 0.0 copy-start
  9.0 1.2 copy-done
  10.2 0.7 copy-done.1
  10.9 0.1 shard_map.83
  10.9 21.7 %all_to_all.20.recv_ref = bf16[16,64,512]{2,1,0:T(8,128)(2,1)S(1)} all-to-all(bf16[16,64,512]{2,1,0:T(8,128)(2,1)S(1)} %shard_map.83), channel_id=1, replica_groups=mesh['prompt'=32,'rollout'=16] {'rollout'}, dimensions={0} | all-to-all | bytes 2097152 | tf_op jit(solution)/shard_map/all_to_all | solution.py:253
  32.7 0.6 shard_map.84
  33.3 17.1 %all_to_all.21.refs_0_ = bf16[4,384,512]{2,1,0:T(8,128)(2,1)S(1)} all-to-all(bf16[4,384,512]{2,1,0:T(8,128)(2,1)S(1)} %shard_map.84), channel_id=1, replica_groups={{0,1,2,3},{4,5,6,7},{8,9,10,11},{12,13,14,15},{16,20,24,28},{17,21,25,2..., dimensions={0} | all-to-all | bytes 3145728 | tf_op jit(solution)/shard_map/all_to_all | solution.py:53
  50.4 1.3 fusion.6
  51.7 2.6 %collective-permute-start.2 = (bf16[2,384,512]{2,1,0:T(8,128)(2,1)}, bf16[2,384,512]{2,1,0:T(8,128)(2,1)S(1)}, u32[]{:S(2)}, u32[]{:S(2)}) collective-permute-start(bf16[2,384,512]{2,1,0:T(8,128)(2,1)} %get-tuple-element.5), channel_id=1, source_target_pairs={{0,12},{4,0},{8,4},{12,8},{1,13},{5,1},{9,5},{13,9},{2,14},{6,2},{... | collective-permute-start | bytes 2359304 | tf_op jit(solution)/shard_map/ppermute | solution.py:62
  54.2 3.3 %collective-permute-start = (bf16[2,384,512]{2,1,0:T(8,128)(2,1)}, bf16[2,384,512]{2,1,0:T(8,128)(2,1)}, u32[]{:S(2)}, u32[]{:S(2)}) collective-permute-start(bf16[2,384,512]{2,1,0:T(8,128)(2,1)} %get-tuple-element.6), channel_id=1, source_target_pairs={{0,4},{4,8},{8,12},{12,0},{1,5},{5,9},{9,13},{13,1},{2,6},{6,10},{... | collective-permute-start | bytes 2359304 | tf_op jit(solution)/shard_map/ppermute | solution.py:62
  57.5 1.9 %collective-permute-start.1 = (bf16[2,384,512]{2,1,0:T(8,128)(2,1)}, bf16[2,384,512]{2,1,0:T(8,128)(2,1)}, u32[]{:S(2)}, u32[]{:S(2)}) collective-permute-start(bf16[2,384,512]{2,1,0:T(8,128)(2,1)} %get-tuple-element.5), channel_id=1, source_target_pairs={{0,4},{4,8},{8,12},{12,0},{1,5},{5,9},{9,13},{13,1},{2,6},{6,10},{... | collective-permute-start | bytes 2359304 | tf_op jit(solution)/shard_map/ppermute | solution.py:62
  59.4 5.1 %collective-permute-start.3 = (bf16[2,384,512]{2,1,0:T(8,128)(2,1)}, bf16[2,384,512]{2,1,0:T(8,128)(2,1)}, u32[]{:S(2)}, u32[]{:S(2)}) collective-permute-start(bf16[2,384,512]{2,1,0:T(8,128)(2,1)} %get-tuple-element.6), channel_id=1, source_target_pairs={{0,12},{4,0},{8,4},{12,8},{1,13},{5,1},{9,5},{13,9},{2,14},{6,2},{... | collective-permute-start | bytes 2359304 | tf_op jit(solution)/shard_map/ppermute | solution.py:62
  64.6 1.2 collective-permute-done.2.refs_3_
  65.7 3.8 %collective-permute-start.5 = (bf16[2,384,512]{2,1,0:T(8,128)(2,1)S(1)}, bf16[2,384,512]{2,1,0:T(8,128)(2,1)}, u32[]{:S(2)}, u32[]{:S(2)}) collective-permute-start(bf16[2,384,512]{2,1,0:T(8,128)(2,1)S(1)} %collective-permute-done.2.refs_3_), channel_id=1, source_target_pairs={{0,12},{4,0},{8,4},{12,8},{1,13},{5,1},{9,5},{13,9},{2,14},{6,2},{... | collective-permute-start | bytes 2359304 | tf_op jit(solution)/shard_map/ppermute | solution.py:62
  69.5 0.1 collective-permute-done.refs_1_
  69.6 2.0 %collective-permute-start.4 = (bf16[2,384,512]{2,1,0:T(8,128)(2,1)}, bf16[2,384,512]{2,1,0:T(8,128)(2,1)}, u32[]{:S(2)}, u32[]{:S(2)}) collective-permute-start(bf16[2,384,512]{2,1,0:T(8,128)(2,1)} %collective-permute-done.refs_1_), channel_id=1, source_target_pairs={{0,4},{4,8},{8,12},{12,0},{1,5},{5,9},{9,13},{13,1},{2,6},{6,10},{... | collective-permute-start | bytes 2359304 | tf_op jit(solution)/shard_map/ppermute | solution.py:62
  71.7 0.0 copy-done.2
  71.7 0.2 copy.11
  71.9 0.2 fusion.3
  72.2 5.8 %collective-permute-done.1.refs_2_ = bf16[2,384,512]{2,1,0:T(8,128)(2,1)} collective-permute-done((bf16[2,384,512]{2,1,0:T(8,128)(2,1)}, bf16[2,384,512]{2,1,0:T(8,128)(2,1)}, u32[]{:S(2)}, u32[]{:S(2)}) %collective-permute-start.1) | collective-permute-done | bytes 786464 | tf_op jit(solution)/shard_map/ppermute | solution.py:62
  78.1 0.0 collective-permute-done.3.refs_4_
  78.1 4.6 %collective-permute-done.5.refs_6_ = bf16[2,384,512]{2,1,0:T(8,128)(2,1)} collective-permute-done((bf16[2,384,512]{2,1,0:T(8,128)(2,1)S(1)}, bf16[2,384,512]{2,1,0:T(8,128)(2,1)}, u32[]{:S(2)}, u32[]{:S(2)}) %collective-permute-start.5) | collective-permute-done | bytes 786464 | tf_op jit(solution)/shard_map/ppermute | solution.py:62
  82.7 3.8 %collective-permute-done.4.refs_5_ = bf16[2,384,512]{2,1,0:T(8,128)(2,1)} collective-permute-done((bf16[2,384,512]{2,1,0:T(8,128)(2,1)}, bf16[2,384,512]{2,1,0:T(8,128)(2,1)}, u32[]{:S(2)}, u32[]{:S(2)}) %collective-permute-start.4) | collective-permute-done | bytes 786464 | tf_op jit(solution)/shard_map/ppermute | solution.py:62
  86.5 7.5 %all-gather.3.cloned.1.call-done = bf16[16896,256]{1,0:T(8,128)(2,1)} async-done(((bf16[528,256]{1,0:T(8,128)(2,1)}), bf16[16896,256]{1,0:T(8,128)(2,1)}) %all-gather.3.cloned.1.call-update) | async-done | bytes 8650768 | tf_op jit(solution)/shard_map/all_gather | solution.py:248
  94.0 9.1 %shard_map.85 = bf16[384,5120]{1,0:T(8,128)(2,1)S(1)} custom-call(bf16[4,4,2,528,256]{4,3,2,1,0:T(8,128)(2,1)} %bitcast.14, bf16[4,384,512]{2,1,0:T(8,128)(2,1)S(1)} %all_to_all.21.refs_0_, bf16[2,384,512]{2,1,0:T(8,128)(2,1)} %collective-permute-done.refs_1_, bf16[2,384,512]{2,1,0:T(8,128)(2,1)} %collective-permute-done.1.refs_2_, ...), custom_call_target="tpu_custom_call" | custom-call | flops 3221225472 | bytes 16777216 | tf_op jit(solution)/shard_map/pallas_call | solution.py:264
  103.1 28.9 %all_to_all.22.recv_ref = bf16[4,96,5120]{2,1,0:T(8,128)(2,1)S(1)} all-to-all(bf16[4,96,5120]{2,1,0:T(8,128)(2,1)S(1)} %bitcast.9), channel_id=1, replica_groups={{0,1,2,3},{4,5,6,7},{8,9,10,11},{12,13,14,15},{16,20,24,28},{17,21,25,2..., dimensions={0} | all-to-all | bytes 7864320 | tf_op jit(solution)/shard_map/all_to_all | solution.py:53
  131.9 0.5 shard_map.86
  132.4 14.6 %all_to_all.23.recv_ref = bf16[4,24,5120]{2,1,0:T(8,128)(2,1)S(1)} all-to-all(bf16[4,24,5120]{2,1,0:T(8,128)(2,1)S(1)} %bitcast.10), channel_id=1, replica_groups={{0,4,8,12},{1,5,9,13},{2,6,10,14},{3,7,11,15},{16,17,18,19},{20,21,22,2..., dimensions={0} | all-to-all | bytes 1966080 | tf_op jit(solution)/shard_map/all_to_all | solution.py:53
  147.0 1.9 %shard_map.87 = bf16[24,5120]{1,0:T(8,128)(2,1)} custom-call(bf16[4,24,5120]{2,1,0:T(8,128)(2,1)S(1)} %all_to_all.23.recv_ref, bf16[24,5120]{1,0:T(8,128)(2,1)} %patches_hbm.1, f32[1280]{0:T(1024)} %gain_hbm.1), custom_call_target="tpu_custom_call" | custom-call | tf_op jit(solution)/shard_map/pallas_call | solution.py:284
  (3 shorter events, 0.0 us)
Async XLA Ops:
  6.5 87.4 %all-gather.3.cloned.1.call-start = ((), (), s32[]{:S(2)}) async-start(), calls=%async_computation.4 | async-start | bytes 8921088 | tf_op jit(solution)/shard_map/all_gather | solution.py:248
  9.0 1.2 copy-start
  10.2 0.7 copy-start.1
  32.7 39.0 %copy-start.2 = (bf16[384,320]{0,1:T(8,128)(2,1)S(1)}, bf16[384,320]{0,1:T(8,128)(2,1)}, u32[]{:S(2)}) copy-start(bf16[384,320]{0,1:T(8,128)(2,1)} %param.11) | copy-start | bytes 737284
  51.7 14.1 %collective-permute-start.2 = (bf16[2,384,512]{2,1,0:T(8,128)(2,1)}, bf16[2,384,512]{2,1,0:T(8,128)(2,1)S(1)}, u32[]{:S(2)}, u32[]{:S(2)}) collective-permute-start(bf16[2,384,512]{2,1,0:T(8,128)(2,1)} %get-tuple-element.5), channel_id=1, source_target_pairs={{0,12},{4,0},{8,4},{12,8},{1,13},{5,1},{9,5},{13,9},{2,14},{6,2},{... | collective-permute-start | bytes 2359304 | tf_op jit(solution)/shard_map/ppermute | solution.py:62
  54.2 15.4 %collective-permute-start = (bf16[2,384,512]{2,1,0:T(8,128)(2,1)}, bf16[2,384,512]{2,1,0:T(8,128)(2,1)}, u32[]{:S(2)}, u32[]{:S(2)}) collective-permute-start(bf16[2,384,512]{2,1,0:T(8,128)(2,1)} %get-tuple-element.6), channel_id=1, source_target_pairs={{0,4},{4,8},{8,12},{12,0},{1,5},{5,9},{9,13},{13,1},{2,6},{6,10},{... | collective-permute-start | bytes 2359304 | tf_op jit(solution)/shard_map/ppermute | solution.py:62
  57.5 20.6 %collective-permute-start.1 = (bf16[2,384,512]{2,1,0:T(8,128)(2,1)}, bf16[2,384,512]{2,1,0:T(8,128)(2,1)}, u32[]{:S(2)}, u32[]{:S(2)}) collective-permute-start(bf16[2,384,512]{2,1,0:T(8,128)(2,1)} %get-tuple-element.5), channel_id=1, source_target_pairs={{0,4},{4,8},{8,12},{12,0},{1,5},{5,9},{9,13},{13,1},{2,6},{6,10},{... | collective-permute-start | bytes 2359304 | tf_op jit(solution)/shard_map/ppermute | solution.py:62
  59.4 18.6 %collective-permute-start.3 = (bf16[2,384,512]{2,1,0:T(8,128)(2,1)}, bf16[2,384,512]{2,1,0:T(8,128)(2,1)}, u32[]{:S(2)}, u32[]{:S(2)}) collective-permute-start(bf16[2,384,512]{2,1,0:T(8,128)(2,1)} %get-tuple-element.6), channel_id=1, source_target_pairs={{0,12},{4,0},{8,4},{12,8},{1,13},{5,1},{9,5},{13,9},{2,14},{6,2},{... | collective-permute-start | bytes 2359304 | tf_op jit(solution)/shard_map/ppermute | solution.py:62
  65.7 17.0 %collective-permute-start.5 = (bf16[2,384,512]{2,1,0:T(8,128)(2,1)S(1)}, bf16[2,384,512]{2,1,0:T(8,128)(2,1)}, u32[]{:S(2)}, u32[]{:S(2)}) collective-permute-start(bf16[2,384,512]{2,1,0:T(8,128)(2,1)S(1)} %collective-permute-done.2.refs_3_), channel_id=1, source_target_pairs={{0,12},{4,0},{8,4},{12,8},{1,13},{5,1},{9,5},{13,9},{2,14},{6,2},{... | collective-permute-start | bytes 2359304 | tf_op jit(solution)/shard_map/ppermute | solution.py:62
  69.6 16.9 %collective-permute-start.4 = (bf16[2,384,512]{2,1,0:T(8,128)(2,1)}, bf16[2,384,512]{2,1,0:T(8,128)(2,1)}, u32[]{:S(2)}, u32[]{:S(2)}) collective-permute-start(bf16[2,384,512]{2,1,0:T(8,128)(2,1)} %collective-permute-done.refs_1_), channel_id=1, source_target_pairs={{0,4},{4,8},{8,12},{12,0},{1,5},{5,9},{9,13},{13,1},{2,6},{6,10},{... | collective-permute-start | bytes 2359304 | tf_op jit(solution)/shard_map/ppermute | solution.py:62
Sparse Core Ops, SparseCore 0:
  9.5 84.4 all-gather.2

commit v12 on v11

--- a/solution.py
+++ b/solution.py
@@ -139,17 +139,16 @@
     copies, late = [], []
     for n, (offset, parts) in enumerate(GATHERED):
         other = lax.rem(second + offset, SIDE)
-        by_row = pltpu.make_async_copy(w_ref.at[other, :, :, 0:HID_OWN], w2.at[n], sems2.at[n, 0])
-        by_col = pltpu.make_async_copy(w_ref.at[:, other, :, 0:HID_OWN], w2.at[n], sems2.at[n, 0])
-        pl.when(even)(by_row.start)
-        pl.when(jnp.logical_not(even))(by_col.start)
-        group = [by_row]
+        count = SIDE // len(parts)
         for h, (operand, k) in enumerate(parts):
-            count = SIDE // len(parts)
-            copy = pltpu.make_async_copy(sums[operand], s.at[n, k : k + count], sems2.at[n, h + 1])
+            span = slice(k, k + count)
+            by_row = pltpu.make_async_copy(w_ref.at[other, span, :, 0:HID_OWN], w2.at[n, span], sems2.at[n, h])
+            by_col = pltpu.make_async_copy(w_ref.at[span, other, :, 0:HID_OWN], w2.at[n, span], sems2.at[n, h])
+            pl.when(even)(by_row.start)
+            pl.when(jnp.logical_not(even))(by_col.start)
+            copy = pltpu.make_async_copy(sums[operand], s.at[n, span], sems2.at[n, h + 2])
             copy.start()
-            group.append(copy)
-        copies.append(group)
+            copies.append((n, span, by_row, copy))
     for q in range(SIDE):
         pair = [
             pltpu.make_async_copy(w_ref.at[q, :, :, HID_OWN:base], w1.at[q], sems1.at[q, 0]),
@@ -159,10 +158,10 @@
             copy.start()
         late.append(pair)
     hidden = None
-    for n in range(SIDE):
-        for copy in copies[n]:
+    for n, span, *group in copies:
+        for copy in group:
             copy.wait()
-        for k in range(SIDE):
+        for k in range(span.start, span.stop):
             block = s[n, k]
             part = dot_t(w2[n, k, 0], block[:, :W2_COLS]) + dot_t(w2[n, k, 1], block[:, W2_COLS:])
             hidden = part if hidden is None else hidden + part
@@ -178,20 +177,16 @@
         out_ref[:, width * q : width * (q + 1)] = part.astype(BF16)
 
 
-def add_kernel(recv_ref, out_ref):
+def add_kernel(recv_ref, patches_ref, gain_ref, out_ref, near_patches_ref, near_gain_ref):
     total = recv_ref[0].astype(F32)
     for k in range(1, SIDE):
         total = total + recv_ref[k].astype(F32)
     out_ref[...] = total.astype(BF16)
-
-
-def norm_kernel(recv_ref, patches_hbm, gain_hbm, out_ref, patches_ref, gain_ref, sems):
-    copies = [
-        pltpu.make_async_copy(patches_hbm, patches_ref, sems.at[0]),
-        pltpu.make_async_copy(gain_hbm, gain_ref, sems.at[1]),
-    ]
-    for copy in copies:
-        copy.start()
+    near_patches_ref[...] = patches_ref[...]
+    near_gain_ref[...] = gain_ref[...]
+
+
+def norm_kernel(recv_ref, patches_ref, gain_ref, out_ref):
     sums = []
     for m in range(MERGE):
         cols = slice(m * VIT, (m + 1) * VIT)
@@ -199,8 +194,6 @@
         for k in range(1, SIDE):
             upstream = upstream + recv_ref[k, :, cols].astype(F32)
         sums.append(upstream)
-    for copy in copies:
-        copy.wait()
     gain = gain_ref[...][None]
     for m in range(MERGE):
         cols = slice(m * VIT, (m + 1) * VIT)
@@ -271,7 +264,7 @@
             pltpu.VMEM((SIDE, SIDE, 2, HID_OWN, W2_COLS), BF16),
             pltpu.VMEM((SIDE, SIDE, 2, IN_OWN, 256), BF16),
             pltpu.VMEM((SIDE, SIDE, 2, TAIL, 256), BF16),
-            pltpu.SemaphoreType.DMA((SIDE, 3)),
+            pltpu.SemaphoreType.DMA((SIDE, 4)),
             pltpu.SemaphoreType.DMA((SIDE, 2)),
         ],
         cost_estimate=pl.CostEstimate(flops=3 << 30, bytes_accessed=16 << 20, transcendentals=0),
@@ -279,18 +272,15 @@
     )(pinned(weights), line, a1, a2, b1, b2, a3, b3, slope)
 
     halfway = exchange(partial.reshape(SIDE, SIDE * OWN, HID), 0)
-    halfway = call(add_kernel, (SIDE * OWN, HID), [VMEM], moved=5 << 20, fast=True)(halfway)
+    halfway, near_patches, near_gain = pl.pallas_call(
+        add_kernel,
+        out_shape=[pltpu.VMEM((SIDE * OWN, HID), BF16), pltpu.VMEM((OWN, HID), BF16), pltpu.VMEM((VIT,), F32)],
+        in_specs=[VMEM] * 3,
+        out_specs=[VMEM] * 3,
+        compiler_params=pltpu.CompilerParams(vmem_limit_bytes=16 << 20),
+    )(halfway, patches, ln_gain)
     last = exchange(halfway.reshape(SIDE, OWN, HID), 1)
-    return call(
-        norm_kernel,
-        (OWN, HID),
-        [VMEM, ANY, ANY],
-        scratch=[
-            pltpu.VMEM((OWN, HID), BF16),
-            pltpu.VMEM((VIT,), F32),
-            pltpu.SemaphoreType.DMA((2,)),
-        ],
-    )(last, pinned(patches), pinned(ln_gain))
+    return call(norm_kernel, (OWN, HID), [VMEM] * 3)(last, near_patches, near_gain)
 
 
 def solution(mesh):

time: 157 us -> 156 us (level)
  no operation moved by 1% of the time
where the time goes in v12:
time: 156 us; the launch traced here: 155 us
  blocking collectives  82.4 us (53%)
  waiting for transfers between devices  23.1 us (15%)
  starting transfers between devices  18.7 us (12%)
  between operations  14.2 us (9%)
  Pallas kernels  12.8 us (8%)
  local copies, waits for them, and re-layouts  3.34 us (2%)
    all_to_all x3, blocking collectives, exchange(): lax.all_to_all(blocks, AXES, split_axis=0, concat_axis=0, axis_index_grou...  60.7 us
    all_to_all x1, blocking collectives, per_device(): lax.all_to_all(outgoing, 'rollout', split_axis=0, concat_axis=0, tiled=True)  21.7 us
    ppermute x6, starting transfers between devices, shift(): return lax.ppermute(value, AXES, pairs)  18.7 us
    ppermute x6, waiting for transfers between devices, shift(): return lax.ppermute(value, AXES, pairs)  15.5 us
    pallas_call x1, Pallas kernels, per_device(): pl.pallas_call(mlp_kernel, out_shape=pltpu.VMEM((ROWS, HID), BF16), in_sp...  8.78 us
    all_gather x1, waiting for transfers between devices, per_device(): weights = lax.all_gather(weights, 'prompt', axis=0, tiled=False)  7.5 us
  transfers between devices with their start and end apart: 7, of which 6 were waited for; matrix products, arithmetic and copies ran while one was open for 1% of the time, Pallas kernels for 0%

profile of v12, /device:TPU:6, one launch (start us, length us, event | category | flops | bytes accessed | tf_op | source)
XLA Modules:
  0.0 154.8 jit_solution(2726496149522107750)
XLA Ops:
  6.5 1.8 %shard_map.82 = bf16[528,256]{1,0:T(8,128)(2,1)} custom-call(bf16[320,256]{1,0:T(8,128)(2,1)} %w2_ref.1, bf16[160,320]{1,0:T(8,128)(2,1)} %w1_ref.1), custom_call_target="tpu_custom_call" | custom-call | tf_op jit(solution)/shard_map/pallas_call | solution.py:230
  8.3 0.0 all-gather.3.cloned.1.call-update
  9.0 0.0 copy-start
  9.0 1.2 copy-done
  10.2 0.7 copy-done.3
  10.9 0.1 shard_map.83
  10.9 21.7 %all_to_all.20.recv_ref = bf16[16,64,512]{2,1,0:T(8,128)(2,1)S(1)} all-to-all(bf16[16,64,512]{2,1,0:T(8,128)(2,1)S(1)} %shard_map.83), channel_id=1, replica_groups=mesh['prompt'=32,'rollout'=16] {'rollout'}, dimensions={0} | all-to-all | bytes 2097152 | tf_op jit(solution)/shard_map/all_to_all | solution.py:246
  32.7 0.6 shard_map.84
  33.3 17.1 %all_to_all.21.refs_0_ = bf16[4,384,512]{2,1,0:T(8,128)(2,1)S(1)} all-to-all(bf16[4,384,512]{2,1,0:T(8,128)(2,1)S(1)} %shard_map.84), channel_id=1, replica_groups={{0,1,2,3},{4,5,6,7},{8,9,10,11},{12,13,14,15},{16,20,24,28},{17,21,25,2..., dimensions={0} | all-to-all | bytes 3145728 | tf_op jit(solution)/shard_map/all_to_all | solution.py:53
  50.4 1.3 fusion.6
  51.7 2.6 %collective-permute-start.2 = (bf16[2,384,512]{2,1,0:T(8,128)(2,1)}, bf16[2,384,512]{2,1,0:T(8,128)(2,1)S(1)}, u32[]{:S(2)}, u32[]{:S(2)}) collective-permute-start(bf16[2,384,512]{2,1,0:T(8,128)(2,1)} %get-tuple-element.11), channel_id=1, source_target_pairs={{0,12},{4,0},{8,4},{12,8},{1,13},{5,1},{9,5},{13,9},{2,14},{6,2},{... | collective-permute-start | bytes 2359304 | tf_op jit(solution)/shard_map/ppermute | solution.py:62
  54.2 3.3 %collective-permute-start = (bf16[2,384,512]{2,1,0:T(8,128)(2,1)}, bf16[2,384,512]{2,1,0:T(8,128)(2,1)}, u32[]{:S(2)}, u32[]{:S(2)}) collective-permute-start(bf16[2,384,512]{2,1,0:T(8,128)(2,1)} %get-tuple-element.12), channel_id=1, source_target_pairs={{0,4},{4,8},{8,12},{12,0},{1,5},{5,9},{9,13},{13,1},{2,6},{6,10},{... | collective-permute-start | bytes 2359304 | tf_op jit(solution)/shard_map/ppermute | solution.py:62
  57.5 1.9 %collective-permute-start.1 = (bf16[2,384,512]{2,1,0:T(8,128)(2,1)}, bf16[2,384,512]{2,1,0:T(8,128)(2,1)}, u32[]{:S(2)}, u32[]{:S(2)}) collective-permute-start(bf16[2,384,512]{2,1,0:T(8,128)(2,1)} %get-tuple-element.11), channel_id=1, source_target_pairs={{0,4},{4,8},{8,12},{12,0},{1,5},{5,9},{9,13},{13,1},{2,6},{6,10},{... | collective-permute-start | bytes 2359304 | tf_op jit(solution)/shard_map/ppermute | solution.py:62
  59.4 5.1 %collective-permute-start.3 = (bf16[2,384,512]{2,1,0:T(8,128)(2,1)}, bf16[2,384,512]{2,1,0:T(8,128)(2,1)}, u32[]{:S(2)}, u32[]{:S(2)}) collective-permute-start(bf16[2,384,512]{2,1,0:T(8,128)(2,1)} %get-tuple-element.12), channel_id=1, source_target_pairs={{0,12},{4,0},{8,4},{12,8},{1,13},{5,1},{9,5},{13,9},{2,14},{6,2},{... | collective-permute-start | bytes 2359304 | tf_op jit(solution)/shard_map/ppermute | solution.py:62
  64.6 1.2 collective-permute-done.2.refs_3_
  65.7 3.8 %collective-permute-start.5 = (bf16[2,384,512]{2,1,0:T(8,128)(2,1)S(1)}, bf16[2,384,512]{2,1,0:T(8,128)(2,1)}, u32[]{:S(2)}, u32[]{:S(2)}) collective-permute-start(bf16[2,384,512]{2,1,0:T(8,128)(2,1)S(1)} %collective-permute-done.2.refs_3_), channel_id=1, source_target_pairs={{0,12},{4,0},{8,4},{12,8},{1,13},{5,1},{9,5},{13,9},{2,14},{6,2},{... | collective-permute-start | bytes 2359304 | tf_op jit(solution)/shard_map/ppermute | solution.py:62
  69.5 0.1 collective-permute-done.refs_1_
  69.6 2.0 %collective-permute-start.4 = (bf16[2,384,512]{2,1,0:T(8,128)(2,1)}, bf16[2,384,512]{2,1,0:T(8,128)(2,1)}, u32[]{:S(2)}, u32[]{:S(2)}) collective-permute-start(bf16[2,384,512]{2,1,0:T(8,128)(2,1)} %collective-permute-done.refs_1_), channel_id=1, source_target_pairs={{0,4},{4,8},{8,12},{12,0},{1,5},{5,9},{9,13},{13,1},{2,6},{6,10},{... | collective-permute-start | bytes 2359304 | tf_op jit(solution)/shard_map/ppermute | solution.py:62
  71.7 0.2 copy.11
  71.9 0.2 fusion.3
  72.2 5.8 %collective-permute-done.1.refs_2_ = bf16[2,384,512]{2,1,0:T(8,128)(2,1)} collective-permute-done((bf16[2,384,512]{2,1,0:T(8,128)(2,1)}, bf16[2,384,512]{2,1,0:T(8,128)(2,1)}, u32[]{:S(2)}, u32[]{:S(2)}) %collective-permute-start.1) | collective-permute-done | bytes 786464 | tf_op jit(solution)/shard_map/ppermute | solution.py:62
  78.1 0.0 collective-permute-done.3.refs_4_
  78.1 4.6 %collective-permute-done.5.refs_6_ = bf16[2,384,512]{2,1,0:T(8,128)(2,1)} collective-permute-done((bf16[2,384,512]{2,1,0:T(8,128)(2,1)S(1)}, bf16[2,384,512]{2,1,0:T(8,128)(2,1)}, u32[]{:S(2)}, u32[]{:S(2)}) %collective-permute-start.5) | collective-permute-done | bytes 786464 | tf_op jit(solution)/shard_map/ppermute | solution.py:62
  82.7 3.8 %collective-permute-done.4.refs_5_ = bf16[2,384,512]{2,1,0:T(8,128)(2,1)} collective-permute-done((bf16[2,384,512]{2,1,0:T(8,128)(2,1)}, bf16[2,384,512]{2,1,0:T(8,128)(2,1)}, u32[]{:S(2)}, u32[]{:S(2)}) %collective-permute-start.4) | collective-permute-done | bytes 786464 | tf_op jit(solution)/shard_map/ppermute | solution.py:62
  86.5 7.5 %all-gather.3.cloned.1.call-done = bf16[16896,256]{1,0:T(8,128)(2,1)} async-done(((bf16[528,256]{1,0:T(8,128)(2,1)}), bf16[16896,256]{1,0:T(8,128)(2,1)}) %all-gather.3.cloned.1.call-update) | async-done | bytes 8650768 | tf_op jit(solution)/shard_map/all_gather | solution.py:241
  94.0 8.8 %shard_map.85 = bf16[384,5120]{1,0:T(8,128)(2,1)S(1)} custom-call(bf16[4,4,2,528,256]{4,3,2,1,0:T(8,128)(2,1)} %bitcast.14, bf16[4,384,512]{2,1,0:T(8,128)(2,1)S(1)} %all_to_all.21.refs_0_, bf16[2,384,512]{2,1,0:T(8,128)(2,1)} %collective-permute-done.refs_1_, bf16[2,384,512]{2,1,0:T(8,128)(2,1)} %collective-permute-done.1.refs_2_, ...), custom_call_target="tpu_custom_call" | custom-call | flops 3221225472 | bytes 16777216 | tf_op jit(solution)/shard_map/pallas_call | solution.py:257
  102.8 0.0 copy-start.1
  102.8 0.0 copy-start.2
  102.8 29.0 %all_to_all.22.recv_ref = bf16[4,96,5120]{2,1,0:T(8,128)(2,1)S(1)} all-to-all(bf16[4,96,5120]{2,1,0:T(8,128)(2,1)S(1)} %bitcast.9), channel_id=1, replica_groups={{0,1,2,3},{4,5,6,7},{8,9,10,11},{12,13,14,15},{16,20,24,28},{17,21,25,2..., dimensions={0} | all-to-all | bytes 7864320 | tf_op jit(solution)/shard_map/all_to_all | solution.py:53
  131.8 0.5 shard_map.86
  132.3 14.6 %all_to_all.23.recv_ref = bf16[4,24,5120]{2,1,0:T(8,128)(2,1)S(1)} all-to-all(bf16[4,24,5120]{2,1,0:T(8,128)(2,1)S(1)} %bitcast.11), channel_id=1, replica_groups={{0,4,8,12},{1,5,9,13},{2,6,10,14},{3,7,11,15},{16,17,18,19},{20,21,22,2..., dimensions={0} | all-to-all | bytes 1966080 | tf_op jit(solution)/shard_map/all_to_all | solution.py:53
  146.9 1.0 shard_map.87
  (7 shorter events, 0.1 us)
Async XLA Ops:
  6.5 87.5 %all-gather.3.cloned.1.call-start = ((), (), s32[]{:S(2)}) async-start(), calls=%async_computation.4 | async-start | bytes 8921088 | tf_op jit(solution)/shard_map/all_gather | solution.py:241
  9.0 1.2 copy-start
  10.2 0.7 copy-start.3
  32.7 39.0 %copy-start.4 = (bf16[384,320]{0,1:T(8,128)(2,1)S(1)}, bf16[384,320]{0,1:T(8,128)(2,1)}, u32[]{:S(2)}) copy-start(bf16[384,320]{0,1:T(8,128)(2,1)} %param.11) | copy-start | bytes 737284
  51.7 14.1 %collective-permute-start.2 = (bf16[2,384,512]{2,1,0:T(8,128)(2,1)}, bf16[2,384,512]{2,1,0:T(8,128)(2,1)S(1)}, u32[]{:S(2)}, u32[]{:S(2)}) collective-permute-start(bf16[2,384,512]{2,1,0:T(8,128)(2,1)} %get-tuple-element.11), channel_id=1, source_target_pairs={{0,12},{4,0},{8,4},{12,8},{1,13},{5,1},{9,5},{13,9},{2,14},{6,2},{... | collective-permute-start | bytes 2359304 | tf_op jit(solution)/shard_map/ppermute | solution.py:62
  54.2 15.4 %collective-permute-start = (bf16[2,384,512]{2,1,0:T(8,128)(2,1)}, bf16[2,384,512]{2,1,0:T(8,128)(2,1)}, u32[]{:S(2)}, u32[]{:S(2)}) collective-permute-start(bf16[2,384,512]{2,1,0:T(8,128)(2,1)} %get-tuple-element.12), channel_id=1, source_target_pairs={{0,4},{4,8},{8,12},{12,0},{1,5},{5,9},{9,13},{13,1},{2,6},{6,10},{... | collective-permute-start | bytes 2359304 | tf_op jit(solution)/shard_map/ppermute | solution.py:62
  57.5 20.6 %collective-permute-start.1 = (bf16[2,384,512]{2,1,0:T(8,128)(2,1)}, bf16[2,384,512]{2,1,0:T(8,128)(2,1)}, u32[]{:S(2)}, u32[]{:S(2)}) collective-permute-start(bf16[2,384,512]{2,1,0:T(8,128)(2,1)} %get-tuple-element.11), channel_id=1, source_target_pairs={{0,4},{4,8},{8,12},{12,0},{1,5},{5,9},{9,13},{13,1},{2,6},{6,10},{... | collective-permute-start | bytes 2359304 | tf_op jit(solution)/shard_map/ppermute | solution.py:62
  59.4 18.6 %collective-permute-start.3 = (bf16[2,384,512]{2,1,0:T(8,128)(2,1)}, bf16[2,384,512]{2,1,0:T(8,128)(2,1)}, u32[]{:S(2)}, u32[]{:S(2)}) collective-permute-start(bf16[2,384,512]{2,1,0:T(8,128)(2,1)} %get-tuple-element.12), channel_id=1, source_target_pairs={{0,12},{4,0},{8,4},{12,8},{1,13},{5,1},{9,5},{13,9},{2,14},{6,2},{... | collective-permute-start | bytes 2359304 | tf_op jit(solution)/shard_map/ppermute | solution.py:62
  65.7 17.0 %collective-permute-start.5 = (bf16[2,384,512]{2,1,0:T(8,128)(2,1)S(1)}, bf16[2,384,512]{2,1,0:T(8,128)(2,1)}, u32[]{:S(2)}, u32[]{:S(2)}) collective-permute-start(bf16[2,384,512]{2,1,0:T(8,128)(2,1)S(1)} %collective-permute-done.2.refs_3_), channel_id=1, source_target_pairs={{0,12},{4,0},{8,4},{12,8},{1,13},{5,1},{9,5},{13,9},{2,14},{6,2},{... | collective-permute-start | bytes 2359304 | tf_op jit(solution)/shard_map/ppermute | solution.py:62
  69.6 16.9 %collective-permute-start.4 = (bf16[2,384,512]{2,1,0:T(8,128)(2,1)}, bf16[2,384,512]{2,1,0:T(8,128)(2,1)}, u32[]{:S(2)}, u32[]{:S(2)}) collective-permute-start(bf16[2,384,512]{2,1,0:T(8,128)(2,1)} %collective-permute-done.refs_1_), channel_id=1, source_target_pairs={{0,4},{4,8},{8,12},{12,0},{1,5},{5,9},{9,13},{13,1},{2,6},{6,10},{... | collective-permute-start | bytes 2359304 | tf_op jit(solution)/shard_map/ppermute | solution.py:62
  102.8 29.0 %copy-start.1 = (bf16[24,5120]{1,0:T(8,128)(2,1)S(1)}, bf16[24,5120]{1,0:T(8,128)(2,1)}, u32[]{:S(2)}) copy-start(bf16[24,5120]{1,0:T(8,128)(2,1)} %patches_ref.1) | copy-start | bytes 737284
  102.8 29.0 %copy-start.2 = (f32[1280]{0:T(1024)S(1)}, f32[1280]{0:T(1024)}, u32[]{:S(2)}) copy-start(f32[1280]{0:T(1024)} %gain_ref.1) | copy-start | bytes 15364
Sparse Core Ops, SparseCore 0:
  9.5 84.4 all-gather.2

commit v13 on v12

--- a/solution.py
+++ b/solution.py
@@ -43,7 +43,7 @@
     groups = []
     for prompt in range(PROMPTS):
         for other in range(SIDE):
-            along_x = (prompt % 2 == 0) == (phase == 0)
+            along_x = (prompt % 2 == 1) == (phase == 0)
             line = [(other * SIDE + i) if along_x else (i * SIDE + other) for i in range(SIDE)]
             groups.append([prompt * ROLLOUTS + r for r in line])
     return groups
@@ -64,8 +64,8 @@
 
 def place_in_plane():
     rollout = lax.axis_index("rollout")
-    even = lax.axis_index("prompt") % 2 == 0
-    return even, jnp.where(even, rollout // SIDE, rollout % SIDE)
+    x_first = lax.axis_index("prompt") % 2 == 1
+    return x_first, jnp.where(x_first, rollout // SIDE, rollout % SIDE)
 
 
 def weights_kernel(w2_ref, w1_ref, out_ref, block, w1, sems):
@@ -88,11 +88,11 @@
 
 
 def pack_kernel(count_ref, ids_ref, grads_ref, out_ref, meta):
-    even, _ = place_in_plane()
+    x_first, _ = place_in_plane()
     ids = ids_ref[...]
     owner = (ids * 2731) >> 16
     turned = (owner & 3) * SIDE + (owner >> 2)
-    place = jnp.where(even, turned, owner) * OWN + ids - owner * OWN + 1
+    place = jnp.where(x_first, turned, owner) * OWN + ids - owner * OWN + 1
     live = lax.broadcasted_iota(jnp.int32, (1, SLOTS), 1) < count_ref[0, 0]
     place = jnp.where(live, place, 0)
     meta[...] = jnp.zeros((8, COLS), F32)
@@ -134,7 +134,7 @@
 
 def mlp_kernel(w_ref, *refs):
     sums, (slope_ref, out_ref, s, w2, w1, w1_tail, sems2, sems1) = refs[:7], refs[7:]
-    even, second = place_in_plane()
+    x_first, second = place_in_plane()
     base = HID_OWN + IN_OWN
     copies, late = [], []
     for n, (offset, parts) in enumerate(GATHERED):
@@ -144,8 +144,8 @@
             span = slice(k, k + count)
             by_row = pltpu.make_async_copy(w_ref.at[other, span, :, 0:HID_OWN], w2.at[n, span], sems2.at[n, h])
             by_col = pltpu.make_async_copy(w_ref.at[span, other, :, 0:HID_OWN], w2.at[n, span], sems2.at[n, h])
-            pl.when(even)(by_row.start)
-            pl.when(jnp.logical_not(even))(by_col.start)
+            pl.when(x_first)(by_row.start)
+            pl.when(jnp.logical_not(x_first))(by_col.start)
             copy = pltpu.make_async_copy(sums[operand], s.at[n, span], sems2.at[n, h + 2])
             copy.start()
             copies.append((n, span, by_row, copy))
@@ -250,9 +250,9 @@
     a2, b2 = shift(line[2:], 1, 1), shift(line[:2], 1, -1)
     a3, b3 = shift(a1, 1, 1), shift(b1, 1, -1)
 
-    even = lax.axis_index("prompt") % 2 == 0
+    x_first = lax.axis_index("prompt") % 2 == 1
     slope = gelu_slope(pre_act.astype(F32)).reshape(SIDE, SIDE, OWN, HID_OWN)
-    slope = jnp.where(even, slope.transpose(1, 0, 2, 3), slope).reshape(ROWS, HID_OWN)
+    slope = jnp.where(x_first, slope.transpose(1, 0, 2, 3), slope).reshape(ROWS, HID_OWN)
     weights = weights.reshape(SIDE, SIDE, 2, W_ROWS, 256)
     partial = pl.pallas_call(
         mlp_kernel,

time: 156 us -> 156 us (level)
    ppermute x6, waiting for transfers between devices: 15.5 us -> 13.7 us  [shift(): return lax.ppermute(value, AXES, pairs)]
  transfers between devices with their start and end apart: 7 -> 7, of which waited for: 6 -> 5; matrix products, arithmetic and copies ran while one was open for 1% -> 1% of each run, Pallas kernels for 0% -> 0%
where the time goes in v13:
time: 156 us; the launch traced here: 155 us
  blocking collectives  81.8 us (52%)
  waiting for transfers between devices  22.3 us (14%)
  starting transfers between devices  20 us (13%)
  between operations  14.2 us (9%)
  Pallas kernels  12.8 us (8%)
  local copies, waits for them, and re-layouts  3.34 us (2%)
    all_to_all x3, blocking collectives, exchange(): lax.all_to_all(blocks, AXES, split_axis=0, concat_axis=0, axis_index_grou...  60.1 us
    all_to_all x1, blocking collectives, per_device(): lax.all_to_all(outgoing, 'rollout', split_axis=0, concat_axis=0, tiled=True)  21.7 us
    ppermute x6, starting transfers between devices, shift(): return lax.ppermute(value, AXES, pairs)  20 us
    ppermute x6, waiting for transfers between devices, shift(): return lax.ppermute(value, AXES, pairs)  13.7 us
    pallas_call x1, Pallas kernels, per_device(): pl.pallas_call(mlp_kernel, out_shape=pltpu.VMEM((ROWS, HID), BF16), in_sp...  8.78 us
    all_gather x1, waiting for transfers between devices, per_device(): weights = lax.all_gather(weights, 'prompt', axis=0, tiled=False)  8.64 us
  transfers between devices with their start and end apart: 7, of which 5 were waited for; matrix products, arithmetic and copies ran while one was open for 1% of the time, Pallas kernels for 0%

profile of v13, /device:TPU:6, one launch (start us, length us, event | category | flops | bytes accessed | tf_op | source)
XLA Modules:
  0.0 154.8 jit_solution(5120840075298385288)
XLA Ops:
  6.5 1.8 %shard_map.82 = bf16[528,256]{1,0:T(8,128)(2,1)} custom-call(bf16[320,256]{1,0:T(8,128)(2,1)} %w2_ref.1, bf16[160,320]{1,0:T(8,128)(2,1)} %w1_ref.1), custom_call_target="tpu_custom_call" | custom-call | tf_op jit(solution)/shard_map/pallas_call | solution.py:230
  8.3 0.0 all-gather.3.cloned.1.call-update
  9.0 0.0 copy-start
  9.0 1.2 copy-done
  10.2 0.7 copy-done.3
  10.9 0.1 shard_map.83
  10.9 21.7 %all_to_all.20.recv_ref = bf16[16,64,512]{2,1,0:T(8,128)(2,1)S(1)} all-to-all(bf16[16,64,512]{2,1,0:T(8,128)(2,1)S(1)} %shard_map.83), channel_id=1, replica_groups=mesh['prompt'=32,'rollout'=16] {'rollout'}, dimensions={0} | all-to-all | bytes 2097152 | tf_op jit(solution)/shard_map/all_to_all | solution.py:246
  32.7 0.6 shard_map.84
  33.3 16.5 %all_to_all.21.refs_0_ = bf16[4,384,512]{2,1,0:T(8,128)(2,1)S(1)} all-to-all(bf16[4,384,512]{2,1,0:T(8,128)(2,1)S(1)} %shard_map.84), channel_id=1, replica_groups={{0,4,8,12},{1,5,9,13},{2,6,10,14},{3,7,11,15},{16,17,18,19},{20,21,22,2..., dimensions={0} | all-to-all | bytes 3145728 | tf_op jit(solution)/shard_map/all_to_all | solution.py:53
  49.8 1.3 fusion.6
  51.1 2.7 %collective-permute-start.2 = (bf16[2,384,512]{2,1,0:T(8,128)(2,1)}, bf16[2,384,512]{2,1,0:T(8,128)(2,1)S(1)}, u32[]{:S(2)}, u32[]{:S(2)}) collective-permute-start(bf16[2,384,512]{2,1,0:T(8,128)(2,1)} %get-tuple-element.11), channel_id=1, source_target_pairs={{0,3},{1,0},{2,1},{3,2},{4,7},{5,4},{6,5},{7,6},{8,11},{9,8},{10,9... | collective-permute-start | bytes 2359304 | tf_op jit(solution)/shard_map/ppermute | solution.py:62
  53.7 4.4 %collective-permute-start = (bf16[2,384,512]{2,1,0:T(8,128)(2,1)}, bf16[2,384,512]{2,1,0:T(8,128)(2,1)}, u32[]{:S(2)}, u32[]{:S(2)}) collective-permute-start(bf16[2,384,512]{2,1,0:T(8,128)(2,1)} %get-tuple-element.12), channel_id=1, source_target_pairs={{0,1},{1,2},{2,3},{3,0},{4,5},{5,6},{6,7},{7,4},{8,9},{9,10},{10,1... | collective-permute-start | bytes 2359304 | tf_op jit(solution)/shard_map/ppermute | solution.py:62
  58.1 3.4 %collective-permute-start.1 = (bf16[2,384,512]{2,1,0:T(8,128)(2,1)}, bf16[2,384,512]{2,1,0:T(8,128)(2,1)}, u32[]{:S(2)}, u32[]{:S(2)}) collective-permute-start(bf16[2,384,512]{2,1,0:T(8,128)(2,1)} %get-tuple-element.11), channel_id=1, source_target_pairs={{0,1},{1,2},{2,3},{3,0},{4,5},{5,6},{6,7},{7,4},{8,9},{9,10},{10,1... | collective-permute-start | bytes 2359304 | tf_op jit(solution)/shard_map/ppermute | solution.py:62
  61.5 2.5 %collective-permute-start.3 = (bf16[2,384,512]{2,1,0:T(8,128)(2,1)}, bf16[2,384,512]{2,1,0:T(8,128)(2,1)}, u32[]{:S(2)}, u32[]{:S(2)}) collective-permute-start(bf16[2,384,512]{2,1,0:T(8,128)(2,1)} %get-tuple-element.12), channel_id=1, source_target_pairs={{0,3},{1,0},{2,1},{3,2},{4,7},{5,4},{6,5},{7,6},{8,11},{9,8},{10,9... | collective-permute-start | bytes 2359304 | tf_op jit(solution)/shard_map/ppermute | solution.py:62
  64.0 2.4 %collective-permute-done.2.refs_3_ = bf16[2,384,512]{2,1,0:T(8,128)(2,1)S(1)} collective-permute-done((bf16[2,384,512]{2,1,0:T(8,128)(2,1)}, bf16[2,384,512]{2,1,0:T(8,128)(2,1)S(1)}, u32[]{:S(2)}, u32[]{:S(2)}) %collective-permute-start.2) | collective-permute-done | bytes 786464 | tf_op jit(solution)/shard_map/ppermute | solution.py:62
  66.3 1.9 %collective-permute-start.5 = (bf16[2,384,512]{2,1,0:T(8,128)(2,1)S(1)}, bf16[2,384,512]{2,1,0:T(8,128)(2,1)}, u32[]{:S(2)}, u32[]{:S(2)}) collective-permute-start(bf16[2,384,512]{2,1,0:T(8,128)(2,1)S(1)} %collective-permute-done.2.refs_3_), channel_id=1, source_target_pairs={{0,3},{1,0},{2,1},{3,2},{4,7},{5,4},{6,5},{7,6},{8,11},{9,8},{10,9... | collective-permute-start | bytes 2359304 | tf_op jit(solution)/shard_map/ppermute | solution.py:62
  68.3 0.0 collective-permute-done.refs_1_
  68.3 5.2 %collective-permute-start.4 = (bf16[2,384,512]{2,1,0:T(8,128)(2,1)}, bf16[2,384,512]{2,1,0:T(8,128)(2,1)}, u32[]{:S(2)}, u32[]{:S(2)}) collective-permute-start(bf16[2,384,512]{2,1,0:T(8,128)(2,1)} %collective-permute-done.refs_1_), channel_id=1, source_target_pairs={{0,1},{1,2},{2,3},{3,0},{4,5},{5,6},{6,7},{7,4},{8,9},{9,10},{10,1... | collective-permute-start | bytes 2359304 | tf_op jit(solution)/shard_map/ppermute | solution.py:62
  73.5 0.2 copy.11
  73.8 0.2 fusion.3
  74.1 2.3 %collective-permute-done.1.refs_2_ = bf16[2,384,512]{2,1,0:T(8,128)(2,1)} collective-permute-done((bf16[2,384,512]{2,1,0:T(8,128)(2,1)}, bf16[2,384,512]{2,1,0:T(8,128)(2,1)}, u32[]{:S(2)}, u32[]{:S(2)}) %collective-permute-start.1) | collective-permute-done | bytes 786464 | tf_op jit(solution)/shard_map/ppermute | solution.py:62
  76.4 0.5 collective-permute-done.3.refs_4_
  76.9 8.4 %collective-permute-done.5.refs_6_ = bf16[2,384,512]{2,1,0:T(8,128)(2,1)} collective-permute-done((bf16[2,384,512]{2,1,0:T(8,128)(2,1)S(1)}, bf16[2,384,512]{2,1,0:T(8,128)(2,1)}, u32[]{:S(2)}, u32[]{:S(2)}) %collective-permute-start.5) | collective-permute-done | bytes 786464 | tf_op jit(solution)/shard_map/ppermute | solution.py:62
  85.3 0.0 collective-permute-done.4.refs_5_
  85.3 8.6 %all-gather.3.cloned.1.call-done = bf16[16896,256]{1,0:T(8,128)(2,1)} async-done(((bf16[528,256]{1,0:T(8,128)(2,1)}), bf16[16896,256]{1,0:T(8,128)(2,1)}) %all-gather.3.cloned.1.call-update) | async-done | bytes 8650768 | tf_op jit(solution)/shard_map/all_gather | solution.py:241
  94.0 8.8 %shard_map.85 = bf16[384,5120]{1,0:T(8,128)(2,1)S(1)} custom-call(bf16[4,4,2,528,256]{4,3,2,1,0:T(8,128)(2,1)} %bitcast.14, bf16[4,384,512]{2,1,0:T(8,128)(2,1)S(1)} %all_to_all.21.refs_0_, bf16[2,384,512]{2,1,0:T(8,128)(2,1)} %collective-permute-done.refs_1_, bf16[2,384,512]{2,1,0:T(8,128)(2,1)} %collective-permute-done.1.refs_2_, ...), custom_call_target="tpu_custom_call" | custom-call | flops 3221225472 | bytes 16777216 | tf_op jit(solution)/shard_map/pallas_call | solution.py:257
  102.8 0.0 copy-start.1
  102.8 0.0 copy-start.2
  102.8 30.6 %all_to_all.22.recv_ref = bf16[4,96,5120]{2,1,0:T(8,128)(2,1)S(1)} all-to-all(bf16[4,96,5120]{2,1,0:T(8,128)(2,1)S(1)} %bitcast.9), channel_id=1, replica_groups={{0,4,8,12},{1,5,9,13},{2,6,10,14},{3,7,11,15},{16,17,18,19},{20,21,22,2..., dimensions={0} | all-to-all | bytes 7864320 | tf_op jit(solution)/shard_map/all_to_all | solution.py:53
  133.4 0.5 shard_map.86
  133.9 13.0 %all_to_all.23.recv_ref = bf16[4,24,5120]{2,1,0:T(8,128)(2,1)S(1)} all-to-all(bf16[4,24,5120]{2,1,0:T(8,128)(2,1)S(1)} %bitcast.11), channel_id=1, replica_groups={{0,1,2,3},{4,5,6,7},{8,9,10,11},{12,13,14,15},{16,20,24,28},{17,21,25,2..., dimensions={0} | all-to-all | bytes 1966080 | tf_op jit(solution)/shard_map/all_to_all | solution.py:53
  146.9 1.0 shard_map.87
  (7 shorter events, 0.1 us)
Async XLA Ops:
  6.5 87.4 %all-gather.3.cloned.1.call-start = ((), (), s32[]{:S(2)}) async-start(), calls=%async_computation.4 | async-start | bytes 8921088 | tf_op jit(solution)/shard_map/all_gather | solution.py:241
  9.0 1.2 copy-start
  10.2 0.7 copy-start.3
  32.7 40.8 %copy-start.4 = (bf16[384,320]{0,1:T(8,128)(2,1)S(1)}, bf16[384,320]{0,1:T(8,128)(2,1)}, u32[]{:S(2)}) copy-start(bf16[384,320]{0,1:T(8,128)(2,1)} %param.11) | copy-start | bytes 737284
  51.1 15.3 %collective-permute-start.2 = (bf16[2,384,512]{2,1,0:T(8,128)(2,1)}, bf16[2,384,512]{2,1,0:T(8,128)(2,1)S(1)}, u32[]{:S(2)}, u32[]{:S(2)}) collective-permute-start(bf16[2,384,512]{2,1,0:T(8,128)(2,1)} %get-tuple-element.11), channel_id=1, source_target_pairs={{0,3},{1,0},{2,1},{3,2},{4,7},{5,4},{6,5},{7,6},{8,11},{9,8},{10,9... | collective-permute-start | bytes 2359304 | tf_op jit(solution)/shard_map/ppermute | solution.py:62
  53.7 14.5 %collective-permute-start = (bf16[2,384,512]{2,1,0:T(8,128)(2,1)}, bf16[2,384,512]{2,1,0:T(8,128)(2,1)}, u32[]{:S(2)}, u32[]{:S(2)}) collective-permute-start(bf16[2,384,512]{2,1,0:T(8,128)(2,1)} %get-tuple-element.12), channel_id=1, source_target_pairs={{0,1},{1,2},{2,3},{3,0},{4,5},{5,6},{6,7},{7,4},{8,9},{9,10},{10,1... | collective-permute-start | bytes 2359304 | tf_op jit(solution)/shard_map/ppermute | solution.py:62
  58.1 18.2 %collective-permute-start.1 = (bf16[2,384,512]{2,1,0:T(8,128)(2,1)}, bf16[2,384,512]{2,1,0:T(8,128)(2,1)}, u32[]{:S(2)}, u32[]{:S(2)}) collective-permute-start(bf16[2,384,512]{2,1,0:T(8,128)(2,1)} %get-tuple-element.11), channel_id=1, source_target_pairs={{0,1},{1,2},{2,3},{3,0},{4,5},{5,6},{6,7},{7,4},{8,9},{9,10},{10,1... | collective-permute-start | bytes 2359304 | tf_op jit(solution)/shard_map/ppermute | solution.py:62
  61.5 15.4 %collective-permute-start.3 = (bf16[2,384,512]{2,1,0:T(8,128)(2,1)}, bf16[2,384,512]{2,1,0:T(8,128)(2,1)}, u32[]{:S(2)}, u32[]{:S(2)}) collective-permute-start(bf16[2,384,512]{2,1,0:T(8,128)(2,1)} %get-tuple-element.12), channel_id=1, source_target_pairs={{0,3},{1,0},{2,1},{3,2},{4,7},{5,4},{6,5},{7,6},{8,11},{9,8},{10,9... | collective-permute-start | bytes 2359304 | tf_op jit(solution)/shard_map/ppermute | solution.py:62
  66.3 19.0 %collective-permute-start.5 = (bf16[2,384,512]{2,1,0:T(8,128)(2,1)S(1)}, bf16[2,384,512]{2,1,0:T(8,128)(2,1)}, u32[]{:S(2)}, u32[]{:S(2)}) collective-permute-start(bf16[2,384,512]{2,1,0:T(8,128)(2,1)S(1)} %collective-permute-done.2.refs_3_), channel_id=1, source_target_pairs={{0,3},{1,0},{2,1},{3,2},{4,7},{5,4},{6,5},{7,6},{8,11},{9,8},{10,9... | collective-permute-start | bytes 2359304 | tf_op jit(solution)/shard_map/ppermute | solution.py:62
  68.3 17.1 %collective-permute-start.4 = (bf16[2,384,512]{2,1,0:T(8,128)(2,1)}, bf16[2,384,512]{2,1,0:T(8,128)(2,1)}, u32[]{:S(2)}, u32[]{:S(2)}) collective-permute-start(bf16[2,384,512]{2,1,0:T(8,128)(2,1)} %collective-permute-done.refs_1_), channel_id=1, source_target_pairs={{0,1},{1,2},{2,3},{3,0},{4,5},{5,6},{6,7},{7,4},{8,9},{9,10},{10,1... | collective-permute-start | bytes 2359304 | tf_op jit(solution)/shard_map/ppermute | solution.py:62
  102.8 30.6 %copy-start.1 = (bf16[24,5120]{1,0:T(8,128)(2,1)S(1)}, bf16[24,5120]{1,0:T(8,128)(2,1)}, u32[]{:S(2)}) copy-start(bf16[24,5120]{1,0:T(8,128)(2,1)} %patches_ref.1) | copy-start | bytes 737284
  102.8 30.6 %copy-start.2 = (f32[1280]{0:T(1024)S(1)}, f32[1280]{0:T(1024)}, u32[]{:S(2)}) copy-start(f32[1280]{0:T(1024)} %gain_ref.1) | copy-start | bytes 15364
Sparse Core Ops, SparseCore 0:
  9.5 84.4 all-gather.2

commit v14 on v12

--- a/solution.py
+++ b/solution.py
@@ -23,6 +23,7 @@
 RUNS = (48, 48, 32, 32)
 TAIL = 48
 W_ROWS = HID_OWN + IN_OWN + TAIL
+LINE_ROWS = SIDE * OWN
 AXES = ("prompt", "rollout")
 F32 = jnp.float32
 BF16 = jnp.bfloat16
@@ -65,7 +66,8 @@
 def place_in_plane():
     rollout = lax.axis_index("rollout")
     even = lax.axis_index("prompt") % 2 == 0
-    return even, jnp.where(even, rollout // SIDE, rollout % SIDE)
+    y, x = rollout // SIDE, rollout % SIDE
+    return even, jnp.where(even, x, y), jnp.where(even, y, x)
 
 
 def weights_kernel(w2_ref, w1_ref, out_ref, block, w1, sems):
@@ -88,7 +90,7 @@
 
 
 def pack_kernel(count_ref, ids_ref, grads_ref, out_ref, meta):
-    even, _ = place_in_plane()
+    even, _, _ = place_in_plane()
     ids = ids_ref[...]
     owner = (ids * 2731) >> 16
     turned = (owner & 3) * SIDE + (owner >> 2)
@@ -133,8 +135,9 @@
 
 
 def mlp_kernel(w_ref, *refs):
-    sums, (slope_ref, out_ref, s, w2, w1, w1_tail, sems2, sems1) = refs[:7], refs[7:]
-    even, second = place_in_plane()
+    sums, outs = refs[:7], refs[8:13]
+    slope_ref, (s, w2, w1, w1_tail, act_ref, sems2, sems1) = refs[7], refs[13:]
+    even, first, second = place_in_plane()
     base = HID_OWN + IN_OWN
     copies, late = [], []
     for n, (offset, parts) in enumerate(GATHERED):
@@ -165,7 +168,12 @@
             block = s[n, k]
             part = dot_t(w2[n, k, 0], block[:, :W2_COLS]) + dot_t(w2[n, k, 1], block[:, W2_COLS:])
             hidden = part if hidden is None else hidden + part
-    act = (hidden.T * slope_ref[...]).astype(BF16)
+    act_ref[...] = (hidden.T * slope_ref[...]).astype(BF16)
+    blocks = []
+    for by in (2, 1, 3, 0):
+        at = pl.multiple_of(lax.rem(first + by, SIDE) * LINE_ROWS, LINE_ROWS)
+        blocks.append(act_ref[pl.ds(at, LINE_ROWS), :])
+    act = jnp.concatenate(blocks, axis=0)
     width = HID // SIDE
     for q in range(SIDE):
         for copy in late[q]:
@@ -174,13 +182,23 @@
         runs = [fold[:, :, :rows, 64 * n : 64 * n + 64] for n, rows in enumerate(RUNS)]
         tail = jnp.concatenate(runs, axis=2).reshape(width, 64)
         part = dot_t(act[:, 0:256], w1[q].reshape(width, 256)) + dot_t(act[:, 256:], tail)
-        out_ref[:, width * q : width * (q + 1)] = part.astype(BF16)
-
-
-def add_kernel(recv_ref, patches_ref, gain_ref, out_ref, near_patches_ref, near_gain_ref):
-    total = recv_ref[0].astype(F32)
-    for k in range(1, SIDE):
-        total = total + recv_ref[k].astype(F32)
+        at = 0
+        for out_ref in outs:
+            rows = out_ref.shape[0]
+            out_ref[:, width * q : width * (q + 1)] = part[at : at + rows].astype(BF16)
+            at += rows
+
+
+def relay_kernel(right_ref, left_ref, low_ref, high_ref, right_out, left_out):
+    half = LINE_ROWS // 2
+    right_out[0:half] = (right_ref[0:half].astype(F32) + low_ref[...].astype(F32)).astype(BF16)
+    right_out[half:] = right_ref[half:]
+    left_out[0:half] = left_ref[0:half]
+    left_out[half:] = (left_ref[half:].astype(F32) + high_ref[...].astype(F32)).astype(BF16)
+
+
+def add_kernel(own_ref, a_ref, b_ref, patches_ref, gain_ref, out_ref, near_patches_ref, near_gain_ref):
+    total = own_ref[...].astype(F32) + a_ref[...].astype(F32) + b_ref[...].astype(F32)
     out_ref[...] = total.astype(BF16)
     near_patches_ref[...] = patches_ref[...]
     near_gain_ref[...] = gain_ref[...]
@@ -254,16 +272,17 @@
     slope = gelu_slope(pre_act.astype(F32)).reshape(SIDE, SIDE, OWN, HID_OWN)
     slope = jnp.where(even, slope.transpose(1, 0, 2, 3), slope).reshape(ROWS, HID_OWN)
     weights = weights.reshape(SIDE, SIDE, 2, W_ROWS, 256)
-    partial = pl.pallas_call(
+    far_low, far_high, right, left, own = pl.pallas_call(
         mlp_kernel,
-        out_shape=pltpu.VMEM((ROWS, HID), BF16),
+        out_shape=[pltpu.VMEM((rows, HID), BF16) for rows in (48, 48, 96, 96, 96)],
         in_specs=[ANY] * 8 + [VMEM],
-        out_specs=VMEM,
+        out_specs=[VMEM] * 5,
         scratch_shapes=[
             pltpu.VMEM((SIDE, SIDE, ROWS, COLS), BF16),
             pltpu.VMEM((SIDE, SIDE, 2, HID_OWN, W2_COLS), BF16),
             pltpu.VMEM((SIDE, SIDE, 2, IN_OWN, 256), BF16),
             pltpu.VMEM((SIDE, SIDE, 2, TAIL, 256), BF16),
+            pltpu.VMEM((ROWS, HID_OWN), BF16),
             pltpu.SemaphoreType.DMA((SIDE, 4)),
             pltpu.SemaphoreType.DMA((SIDE, 2)),
         ],
@@ -271,14 +290,22 @@
         compiler_params=pltpu.CompilerParams(vmem_limit_bytes=24 << 20),
     )(pinned(weights), line, a1, a2, b1, b2, a3, b3, slope)
 
-    halfway = exchange(partial.reshape(SIDE, SIDE * OWN, HID), 0)
+    low, high = shift(far_low, 0, 1), shift(far_high, 0, -1)
+    right, left = pl.pallas_call(
+        relay_kernel,
+        out_shape=[pltpu.VMEM((LINE_ROWS, HID), BF16)] * 2,
+        in_specs=[VMEM] * 4,
+        out_specs=[VMEM] * 2,
+        compiler_params=pltpu.CompilerParams(vmem_limit_bytes=16 << 20),
+    )(right, left, low, high)
+    from_left, from_right = shift(right, 0, 1), shift(left, 0, -1)
     halfway, near_patches, near_gain = pl.pallas_call(
         add_kernel,
         out_shape=[pltpu.VMEM((SIDE * OWN, HID), BF16), pltpu.VMEM((OWN, HID), BF16), pltpu.VMEM((VIT,), F32)],
-        in_specs=[VMEM] * 3,
+        in_specs=[VMEM] * 5,
         out_specs=[VMEM] * 3,
         compiler_params=pltpu.CompilerParams(vmem_limit_bytes=16 << 20),
-    )(halfway, patches, ln_gain)
+    )(own, from_left, from_right, patches, ln_gain)
     last = exchange(halfway.reshape(SIDE, OWN, HID), 1)
     return call(norm_kernel, (OWN, HID), [VMEM] * 3)(last, near_patches, near_gain)
 

time: 156 us -> 160 us (1.026)
  blocking collectives: 82.4 us -> 53.5 us
  waiting for transfers between devices: 23.1 us -> 44.9 us
  starting transfers between devices: 18.7 us -> 30.5 us
    all_to_all x3 -> x2, blocking collectives: 60.7 us -> 31.7 us  [exchange(): lax.all_to_all(blocks, AXES, split_axis=0, concat_axis=0, axis_index_grou...]
    ppermute x6 -> x10, waiting for transfers between devices: 15.5 us -> 37.3 us  [shift(): return lax.ppermute(value, AXES, pairs)]
    ppermute x6 -> x10, starting transfers between devices: 18.7 us -> 30.5 us  [shift(): return lax.ppermute(value, AXES, pairs)]
    pallas_call x1 -> x2, Pallas kernels: 8.78 us -> 9.09 us  [the longest x1 8.83 us: per_device(): pl.pallas_call(mlp_kernel, out_shape=[pltpu.VMEM((rows, HID), BF16) for r...]
  transfers between devices with their start and end apart: 7 -> 11, of which waited for: 6 -> 10; matrix products, arithmetic and copies ran while one was open for 1% -> 1% of each run, Pallas kernels for 0% -> 0%
where the time goes in v14:
time: 160 us
  blocking collectives  53.5 us (33%)
  waiting for transfers between devices  44.9 us (28%)
  starting transfers between devices  30.5 us (19%)
  between operations  14.2 us (9%)
  Pallas kernels  13 us (8%)
  local copies, waits for them, and re-layouts  3.34 us (2%)
    ppermute x10, waiting for transfers between devices, shift(): return lax.ppermute(value, AXES, pairs)  37.3 us
    all_to_all x2, blocking collectives, exchange(): lax.all_to_all(blocks, AXES, split_axis=0, concat_axis=0, axis_index_grou...  31.7 us
    ppermute x10, starting transfers between devices, shift(): return lax.ppermute(value, AXES, pairs)  30.5 us
    all_to_all x1, blocking collectives, per_device(): lax.all_to_all(outgoing, 'rollout', split_axis=0, concat_axis=0, tiled=True)  21.7 us
    pallas_call x1, Pallas kernels, per_device(): pl.pallas_call(mlp_kernel, out_shape=[pltpu.VMEM((rows, HID), BF16) for r...  8.83 us
    all_gather x1, waiting for transfers between devices, per_device(): weights = lax.all_gather(weights, 'prompt', axis=0, tiled=False)  7.5 us
  transfers between devices with their start and end apart: 11, of which 10 were waited for; matrix products, arithmetic and copies ran while one was open for 1% of the time, Pallas kernels for 0%

profile of v14, /device:TPU:6, one launch (start us, length us, event | category | flops | bytes accessed | tf_op | source)
XLA Modules:
  0.0 159.7 jit_solution(8997627276896557008)
XLA Ops:
  6.5 1.8 %shard_map.82 = bf16[528,256]{1,0:T(8,128)(2,1)} custom-call(bf16[320,256]{1,0:T(8,128)(2,1)} %w2_ref.1, bf16[160,320]{1,0:T(8,128)(2,1)} %w1_ref.1), custom_call_target="tpu_custom_call" | custom-call | tf_op jit(solution)/shard_map/pallas_call | solution.py:248
  9.0 1.2 copy-done
  10.2 0.7 copy-done.3
  10.9 21.7 %all_to_all.15.recv_ref = bf16[16,64,512]{2,1,0:T(8,128)(2,1)S(1)} all-to-all(bf16[16,64,512]{2,1,0:T(8,128)(2,1)S(1)} %shard_map.83), channel_id=1, replica_groups=mesh['prompt'=32,'rollout'=16] {'rollout'}, dimensions={0} | all-to-all | bytes 2097152 | tf_op jit(solution)/shard_map/all_to_all | solution.py:264
  32.7 0.6 shard_map.84
  33.3 17.1 %all_to_all.16.refs_0_ = bf16[4,384,512]{2,1,0:T(8,128)(2,1)S(1)} all-to-all(bf16[4,384,512]{2,1,0:T(8,128)(2,1)S(1)} %shard_map.84), channel_id=1, replica_groups={{0,1,2,3},{4,5,6,7},{8,9,10,11},{12,13,14,15},{16,20,24,28},{17,21,25,2..., dimensions={0} | all-to-all | bytes 3145728 | tf_op jit(solution)/shard_map/all_to_all | solution.py:54
  50.4 1.3 fusion.6
  51.6 2.6 %collective-permute-start.2 = (bf16[2,384,512]{2,1,0:T(8,128)(2,1)}, bf16[2,384,512]{2,1,0:T(8,128)(2,1)S(1)}, u32[]{:S(2)}, u32[]{:S(2)}) collective-permute-start(bf16[2,384,512]{2,1,0:T(8,128)(2,1)} %get-tuple-element.25), channel_id=1, source_target_pairs={{0,12},{4,0},{8,4},{12,8},{1,13},{5,1},{9,5},{13,9},{2,14},{6,2},{... | collective-permute-start | bytes 2359304 | tf_op jit(solution)/shard_map/ppermute | solution.py:63
  54.2 3.3 %collective-permute-start = (bf16[2,384,512]{2,1,0:T(8,128)(2,1)}, bf16[2,384,512]{2,1,0:T(8,128)(2,1)}, u32[]{:S(2)}, u32[]{:S(2)}) collective-permute-start(bf16[2,384,512]{2,1,0:T(8,128)(2,1)} %get-tuple-element.26), channel_id=1, source_target_pairs={{0,4},{4,8},{8,12},{12,0},{1,5},{5,9},{9,13},{13,1},{2,6},{6,10},{... | collective-permute-start | bytes 2359304 | tf_op jit(solution)/shard_map/ppermute | solution.py:63
  57.5 1.9 %collective-permute-start.1 = (bf16[2,384,512]{2,1,0:T(8,128)(2,1)}, bf16[2,384,512]{2,1,0:T(8,128)(2,1)}, u32[]{:S(2)}, u32[]{:S(2)}) collective-permute-start(bf16[2,384,512]{2,1,0:T(8,128)(2,1)} %get-tuple-element.25), channel_id=1, source_target_pairs={{0,4},{4,8},{8,12},{12,0},{1,5},{5,9},{9,13},{13,1},{2,6},{6,10},{... | collective-permute-start | bytes 2359304 | tf_op jit(solution)/shard_map/ppermute | solution.py:63
  59.4 5.1 %collective-permute-start.3 = (bf16[2,384,512]{2,1,0:T(8,128)(2,1)}, bf16[2,384,512]{2,1,0:T(8,128)(2,1)}, u32[]{:S(2)}, u32[]{:S(2)}) collective-permute-start(bf16[2,384,512]{2,1,0:T(8,128)(2,1)} %get-tuple-element.26), channel_id=1, source_target_pairs={{0,12},{4,0},{8,4},{12,8},{1,13},{5,1},{9,5},{13,9},{2,14},{6,2},{... | collective-permute-start | bytes 2359304 | tf_op jit(solution)/shard_map/ppermute | solution.py:63
  64.5 1.2 collective-permute-done.2.refs_3_
  65.7 3.8 %collective-permute-start.5 = (bf16[2,384,512]{2,1,0:T(8,128)(2,1)S(1)}, bf16[2,384,512]{2,1,0:T(8,128)(2,1)}, u32[]{:S(2)}, u32[]{:S(2)}) collective-permute-start(bf16[2,384,512]{2,1,0:T(8,128)(2,1)S(1)} %collective-permute-done.2.refs_3_), channel_id=1, source_target_pairs={{0,12},{4,0},{8,4},{12,8},{1,13},{5,1},{9,5},{13,9},{2,14},{6,2},{... | collective-permute-start | bytes 2359304 | tf_op jit(solution)/shard_map/ppermute | solution.py:63
  69.6 2.0 %collective-permute-start.4 = (bf16[2,384,512]{2,1,0:T(8,128)(2,1)}, bf16[2,384,512]{2,1,0:T(8,128)(2,1)}, u32[]{:S(2)}, u32[]{:S(2)}) collective-permute-start(bf16[2,384,512]{2,1,0:T(8,128)(2,1)} %collective-permute-done.refs_1_), channel_id=1, source_target_pairs={{0,4},{4,8},{8,12},{12,0},{1,5},{5,9},{9,13},{13,1},{2,6},{6,10},{... | collective-permute-start | bytes 2359304 | tf_op jit(solution)/shard_map/ppermute | solution.py:63
  71.9 0.2 fusion.3
  72.2 5.8 %collective-permute-done.1.refs_2_ = bf16[2,384,512]{2,1,0:T(8,128)(2,1)} collective-permute-done((bf16[2,384,512]{2,1,0:T(8,128)(2,1)}, bf16[2,384,512]{2,1,0:T(8,128)(2,1)}, u32[]{:S(2)}, u32[]{:S(2)}) %collective-permute-start.1) | collective-permute-done | bytes 786464 | tf_op jit(solution)/shard_map/ppermute | solution.py:63
  78.0 4.6 %collective-permute-done.5.refs_6_ = bf16[2,384,512]{2,1,0:T(8,128)(2,1)} collective-permute-done((bf16[2,384,512]{2,1,0:T(8,128)(2,1)S(1)}, bf16[2,384,512]{2,1,0:T(8,128)(2,1)}, u32[]{:S(2)}, u32[]{:S(2)}) %collective-permute-start.5) | collective-permute-done | bytes 786464 | tf_op jit(solution)/shard_map/ppermute | solution.py:63
  82.7 3.8 %collective-permute-done.4.refs_5_ = bf16[2,384,512]{2,1,0:T(8,128)(2,1)} collective-permute-done((bf16[2,384,512]{2,1,0:T(8,128)(2,1)}, bf16[2,384,512]{2,1,0:T(8,128)(2,1)}, u32[]{:S(2)}, u32[]{:S(2)}) %collective-permute-start.4) | collective-permute-done | bytes 786464 | tf_op jit(solution)/shard_map/ppermute | solution.py:63
  86.5 7.5 %all-gather.3.cloned.1.call-done = bf16[16896,256]{1,0:T(8,128)(2,1)} async-done(((bf16[528,256]{1,0:T(8,128)(2,1)}), bf16[16896,256]{1,0:T(8,128)(2,1)}) %all-gather.3.cloned.1.call-update) | async-done | bytes 8650768 | tf_op jit(solution)/shard_map/all_gather | solution.py:259
  94.0 8.8 %shard_map.85 = (bf16[48,5120]{1,0:T(8,128)(2,1)S(1)}, bf16[48,5120]{1,0:T(8,128)(2,1)S(1)}, bf16[96,5120]{1,0:T(8,128)(2,1)S(1)}, bf16[96,5120]{1,0:T(8,128)(2,1)S(1)}, bf16[96,5120]{1,0:T(8,128)(2,1)S(1)}) custom-call(bf16[4,4,2,528,256]{4,3,2,1,0:T(8,128)(2,1)} %bitcast.12, bf16[4,384,512]{2,1,0:T(8,128)(2,1)S(1)} %all_to_all.16.refs_0_, ...), custom_call_target="tpu_custom_call" | custom-call | flops 3221225472 | bytes 16777216 | tf_op jit(solution)/shard_map/pallas_call | solution.py:275
  102.8 2.6 %collective-permute-start.6 = (bf16[48,5120]{1,0:T(8,128)(2,1)S(1)}, bf16[48,5120]{1,0:T(8,128)(2,1)S(1)}, u32[]{:S(2)}, u32[]{:S(2)}) collective-permute-start(bf16[48,5120]{1,0:T(8,128)(2,1)S(1)} %get-tuple-element.18), channel_id=1, source_target_pairs={{0,1},{1,2},{2,3},{3,0},{4,5},{5,6},{6,7},{7,4},{8,9},{9,10},{10,1... | collective-permute-start | bytes 1474568 | tf_op jit(solution)/shard_map/ppermute | solution.py:63
  105.4 3.4 %collective-permute-start.7 = (bf16[48,5120]{1,0:T(8,128)(2,1)S(1)}, bf16[48,5120]{1,0:T(8,128)(2,1)S(1)}, u32[]{:S(2)}, u32[]{:S(2)}) collective-permute-start(bf16[48,5120]{1,0:T(8,128)(2,1)S(1)} %get-tuple-element.19), channel_id=1, source_target_pairs={{0,3},{1,0},{2,1},{3,2},{4,7},{5,4},{6,5},{7,6},{8,11},{9,8},{10,9... | collective-permute-start | bytes 1474568 | tf_op jit(solution)/shard_map/ppermute | solution.py:63
  108.8 4.9 %collective-permute-done.6.low_ref = bf16[48,5120]{1,0:T(8,128)(2,1)S(1)} collective-permute-done((bf16[48,5120]{1,0:T(8,128)(2,1)S(1)}, bf16[48,5120]{1,0:T(8,128)(2,1)S(1)}, u32[]{:S(2)}, u32[]{:S(2)}) %collective-permute-start.6) | collective-permute-done | bytes 491552 | tf_op jit(solution)/shard_map/ppermute | solution.py:63
  113.7 3.7 %collective-permute-done.7.high_ref = bf16[48,5120]{1,0:T(8,128)(2,1)S(1)} collective-permute-done((bf16[48,5120]{1,0:T(8,128)(2,1)S(1)}, bf16[48,5120]{1,0:T(8,128)(2,1)S(1)}, u32[]{:S(2)}, u32[]{:S(2)}) %collective-permute-start.7) | collective-permute-done | bytes 491552 | tf_op jit(solution)/shard_map/ppermute | solution.py:63
  117.3 0.3 shard_map.86
  117.6 1.9 %collective-permute-start.8 = (bf16[96,5120]{1,0:T(8,128)(2,1)S(1)}, bf16[96,5120]{1,0:T(8,128)(2,1)S(1)}, u32[]{:S(2)}, u32[]{:S(2)}) collective-permute-start(bf16[96,5120]{1,0:T(8,128)(2,1)S(1)} %get-tuple-element.20), channel_id=1, source_target_pairs={{0,1},{1,2},{2,3},{3,0},{4,5},{5,6},{6,7},{7,4},{8,9},{9,10},{10,1... | collective-permute-start | bytes 2949128 | tf_op jit(solution)/shard_map/ppermute | solution.py:63
  119.5 3.9 %collective-permute-start.9 = (bf16[96,5120]{1,0:T(8,128)(2,1)S(1)}, bf16[96,5120]{1,0:T(8,128)(2,1)S(1)}, u32[]{:S(2)}, u32[]{:S(2)}) collective-permute-start(bf16[96,5120]{1,0:T(8,128)(2,1)S(1)} %get-tuple-element.21), channel_id=1, source_target_pairs={{0,3},{1,0},{2,1},{3,2},{4,7},{5,4},{6,5},{7,6},{8,11},{9,8},{10,9... | collective-permute-start | bytes 2949128 | tf_op jit(solution)/shard_map/ppermute | solution.py:63
  123.5 10.1 %collective-permute-done.8.a_ref = bf16[96,5120]{1,0:T(8,128)(2,1)S(1)} collective-permute-done((bf16[96,5120]{1,0:T(8,128)(2,1)S(1)}, bf16[96,5120]{1,0:T(8,128)(2,1)S(1)}, u32[]{:S(2)}, u32[]{:S(2)}) %collective-permute-start.8) | collective-permute-done | bytes 983072 | tf_op jit(solution)/shard_map/ppermute | solution.py:63
  133.6 3.1 %collective-permute-done.9.b_ref = bf16[96,5120]{1,0:T(8,128)(2,1)S(1)} collective-permute-done((bf16[96,5120]{1,0:T(8,128)(2,1)S(1)}, bf16[96,5120]{1,0:T(8,128)(2,1)S(1)}, u32[]{:S(2)}, u32[]{:S(2)}) %collective-permute-start.9) | collective-permute-done | bytes 983072 | tf_op jit(solution)/shard_map/ppermute | solution.py:63
  136.7 0.4 shard_map.87
  137.1 14.7 %all_to_all.17.recv_ref = bf16[4,24,5120]{2,1,0:T(8,128)(2,1)S(1)} all-to-all(bf16[4,24,5120]{2,1,0:T(8,128)(2,1)S(1)} %bitcast.9), channel_id=1, replica_groups={{0,4,8,12},{1,5,9,13},{2,6,10,14},{3,7,11,15},{16,17,18,19},{20,21,22,2..., dimensions={0} | all-to-all | bytes 1966080 | tf_op jit(solution)/shard_map/all_to_all | solution.py:54
  151.8 1.0 shard_map.88
  (15 shorter events, 0.5 us)
Async XLA Ops:
  6.5 87.4 %all-gather.3.cloned.1.call-start = ((), (), s32[]{:S(2)}) async-start(), calls=%async_computation.3 | async-start | bytes 8921088 | tf_op jit(solution)/shard_map/all_gather | solution.py:259
  9.0 1.2 copy-start
  10.2 0.7 copy-start.3
  50.3 21.3 %copy-start.4 = (bf16[384,320]{0,1:T(8,128)(2,1)S(1)}, bf16[384,320]{0,1:T(8,128)(2,1)}, u32[]{:S(2)}) copy-start(bf16[384,320]{0,1:T(8,128)(2,1)} %param.11) | copy-start | bytes 737284
  51.6 14.1 %collective-permute-start.2 = (bf16[2,384,512]{2,1,0:T(8,128)(2,1)}, bf16[2,384,512]{2,1,0:T(8,128)(2,1)S(1)}, u32[]{:S(2)}, u32[]{:S(2)}) collective-permute-start(bf16[2,384,512]{2,1,0:T(8,128)(2,1)} %get-tuple-element.25), channel_id=1, source_target_pairs={{0,12},{4,0},{8,4},{12,8},{1,13},{5,1},{9,5},{13,9},{2,14},{6,2},{... | collective-permute-start | bytes 2359304 | tf_op jit(solution)/shard_map/ppermute | solution.py:63
  54.2 15.4 %collective-permute-start = (bf16[2,384,512]{2,1,0:T(8,128)(2,1)}, bf16[2,384,512]{2,1,0:T(8,128)(2,1)}, u32[]{:S(2)}, u32[]{:S(2)}) collective-permute-start(bf16[2,384,512]{2,1,0:T(8,128)(2,1)} %get-tuple-element.26), channel_id=1, source_target_pairs={{0,4},{4,8},{8,12},{12,0},{1,5},{5,9},{9,13},{13,1},{2,6},{6,10},{... | collective-permute-start | bytes 2359304 | tf_op jit(solution)/shard_map/ppermute | solution.py:63
  57.5 20.6 %collective-permute-start.1 = (bf16[2,384,512]{2,1,0:T(8,128)(2,1)}, bf16[2,384,512]{2,1,0:T(8,128)(2,1)}, u32[]{:S(2)}, u32[]{:S(2)}) collective-permute-start(bf16[2,384,512]{2,1,0:T(8,128)(2,1)} %get-tuple-element.25), channel_id=1, source_target_pairs={{0,4},{4,8},{8,12},{12,0},{1,5},{5,9},{9,13},{13,1},{2,6},{6,10},{... | collective-permute-start | bytes 2359304 | tf_op jit(solution)/shard_map/ppermute | solution.py:63
  59.4 18.6 %collective-permute-start.3 = (bf16[2,384,512]{2,1,0:T(8,128)(2,1)}, bf16[2,384,512]{2,1,0:T(8,128)(2,1)}, u32[]{:S(2)}, u32[]{:S(2)}) collective-permute-start(bf16[2,384,512]{2,1,0:T(8,128)(2,1)} %get-tuple-element.26), channel_id=1, source_target_pairs={{0,12},{4,0},{8,4},{12,8},{1,13},{5,1},{9,5},{13,9},{2,14},{6,2},{... | collective-permute-start | bytes 2359304 | tf_op jit(solution)/shard_map/ppermute | solution.py:63
  65.7 17.0 %collective-permute-start.5 = (bf16[2,384,512]{2,1,0:T(8,128)(2,1)S(1)}, bf16[2,384,512]{2,1,0:T(8,128)(2,1)}, u32[]{:S(2)}, u32[]{:S(2)}) collective-permute-start(bf16[2,384,512]{2,1,0:T(8,128)(2,1)S(1)} %collective-permute-done.2.refs_3_), channel_id=1, source_target_pairs={{0,12},{4,0},{8,4},{12,8},{1,13},{5,1},{9,5},{13,9},{2,14},{6,2},{... | collective-permute-start | bytes 2359304 | tf_op jit(solution)/shard_map/ppermute | solution.py:63
  69.6 16.9 %collective-permute-start.4 = (bf16[2,384,512]{2,1,0:T(8,128)(2,1)}, bf16[2,384,512]{2,1,0:T(8,128)(2,1)}, u32[]{:S(2)}, u32[]{:S(2)}) collective-permute-start(bf16[2,384,512]{2,1,0:T(8,128)(2,1)} %collective-permute-done.refs_1_), channel_id=1, source_target_pairs={{0,4},{4,8},{8,12},{12,0},{1,5},{5,9},{9,13},{13,1},{2,6},{6,10},{... | collective-permute-start | bytes 2359304 | tf_op jit(solution)/shard_map/ppermute | solution.py:63
  102.8 33.9 %copy-start.1 = (bf16[24,5120]{1,0:T(8,128)(2,1)S(1)}, bf16[24,5120]{1,0:T(8,128)(2,1)}, u32[]{:S(2)}) copy-start(bf16[24,5120]{1,0:T(8,128)(2,1)} %patches_ref.1) | copy-start | bytes 737284
  102.8 33.9 %copy-start.2 = (f32[1280]{0:T(1024)S(1)}, f32[1280]{0:T(1024)}, u32[]{:S(2)}) copy-start(f32[1280]{0:T(1024)} %gain_ref.1) | copy-start | bytes 15364
  102.8 10.9 %collective-permute-start.6 = (bf16[48,5120]{1,0:T(8,128)(2,1)S(1)}, bf16[48,5120]{1,0:T(8,128)(2,1)S(1)}, u32[]{:S(2)}, u32[]{:S(2)}) collective-permute-start(bf16[48,5120]{1,0:T(8,128)(2,1)S(1)} %get-tuple-element.18), channel_id=1, source_target_pairs={{0,1},{1,2},{2,3},{3,0},{4,5},{5,6},{6,7},{7,4},{8,9},{9,10},{10,1... | collective-permute-start | bytes 1474568 | tf_op jit(solution)/shard_map/ppermute | solution.py:63
  105.4 11.9 %collective-permute-start.7 = (bf16[48,5120]{1,0:T(8,128)(2,1)S(1)}, bf16[48,5120]{1,0:T(8,128)(2,1)S(1)}, u32[]{:S(2)}, u32[]{:S(2)}) collective-permute-start(bf16[48,5120]{1,0:T(8,128)(2,1)S(1)} %get-tuple-element.19), channel_id=1, source_target_pairs={{0,3},{1,0},{2,1},{3,2},{4,7},{5,4},{6,5},{7,6},{8,11},{9,8},{10,9... | collective-permute-start | bytes 1474568 | tf_op jit(solution)/shard_map/ppermute | solution.py:63
  117.6 16.0 %collective-permute-start.8 = (bf16[96,5120]{1,0:T(8,128)(2,1)S(1)}, bf16[96,5120]{1,0:T(8,128)(2,1)S(1)}, u32[]{:S(2)}, u32[]{:S(2)}) collective-permute-start(bf16[96,5120]{1,0:T(8,128)(2,1)S(1)} %get-tuple-element.20), channel_id=1, source_target_pairs={{0,1},{1,2},{2,3},{3,0},{4,5},{5,6},{6,7},{7,4},{8,9},{9,10},{10,1... | collective-permute-start | bytes 2949128 | tf_op jit(solution)/shard_map/ppermute | solution.py:63
  119.5 17.2 %collective-permute-start.9 = (bf16[96,5120]{1,0:T(8,128)(2,1)S(1)}, bf16[96,5120]{1,0:T(8,128)(2,1)S(1)}, u32[]{:S(2)}, u32[]{:S(2)}) collective-permute-start(bf16[96,5120]{1,0:T(8,128)(2,1)S(1)} %get-tuple-element.21), channel_id=1, source_target_pairs={{0,3},{1,0},{2,1},{3,2},{4,7},{5,4},{6,5},{7,6},{8,11},{9,8},{10,9... | collective-permute-start | bytes 2949128 | tf_op jit(solution)/shard_map/ppermute | solution.py:63
Sparse Core Ops, SparseCore 0:
  9.5 84.4 all-gather.2

commit v15 on v12

--- a/solution.py
+++ b/solution.py
@@ -133,7 +133,7 @@
 
 
 def mlp_kernel(w_ref, *refs):
-    sums, (slope_ref, out_ref, s, w2, w1, w1_tail, sems2, sems1) = refs[:7], refs[7:]
+    sums, (slope_hbm, out_ref, s, w2, w1, w1_tail, slope_ref, sems2, sems1, slope_sem) = refs[:7], refs[7:]
     even, second = place_in_plane()
     base = HID_OWN + IN_OWN
     copies, late = [], []
@@ -149,6 +149,8 @@
             copy = pltpu.make_async_copy(sums[operand], s.at[n, span], sems2.at[n, h + 2])
             copy.start()
             copies.append((n, span, by_row, copy))
+    get_slope = pltpu.make_async_copy(slope_hbm, slope_ref, slope_sem.at[0])
+    get_slope.start()
     for q in range(SIDE):
         pair = [
             pltpu.make_async_copy(w_ref.at[q, :, :, HID_OWN:base], w1.at[q], sems1.at[q, 0]),
@@ -165,6 +167,7 @@
             block = s[n, k]
             part = dot_t(w2[n, k, 0], block[:, :W2_COLS]) + dot_t(w2[n, k, 1], block[:, W2_COLS:])
             hidden = part if hidden is None else hidden + part
+    get_slope.wait()
     act = (hidden.T * slope_ref[...]).astype(BF16)
     width = HID // SIDE
     for q in range(SIDE):
@@ -257,15 +260,17 @@
     partial = pl.pallas_call(
         mlp_kernel,
         out_shape=pltpu.VMEM((ROWS, HID), BF16),
-        in_specs=[ANY] * 8 + [VMEM],
+        in_specs=[ANY] * 9,
         out_specs=VMEM,
         scratch_shapes=[
             pltpu.VMEM((SIDE, SIDE, ROWS, COLS), BF16),
             pltpu.VMEM((SIDE, SIDE, 2, HID_OWN, W2_COLS), BF16),
             pltpu.VMEM((SIDE, SIDE, 2, IN_OWN, 256), BF16),
             pltpu.VMEM((SIDE, SIDE, 2, TAIL, 256), BF16),
+            pltpu.VMEM((ROWS, HID_OWN), F32),
             pltpu.SemaphoreType.DMA((SIDE, 4)),
             pltpu.SemaphoreType.DMA((SIDE, 2)),
+            pltpu.SemaphoreType.DMA((1,)),
         ],
         cost_estimate=pl.CostEstimate(flops=3 << 30, bytes_accessed=16 << 20, transcendentals=0),
         compiler_params=pltpu.CompilerParams(vmem_limit_bytes=24 << 20),

time: 156 us -> 156 us (level)
  no operation moved by 1% of the time
where the time goes in v15:
time: 156 us; the launch traced here: 154 us
  blocking collectives  82.4 us (53%)
  waiting for transfers between devices  23.1 us (15%)
  starting transfers between devices  18.7 us (12%)
  between operations  14.2 us (9%)
  Pallas kernels  12.5 us (8%)
  local copies, waits for them, and re-layouts  3.34 us (2%)
    all_to_all x3, blocking collectives, exchange(): lax.all_to_all(blocks, AXES, split_axis=0, concat_axis=0, axis_index_grou...  60.7 us
    all_to_all x1, blocking collectives, per_device(): lax.all_to_all(outgoing, 'rollout', split_axis=0, concat_axis=0, tiled=True)  21.7 us
    ppermute x6, starting transfers between devices, shift(): return lax.ppermute(value, AXES, pairs)  18.7 us
    ppermute x6, waiting for transfers between devices, shift(): return lax.ppermute(value, AXES, pairs)  15.5 us
    pallas_call x1, Pallas kernels, per_device(): pl.pallas_call(mlp_kernel, out_shape=pltpu.VMEM((ROWS, HID), BF16), in_sp...  8.46 us
    all_gather x1, waiting for transfers between devices, per_device(): weights = lax.all_gather(weights, 'prompt', axis=0, tiled=False)  7.5 us
  transfers between devices with their start and end apart: 7, of which 6 were waited for; matrix products, arithmetic and copies ran while one was open for 1% of the time, Pallas kernels for 0%

profile of v15, /device:TPU:6, one launch (start us, length us, event | category | flops | bytes accessed | tf_op | source)
XLA Modules:
  0.0 154.5 jit_solution(15820206755013897943)
XLA Ops:
  6.5 1.8 %shard_map.82 = bf16[528,256]{1,0:T(8,128)(2,1)} custom-call(bf16[320,256]{1,0:T(8,128)(2,1)} %w2_ref.1, bf16[160,320]{1,0:T(8,128)(2,1)} %w1_ref.1), custom_call_target="tpu_custom_call" | custom-call | tf_op jit(solution)/shard_map/pallas_call | solution.py:233
  8.3 0.0 all-gather.3.cloned.1.call-update
  9.0 0.0 copy-start
  9.0 1.2 copy-done
  10.2 0.7 copy-done.3
  10.9 0.1 shard_map.83
  10.9 21.7 %all_to_all.20.recv_ref = bf16[16,64,512]{2,1,0:T(8,128)(2,1)S(1)} all-to-all(bf16[16,64,512]{2,1,0:T(8,128)(2,1)S(1)} %shard_map.83), channel_id=1, replica_groups=mesh['prompt'=32,'rollout'=16] {'rollout'}, dimensions={0} | all-to-all | bytes 2097152 | tf_op jit(solution)/shard_map/all_to_all | solution.py:249
  32.7 0.6 shard_map.84
  33.3 17.1 %all_to_all.21.refs_0_ = bf16[4,384,512]{2,1,0:T(8,128)(2,1)S(1)} all-to-all(bf16[4,384,512]{2,1,0:T(8,128)(2,1)S(1)} %shard_map.84), channel_id=1, replica_groups={{0,1,2,3},{4,5,6,7},{8,9,10,11},{12,13,14,15},{16,20,24,28},{17,21,25,2..., dimensions={0} | all-to-all | bytes 3145728 | tf_op jit(solution)/shard_map/all_to_all | solution.py:53
  50.4 1.3 fusion.6
  51.7 2.6 %collective-permute-start.2 = (bf16[2,384,512]{2,1,0:T(8,128)(2,1)}, bf16[2,384,512]{2,1,0:T(8,128)(2,1)S(1)}, u32[]{:S(2)}, u32[]{:S(2)}) collective-permute-start(bf16[2,384,512]{2,1,0:T(8,128)(2,1)} %get-tuple-element.11), channel_id=1, source_target_pairs={{0,12},{4,0},{8,4},{12,8},{1,13},{5,1},{9,5},{13,9},{2,14},{6,2},{... | collective-permute-start | bytes 2359304 | tf_op jit(solution)/shard_map/ppermute | solution.py:62
  54.2 3.3 %collective-permute-start = (bf16[2,384,512]{2,1,0:T(8,128)(2,1)}, bf16[2,384,512]{2,1,0:T(8,128)(2,1)}, u32[]{:S(2)}, u32[]{:S(2)}) collective-permute-start(bf16[2,384,512]{2,1,0:T(8,128)(2,1)} %get-tuple-element.12), channel_id=1, source_target_pairs={{0,4},{4,8},{8,12},{12,0},{1,5},{5,9},{9,13},{13,1},{2,6},{6,10},{... | collective-permute-start | bytes 2359304 | tf_op jit(solution)/shard_map/ppermute | solution.py:62
  57.5 1.9 %collective-permute-start.1 = (bf16[2,384,512]{2,1,0:T(8,128)(2,1)}, bf16[2,384,512]{2,1,0:T(8,128)(2,1)}, u32[]{:S(2)}, u32[]{:S(2)}) collective-permute-start(bf16[2,384,512]{2,1,0:T(8,128)(2,1)} %get-tuple-element.11), channel_id=1, source_target_pairs={{0,4},{4,8},{8,12},{12,0},{1,5},{5,9},{9,13},{13,1},{2,6},{6,10},{... | collective-permute-start | bytes 2359304 | tf_op jit(solution)/shard_map/ppermute | solution.py:62
  59.4 5.1 %collective-permute-start.3 = (bf16[2,384,512]{2,1,0:T(8,128)(2,1)}, bf16[2,384,512]{2,1,0:T(8,128)(2,1)}, u32[]{:S(2)}, u32[]{:S(2)}) collective-permute-start(bf16[2,384,512]{2,1,0:T(8,128)(2,1)} %get-tuple-element.12), channel_id=1, source_target_pairs={{0,12},{4,0},{8,4},{12,8},{1,13},{5,1},{9,5},{13,9},{2,14},{6,2},{... | collective-permute-start | bytes 2359304 | tf_op jit(solution)/shard_map/ppermute | solution.py:62
  64.6 1.2 collective-permute-done.2.refs_3_
  65.7 3.8 %collective-permute-start.5 = (bf16[2,384,512]{2,1,0:T(8,128)(2,1)S(1)}, bf16[2,384,512]{2,1,0:T(8,128)(2,1)}, u32[]{:S(2)}, u32[]{:S(2)}) collective-permute-start(bf16[2,384,512]{2,1,0:T(8,128)(2,1)S(1)} %collective-permute-done.2.refs_3_), channel_id=1, source_target_pairs={{0,12},{4,0},{8,4},{12,8},{1,13},{5,1},{9,5},{13,9},{2,14},{6,2},{... | collective-permute-start | bytes 2359304 | tf_op jit(solution)/shard_map/ppermute | solution.py:62
  69.5 0.1 collective-permute-done.refs_1_
  69.6 2.0 %collective-permute-start.4 = (bf16[2,384,512]{2,1,0:T(8,128)(2,1)}, bf16[2,384,512]{2,1,0:T(8,128)(2,1)}, u32[]{:S(2)}, u32[]{:S(2)}) collective-permute-start(bf16[2,384,512]{2,1,0:T(8,128)(2,1)} %collective-permute-done.refs_1_), channel_id=1, source_target_pairs={{0,4},{4,8},{8,12},{12,0},{1,5},{5,9},{9,13},{13,1},{2,6},{6,10},{... | collective-permute-start | bytes 2359304 | tf_op jit(solution)/shard_map/ppermute | solution.py:62
  71.7 0.2 copy.11
  71.9 0.2 fusion.3
  72.2 5.8 %collective-permute-done.1.refs_2_ = bf16[2,384,512]{2,1,0:T(8,128)(2,1)} collective-permute-done((bf16[2,384,512]{2,1,0:T(8,128)(2,1)}, bf16[2,384,512]{2,1,0:T(8,128)(2,1)}, u32[]{:S(2)}, u32[]{:S(2)}) %collective-permute-start.1) | collective-permute-done | bytes 786464 | tf_op jit(solution)/shard_map/ppermute | solution.py:62
  78.1 0.0 collective-permute-done.3.refs_4_
  78.1 4.6 %collective-permute-done.5.refs_6_ = bf16[2,384,512]{2,1,0:T(8,128)(2,1)} collective-permute-done((bf16[2,384,512]{2,1,0:T(8,128)(2,1)S(1)}, bf16[2,384,512]{2,1,0:T(8,128)(2,1)}, u32[]{:S(2)}, u32[]{:S(2)}) %collective-permute-start.5) | collective-permute-done | bytes 786464 | tf_op jit(solution)/shard_map/ppermute | solution.py:62
  82.7 3.8 %collective-permute-done.4.refs_5_ = bf16[2,384,512]{2,1,0:T(8,128)(2,1)} collective-permute-done((bf16[2,384,512]{2,1,0:T(8,128)(2,1)}, bf16[2,384,512]{2,1,0:T(8,128)(2,1)}, u32[]{:S(2)}, u32[]{:S(2)}) %collective-permute-start.4) | collective-permute-done | bytes 786464 | tf_op jit(solution)/shard_map/ppermute | solution.py:62
  86.5 7.5 %all-gather.3.cloned.1.call-done = bf16[16896,256]{1,0:T(8,128)(2,1)} async-done(((bf16[528,256]{1,0:T(8,128)(2,1)}), bf16[16896,256]{1,0:T(8,128)(2,1)}) %all-gather.3.cloned.1.call-update) | async-done | bytes 8650768 | tf_op jit(solution)/shard_map/all_gather | solution.py:244
  94.0 8.5 %shard_map.85 = bf16[384,5120]{1,0:T(8,128)(2,1)S(1)} custom-call(bf16[4,4,2,528,256]{4,3,2,1,0:T(8,128)(2,1)} %bitcast.14, bf16[4,384,512]{2,1,0:T(8,128)(2,1)S(1)} %all_to_all.21.refs_0_, bf16[2,384,512]{2,1,0:T(8,128)(2,1)} %collective-permute-done.refs_1_, bf16[2,384,512]{2,1,0:T(8,128)(2,1)} %collective-permute-done.1.refs_2_, ...), custom_call_target="tpu_custom_call" | custom-call | flops 3221225472 | bytes 16777216 | tf_op jit(solution)/shard_map/pallas_call | solution.py:260
  102.5 0.0 copy-start.1
  102.5 0.0 copy-start.2
  102.5 29.0 %all_to_all.22.recv_ref = bf16[4,96,5120]{2,1,0:T(8,128)(2,1)S(1)} all-to-all(bf16[4,96,5120]{2,1,0:T(8,128)(2,1)S(1)} %bitcast.9), channel_id=1, replica_groups={{0,1,2,3},{4,5,6,7},{8,9,10,11},{12,13,14,15},{16,20,24,28},{17,21,25,2..., dimensions={0} | all-to-all | bytes 7864320 | tf_op jit(solution)/shard_map/all_to_all | solution.py:53
  131.5 0.5 shard_map.86
  131.9 14.6 %all_to_all.23.recv_ref = bf16[4,24,5120]{2,1,0:T(8,128)(2,1)S(1)} all-to-all(bf16[4,24,5120]{2,1,0:T(8,128)(2,1)S(1)} %bitcast.11), channel_id=1, replica_groups={{0,4,8,12},{1,5,9,13},{2,6,10,14},{3,7,11,15},{16,17,18,19},{20,21,22,2..., dimensions={0} | all-to-all | bytes 1966080 | tf_op jit(solution)/shard_map/all_to_all | solution.py:53
  146.6 1.0 shard_map.87
  (7 shorter events, 0.1 us)
Async XLA Ops:
  6.5 87.5 %all-gather.3.cloned.1.call-start = ((), (), s32[]{:S(2)}) async-start(), calls=%async_computation.4 | async-start | bytes 8921088 | tf_op jit(solution)/shard_map/all_gather | solution.py:244
  9.0 1.2 copy-start
  10.2 0.7 copy-start.3
  32.7 39.0 %copy-start.4 = (bf16[384,320]{0,1:T(8,128)(2,1)S(1)}, bf16[384,320]{0,1:T(8,128)(2,1)}, u32[]{:S(2)}) copy-start(bf16[384,320]{0,1:T(8,128)(2,1)} %param.11) | copy-start | bytes 737284
  51.7 14.1 %collective-permute-start.2 = (bf16[2,384,512]{2,1,0:T(8,128)(2,1)}, bf16[2,384,512]{2,1,0:T(8,128)(2,1)S(1)}, u32[]{:S(2)}, u32[]{:S(2)}) collective-permute-start(bf16[2,384,512]{2,1,0:T(8,128)(2,1)} %get-tuple-element.11), channel_id=1, source_target_pairs={{0,12},{4,0},{8,4},{12,8},{1,13},{5,1},{9,5},{13,9},{2,14},{6,2},{... | collective-permute-start | bytes 2359304 | tf_op jit(solution)/shard_map/ppermute | solution.py:62
  54.2 15.4 %collective-permute-start = (bf16[2,384,512]{2,1,0:T(8,128)(2,1)}, bf16[2,384,512]{2,1,0:T(8,128)(2,1)}, u32[]{:S(2)}, u32[]{:S(2)}) collective-permute-start(bf16[2,384,512]{2,1,0:T(8,128)(2,1)} %get-tuple-element.12), channel_id=1, source_target_pairs={{0,4},{4,8},{8,12},{12,0},{1,5},{5,9},{9,13},{13,1},{2,6},{6,10},{... | collective-permute-start | bytes 2359304 | tf_op jit(solution)/shard_map/ppermute | solution.py:62
  57.5 20.6 %collective-permute-start.1 = (bf16[2,384,512]{2,1,0:T(8,128)(2,1)}, bf16[2,384,512]{2,1,0:T(8,128)(2,1)}, u32[]{:S(2)}, u32[]{:S(2)}) collective-permute-start(bf16[2,384,512]{2,1,0:T(8,128)(2,1)} %get-tuple-element.11), channel_id=1, source_target_pairs={{0,4},{4,8},{8,12},{12,0},{1,5},{5,9},{9,13},{13,1},{2,6},{6,10},{... | collective-permute-start | bytes 2359304 | tf_op jit(solution)/shard_map/ppermute | solution.py:62
  59.4 18.6 %collective-permute-start.3 = (bf16[2,384,512]{2,1,0:T(8,128)(2,1)}, bf16[2,384,512]{2,1,0:T(8,128)(2,1)}, u32[]{:S(2)}, u32[]{:S(2)}) collective-permute-start(bf16[2,384,512]{2,1,0:T(8,128)(2,1)} %get-tuple-element.12), channel_id=1, source_target_pairs={{0,12},{4,0},{8,4},{12,8},{1,13},{5,1},{9,5},{13,9},{2,14},{6,2},{... | collective-permute-start | bytes 2359304 | tf_op jit(solution)/shard_map/ppermute | solution.py:62
  65.7 17.0 %collective-permute-start.5 = (bf16[2,384,512]{2,1,0:T(8,128)(2,1)S(1)}, bf16[2,384,512]{2,1,0:T(8,128)(2,1)}, u32[]{:S(2)}, u32[]{:S(2)}) collective-permute-start(bf16[2,384,512]{2,1,0:T(8,128)(2,1)S(1)} %collective-permute-done.2.refs_3_), channel_id=1, source_target_pairs={{0,12},{4,0},{8,4},{12,8},{1,13},{5,1},{9,5},{13,9},{2,14},{6,2},{... | collective-permute-start | bytes 2359304 | tf_op jit(solution)/shard_map/ppermute | solution.py:62
  69.6 16.9 %collective-permute-start.4 = (bf16[2,384,512]{2,1,0:T(8,128)(2,1)}, bf16[2,384,512]{2,1,0:T(8,128)(2,1)}, u32[]{:S(2)}, u32[]{:S(2)}) collective-permute-start(bf16[2,384,512]{2,1,0:T(8,128)(2,1)} %collective-permute-done.refs_1_), channel_id=1, source_target_pairs={{0,4},{4,8},{8,12},{12,0},{1,5},{5,9},{9,13},{13,1},{2,6},{6,10},{... | collective-permute-start | bytes 2359304 | tf_op jit(solution)/shard_map/ppermute | solution.py:62
  102.5 29.0 %copy-start.1 = (bf16[24,5120]{1,0:T(8,128)(2,1)S(1)}, bf16[24,5120]{1,0:T(8,128)(2,1)}, u32[]{:S(2)}) copy-start(bf16[24,5120]{1,0:T(8,128)(2,1)} %patches_ref.1) | copy-start | bytes 737284
  102.5 29.0 %copy-start.2 = (f32[1280]{0:T(1024)S(1)}, f32[1280]{0:T(1024)}, u32[]{:S(2)}) copy-start(f32[1280]{0:T(1024)} %gain_ref.1) | copy-start | bytes 15364
Sparse Core Ops, SparseCore 0:
  9.5 84.4 all-gather.2
